TPU v7x, 32 devices: a whole 2x2x4 slice. The times are simulated.
32 devices in a mesh: inline: 16 (over z, y, core), shot: 2 (over x).
Axes of the slice: x: 2, y: 2, z: 4, core: 2. Of those that a mesh axis runs over, the one named last changes fastest.
Arguments:
- source: bfloat16 [8, 512, 32, 256], P('shot', 'inline'), may hold values from -6 to 6
- receiver: bfloat16 [8, 512, 32, 256], P('shot', 'inline'), may hold values from -6 to 6
Outputs:
- offset_image: float32 [129, 512, 256], P(None, 'inline', 'shot')
All inputs are finite; a program needn't handle non-finite values.
Results may differ from a plain program's by a relative error of at most 0.0003.
Values may be sent and summed in bfloat16 or wider, within the bound.
No kernel may reach another device: no remote copies, remote signals or barrier semaphores. Data moves between devices by JAX's collectives and lax.ppermute only.
A program may use at most 192 MiB of HBM per device.

v0:
```python
import jax
import jax.numpy as jnp
from jax import lax
from jax.sharding import PartitionSpec as P


def shifted(value, axis, steps):
    count = lax.axis_size(axis)
    initial, last = (max(0, -steps), min(count, count - steps))
    return lax.ppermute(value, axis, [(source, source + steps) for source in range(initial, last)])


def band_rows(product, width, lags):
    rows = product.shape[0]
    cross = product.shape[2]
    flat = product.reshape(rows * width, cross)
    flat = jnp.pad(flat, ((0, rows), (0, 0)))
    skewed = flat.reshape(rows, width + 1, cross)[:, :lags, :]
    return jnp.transpose(skewed, (1, 0, 2))


def direct_shift(slab, offset):
    return shifted(slab, "inline", offset)


def extend(receiver):
    near_left = direct_shift(receiver, 1)
    far_left = direct_shift(receiver, 2)
    near_right = direct_shift(receiver, -1)
    far_right = direct_shift(receiver, -2)
    return jnp.concatenate((far_left, near_left, receiver, near_right, far_right), axis=1)


def correlate(source, receiver):
    cells = source.shape[1]
    lag_half = 2 * cells
    extended = extend(receiver)
    width = cells + 2 * lag_half
    product = jnp.einsum("sity,szty->izy", source, extended, preferred_element_type=jnp.float32)
    return band_rows(product, width, 2 * lag_half + 1)


def on_device(source, receiver):
    times = source.shape[2]
    moved_source, moved_receiver = (
        lax.all_to_all(source, "shot", split_axis=3, concat_axis=0, tiled=True),
        lax.all_to_all(receiver, "shot", split_axis=3, concat_axis=0, tiled=True),
    )
    all_shots = moved_source.shape[0]
    summed = correlate(moved_source, moved_receiver)
    return summed * (1.0 / (times * all_shots) ** 0.5)


def solution(mesh):
    placed = (P("shot", "inline", None, None), P("shot", "inline", None, None))
    return jax.shard_map(
        on_device, mesh=mesh, in_specs=placed, out_specs=P(None, "inline", "shot"), check_vma=False
    )
```

profile of v0, /device:TPU:0, one launch (start us, length us, event | category | flops | bytes accessed | tf_op | source)
XLA Modules:
  0.0 333.8 jit_solution(14233737789096519494)
XLA Ops:
  0.0 12.5 %copy.9 = bf16[4,32,32,256]{2,1,0,3:T(8,128)(2,1)} copy(bf16[4,32,32,256]{3,2,1,0:T(8,128)(2,1)} %param.3) | data formatting | bytes 4194304 | tf_op args[1]
  12.5 10.2 %reshape.11 = bf16[2,2,262144]{2,1,0:T(2,128)(2,1)S(1)} reshape(bf16[256,4,32,32]{3,2,1,0:T(8,128)(2,1)} %bitcast.25) | data formatting | bytes 4194304
  22.7 29.7 %all_to_all.36 = bf16[2,2,262144]{2,1,0:T(2,128)(2,1)} all-to-all(bf16[2,2,262144]{2,1,0:T(2,128)(2,1)S(1)} %reshape.11), channel_id=1, replica_groups=mesh['inline'=16,'shot'=2] {'shot'}, dimensions={0} | all-to-all | bytes 4194304 | tf_op jit(solution)/shard_map/all_to_all | solution.py:47
  52.4 7.6 %reshape.12 = bf16[256,4,32,32]{3,2,1,0:T(8,128)(2,1)} reshape(bf16[2,2,262144]{2,1,0:T(2,128)(2,1)} %all_to_all.36) | data formatting | bytes 4194304
  60.0 12.0 %copy.10 = bf16[4,32,32,2,128]{1,2,0,3,4:T(8,128)(2,1)} copy(bf16[4,32,32,2,128]{2,1,0,4,3:T(8,128)(2,1)} %bitcast.27) | data formatting | bytes 4194304 | tf_op jit(solution)/shard_map/all_to_all | solution.py:47
  72.0 0.0 copy-start
  72.0 13.4 %copy.11 = bf16[8,32,32,128]{3,2,1,0:T(8,128)(2,1)} copy(bf16[8,32,32,128]{1,2,0,3:T(8,128)(2,1)} %bitcast.22) | data formatting | bytes 4194304 | tf_op jit(solution)/shard_map/all_to_all | solution.py:47
  85.4 5.1 %collective-permute-start = (bf16[8,32,32,128]{3,2,1,0:T(8,128)(2,1)}, bf16[8,32,32,128]{3,2,1,0:T(8,128)(2,1)}, u32[]{:S(2)}, u32[]{:S(2)}) collective-permute-start(bf16[8,32,32,128]{3,2,1,0:T(8,128)(2,1)} %copy.11), channel_id=1, source_target_pairs={{0,4},{2,6},{4,8},{6,10},{8,12},{10,14},{12,16},{14,18},{16,20},{1... | collective-permute-start | bytes 6291464 | tf_op jit(solution)/shard_map/ppermute | solution.py:10
  90.5 2.6 collective-permute-start.1
  93.1 1.3 collective-permute-start.2
  94.4 1.5 collective-permute-start.3
  95.9 0.0 copy-done
  95.9 12.0 %copy.19 = bf16[4,32,32,256]{2,1,0,3:T(8,128)(2,1)} copy(bf16[4,32,32,256]{3,2,1,0:T(8,128)(2,1)S(1)} %copy-done) | data formatting | bytes 4194304 | tf_op args[0]
  107.9 10.2 %reshape.9 = bf16[2,2,262144]{2,1,0:T(2,128)(2,1)S(1)} reshape(bf16[256,4,32,32]{3,2,1,0:T(8,128)(2,1)} %bitcast.26) | data formatting | bytes 4194304
  118.1 29.6 %all_to_all.37 = bf16[2,2,262144]{2,1,0:T(2,128)(2,1)} all-to-all(bf16[2,2,262144]{2,1,0:T(2,128)(2,1)S(1)} %reshape.9), channel_id=1, replica_groups=mesh['inline'=16,'shot'=2] {'shot'}, dimensions={0} | all-to-all | bytes 4194304 | tf_op jit(solution)/shard_map/all_to_all | solution.py:46
  147.6 7.6 %reshape.10 = bf16[256,4,32,32]{3,2,1,0:T(8,128)(2,1)} reshape(bf16[2,2,262144]{2,1,0:T(2,128)(2,1)} %all_to_all.37) | data formatting | bytes 4194304
  155.2 10.3 %copy.20 = bf16[4,32,32,2,128]{2,1,0,3,4:T(8,128)(2,1)} copy(bf16[4,32,32,2,128]{2,1,0,4,3:T(8,128)(2,1)} %bitcast.28) | data formatting | bytes 4194304 | tf_op jit(solution)/shard_map/all_to_all | solution.py:46
  165.6 37.4 %collective-permute-done = bf16[8,32,32,128]{3,2,1,0:T(8,128)(2,1)} collective-permute-done((bf16[8,32,32,128]{3,2,1,0:T(8,128)(2,1)}, bf16[8,32,32,128]{3,2,1,0:T(8,128)(2,1)}, u32[]{:S(2)}, u32[]{:S(2)}) %collective-permute-start) | collective-permute-done | bytes 2097184 | tf_op jit(solution)/shard_map/ppermute | solution.py:10
  203.0 15.3 %copy.15 = bf16[8,32,32,128]{1,2,0,3:T(8,128)(2,1)} copy(bf16[8,32,32,128]{3,2,1,0:T(8,128)(2,1)} %collective-permute-done) | data formatting | bytes 4194304 | tf_op jit(solution)/shard_map/ppermute | solution.py:10
  218.3 0.0 collective-permute-done.1
  218.3 15.2 %copy.16 = bf16[8,32,32,128]{1,2,0,3:T(8,128)(2,1)} copy(bf16[8,32,32,128]{3,2,1,0:T(8,128)(2,1)} %collective-permute-done.1) | data formatting | bytes 4194304 | tf_op jit(solution)/shard_map/ppermute | solution.py:10
  233.5 0.0 collective-permute-done.2
  233.5 15.3 %copy.17 = bf16[8,32,32,128]{1,2,0,3:T(8,128)(2,1)} copy(bf16[8,32,32,128]{3,2,1,0:T(8,128)(2,1)} %collective-permute-done.2) | data formatting | bytes 4194304 | tf_op jit(solution)/shard_map/ppermute | solution.py:10
  248.8 0.0 collective-permute-done.3
  248.8 15.2 %copy.18 = bf16[8,32,32,128]{1,2,0,3:T(8,128)(2,1)} copy(bf16[8,32,32,128]{3,2,1,0:T(8,128)(2,1)} %collective-permute-done.3) | data formatting | bytes 4194304 | tf_op jit(solution)/shard_map/ppermute | solution.py:10
  264.0 44.4 %concatenate.3 = bf16[8,160,32,128]{1,2,0,3:T(8,128)(2,1)} concatenate(bf16[8,32,32,128]{1,2,0,3:T(8,128)(2,1)} %copy.15, bf16[8,32,32,128]{1,2,0,3:T(8,128)(2,1)} %copy.16, bf16[8,32,32,128]{1,2,0,3:T(8,128)(2,1)} %bitcast.23, bf16[8,32,32,128]{1,2,0,3:T(8,128)(2,1)} %copy.17, bf16[8,32,32,128]{1,2,0,3:T(8,128)(2,1)} %copy.18), dimensions={1} | concatenate | bytes 20971520 | tf_op jit(solution)/shard_map/concatenate | solution.py:31
  308.4 13.4 %convolution_bitcast_fusion = f32[32,160,128]{1,0,2:T(8,128)} fusion(bf16[8,32,32,128]{2,1,0,3:T(8,128)(2,1)} %bitcast.24, bf16[8,160,32,128]{1,2,0,3:T(8,128)(2,1)} %concatenate.3), kind=kOutput, calls=%fused_computation.2 | convolution fusion | flops 335544320 | bytes 15204352 | tf_op jit(solution)/shard_map/sity,szty->izy/dot_general | solution.py:39
  321.9 4.9 %copy.21 = f32[32,160,128]{2,1,0:T(8,128)} copy(f32[32,160,128]{1,0,2:T(8,128)} %convolution_bitcast_fusion) | data formatting | bytes 5242880 | tf_op jit(solution)/shard_map/sity,szty->izy/transpose | solution.py:39
  326.8 1.9 pad.4
  328.7 1.7 reshape.7
  330.4 1.8 fusion
  332.1 1.7 copy.22
Async XLA Ops:
  72.0 23.9 %copy-start = (bf16[4,32,32,256]{3,2,1,0:T(8,128)(2,1)S(1)}, bf16[4,32,32,256]{3,2,1,0:T(8,128)(2,1)}, u32[]{:S(2)}) copy-start(bf16[4,32,32,256]{3,2,1,0:T(8,128)(2,1)} %param.2) | copy-start | bytes 6291460
  85.4 117.6 %collective-permute-start = (bf16[8,32,32,128]{3,2,1,0:T(8,128)(2,1)}, bf16[8,32,32,128]{3,2,1,0:T(8,128)(2,1)}, u32[]{:S(2)}, u32[]{:S(2)}) collective-permute-start(bf16[8,32,32,128]{3,2,1,0:T(8,128)(2,1)} %copy.11), channel_id=1, source_target_pairs={{0,4},{2,6},{4,8},{6,10},{8,12},{10,14},{12,16},{14,18},{16,20},{1... | collective-permute-start | bytes 6291464 | tf_op jit(solution)/shard_map/ppermute | solution.py:10
  90.5 127.8 %collective-permute-start.1 = (bf16[8,32,32,128]{3,2,1,0:T(8,128)(2,1)}, bf16[8,32,32,128]{3,2,1,0:T(8,128)(2,1)}, u32[]{:S(2)}, u32[]{:S(2)}) collective-permute-start(bf16[8,32,32,128]{3,2,1,0:T(8,128)(2,1)} %copy.11), channel_id=1, source_target_pairs={{0,2},{2,4},{4,6},{6,8},{8,10},{10,12},{12,14},{14,16},{16,18},{18... | collective-permute-start | bytes 6291464 | tf_op jit(solution)/shard_map/ppermute | solution.py:10
  93.1 140.4 %collective-permute-start.2 = (bf16[8,32,32,128]{3,2,1,0:T(8,128)(2,1)}, bf16[8,32,32,128]{3,2,1,0:T(8,128)(2,1)}, u32[]{:S(2)}, u32[]{:S(2)}) collective-permute-start(bf16[8,32,32,128]{3,2,1,0:T(8,128)(2,1)} %copy.11), channel_id=1, source_target_pairs={{2,0},{4,2},{6,4},{8,6},{10,8},{12,10},{14,12},{16,14},{18,16},{20... | collective-permute-start | bytes 6291464 | tf_op jit(solution)/shard_map/ppermute | solution.py:10
  94.4 154.3 %collective-permute-start.3 = (bf16[8,32,32,128]{3,2,1,0:T(8,128)(2,1)}, bf16[8,32,32,128]{3,2,1,0:T(8,128)(2,1)}, u32[]{:S(2)}, u32[]{:S(2)}) collective-permute-start(bf16[8,32,32,128]{3,2,1,0:T(8,128)(2,1)} %copy.11), channel_id=1, source_target_pairs={{4,0},{6,2},{8,4},{10,6},{12,8},{14,10},{16,12},{18,14},{20,16},{2... | collective-permute-start | bytes 6291464 | tf_op jit(solution)/shard_map/ppermute | solution.py:10
where the time goes:
time: 341 us; the launch traced here: 334 us
  local copies, waits for them, and re-layouts  211 us (62%)
  blocking collectives  59.2 us (17%)
  waiting for transfers between devices  37.4 us (11%)
  matrix products  13.4 us (4%)
  starting transfers between devices  10.4 us (3%)
    ppermute x4, local copies, waits for them, and re-layouts, shifted(): lax.ppermute(value, axis, [(source, source + steps) for source in range(i...  61 us
    unnamed x8, local copies, waits for them, and re-layouts  60.1 us
    concatenate x1, local copies, waits for them, and re-layouts, extend(): jnp.concatenate((far_left, near_left, receiver, near_right, far_right), a...  44.4 us
    ppermute x4, waiting for transfers between devices, shifted(): lax.ppermute(value, axis, [(source, source + steps) for source in range(i...  37.4 us
    all_to_all x1, blocking collectives, on_device(): lax.all_to_all(receiver, 'shot', split_axis=3, concat_axis=0, tiled=True)  29.7 us
    all_to_all x1, blocking collectives, on_device(): lax.all_to_all(source, 'shot', split_axis=3, concat_axis=0, tiled=True)  29.6 us
    all_to_all x2, local copies, waits for them, and re-layouts, on_device(): lax.all_to_all(receiver, 'shot', split_axis=3, concat_axis=0, tiled=True)  25.4 us
    dot_general x1, matrix products, correlate(): jnp.einsum('sity,szty->izy', source, extended, preferred_element_type=jnp...  13.4 us
  transfers between devices with their start and end apart: 4, of which 1 were waited for; matrix products, arithmetic and copies ran while one was open for 26% of the time, Pallas kernels for 0%

commit v1 on v0

v1 whole, which is shorter than its diff:
```python
import functools

import jax
import jax.numpy as jnp
from jax import lax
from jax.experimental import pallas as pl
from jax.experimental.pallas import tpu as pltpu
from jax.sharding import PartitionSpec as P

LANES = 128
ROWS = 16
VMEM_BYTES = 48 * 1024 * 1024


def shifted(value, axis, steps):
    count = lax.axis_size(axis)
    initial, last = (max(0, -steps), min(count, count - steps))
    return lax.ppermute(value, axis, [(source, source + steps) for source in range(initial, last)])


def band_rows(product, width, lags):
    rows = product.shape[0]
    cross = product.shape[2]
    flat = product.reshape(rows * width, cross)
    flat = jnp.pad(flat, ((0, rows), (0, 0)))
    skewed = flat.reshape(rows, width + 1, cross)[:, :lags, :]
    return jnp.transpose(skewed, (1, 0, 2))


def plain(source, receiver, scale):
    source, receiver = (
        lax.all_to_all(value, "shot", split_axis=3, concat_axis=0, tiled=True) for value in (source, receiver)
    )
    cells = source.shape[1]
    slabs = [receiver if step == 0 else shifted(receiver, "inline", -step) for step in (-2, -1, 0, 1, 2)]
    width = 5 * cells
    product = jnp.einsum(
        "sity,szty->izy", source, jnp.concatenate(slabs, axis=1), preferred_element_type=jnp.float32
    )
    return band_rows(product, width, 4 * cells + 1) * scale


def turn_body(half_ref, raw_ref, turned_ref, rows_ref):
    shots, cells, times, cross = raw_ref.shape
    for cell in range(cells):
        tile = raw_ref[:, cell].reshape(shots * times, cross).astype(jnp.float32)
        rows_ref[pl.ds(cell, cross, stride=cells), :] = tile.T
    turned_ref[...] = rows_ref[...].reshape(turned_ref.shape).astype(turned_ref.dtype)


def turn(raw, half):
    shots, cells, times, _ = raw.shape
    depth = shots * times
    return pl.pallas_call(
        turn_body,
        grid_spec=pltpu.PrefetchScalarGridSpec(
            num_scalar_prefetch=1,
            grid=(cells // ROWS,),
            in_specs=[pl.BlockSpec((shots, ROWS, times, LANES), lambda step, half: (0, step, 0, half[0]))],
            out_specs=pl.BlockSpec((LANES, ROWS, depth), lambda step, half: (0, step, 0)),
            scratch_shapes=[pltpu.VMEM((LANES * ROWS, depth), jnp.float32)],
        ),
        out_shape=jax.ShapeDtypeStruct((LANES, cells, depth), raw.dtype),
        compiler_params=pltpu.CompilerParams(vmem_limit_bytes=VMEM_BYTES),
        cost_estimate=pl.CostEstimate(flops=0, bytes_accessed=raw.size * 2, transcendentals=0),
        name="turn",
    )(half, raw)


def image_body(scale, cells, where_ref, *refs):
    sources, slots, image_ref = (refs[:2], [refs[2 + 2 * j : 4 + 2 * j] for j in range(5)], refs[12])
    wide_ref, narrow_ref, skewed_ref, sem = refs[13:]
    block = sources[0].shape[0]
    step = pl.program_id(0)

    def rows_of(pair, cross):
        return jnp.concatenate([part[cross] for part in pair], axis=1)

    dims = (((1,), (1,)), ((), ()))
    for cross in range(block):
        left = rows_of(sources, cross)
        right = [rows_of(pair, cross) for pair in slots]
        place = pl.ds(pl.multiple_of((step * block + cross) * cells, cells), cells)
        wide_ref[place, :] = lax.dot_general(
            left, jnp.concatenate(right[:4], axis=0), dims, preferred_element_type=jnp.float32
        )
        narrow_ref[place, :cells] = lax.dot_general(left, right[4], dims, preferred_element_type=jnp.float32)

    @pl.when(step == pl.num_programs(0) - 1)
    def _():
        for cell in range(cells):
            every = pl.ds(cell, LANES, stride=cells)
            turned = [wide_ref[every, :].T, narrow_ref[every, :].T[:cells]]
            pieces = [turned[0][cells * j : cells * (j + 1)] for j in range(4)] + [turned[1]]
            for j, piece in enumerate(pieces):
                lag = (where_ref[j] + 3) * cells - cell
                skewed_ref[pl.ds(lag * cells + cell, cells, stride=cells), :] = piece * scale
        copy = pltpu.make_async_copy(
            skewed_ref.at[pl.ds(cells * cells, image_ref.shape[0])], image_ref, sem
        )
        copy.start()
        copy.wait()


def image(scale, where, sources, slots):
    _, cells, depth = sources[0].shape
    lags = 4 * cells + 1
    block = 16
    spec = pl.BlockSpec((block, cells, depth), lambda step, where: (step, 0, 0))
    flat = [part for pair in (sources, *slots) for part in pair]
    return pl.pallas_call(
        functools.partial(image_body, scale, cells),
        grid_spec=pltpu.PrefetchScalarGridSpec(
            num_scalar_prefetch=1,
            grid=(LANES // block,),
            in_specs=[spec] * len(flat),
            out_specs=pl.BlockSpec(memory_space=pl.ANY),
            scratch_shapes=[
                pltpu.VMEM((LANES * cells, 4 * cells), jnp.float32),
                pltpu.VMEM((LANES * cells, LANES), jnp.float32),
                pltpu.VMEM(((lags + 2 * cells) * cells, LANES), jnp.float32),
                pltpu.SemaphoreType.DMA(()),
            ],
        ),
        out_shape=jax.ShapeDtypeStruct((lags * cells, LANES), jnp.float32),
        compiler_params=pltpu.CompilerParams(vmem_limit_bytes=VMEM_BYTES),
        name="image",
    )(where, *flat).reshape(lags, cells, LANES)


def routed(source, receiver, scale):
    count = lax.axis_size("inline")
    own = lax.axis_index("inline")
    core, odd = own % 2, own // 2 % 2
    half = lax.axis_index("shot")

    def across(value):
        return lax.ppermute(value, "shot", [(0, 1), (1, 0)])

    def along_y(value):
        return lax.ppermute(value, "inline", [(index, index ^ 2) for index in range(count)])

    def along_z(value):
        pairs = [(index, index + (4 if index // 2 % 2 == 0 else -4)) for index in range(count)]
        return lax.ppermute(value, "inline", [pair for pair in pairs if 0 <= pair[1] < count])

    def to_core(value):
        return lax.ppermute(value, "inline", [(index, index ^ 1) for index in range(count)])

    here, there = (jnp.full((1,), index, jnp.int32) for index in (half, 1 - half))
    sent = turn(receiver, there)
    kept = turn(receiver, here)
    slots = []
    for part in (kept, across(sent)):
        from_y = along_y(part)
        from_z = along_z(from_y)
        twin = to_core(part)
        shared = jnp.where(core == odd, to_core(from_z), to_core(from_y))
        slots.append((from_y, from_z, part, twin, shared))
    sources = (turn(source, here), across(turn(source, there)))
    where = jnp.stack([2 - 4 * odd, 4 * odd - 2, 0 * odd, 1 - 2 * core, 2 * core - 1]).astype(jnp.int32)
    return image(scale, where, sources, list(zip(*slots)))


def on_device(source, receiver):
    shots, cells, times, cross = source.shape
    groups, count = lax.axis_size("shot"), lax.axis_size("inline")
    scale = 1.0 / (times * shots * groups) ** 0.5
    fits = (
        groups == 2
        and count % 4 == 0
        and cross == 2 * LANES
        and shots * times == LANES
        and 4 * cells == LANES
        and times % ROWS == 0
    )
    return routed(source, receiver, scale) if fits else plain(source, receiver, scale)


def solution(mesh):
    placed = (P("shot", "inline", None, None), P("shot", "inline", None, None))
    return jax.shard_map(
        on_device, mesh=mesh, in_specs=placed, out_specs=P(None, "inline", "shot"), check_vma=False
    )
```

time: 341 us -> 122 us (0.36); the launches traced: 334 us -> 121 us
  local copies, waits for them, and re-layouts: 211 us -> 5.01 us
  blocking collectives: 59.2 us -> 0 us
  waiting for transfers between devices: 37.4 us -> 75.6 us
  Pallas kernels: 0 us -> 19.8 us
  matrix products: 13.4 us -> 0 us
  starting transfers between devices: 10.4 us -> 16.1 us
    ppermute x4 -> x0, local copies, waits for them, and re-layouts: 61 us -> none  [shifted(): lax.ppermute(value, axis, [(source, source + steps) for source in range(i...]
    all_to_all x2 -> x0, blocking collectives: 59.2 us -> none  [the longest x1 29.7 us: on_device(): lax.all_to_all(receiver, 'shot', split_axis=3, concat_axis=0, tiled=True)]
    unnamed x8 -> x22, local copies, waits for them, and re-layouts: 60.1 us -> 4.93 us
    concatenate x1 -> x0, local copies, waits for them, and re-layouts: 44.4 us -> none  [extend(): jnp.concatenate((far_left, near_left, receiver, near_right, far_right), a...]
    ppermute x4 -> x12, waiting for transfers between devices: 37.4 us -> 75.6 us  [the longest x2 37 us: across(): return lax.ppermute(value, 'shot', [(0, 1), (1, 0)])]
    all_to_all x3 -> x0, local copies, waits for them, and re-layouts: 35.7 us -> none  [the longest x2 25.4 us: on_device(): lax.all_to_all(receiver, 'shot', split_axis=3, concat_axis=0, tiled=True)]
    pallas_call x0 -> x5, Pallas kernels: none -> 19.8 us  [the longest x1 14.6 us: image(): pl.pallas_call(functools.partial(image_body, scale, cells), grid_spec=plt...]
    dot_general x1 -> x0, matrix products: 13.4 us -> none  [correlate(): jnp.einsum('sity,szty->izy', source, extended, preferred_element_type=jnp...]
  transfers between devices with their start and end apart: 4 -> 12, of which waited for: 1 -> 5; matrix products, arithmetic and copies ran while one was open for 26% -> 4% of each run, Pallas kernels for 0% -> 3%
where the time goes in v1:
time: 122 us; the launch traced here: 121 us
  waiting for transfers between devices  75.6 us (62%)
  Pallas kernels  19.8 us (16%)
  starting transfers between devices  16.1 us (13%)
  local copies, waits for them, and re-layouts  5.01 us (4%)
  other arithmetic  4.85 us (4%)
    ppermute x2, waiting for transfers between devices, across(): return lax.ppermute(value, 'shot', [(0, 1), (1, 0)])  37 us
    ppermute x2, waiting for transfers between devices, along_y(): lax.ppermute(value, 'inline', [(index, index ^ 2) for index in range(coun...  19.7 us
    ppermute x2, waiting for transfers between devices, along_z(): lax.ppermute(value, 'inline', [pair for pair in pairs if 0 <= pair[1] < c...  18.9 us
    pallas_call x1, Pallas kernels, image(): pl.pallas_call(functools.partial(image_body, scale, cells), grid_spec=plt...  14.6 us
    ppermute x2, starting transfers between devices, along_z(): lax.ppermute(value, 'inline', [pair for pair in pairs if 0 <= pair[1] < c...  8.07 us
    pallas_call x4, Pallas kernels, turn(): pl.pallas_call(turn_body, grid_spec=pltpu.PrefetchScalarGridSpec(num_scal...  5.14 us
    unnamed x22, local copies, waits for them, and re-layouts  4.93 us
    select_n x2, other arithmetic, routed(): shared = jnp.where(core == odd, to_core(from_z), to_core(from_y))  4.85 us
  transfers between devices with their start and end apart: 12, of which 5 were waited for; matrix products, arithmetic and copies ran while one was open for 4% of the time, Pallas kernels for 3%

profile of v1, /device:TPU:0, one launch (start us, length us, event | category | flops | bytes accessed | tf_op | source)
XLA Modules:
  0.0 121.5 jit_solution(15283077340023596725)
XLA Ops:
  0.0 0.0 copy-start
  0.0 1.6 %copy-done = bf16[4,32,32,256]{3,2,1,0:T(8,128)(2,1)S(1)} copy-done((bf16[4,32,32,256]{3,2,1,0:T(8,128)(2,1)S(1)}, bf16[4,32,32,256]{3,2,1,0:T(8,128)(2,1)}, u32[]{:S(2)}) %copy-start) | copy-done | bytes 2097176
  1.6 1.1 turn.7
  2.7 0.0 copy-start.1
  2.7 3.0 %collective-permute-start.2 = (bf16[128,32,128]{2,1,0:T(8,128)(2,1)S(1)}, bf16[128,32,128]{2,1,0:T(8,128)(2,1)}, u32[]{:S(2)}, u32[]{:S(2)}) collective-permute-start(bf16[128,32,128]{2,1,0:T(8,128)(2,1)S(1)} %turn.7), channel_id=1, source_target_pairs={{0,1},{1,0},{2,3},{3,2},{4,5},{5,4},{6,7},{7,6},{8,9},{9,8},{10,11... | collective-permute-start | bytes 3145736 | tf_op jit(solution)/shard_map/ppermute | solution.py:138
  5.7 1.1 turn.6.refs_6_
  6.8 0.0 copy-start.2
  6.8 1.6 %collective-permute-start.1 = (bf16[128,32,128]{2,1,0:T(8,128)(2,1)S(1)}, bf16[128,32,128]{2,1,0:T(8,128)(2,1)S(1)}, u32[]{:S(2)}, u32[]{:S(2)}) collective-permute-start(bf16[128,32,128]{2,1,0:T(8,128)(2,1)S(1)} %turn.6.refs_6_), channel_id=1, source_target_pairs={{0,4},{2,6},{4,0},{6,2},{8,12},{10,14},{12,8},{14,10},{16,20},{18,... | collective-permute-start | bytes 3145736 | tf_op jit(solution)/shard_map/ppermute | solution.py:141
  8.4 20.6 %collective-permute-done.2.refs_7_ = bf16[128,32,128]{2,1,0:T(8,128)(2,1)} collective-permute-done((bf16[128,32,128]{2,1,0:T(8,128)(2,1)S(1)}, bf16[128,32,128]{2,1,0:T(8,128)(2,1)}, u32[]{:S(2)}, u32[]{:S(2)}) %collective-permute-start.2) | collective-permute-done | bytes 1048608 | tf_op jit(solution)/shard_map/ppermute | solution.py:138
  29.0 1.8 %collective-permute-start.3 = (bf16[128,32,128]{2,1,0:T(8,128)(2,1)}, bf16[128,32,128]{2,1,0:T(8,128)(2,1)}, u32[]{:S(2)}, u32[]{:S(2)}) collective-permute-start(bf16[128,32,128]{2,1,0:T(8,128)(2,1)} %collective-permute-done.2.refs_7_), channel_id=1, source_target_pairs={{0,4},{2,6},{4,0},{6,2},{8,12},{10,14},{12,8},{14,10},{16,20},{18,... | collective-permute-start | bytes 3145736 | tf_op jit(solution)/shard_map/ppermute | solution.py:141
  30.7 1.1 collective-permute-done.1.refs_2_
  31.9 3.6 %collective-permute-start.4 = (bf16[128,32,128]{2,1,0:T(8,128)(2,1)S(1)}, bf16[128,32,128]{2,1,0:T(8,128)(2,1)S(1)}, u32[]{:S(2)}, u32[]{:S(2)}) collective-permute-start(bf16[128,32,128]{2,1,0:T(8,128)(2,1)S(1)} %collective-permute-done.1.refs_2_), channel_id=1, source_target_pairs={{0,8},{2,10},{8,16},{10,18},{12,4},{14,6},{16,24},{18,26},{20,12},... | collective-permute-start | bytes 3145736 | tf_op jit(solution)/shard_map/ppermute | solution.py:145
  35.5 18.6 %collective-permute-done.3.refs_3_ = bf16[128,32,128]{2,1,0:T(8,128)(2,1)} collective-permute-done((bf16[128,32,128]{2,1,0:T(8,128)(2,1)}, bf16[128,32,128]{2,1,0:T(8,128)(2,1)}, u32[]{:S(2)}, u32[]{:S(2)}) %collective-permute-start.3) | collective-permute-done | bytes 1048608 | tf_op jit(solution)/shard_map/ppermute | solution.py:141
  54.1 4.5 %collective-permute-start.5 = (bf16[128,32,128]{2,1,0:T(8,128)(2,1)}, bf16[128,32,128]{2,1,0:T(8,128)(2,1)}, u32[]{:S(2)}, u32[]{:S(2)}) collective-permute-start(bf16[128,32,128]{2,1,0:T(8,128)(2,1)} %collective-permute-done.3.refs_3_), channel_id=1, source_target_pairs={{0,8},{2,10},{8,16},{10,18},{12,4},{14,6},{16,24},{18,26},{20,12},... | collective-permute-start | bytes 3145736 | tf_op jit(solution)/shard_map/ppermute | solution.py:145
  58.5 0.0 collective-permute-start.9
  58.5 0.0 copy-start.5
  58.5 1.0 copy-done.5
  59.5 0.0 collective-permute-done.4.refs_4_
  59.5 0.5 collective-permute-start.8
  60.1 0.1 collective-permute-start.11
  60.1 18.9 %collective-permute-done.5.refs_5_ = bf16[128,32,128]{2,1,0:T(8,128)(2,1)} collective-permute-done((bf16[128,32,128]{2,1,0:T(8,128)(2,1)}, bf16[128,32,128]{2,1,0:T(8,128)(2,1)}, u32[]{:S(2)}, u32[]{:S(2)}) %collective-permute-start.5) | collective-permute-done | bytes 1048608 | tf_op jit(solution)/shard_map/ppermute | solution.py:145
  79.0 0.0 collective-permute-start.10
  79.0 0.5 collective-permute-start.6
  79.5 0.0 copy-done.1
  79.5 1.9 %turn.5 = bf16[128,32,128]{2,1,0:T(8,128)(2,1)} custom-call(s32[1]{0:T(128)} %bitcast.5.half_ref, bf16[4,32,32,256]{3,2,1,0:T(8,128)(2,1)S(1)} %copy-done.1), custom_call_target="tpu_custom_call" | custom-call | bytes 2097152 | tf_op jit(solution)/shard_map/turn/pallas_call | solution.py:54
  81.4 0.0 collective-permute-done.9
  81.4 0.0 copy-done.7
  81.4 0.6 collective-permute-start
  82.0 0.0 collective-permute-done.8
  82.0 0.4 copy-done.9
  82.4 1.0 copy-done.10
  83.3 0.0 collective-permute-start.7
  83.3 1.1 turn.4.refs_0_
  84.4 0.0 copy-done.2
  84.5 0.0 copy-start.3
  84.5 1.0 copy-done.3
  85.4 0.1 stack.19.where_ref
  85.5 2.4 %broadcast_select_fusion.1.refs_10_ = bf16[128,32,128]{2,1,0:T(8,128)(2,1)} fusion(bf16[128,32,128]{2,1,0:T(8,128)(2,1)} %copy-done.10, bf16[128,32,128]{2,1,0:T(8,128)(2,1)} %copy-done.9, pred[]{:T(512)S(6)} %eq.7), kind=kLoop, calls=%fused_computation.1 | loop fusion | flops 524288 | bytes 3145729 | tf_op jit(solution)/shard_map/jit(_where)/select_n | solution.py:158
  87.9 0.0 collective-permute-done.11
  87.9 0.0 collective-permute-done.10
  87.9 2.5 %broadcast_select_fusion.refs_11_ = bf16[128,32,128]{2,1,0:T(8,128)(2,1)} fusion(bf16[128,32,128]{2,1,0:T(8,128)(2,1)} %collective-permute-done.10, bf16[128,32,128]{2,1,0:T(8,128)(2,1)} %collective-permute-done.11, pred[]{:T(512)S(6)} %eq.7), kind=kLoop, calls=%fused_computation | loop fusion | flops 524288 | bytes 3145729 | tf_op jit(solution)/shard_map/jit(_where)/select_n | solution.py:158
  90.4 16.4 %collective-permute-done.refs_1_ = bf16[128,32,128]{2,1,0:T(8,128)(2,1)} collective-permute-done((bf16[128,32,128]{2,1,0:T(8,128)(2,1)}, bf16[128,32,128]{2,1,0:T(8,128)(2,1)}, u32[]{:S(2)}, u32[]{:S(2)}) %collective-permute-start) | collective-permute-done | bytes 1048608 | tf_op jit(solution)/shard_map/ppermute | solution.py:138
  106.8 0.0 collective-permute-done.6.refs_8_
  106.8 0.0 collective-permute-done.7.refs_9_
  106.8 0.0 copy-done.4
  106.8 0.0 copy-done.6
  106.8 0.0 copy-done.8
  106.9 14.6 %image.1 = f32[4128,128]{1,0:T(8,128)} custom-call(s32[5]{0:T(128)S(1)} %stack.19.where_ref, bf16[128,32,128]{2,1,0:T(8,128)(2,1)S(1)} %copy-done.4, bf16[128,32,128]{2,1,0:T(8,128)(2,1)} %collective-permute-done.refs_1_, bf16[128,32,128]{2,1,0:T(8,128)(2,1)S(1)} %copy-done.6, bf16[128,32,128]{2,1,0:T(8,128)(2,1)} %collective-permute-done.3.refs_3_, ...), custom_call_target="tpu_custom_call" | custom-call | tf_op jit(solution)/shard_map/image/pallas_call | solution.py:111
  (6 shorter events, 0.0 us)
Async XLA Ops:
  0.0 1.6 %copy-start = (bf16[4,32,32,256]{3,2,1,0:T(8,128)(2,1)S(1)}, bf16[4,32,32,256]{3,2,1,0:T(8,128)(2,1)}, u32[]{:S(2)}) copy-start(bf16[4,32,32,256]{3,2,1,0:T(8,128)(2,1)} %raw_ref.7) | copy-start | bytes 6291460
  2.7 76.8 %copy-start.1 = (bf16[4,32,32,256]{3,2,1,0:T(8,128)(2,1)S(1)}, bf16[4,32,32,256]{3,2,1,0:T(8,128)(2,1)}, u32[]{:S(2)}) copy-start(bf16[4,32,32,256]{3,2,1,0:T(8,128)(2,1)} %raw_ref.5) | copy-start | bytes 6291460
  2.7 26.3 %collective-permute-start.2 = (bf16[128,32,128]{2,1,0:T(8,128)(2,1)S(1)}, bf16[128,32,128]{2,1,0:T(8,128)(2,1)}, u32[]{:S(2)}, u32[]{:S(2)}) collective-permute-start(bf16[128,32,128]{2,1,0:T(8,128)(2,1)S(1)} %turn.7), channel_id=1, source_target_pairs={{0,1},{1,0},{2,3},{3,2},{4,5},{5,4},{6,7},{7,6},{8,9},{9,8},{10,11... | collective-permute-start | bytes 3145736 | tf_op jit(solution)/shard_map/ppermute | solution.py:138
  6.8 77.6 %copy-start.2 = (bf16[128,32,128]{2,1,0:T(8,128)(2,1)}, bf16[128,32,128]{2,1,0:T(8,128)(2,1)S(1)}, u32[]{:S(2)}) copy-start(bf16[128,32,128]{2,1,0:T(8,128)(2,1)S(1)} %turn.6.refs_6_) | copy-start | bytes 3145732
  6.8 25.1 %collective-permute-start.1 = (bf16[128,32,128]{2,1,0:T(8,128)(2,1)S(1)}, bf16[128,32,128]{2,1,0:T(8,128)(2,1)S(1)}, u32[]{:S(2)}, u32[]{:S(2)}) collective-permute-start(bf16[128,32,128]{2,1,0:T(8,128)(2,1)S(1)} %turn.6.refs_6_), channel_id=1, source_target_pairs={{0,4},{2,6},{4,0},{6,2},{8,12},{10,14},{12,8},{14,10},{16,20},{18,... | collective-permute-start | bytes 3145736 | tf_op jit(solution)/shard_map/ppermute | solution.py:141
  29.0 25.1 %collective-permute-start.3 = (bf16[128,32,128]{2,1,0:T(8,128)(2,1)}, bf16[128,32,128]{2,1,0:T(8,128)(2,1)}, u32[]{:S(2)}, u32[]{:S(2)}) collective-permute-start(bf16[128,32,128]{2,1,0:T(8,128)(2,1)} %collective-permute-done.2.refs_7_), channel_id=1, source_target_pairs={{0,4},{2,6},{4,0},{6,2},{8,12},{10,14},{12,8},{14,10},{16,20},{18,... | collective-permute-start | bytes 3145736 | tf_op jit(solution)/shard_map/ppermute | solution.py:141
  31.9 27.7 %collective-permute-start.4 = (bf16[128,32,128]{2,1,0:T(8,128)(2,1)S(1)}, bf16[128,32,128]{2,1,0:T(8,128)(2,1)S(1)}, u32[]{:S(2)}, u32[]{:S(2)}) collective-permute-start(bf16[128,32,128]{2,1,0:T(8,128)(2,1)S(1)} %collective-permute-done.1.refs_2_), channel_id=1, source_target_pairs={{0,8},{2,10},{8,16},{10,18},{12,4},{14,6},{16,24},{18,26},{20,12},... | collective-permute-start | bytes 3145736 | tf_op jit(solution)/shard_map/ppermute | solution.py:145
  54.1 24.9 %collective-permute-start.5 = (bf16[128,32,128]{2,1,0:T(8,128)(2,1)}, bf16[128,32,128]{2,1,0:T(8,128)(2,1)}, u32[]{:S(2)}, u32[]{:S(2)}) collective-permute-start(bf16[128,32,128]{2,1,0:T(8,128)(2,1)} %collective-permute-done.3.refs_3_), channel_id=1, source_target_pairs={{0,8},{2,10},{8,16},{10,18},{12,4},{14,6},{16,24},{18,26},{20,12},... | collective-permute-start | bytes 3145736 | tf_op jit(solution)/shard_map/ppermute | solution.py:145
  58.5 22.8 %collective-permute-start.9 = (bf16[128,32,128]{2,1,0:T(8,128)(2,1)S(1)}, bf16[128,32,128]{2,1,0:T(8,128)(2,1)S(1)}, u32[]{:S(2)}, u32[]{:S(2)}) collective-permute-start(bf16[128,32,128]{2,1,0:T(8,128)(2,1)S(1)} %collective-permute-done.1.refs_2_), channel_id=1, source_target_pairs={{0,2},{2,0},{4,6},{6,4},{8,10},{10,8},{12,14},{14,12},{16,18},{18,... | collective-permute-start | bytes 3145736 | tf_op jit(solution)/shard_map/ppermute | solution.py:148
  58.5 1.0 copy-start.5
  59.5 21.8 %copy-start.7 = (bf16[128,32,128]{2,1,0:T(8,128)(2,1)}, bf16[128,32,128]{2,1,0:T(8,128)(2,1)S(1)}, u32[]{:S(2)}) copy-start(bf16[128,32,128]{2,1,0:T(8,128)(2,1)S(1)} %collective-permute-done.4.refs_4_) | copy-start | bytes 3145732
  59.5 22.5 %collective-permute-start.8 = (bf16[128,32,128]{2,1,0:T(8,128)(2,1)S(1)}, bf16[128,32,128]{2,1,0:T(8,128)(2,1)S(1)}, u32[]{:S(2)}, u32[]{:S(2)}) collective-permute-start(bf16[128,32,128]{2,1,0:T(8,128)(2,1)S(1)} %collective-permute-done.4.refs_4_), channel_id=1, source_target_pairs={{0,2},{2,0},{4,6},{6,4},{8,10},{10,8},{12,14},{14,12},{16,18},{18,... | collective-permute-start | bytes 3145736 | tf_op jit(solution)/shard_map/ppermute | solution.py:148
  60.1 27.8 %collective-permute-start.11 = (bf16[128,32,128]{2,1,0:T(8,128)(2,1)}, bf16[128,32,128]{2,1,0:T(8,128)(2,1)}, u32[]{:S(2)}, u32[]{:S(2)}) collective-permute-start(bf16[128,32,128]{2,1,0:T(8,128)(2,1)} %collective-permute-done.3.refs_3_), channel_id=1, source_target_pairs={{0,2},{2,0},{4,6},{6,4},{8,10},{10,8},{12,14},{14,12},{16,18},{18,... | collective-permute-start | bytes 3145736 | tf_op jit(solution)/shard_map/ppermute | solution.py:148
  79.0 8.9 %collective-permute-start.10 = (bf16[128,32,128]{2,1,0:T(8,128)(2,1)}, bf16[128,32,128]{2,1,0:T(8,128)(2,1)}, u32[]{:S(2)}, u32[]{:S(2)}) collective-permute-start(bf16[128,32,128]{2,1,0:T(8,128)(2,1)} %collective-permute-done.5.refs_5_), channel_id=1, source_target_pairs={{0,2},{2,0},{4,6},{6,4},{8,10},{10,8},{12,14},{14,12},{16,18},{18,... | collective-permute-start | bytes 3145736 | tf_op jit(solution)/shard_map/ppermute | solution.py:148
  79.0 27.8 %collective-permute-start.6 = (bf16[128,32,128]{2,1,0:T(8,128)(2,1)S(1)}, bf16[128,32,128]{2,1,0:T(8,128)(2,1)}, u32[]{:S(2)}, u32[]{:S(2)}) collective-permute-start(bf16[128,32,128]{2,1,0:T(8,128)(2,1)S(1)} %turn.6.refs_6_), channel_id=1, source_target_pairs={{0,2},{2,0},{4,6},{6,4},{8,10},{10,8},{12,14},{14,12},{16,18},{18,... | collective-permute-start | bytes 3145736 | tf_op jit(solution)/shard_map/ppermute | solution.py:148
  81.4 1.0 copy-start.9
  81.4 25.4 %collective-permute-start = (bf16[128,32,128]{2,1,0:T(8,128)(2,1)}, bf16[128,32,128]{2,1,0:T(8,128)(2,1)}, u32[]{:S(2)}, u32[]{:S(2)}) collective-permute-start(bf16[128,32,128]{2,1,0:T(8,128)(2,1)} %turn.5), channel_id=1, source_target_pairs={{0,1},{1,0},{2,3},{3,2},{4,5},{5,4},{6,7},{7,6},{8,9},{9,8},{10,11... | collective-permute-start | bytes 3145736 | tf_op jit(solution)/shard_map/ppermute | solution.py:138
  82.4 1.0 copy-start.10
  83.3 23.5 %collective-permute-start.7 = (bf16[128,32,128]{2,1,0:T(8,128)(2,1)}, bf16[128,32,128]{2,1,0:T(8,128)(2,1)}, u32[]{:S(2)}, u32[]{:S(2)}) collective-permute-start(bf16[128,32,128]{2,1,0:T(8,128)(2,1)} %collective-permute-done.2.refs_7_), channel_id=1, source_target_pairs={{0,2},{2,0},{4,6},{6,4},{8,10},{10,8},{12,14},{14,12},{16,18},{18,... | collective-permute-start | bytes 3145736 | tf_op jit(solution)/shard_map/ppermute | solution.py:148
  84.5 1.0 copy-start.3
  87.9 18.9 %copy-start.4 = (bf16[128,32,128]{2,1,0:T(8,128)(2,1)S(1)}, bf16[128,32,128]{2,1,0:T(8,128)(2,1)}, u32[]{:S(2)}) copy-start(bf16[128,32,128]{2,1,0:T(8,128)(2,1)} %copy-done.3) | copy-start | bytes 3145732
  87.9 19.0 %copy-start.6 = (bf16[128,32,128]{2,1,0:T(8,128)(2,1)S(1)}, bf16[128,32,128]{2,1,0:T(8,128)(2,1)}, u32[]{:S(2)}) copy-start(bf16[128,32,128]{2,1,0:T(8,128)(2,1)} %copy-done.5) | copy-start | bytes 3145732
  87.9 19.0 %copy-start.8 = (bf16[128,32,128]{2,1,0:T(8,128)(2,1)S(1)}, bf16[128,32,128]{2,1,0:T(8,128)(2,1)}, u32[]{:S(2)}) copy-start(bf16[128,32,128]{2,1,0:T(8,128)(2,1)} %copy-done.7) | copy-start | bytes 3145732

commit v2 on v1

v2 whole, which is shorter than its diff:
```python
import functools

import jax
import jax.numpy as jnp
from jax import lax
from jax.experimental import pallas as pl
from jax.experimental.pallas import tpu as pltpu
from jax.sharding import PartitionSpec as P

LANES = 128
ROWS = 16
VMEM_BYTES = 20 * 1024 * 1024
TOP_BYTES = 60 * 1024 * 1024


def shifted(value, axis, steps):
    count = lax.axis_size(axis)
    initial, last = (max(0, -steps), min(count, count - steps))
    return lax.ppermute(value, axis, [(source, source + steps) for source in range(initial, last)])


def band_rows(product, width, lags):
    rows = product.shape[0]
    cross = product.shape[2]
    flat = product.reshape(rows * width, cross)
    flat = jnp.pad(flat, ((0, rows), (0, 0)))
    skewed = flat.reshape(rows, width + 1, cross)[:, :lags, :]
    return jnp.transpose(skewed, (1, 0, 2))


def plain(source, receiver, scale):
    source, receiver = (
        lax.all_to_all(value, "shot", split_axis=3, concat_axis=0, tiled=True) for value in (source, receiver)
    )
    cells = source.shape[1]
    slabs = [receiver if step == 0 else shifted(receiver, "inline", -step) for step in (-2, -1, 0, 1, 2)]
    width = 5 * cells
    product = jnp.einsum(
        "sity,szty->izy", source, jnp.concatenate(slabs, axis=1), preferred_element_type=jnp.float32
    )
    return band_rows(product, width, 4 * cells + 1) * scale


def turn_body(half_ref, raw_ref, *refs):
    *turned_refs, rows_ref = refs
    shots, cells, times, cross = raw_ref.shape
    for cell in range(cells):
        tile = raw_ref[:, cell].reshape(shots * times, cross).astype(jnp.float32)
        rows_ref[pl.ds(cell, cross, stride=cells), :] = tile.T
    share = cross // len(turned_refs)
    for part, turned_ref in enumerate(turned_refs):
        rows = rows_ref[pl.ds(part * share * cells, share * cells), :]
        turned_ref[...] = rows.reshape(turned_ref.shape).astype(turned_ref.dtype)


def turn(raw, half, parts, vmem, after=None):
    shots, cells, times, _ = raw.shape
    depth = shots * times
    extra = [] if after is None else [after]

    def body(half_ref, raw_ref, *refs):
        turn_body(half_ref, raw_ref, *refs[len(extra) :])

    return pl.pallas_call(
        body,
        grid_spec=pltpu.PrefetchScalarGridSpec(
            num_scalar_prefetch=1,
            grid=(cells // ROWS,),
            in_specs=[pl.BlockSpec((shots, ROWS, times, LANES), lambda step, half: (0, step, 0, half[0]))]
            + [pl.BlockSpec(memory_space=pl.ANY)] * len(extra),
            out_specs=[pl.BlockSpec((LANES // parts, ROWS, depth), lambda step, half: (0, step, 0))] * parts,
            scratch_shapes=[pltpu.VMEM((LANES * ROWS, depth), jnp.float32)],
        ),
        out_shape=[jax.ShapeDtypeStruct((LANES // parts, cells, depth), raw.dtype)] * parts,
        compiler_params=pltpu.CompilerParams(vmem_limit_bytes=vmem),
        cost_estimate=pl.CostEstimate(flops=0, bytes_accessed=raw.size * 2, transcendentals=0),
        name="turn",
    )(half, raw, *extra)


DIMS = (((1,), (1,)), ((), ()))


def choose(flag_ref, first, second, chosen):
    @pl.when(flag_ref[SLOTS] == 1)
    def _():
        for to, source in zip(chosen, first):
            to[...] = source[...]

    @pl.when(flag_ref[SLOTS] == 0)
    def _():
        for to, source in zip(chosen, second):
            to[...] = source[...]


def multiply(source_ref, slots, store):
    parts, block = source_ref.shape[:2]
    for part in range(parts):
        for cross in range(block):
            right = [slab[part][cross] for slab in slots]
            right = jnp.concatenate(right, axis=0) if len(right) > 1 else right[0]
            store(part, cross, lax.dot_general(source_ref[part, cross], right, DIMS, preferred_element_type=jnp.float32))


def spread(scale, cells, products_ref, skewed_ref, where_ref, slots):
    for cell in range(cells):
        turned = products_ref[pl.ds(cell, LANES, stride=cells), :].T * scale
        for place, slot in enumerate(slots):
            lag = (where_ref[slot] + 3) * cells - cell
            skewed_ref[pl.ds(lag * cells + cell, cells, stride=cells), :] = turned[cells * place : cells * (place + 1)]


def first_body(cells, where_ref, source_ref, *refs):
    ins, (wide_ref, late_ref), chosen = refs[:12], refs[12:14], refs[14:]
    slots = [ins[2 * j : 2 * j + 2] for j in range(6)]
    choose(where_ref, slots[4], slots[5], chosen)

    def store_wide(part, cross, value):
        wide_ref[part, pl.ds(cross * cells, cells), : 3 * cells] = value

    def store_late(part, cross, value):
        late_ref[part, pl.ds(cross * cells, cells), : 2 * cells] = value

    multiply(source_ref, slots[:3], store_wide)
    multiply(source_ref, [slots[3], chosen], store_late)


def specs_of(block, cells, depth):
    source = pl.BlockSpec((2, block, cells, depth), lambda step, where: (0, step, 0, 0))
    slab = pl.BlockSpec((block, cells, depth), lambda step, where: (step, 0, 0))
    products = pl.BlockSpec((2, block * cells, LANES), lambda step, where: (0, step, 0))
    return source, slab, products


BLOCK = 8
SLOTS = 5


def first(where, source, slots):
    _, half, cells, depth = source.shape
    source_spec, slab, products = specs_of(BLOCK, cells, depth)
    return pl.pallas_call(
        functools.partial(first_body, cells),
        grid_spec=pltpu.PrefetchScalarGridSpec(
            num_scalar_prefetch=1,
            grid=(half // BLOCK,),
            in_specs=[source_spec] + [slab] * 12,
            out_specs=[products] * 2,
            scratch_shapes=[pltpu.VMEM((BLOCK, cells, depth), source.dtype)] * 2,
        ),
        out_shape=[jax.ShapeDtypeStruct((2, half * cells, LANES), jnp.float32)] * 2,
        compiler_params=pltpu.CompilerParams(vmem_limit_bytes=VMEM_BYTES),
        name="first",
    )(where, source, *slots)


def adder(cells, step, half_rows, products_ref, total_ref, width):
    def store(part, cross, value):
        rows = pl.ds(cross * cells, cells)
        place = pl.multiple_of(part * half_rows + (step * BLOCK + cross) * cells, cells)
        total_ref[pl.ds(place, cells), :width] = value + products_ref[part, rows, :width]

    return store


def second_body(scale, cells, where_ref, source_ref, *refs):
    ins, products_ref, skewed_out, total_ref, skewed_ref, sem = refs[:6], *refs[6:]
    step = pl.program_id(0)
    slots = [ins[2 * j : 2 * j + 2] for j in range(3)]
    multiply(source_ref, slots, adder(cells, step, LANES // 2 * cells, products_ref, total_ref, 3 * cells))

    @pl.when(step == pl.num_programs(0) - 1)
    def _():
        spread(scale, cells, total_ref, skewed_ref, where_ref, (0, 1, 2))
        copy = pltpu.make_async_copy(skewed_ref, skewed_out, sem)
        copy.start()
        copy.wait()


def second(scale, where, source, slots, products):
    _, half, cells, depth = source.shape
    source_spec, slab, products_spec = specs_of(BLOCK, cells, depth)
    rows = (4 * cells + 1 + 2 * cells) * cells
    return pl.pallas_call(
        functools.partial(second_body, scale, cells),
        grid_spec=pltpu.PrefetchScalarGridSpec(
            num_scalar_prefetch=1,
            grid=(half // BLOCK,),
            in_specs=[source_spec] + [slab] * 6 + [products_spec],
            out_specs=pl.BlockSpec(memory_space=pl.ANY),
            scratch_shapes=[
                pltpu.VMEM((2 * half * cells, LANES), jnp.float32),
                pltpu.VMEM((rows, LANES), jnp.float32),
                pltpu.SemaphoreType.DMA(()),
            ],
        ),
        out_shape=jax.ShapeDtypeStruct((rows, LANES), jnp.float32),
        compiler_params=pltpu.CompilerParams(vmem_limit_bytes=VMEM_BYTES),
        name="second",
    )(where, source, *slots, products)


def third_body(scale, cells, where_ref, source_ref, *refs):
    ins, (products_ref, skewed_in, image_ref), (total_ref, skewed_ref, in_sem, out_sem) = refs[:6], refs[6:9], refs[9:13]
    chosen = refs[13:]
    step = pl.program_id(0)
    slots = [ins[2 * j : 2 * j + 2] for j in range(3)]
    load = pltpu.make_async_copy(skewed_in, skewed_ref, in_sem)

    @pl.when(step == 0)
    def _():
        load.start()

    choose(where_ref, slots[1], slots[2], chosen)
    multiply(
        source_ref, [slots[0], chosen], adder(cells, step, LANES // 2 * cells, products_ref, total_ref, 2 * cells)
    )

    @pl.when(step == pl.num_programs(0) - 1)
    def _():
        load.wait()
        spread(scale, cells, total_ref, skewed_ref, where_ref, (3, 4))
        copy = pltpu.make_async_copy(skewed_ref.at[pl.ds(cells * cells, image_ref.shape[0])], image_ref, out_sem)
        copy.start()
        copy.wait()


def third(scale, where, source, slots, products, skewed):
    _, half, cells, depth = source.shape
    source_spec, slab, products_spec = specs_of(BLOCK, cells, depth)
    lags = 4 * cells + 1
    return pl.pallas_call(
        functools.partial(third_body, scale, cells),
        grid_spec=pltpu.PrefetchScalarGridSpec(
            num_scalar_prefetch=1,
            grid=(half // BLOCK,),
            in_specs=[source_spec] + [slab] * 6 + [products_spec, pl.BlockSpec(memory_space=pl.ANY)],
            out_specs=pl.BlockSpec(memory_space=pl.ANY),
            scratch_shapes=[
                pltpu.VMEM((2 * half * cells, LANES), jnp.float32),
                pltpu.VMEM(skewed.shape, jnp.float32),
                pltpu.SemaphoreType.DMA(()),
                pltpu.SemaphoreType.DMA(()),
            ]
            + [pltpu.VMEM((BLOCK, cells, depth), source.dtype)] * 2,
        ),
        out_shape=jax.ShapeDtypeStruct((lags * cells, LANES), jnp.float32),
        compiler_params=pltpu.CompilerParams(vmem_limit_bytes=VMEM_BYTES),
        name="third",
    )(where, source, *slots, products, skewed).reshape(lags, cells, LANES)


def routed(source, receiver, scale):
    count = lax.axis_size("inline")
    own = lax.axis_index("inline")
    core, odd = own & 1, (own >> 1) & 1
    half = lax.axis_index("shot")

    def across(value):
        return lax.ppermute(value, "shot", [(0, 1), (1, 0)])

    def along_y(value):
        return lax.ppermute(value, "inline", [(index, index ^ 2) for index in range(count)])

    def along_z(value):
        pairs = [(index, index + (4 if index // 2 % 2 == 0 else -4)) for index in range(count)]
        return lax.ppermute(value, "inline", [pair for pair in pairs if 0 <= pair[1] < count])

    def to_core(value):
        return lax.ppermute(value, "inline", [(index, index ^ 1) for index in range(count)])

    here, there = (jnp.full((1,), index, jnp.int32) for index in (half, 1 - half))
    kept = turn(receiver, here, 2, TOP_BYTES)
    sent = turn(receiver, there, 2, VMEM_BYTES, kept[0])
    moved = [across(part) for part in sent]
    near = turn(source, here, 1, VMEM_BYTES, sent[0])[0]
    far = across(turn(source, there, 1, VMEM_BYTES, moved[1])[0])
    sources = [value.reshape(2, LANES // 2, *value.shape[1:]) for value in (near, far)]
    groups = []
    for parts in (kept, moved):
        from_y = [along_y(part) for part in parts]
        from_z = [along_z(part) for part in from_y]
        twin = [to_core(part) for part in parts]
        shared_y = [to_core(part) for part in from_y]
        shared_z = [to_core(part) for part in from_z]
        groups.append((*from_y, *parts, *twin, *from_z, *shared_y, *shared_z))
    where = jnp.stack(
        [2 - 4 * odd, 0 * odd, 1 - 2 * core, 4 * odd - 2, 2 * core - 1, core ^ odd]
    ).astype(jnp.int32)
    wide, late = first(where, sources[0], groups[0])
    skewed = second(scale, where, sources[1], groups[1][:6], wide)
    return third(scale, where, sources[1], groups[1][6:], late, skewed)


def on_device(source, receiver):
    shots, cells, times, cross = source.shape
    groups, count = lax.axis_size("shot"), lax.axis_size("inline")
    scale = 1.0 / (times * shots * groups) ** 0.5
    fits = (
        groups == 2
        and count % 4 == 0
        and cross == 2 * LANES
        and shots * times == LANES
        and 4 * cells == LANES
        and times % ROWS == 0
    )
    return routed(source, receiver, scale) if fits else plain(source, receiver, scale)


def solution(mesh):
    placed = (P("shot", "inline", None, None), P("shot", "inline", None, None))
    return jax.shard_map(
        on_device, mesh=mesh, in_specs=placed, out_specs=P(None, "inline", "shot"), check_vma=False
    )
```

time: 122 us -> 133 us (1.090)
  waiting for transfers between devices: 75.6 us -> 50.5 us
  local copies, waits for them, and re-layouts: 5.01 us -> 22.3 us
  Pallas kernels: 19.8 us -> 31.9 us
  starting transfers between devices: 16.1 us -> 26.6 us
  other arithmetic: 4.85 us -> 0 us
    ppermute x2 -> x3, waiting for transfers between devices: 37 us -> 0.01 us  [across(): return lax.ppermute(value, 'shot', [(0, 1), (1, 0)])]
    unnamed x22 -> x68, local copies, waits for them, and re-layouts: 4.93 us -> 22.2 us
    pallas_call x5 -> x7, Pallas kernels: 19.8 us -> 31.9 us  [the longest x1 9.72 us: third(): pl.pallas_call(functools.partial(third_body, scale, cells), grid_spec=plt...]
    ppermute x2 -> x4, waiting for transfers between devices: 18.9 us -> 30.9 us  [along_z(): lax.ppermute(value, 'inline', [pair for pair in pairs if 0 <= pair[1] < c...]
    ppermute x2 -> x4, starting transfers between devices: 8.07 us -> 13.6 us  [along_z(): lax.ppermute(value, 'inline', [pair for pair in pairs if 0 <= pair[1] < c...]
    select_n x2 -> x0, other arithmetic: 4.85 us -> none  [routed(): shared = jnp.where(core == odd, to_core(from_z), to_core(from_y))]
    ppermute x2 -> x4, starting transfers between devices: 3.35 us -> 5.44 us  [along_y(): lax.ppermute(value, 'inline', [(index, index ^ 2) for index in range(coun...]
    ppermute x2 -> x3, starting transfers between devices: 3.62 us -> 5.55 us  [across(): return lax.ppermute(value, 'shot', [(0, 1), (1, 0)])]
  transfers between devices with their start and end apart: 12 -> 23, of which waited for: 5 -> 7; matrix products, arithmetic and copies ran while one was open for 4% -> 0% of each run, Pallas kernels for 3% -> 15%
where the time goes in v2:
time: 133 us; the launch traced here: 132 us
  waiting for transfers between devices  50.5 us (38%)
  Pallas kernels  31.9 us (24%)
  starting transfers between devices  26.6 us (20%)
  local copies, waits for them, and re-layouts  22.3 us (17%)
    ppermute x4, waiting for transfers between devices, along_z(): lax.ppermute(value, 'inline', [pair for pair in pairs if 0 <= pair[1] < c...  30.9 us
    unnamed x68, local copies, waits for them, and re-layouts  22.2 us
    ppermute x4, waiting for transfers between devices, along_y(): lax.ppermute(value, 'inline', [(index, index ^ 2) for index in range(coun...  19.6 us
    ppermute x4, starting transfers between devices, along_z(): lax.ppermute(value, 'inline', [pair for pair in pairs if 0 <= pair[1] < c...  13.6 us
    pallas_call x1, Pallas kernels, third(): pl.pallas_call(functools.partial(third_body, scale, cells), grid_spec=plt...  9.72 us
    pallas_call x1, Pallas kernels, second(): pl.pallas_call(functools.partial(second_body, scale, cells), grid_spec=pl...  8.6 us
    pallas_call x4, Pallas kernels, turn(): pl.pallas_call(body, grid_spec=pltpu.PrefetchScalarGridSpec(num_scalar_pr...  6.83 us
    pallas_call x1, Pallas kernels, first(): pl.pallas_call(functools.partial(first_body, cells), grid_spec=pltpu.Pref...  6.77 us
  transfers between devices with their start and end apart: 23, of which 7 were waited for; matrix products, arithmetic and copies ran while one was open for 0% of the time, Pallas kernels for 15%

profile of v2, /device:TPU:0, one launch (start us, length us, event | category | flops | bytes accessed | tf_op | source)
XLA Modules:
  0.0 131.6 jit_solution(17244234989945957953)
XLA Ops:
  0.0 2.9 %turn.4 = (bf16[64,32,128]{2,1,0:T(8,128)(2,1)}, bf16[64,32,128]{2,1,0:T(8,128)(2,1)}) custom-call(s32[1]{0:T(128)} %bitcast.6.half_ref, bf16[4,32,32,256]{3,2,1,0:T(8,128)(2,1)} %raw_ref.5), custom_call_target="tpu_custom_call" | custom-call | bytes 2097152 | tf_op jit(solution)/shard_map/turn/pallas_call | solution.py:64
  2.9 3.0 %collective-permute-start.11 = (bf16[64,32,128]{2,1,0:T(8,128)(2,1)}, bf16[64,32,128]{2,1,0:T(8,128)(2,1)S(1)}, u32[]{:S(2)}, u32[]{:S(2)}) collective-permute-start(bf16[64,32,128]{2,1,0:T(8,128)(2,1)} %get-tuple-element.11.refs_0_.refs_2_), channel_id=1, source_target_pairs={{0,4},{2,6},{4,0},{6,2},{8,12},{10,14},{12,8},{14,10},{16,20},{18,... | collective-permute-start | bytes 1572872 | tf_op jit(solution)/shard_map/ppermute | solution.py:263
  5.9 0.5 collective-permute-start.14
  6.4 1.2 copy-done.7
  7.6 1.1 turn.5
  8.7 2.0 %collective-permute-start = (bf16[64,32,128]{2,1,0:T(8,128)(2,1)S(1)}, bf16[64,32,128]{2,1,0:T(8,128)(2,1)S(1)}, u32[]{:S(2)}, u32[]{:S(2)}) collective-permute-start(bf16[64,32,128]{2,1,0:T(8,128)(2,1)S(1)} %get-tuple-element.12), channel_id=1, source_target_pairs={{0,1},{1,0},{2,3},{3,2},{4,5},{5,4},{6,7},{7,6},{8,9},{9,8},{10,11... | collective-permute-start | bytes 1572872 | tf_op jit(solution)/shard_map/ppermute | solution.py:260
  10.7 8.1 %collective-permute-done.11.refs_0_ = bf16[64,32,128]{2,1,0:T(8,128)(2,1)S(1)} collective-permute-done((bf16[64,32,128]{2,1,0:T(8,128)(2,1)}, bf16[64,32,128]{2,1,0:T(8,128)(2,1)S(1)}, u32[]{:S(2)}, u32[]{:S(2)}) %collective-permute-start.11) | collective-permute-done | bytes 524320 | tf_op jit(solution)/shard_map/ppermute | solution.py:263
  18.8 2.0 %collective-permute-start.2 = (bf16[64,32,128]{2,1,0:T(8,128)(2,1)S(1)}, bf16[64,32,128]{2,1,0:T(8,128)(2,1)S(1)}, u32[]{:S(2)}, u32[]{:S(2)}) collective-permute-start(bf16[64,32,128]{2,1,0:T(8,128)(2,1)S(1)} %get-tuple-element.13.refs_0_), channel_id=1, source_target_pairs={{0,1},{1,0},{2,3},{3,2},{4,5},{5,4},{6,7},{7,6},{8,9},{9,8},{10,11... | collective-permute-start | bytes 1572872 | tf_op jit(solution)/shard_map/ppermute | solution.py:260
  20.8 0.8 copy-done.15
  21.6 7.6 %collective-permute-done.12.refs_1_ = bf16[64,32,128]{2,1,0:T(8,128)(2,1)S(1)} collective-permute-done((bf16[64,32,128]{2,1,0:T(8,128)(2,1)}, bf16[64,32,128]{2,1,0:T(8,128)(2,1)S(1)}, u32[]{:S(2)}, u32[]{:S(2)}) %collective-permute-start.12) | collective-permute-done | bytes 524320 | tf_op jit(solution)/shard_map/ppermute | solution.py:263
  29.2 3.7 %collective-permute-start.15 = (bf16[64,32,128]{2,1,0:T(8,128)(2,1)S(1)}, bf16[64,32,128]{2,1,0:T(8,128)(2,1)S(1)}, u32[]{:S(2)}, u32[]{:S(2)}) collective-permute-start(bf16[64,32,128]{2,1,0:T(8,128)(2,1)S(1)} %collective-permute-done.11.refs_0_), channel_id=1, source_target_pairs={{0,8},{2,10},{8,16},{10,18},{12,4},{14,6},{16,24},{18,26},{20,12},... | collective-permute-start | bytes 1572872 | tf_op jit(solution)/shard_map/ppermute | solution.py:267
  32.9 3.5 %collective-permute-start.16 = (bf16[64,32,128]{2,1,0:T(8,128)(2,1)S(1)}, bf16[64,32,128]{2,1,0:T(8,128)(2,1)S(1)}, u32[]{:S(2)}, u32[]{:S(2)}) collective-permute-start(bf16[64,32,128]{2,1,0:T(8,128)(2,1)S(1)} %collective-permute-done.12.refs_1_), channel_id=1, source_target_pairs={{0,8},{2,10},{8,16},{10,18},{12,4},{14,6},{16,24},{18,26},{20,12},... | collective-permute-start | bytes 1572872 | tf_op jit(solution)/shard_map/ppermute | solution.py:267
  36.5 0.8 copy-done.18
  37.3 0.5 collective-permute-start.18
  37.8 0.8 copy-done.20
  38.6 6.6 %collective-permute-done.15.refs_6_ = bf16[64,32,128]{2,1,0:T(8,128)(2,1)S(1)} collective-permute-done((bf16[64,32,128]{2,1,0:T(8,128)(2,1)S(1)}, bf16[64,32,128]{2,1,0:T(8,128)(2,1)S(1)}, u32[]{:S(2)}, u32[]{:S(2)}) %collective-permute-start.15) | collective-permute-done | bytes 524320 | tf_op jit(solution)/shard_map/ppermute | solution.py:267
  45.3 2.4 %collective-permute-start.5 = (bf16[64,32,128]{2,1,0:T(8,128)(2,1)S(1)}, bf16[64,32,128]{2,1,0:T(8,128)(2,1)}, u32[]{:S(2)}, u32[]{:S(2)}) collective-permute-start(bf16[64,32,128]{2,1,0:T(8,128)(2,1)S(1)} %collective-permute-done.refs_0_.refs_3_), channel_id=1, source_target_pairs={{0,4},{2,6},{4,0},{6,2},{8,12},{10,14},{12,8},{14,10},{16,20},{18,... | collective-permute-start | bytes 1572872 | tf_op jit(solution)/shard_map/ppermute | solution.py:263
  47.7 6.7 %collective-permute-done.16.refs_7_ = bf16[64,32,128]{2,1,0:T(8,128)(2,1)S(1)} collective-permute-done((bf16[64,32,128]{2,1,0:T(8,128)(2,1)S(1)}, bf16[64,32,128]{2,1,0:T(8,128)(2,1)S(1)}, u32[]{:S(2)}, u32[]{:S(2)}) %collective-permute-start.16) | collective-permute-done | bytes 524320 | tf_op jit(solution)/shard_map/ppermute | solution.py:267
  54.4 0.8 copy-done.26
  55.8 1.8 %turn.6 = bf16[128,32,128]{2,1,0:T(8,128)(2,1)} custom-call(s32[1]{0:T(128)} %bitcast.5.half_ref, bf16[4,32,32,256]{3,2,1,0:T(8,128)(2,1)S(1)} %copy-done.1, bf16[64,32,128]{2,1,0:T(8,128)(2,1)S(1)} %collective-permute-done.refs_0_.refs_3_), custom_call_target="tpu_custom_call" | custom-call | bytes 2097152 | tf_op jit(solution)/shard_map/turn/pallas_call | solution.py:64
  57.6 0.8 copy-done.28
  58.4 1.5 %collective-permute-start.1 = (bf16[128,32,128]{2,1,0:T(8,128)(2,1)}, bf16[128,32,128]{2,1,0:T(8,128)(2,1)S(1)}, u32[]{:S(2)}, u32[]{:S(2)}) collective-permute-start(bf16[128,32,128]{2,1,0:T(8,128)(2,1)} %turn.6), channel_id=1, source_target_pairs={{0,1},{1,0},{2,3},{3,2},{4,5},{5,4},{6,7},{7,6},{8,9},{9,8},{10,11... | collective-permute-start | bytes 3145736 | tf_op jit(solution)/shard_map/ppermute | solution.py:260
  59.9 3.9 %collective-permute-done.5.refs_1_ = bf16[64,32,128]{2,1,0:T(8,128)(2,1)} collective-permute-done((bf16[64,32,128]{2,1,0:T(8,128)(2,1)S(1)}, bf16[64,32,128]{2,1,0:T(8,128)(2,1)}, u32[]{:S(2)}, u32[]{:S(2)}) %collective-permute-start.5) | collective-permute-done | bytes 524320 | tf_op jit(solution)/shard_map/ppermute | solution.py:263
  63.9 0.8 copy-done.11
  64.7 4.2 %collective-permute-start.6 = (bf16[64,32,128]{2,1,0:T(8,128)(2,1)}, bf16[64,32,128]{2,1,0:T(8,128)(2,1)}, u32[]{:S(2)}, u32[]{:S(2)}) collective-permute-start(bf16[64,32,128]{2,1,0:T(8,128)(2,1)} %collective-permute-done.5.refs_1_), channel_id=1, source_target_pairs={{0,8},{2,10},{8,16},{10,18},{12,4},{14,6},{16,24},{18,26},{20,12},... | collective-permute-start | bytes 1572872 | tf_op jit(solution)/shard_map/ppermute | solution.py:267
  68.9 0.8 copy-done.13
  69.7 2.1 %collective-permute-start.4 = (bf16[64,32,128]{2,1,0:T(8,128)(2,1)}, bf16[64,32,128]{2,1,0:T(8,128)(2,1)}, u32[]{:S(2)}, u32[]{:S(2)}) collective-permute-start(bf16[64,32,128]{2,1,0:T(8,128)(2,1)} %collective-permute-done.3.refs_0_), channel_id=1, source_target_pairs={{0,8},{2,10},{8,16},{10,18},{12,4},{14,6},{16,24},{18,26},{20,12},... | collective-permute-start | bytes 1572872 | tf_op jit(solution)/shard_map/ppermute | solution.py:267
  71.8 0.8 copy-done.30
  72.9 0.8 copy-done.32
  74.0 6.7 %collective-permute-done.6.refs_1_ = bf16[64,32,128]{2,1,0:T(8,128)(2,1)} collective-permute-done((bf16[64,32,128]{2,1,0:T(8,128)(2,1)}, bf16[64,32,128]{2,1,0:T(8,128)(2,1)}, u32[]{:S(2)}, u32[]{:S(2)}) %collective-permute-start.6) | collective-permute-done | bytes 524320 | tf_op jit(solution)/shard_map/ppermute | solution.py:267
  80.7 10.8 %collective-permute-done.4.refs_0_ = bf16[64,32,128]{2,1,0:T(8,128)(2,1)} collective-permute-done((bf16[64,32,128]{2,1,0:T(8,128)(2,1)}, bf16[64,32,128]{2,1,0:T(8,128)(2,1)}, u32[]{:S(2)}, u32[]{:S(2)}) %collective-permute-start.4) | collective-permute-done | bytes 524320 | tf_op jit(solution)/shard_map/ppermute | solution.py:267
  91.5 1.0 copy-done.16
  92.5 1.1 turn.7
  93.7 1.0 copy-done.3
  94.8 1.2 copy-done.4
  96.0 1.0 copy-done.8
  97.0 1.0 copy-done.17
  98.1 1.0 copy-done.19
  99.1 1.0 copy-done.21
  100.2 1.0 copy-done.23
  101.2 1.0 copy-done.25
  102.2 1.0 copy-done.27
  103.3 1.0 copy-done.29
  104.3 1.0 copy-done.31
  105.4 1.0 copy-done.33
  106.4 6.8 %first.1 = (f32[2,2048,128]{2,1,0:T(8,128)S(1)}, f32[2,2048,128]{2,1,0:T(8,128)S(1)}) custom-call(s32[6]{0:T(128)S(1)} %stack.23.where_ref, bf16[2,64,32,128]{3,2,1,0:T(8,128)(2,1)S(1)} %bitcast.12, bf16[64,32,128]{2,1,0:T(8,128)(2,1)S(1)} %copy-done.19, bf16[64,32,128]{2,1,0:T(8,128)(2,1)S(1)} %copy-done.21, bf16[64,32,128]{2,1,0:T(8,128)(2,1)S(1)} %copy-done.8, ...), custom_call_target="tpu_custom_call" | custom-call | tf_op jit(solution)/shard_map/first/pallas_call | solution.py:142
  113.2 8.6 %second.1.refs_7_ = f32[6176,128]{1,0:T(8,128)S(1)} custom-call(s32[6]{0:T(128)S(1)} %stack.23.where_ref, bf16[2,64,32,128]{3,2,1,0:T(8,128)(2,1)S(1)} %bitcast.10, bf16[64,32,128]{2,1,0:T(8,128)(2,1)} %collective-permute-done.3.refs_0_, bf16[64,32,128]{2,1,0:T(8,128)(2,1)} %collective-permute-done.5.refs_1_, bf16[64,32,128]{2,1,0:T(8,128)(2,1)S(1)} %copy-done.10, ...), custom_call_target="tpu_custom_call" | custom-call | tf_op jit(solution)/shard_map/second/pallas_call | solution.py:184
  121.9 9.7 %third.1 = f32[4128,128]{1,0:T(8,128)} custom-call(s32[6]{0:T(128)S(1)} %stack.23.where_ref, bf16[2,64,32,128]{3,2,1,0:T(8,128)(2,1)S(1)} %bitcast.11, bf16[64,32,128]{2,1,0:T(8,128)(2,1)} %collective-permute-done.4.refs_0_, bf16[64,32,128]{2,1,0:T(8,128)(2,1)} %collective-permute-done.6.refs_1_, bf16[64,32,128]{2,1,0:T(8,128)(2,1)} %collective-permute-done.7.refs_2_, ...), custom_call_target="tpu_custom_call" | custom-call | tf_op jit(solution)/shard_map/third/pallas_call | solution.py:232
  (74 shorter events, 1.3 us)
Async XLA Ops:
  0.0 6.4 %copy-start = (bf16[4,32,32,256]{3,2,1,0:T(8,128)(2,1)S(1)}, bf16[4,32,32,256]{3,2,1,0:T(8,128)(2,1)}, u32[]{:S(2)}) copy-start(bf16[4,32,32,256]{3,2,1,0:T(8,128)(2,1)} %raw_ref.5) | copy-start | bytes 6291460
  2.9 15.9 %collective-permute-start.11 = (bf16[64,32,128]{2,1,0:T(8,128)(2,1)}, bf16[64,32,128]{2,1,0:T(8,128)(2,1)S(1)}, u32[]{:S(2)}, u32[]{:S(2)}) collective-permute-start(bf16[64,32,128]{2,1,0:T(8,128)(2,1)} %get-tuple-element.11.refs_0_.refs_2_), channel_id=1, source_target_pairs={{0,4},{2,6},{4,0},{6,2},{8,12},{10,14},{12,8},{14,10},{16,20},{18,... | collective-permute-start | bytes 1572872 | tf_op jit(solution)/shard_map/ppermute | solution.py:263
  5.8 23.4 %collective-permute-start.12 = (bf16[64,32,128]{2,1,0:T(8,128)(2,1)}, bf16[64,32,128]{2,1,0:T(8,128)(2,1)S(1)}, u32[]{:S(2)}, u32[]{:S(2)}) collective-permute-start(bf16[64,32,128]{2,1,0:T(8,128)(2,1)} %get-tuple-element.14.refs_3_), channel_id=1, source_target_pairs={{0,4},{2,6},{4,0},{6,2},{8,12},{10,14},{12,8},{14,10},{16,20},{18,... | collective-permute-start | bytes 1572872 | tf_op jit(solution)/shard_map/ppermute | solution.py:263
  5.9 27.1 %collective-permute-start.13 = (bf16[64,32,128]{2,1,0:T(8,128)(2,1)}, bf16[64,32,128]{2,1,0:T(8,128)(2,1)}, u32[]{:S(2)}, u32[]{:S(2)}) collective-permute-start(bf16[64,32,128]{2,1,0:T(8,128)(2,1)} %get-tuple-element.11.refs_0_.refs_2_), channel_id=1, source_target_pairs={{0,2},{2,0},{4,6},{6,4},{8,10},{10,8},{12,14},{14,12},{16,18},{18,... | collective-permute-start | bytes 1572872 | tf_op jit(solution)/shard_map/ppermute | solution.py:270
  5.9 30.6 %collective-permute-start.14 = (bf16[64,32,128]{2,1,0:T(8,128)(2,1)}, bf16[64,32,128]{2,1,0:T(8,128)(2,1)}, u32[]{:S(2)}, u32[]{:S(2)}) collective-permute-start(bf16[64,32,128]{2,1,0:T(8,128)(2,1)} %get-tuple-element.14.refs_3_), channel_id=1, source_target_pairs={{0,2},{2,0},{4,6},{6,4},{8,10},{10,8},{12,14},{14,12},{16,18},{18,... | collective-permute-start | bytes 1572872 | tf_op jit(solution)/shard_map/ppermute | solution.py:270
  6.4 49.4 %copy-start.1 = (bf16[4,32,32,256]{3,2,1,0:T(8,128)(2,1)S(1)}, bf16[4,32,32,256]{3,2,1,0:T(8,128)(2,1)}, u32[]{:S(2)}) copy-start(bf16[4,32,32,256]{3,2,1,0:T(8,128)(2,1)} %raw_ref.7) | copy-start | bytes 6291460
  6.4 1.2 copy-start.7
  8.7 82.8 %copy-start.2 = (bf16[4,32,32,256]{3,2,1,0:T(8,128)(2,1)S(1)}, bf16[4,32,32,256]{3,2,1,0:T(8,128)(2,1)}, u32[]{:S(2)}) copy-start(bf16[4,32,32,256]{3,2,1,0:T(8,128)(2,1)} %raw_ref.7) | copy-start | bytes 6291460
  8.7 28.6 %collective-permute-start = (bf16[64,32,128]{2,1,0:T(8,128)(2,1)S(1)}, bf16[64,32,128]{2,1,0:T(8,128)(2,1)S(1)}, u32[]{:S(2)}, u32[]{:S(2)}) collective-permute-start(bf16[64,32,128]{2,1,0:T(8,128)(2,1)S(1)} %get-tuple-element.12), channel_id=1, source_target_pairs={{0,1},{1,0},{2,3},{3,2},{4,5},{5,4},{6,7},{7,6},{8,9},{9,8},{10,11... | collective-permute-start | bytes 1572872 | tf_op jit(solution)/shard_map/ppermute | solution.py:260
  18.8 19.8 %collective-permute-start.2 = (bf16[64,32,128]{2,1,0:T(8,128)(2,1)S(1)}, bf16[64,32,128]{2,1,0:T(8,128)(2,1)S(1)}, u32[]{:S(2)}, u32[]{:S(2)}) collective-permute-start(bf16[64,32,128]{2,1,0:T(8,128)(2,1)S(1)} %get-tuple-element.13.refs_0_), channel_id=1, source_target_pairs={{0,1},{1,0},{2,3},{3,2},{4,5},{5,4},{6,7},{7,6},{8,9},{9,8},{10,11... | collective-permute-start | bytes 1572872 | tf_op jit(solution)/shard_map/ppermute | solution.py:260
  29.2 16.1 %collective-permute-start.15 = (bf16[64,32,128]{2,1,0:T(8,128)(2,1)S(1)}, bf16[64,32,128]{2,1,0:T(8,128)(2,1)S(1)}, u32[]{:S(2)}, u32[]{:S(2)}) collective-permute-start(bf16[64,32,128]{2,1,0:T(8,128)(2,1)S(1)} %collective-permute-done.11.refs_0_), channel_id=1, source_target_pairs={{0,8},{2,10},{8,16},{10,18},{12,4},{14,6},{16,24},{18,26},{20,12},... | collective-permute-start | bytes 1572872 | tf_op jit(solution)/shard_map/ppermute | solution.py:267
  32.9 21.5 %collective-permute-start.16 = (bf16[64,32,128]{2,1,0:T(8,128)(2,1)S(1)}, bf16[64,32,128]{2,1,0:T(8,128)(2,1)S(1)}, u32[]{:S(2)}, u32[]{:S(2)}) collective-permute-start(bf16[64,32,128]{2,1,0:T(8,128)(2,1)S(1)} %collective-permute-done.12.refs_1_), channel_id=1, source_target_pairs={{0,8},{2,10},{8,16},{10,18},{12,4},{14,6},{16,24},{18,26},{20,12},... | collective-permute-start | bytes 1572872 | tf_op jit(solution)/shard_map/ppermute | solution.py:267
  36.5 18.0 %collective-permute-start.17 = (bf16[64,32,128]{2,1,0:T(8,128)(2,1)S(1)}, bf16[64,32,128]{2,1,0:T(8,128)(2,1)S(1)}, u32[]{:S(2)}, u32[]{:S(2)}) collective-permute-start(bf16[64,32,128]{2,1,0:T(8,128)(2,1)S(1)} %collective-permute-done.11.refs_0_), channel_id=1, source_target_pairs={{0,2},{2,0},{4,6},{6,4},{8,10},{10,8},{12,14},{14,12},{16,18},{18,... | collective-permute-start | bytes 1572872 | tf_op jit(solution)/shard_map/ppermute | solution.py:270
  37.3 20.2 %copy-start.5 = (bf16[64,32,128]{2,1,0:T(8,128)(2,1)}, bf16[64,32,128]{2,1,0:T(8,128)(2,1)S(1)}, u32[]{:S(2)}) copy-start(bf16[64,32,128]{2,1,0:T(8,128)(2,1)S(1)} %collective-permute-done.refs_0_.refs_3_) | copy-start | bytes 1572868
  37.3 20.2 %collective-permute-start.18 = (bf16[64,32,128]{2,1,0:T(8,128)(2,1)S(1)}, bf16[64,32,128]{2,1,0:T(8,128)(2,1)S(1)}, u32[]{:S(2)}, u32[]{:S(2)}) collective-permute-start(bf16[64,32,128]{2,1,0:T(8,128)(2,1)S(1)} %collective-permute-done.12.refs_1_), channel_id=1, source_target_pairs={{0,2},{2,0},{4,6},{6,4},{8,10},{10,8},{12,14},{14,12},{16,18},{18,... | collective-permute-start | bytes 1572872 | tf_op jit(solution)/shard_map/ppermute | solution.py:270
  38.6 30.3 %copy-start.9 = (bf16[64,32,128]{2,1,0:T(8,128)(2,1)}, bf16[64,32,128]{2,1,0:T(8,128)(2,1)S(1)}, u32[]{:S(2)}) copy-start(bf16[64,32,128]{2,1,0:T(8,128)(2,1)S(1)} %collective-permute-done.2.refs_2_) | copy-start | bytes 1572868
  38.6 21.3 %collective-permute-start.3 = (bf16[64,32,128]{2,1,0:T(8,128)(2,1)S(1)}, bf16[64,32,128]{2,1,0:T(8,128)(2,1)}, u32[]{:S(2)}, u32[]{:S(2)}) collective-permute-start(bf16[64,32,128]{2,1,0:T(8,128)(2,1)S(1)} %collective-permute-done.2.refs_2_), channel_id=1, source_target_pairs={{0,4},{2,6},{4,0},{6,2},{8,12},{10,14},{12,8},{14,10},{16,20},{18,... | collective-permute-start | bytes 1572872 | tf_op jit(solution)/shard_map/ppermute | solution.py:263
  45.3 26.6 %copy-start.22 = (bf16[64,32,128]{2,1,0:T(8,128)(2,1)}, bf16[64,32,128]{2,1,0:T(8,128)(2,1)S(1)}, u32[]{:S(2)}) copy-start(bf16[64,32,128]{2,1,0:T(8,128)(2,1)S(1)} %collective-permute-done.15.refs_6_) | copy-start | bytes 1572868
  45.3 18.6 %collective-permute-start.5 = (bf16[64,32,128]{2,1,0:T(8,128)(2,1)S(1)}, bf16[64,32,128]{2,1,0:T(8,128)(2,1)}, u32[]{:S(2)}, u32[]{:S(2)}) collective-permute-start(bf16[64,32,128]{2,1,0:T(8,128)(2,1)S(1)} %collective-permute-done.refs_0_.refs_3_), channel_id=1, source_target_pairs={{0,4},{2,6},{4,0},{6,2},{8,12},{10,14},{12,8},{14,10},{16,20},{18,... | collective-permute-start | bytes 1572872 | tf_op jit(solution)/shard_map/ppermute | solution.py:263
  54.4 17.4 %copy-start.24 = (bf16[64,32,128]{2,1,0:T(8,128)(2,1)}, bf16[64,32,128]{2,1,0:T(8,128)(2,1)S(1)}, u32[]{:S(2)}) copy-start(bf16[64,32,128]{2,1,0:T(8,128)(2,1)S(1)} %collective-permute-done.16.refs_7_) | copy-start | bytes 1572868
  54.4 9.4 %collective-permute-start.21 = (bf16[64,32,128]{2,1,0:T(8,128)(2,1)S(1)}, bf16[64,32,128]{2,1,0:T(8,128)(2,1)S(1)}, u32[]{:S(2)}, u32[]{:S(2)}) collective-permute-start(bf16[64,32,128]{2,1,0:T(8,128)(2,1)S(1)} %collective-permute-done.2.refs_2_), channel_id=1, source_target_pairs={{0,2},{2,0},{4,6},{6,4},{8,10},{10,8},{12,14},{14,12},{16,18},{18,... | collective-permute-start | bytes 1572872 | tf_op jit(solution)/shard_map/ppermute | solution.py:270
  55.3 13.6 %collective-permute-start.22 = (bf16[64,32,128]{2,1,0:T(8,128)(2,1)S(1)}, bf16[64,32,128]{2,1,0:T(8,128)(2,1)S(1)}, u32[]{:S(2)}, u32[]{:S(2)}) collective-permute-start(bf16[64,32,128]{2,1,0:T(8,128)(2,1)S(1)} %collective-permute-done.refs_0_.refs_3_), channel_id=1, source_target_pairs={{0,2},{2,0},{4,6},{6,4},{8,10},{10,8},{12,14},{14,12},{16,18},{18,... | collective-permute-start | bytes 1572872 | tf_op jit(solution)/shard_map/ppermute | solution.py:270
  58.4 54.8 %collective-permute-start.1 = (bf16[128,32,128]{2,1,0:T(8,128)(2,1)}, bf16[128,32,128]{2,1,0:T(8,128)(2,1)S(1)}, u32[]{:S(2)}, u32[]{:S(2)}) collective-permute-start(bf16[128,32,128]{2,1,0:T(8,128)(2,1)} %turn.6), channel_id=1, source_target_pairs={{0,1},{1,0},{2,3},{3,2},{4,5},{5,4},{6,7},{7,6},{8,9},{9,8},{10,11... | collective-permute-start | bytes 3145736 | tf_op jit(solution)/shard_map/ppermute | solution.py:260
  59.9 11.9 %collective-permute-start.19 = (bf16[64,32,128]{2,1,0:T(8,128)(2,1)S(1)}, bf16[64,32,128]{2,1,0:T(8,128)(2,1)S(1)}, u32[]{:S(2)}, u32[]{:S(2)}) collective-permute-start(bf16[64,32,128]{2,1,0:T(8,128)(2,1)S(1)} %collective-permute-done.15.refs_6_), channel_id=1, source_target_pairs={{0,2},{2,0},{4,6},{6,4},{8,10},{10,8},{12,14},{14,12},{16,18},{18,... | collective-permute-start | bytes 1572872 | tf_op jit(solution)/shard_map/ppermute | solution.py:270
  63.9 9.0 %collective-permute-start.20 = (bf16[64,32,128]{2,1,0:T(8,128)(2,1)S(1)}, bf16[64,32,128]{2,1,0:T(8,128)(2,1)S(1)}, u32[]{:S(2)}, u32[]{:S(2)}) collective-permute-start(bf16[64,32,128]{2,1,0:T(8,128)(2,1)S(1)} %collective-permute-done.16.refs_7_), channel_id=1, source_target_pairs={{0,2},{2,0},{4,6},{6,4},{8,10},{10,8},{12,14},{14,12},{16,18},{18,... | collective-permute-start | bytes 1572872 | tf_op jit(solution)/shard_map/ppermute | solution.py:270
  64.7 16.0 %collective-permute-start.6 = (bf16[64,32,128]{2,1,0:T(8,128)(2,1)}, bf16[64,32,128]{2,1,0:T(8,128)(2,1)}, u32[]{:S(2)}, u32[]{:S(2)}) collective-permute-start(bf16[64,32,128]{2,1,0:T(8,128)(2,1)} %collective-permute-done.5.refs_1_), channel_id=1, source_target_pairs={{0,8},{2,10},{8,16},{10,18},{12,4},{14,6},{16,24},{18,26},{20,12},... | collective-permute-start | bytes 1572872 | tf_op jit(solution)/shard_map/ppermute | solution.py:267
  69.7 21.8 %collective-permute-start.4 = (bf16[64,32,128]{2,1,0:T(8,128)(2,1)}, bf16[64,32,128]{2,1,0:T(8,128)(2,1)}, u32[]{:S(2)}, u32[]{:S(2)}) collective-permute-start(bf16[64,32,128]{2,1,0:T(8,128)(2,1)} %collective-permute-done.3.refs_0_), channel_id=1, source_target_pairs={{0,8},{2,10},{8,16},{10,18},{12,4},{14,6},{16,24},{18,26},{20,12},... | collective-permute-start | bytes 1572872 | tf_op jit(solution)/shard_map/ppermute | solution.py:267
  72.6 49.2 %collective-permute-start.7 = (bf16[64,32,128]{2,1,0:T(8,128)(2,1)}, bf16[64,32,128]{2,1,0:T(8,128)(2,1)}, u32[]{:S(2)}, u32[]{:S(2)}) collective-permute-start(bf16[64,32,128]{2,1,0:T(8,128)(2,1)} %collective-permute-done.3.refs_0_), channel_id=1, source_target_pairs={{0,2},{2,0},{4,6},{6,4},{8,10},{10,8},{12,14},{14,12},{16,18},{18,... | collective-permute-start | bytes 1572872 | tf_op jit(solution)/shard_map/ppermute | solution.py:270
  73.7 48.2 %collective-permute-start.8 = (bf16[64,32,128]{2,1,0:T(8,128)(2,1)}, bf16[64,32,128]{2,1,0:T(8,128)(2,1)}, u32[]{:S(2)}, u32[]{:S(2)}) collective-permute-start(bf16[64,32,128]{2,1,0:T(8,128)(2,1)} %collective-permute-done.5.refs_1_), channel_id=1, source_target_pairs={{0,2},{2,0},{4,6},{6,4},{8,10},{10,8},{12,14},{14,12},{16,18},{18,... | collective-permute-start | bytes 1572872 | tf_op jit(solution)/shard_map/ppermute | solution.py:270
  80.6 41.2 %collective-permute-start.10 = (bf16[64,32,128]{2,1,0:T(8,128)(2,1)}, bf16[64,32,128]{2,1,0:T(8,128)(2,1)}, u32[]{:S(2)}, u32[]{:S(2)}) collective-permute-start(bf16[64,32,128]{2,1,0:T(8,128)(2,1)} %collective-permute-done.6.refs_1_), channel_id=1, source_target_pairs={{0,2},{2,0},{4,6},{6,4},{8,10},{10,8},{12,14},{14,12},{16,18},{18,... | collective-permute-start | bytes 1572872 | tf_op jit(solution)/shard_map/ppermute | solution.py:270
  91.5 30.4 %collective-permute-start.9 = (bf16[64,32,128]{2,1,0:T(8,128)(2,1)}, bf16[64,32,128]{2,1,0:T(8,128)(2,1)}, u32[]{:S(2)}, u32[]{:S(2)}) collective-permute-start(bf16[64,32,128]{2,1,0:T(8,128)(2,1)} %collective-permute-done.4.refs_0_), channel_id=1, source_target_pairs={{0,2},{2,0},{4,6},{6,4},{8,10},{10,8},{12,14},{14,12},{16,18},{18,... | collective-permute-start | bytes 1572872 | tf_op jit(solution)/shard_map/ppermute | solution.py:270
  91.5 1.0 copy-start.16
  93.6 1.0 copy-start.3
  94.8 1.2 copy-start.4
  96.0 1.0 copy-start.8
  97.0 1.0 copy-start.17
  98.1 1.0 copy-start.19
  99.1 1.0 copy-start.21
  100.1 1.0 copy-start.23
  101.2 1.0 copy-start.25
  102.2 1.0 copy-start.27
  103.3 1.0 copy-start.29
  104.3 1.0 copy-start.31
  105.4 1.0 copy-start.33
  106.4 6.8 %copy-start.6 = (bf16[64,32,128]{2,1,0:T(8,128)(2,1)S(1)}, bf16[64,32,128]{2,1,0:T(8,128)(2,1)}, u32[]{:S(2)}) copy-start(bf16[64,32,128]{2,1,0:T(8,128)(2,1)} %copy-done.5) | copy-start | bytes 1572868
  106.4 6.8 %copy-start.10 = (bf16[64,32,128]{2,1,0:T(8,128)(2,1)S(1)}, bf16[64,32,128]{2,1,0:T(8,128)(2,1)}, u32[]{:S(2)}) copy-start(bf16[64,32,128]{2,1,0:T(8,128)(2,1)} %copy-done.9) | copy-start | bytes 1572868
  106.4 6.8 %copy-start.12 = (bf16[64,32,128]{2,1,0:T(8,128)(2,1)S(1)}, bf16[64,32,128]{2,1,0:T(8,128)(2,1)}, u32[]{:S(2)}) copy-start(bf16[64,32,128]{2,1,0:T(8,128)(2,1)} %copy-done.11) | copy-start | bytes 1572868
  106.4 6.8 %copy-start.14 = (bf16[64,32,128]{2,1,0:T(8,128)(2,1)S(1)}, bf16[64,32,128]{2,1,0:T(8,128)(2,1)}, u32[]{:S(2)}) copy-start(bf16[64,32,128]{2,1,0:T(8,128)(2,1)} %copy-done.13) | copy-start | bytes 1572868
  (9 other events, 7.3 us)

commit v3 on v1

v3 whole, which is shorter than its diff:
```python
import functools

import jax
import jax.numpy as jnp
from jax import lax
from jax.experimental import pallas as pl
from jax.experimental.pallas import tpu as pltpu
from jax.sharding import PartitionSpec as P

LANES = 128
ROWS = 16
VMEM_BYTES = 16 * 1024 * 1024


def shifted(value, axis, steps):
    count = lax.axis_size(axis)
    initial, last = (max(0, -steps), min(count, count - steps))
    return lax.ppermute(value, axis, [(source, source + steps) for source in range(initial, last)])


def band_rows(product, width, lags):
    rows = product.shape[0]
    cross = product.shape[2]
    flat = product.reshape(rows * width, cross)
    flat = jnp.pad(flat, ((0, rows), (0, 0)))
    skewed = flat.reshape(rows, width + 1, cross)[:, :lags, :]
    return jnp.transpose(skewed, (1, 0, 2))


def plain(source, receiver, scale):
    source, receiver = (
        lax.all_to_all(value, "shot", split_axis=3, concat_axis=0, tiled=True) for value in (source, receiver)
    )
    cells = source.shape[1]
    slabs = [receiver if step == 0 else shifted(receiver, "inline", -step) for step in (-2, -1, 0, 1, 2)]
    width = 5 * cells
    product = jnp.einsum(
        "sity,szty->izy", source, jnp.concatenate(slabs, axis=1), preferred_element_type=jnp.float32
    )
    return band_rows(product, width, 4 * cells + 1) * scale


def turn_body(which_ref, raw_ref, *refs):
    own_ref, other_ref, rows_ref = refs[-3:]
    shots, cells, times, cross = raw_ref.shape
    for cell in range(cells):
        tile = raw_ref[:, cell].reshape(shots * times, cross).astype(jnp.float32)
        rows_ref[pl.ds(cell, cross, stride=cells), :] = tile.T
    share = cross // 2 * cells
    for turned_ref, part in ((own_ref, which_ref[1]), (other_ref, 1 - which_ref[1])):
        rows = rows_ref[pl.ds(pl.multiple_of(part * share, share), share), :]
        turned_ref[...] = rows.reshape(turned_ref.shape).astype(turned_ref.dtype)


def turn(raw, half, core):
    shots, cells, times, _ = raw.shape
    depth = shots * times
    share = LANES // 2
    return pl.pallas_call(
        turn_body,
        grid_spec=pltpu.PrefetchScalarGridSpec(
            num_scalar_prefetch=1,
            grid=(cells // ROWS,),
            in_specs=[pl.BlockSpec((shots, ROWS, times, LANES), lambda step, which: (0, step, 0, which[0]))],
            out_specs=[pl.BlockSpec((share, ROWS, depth), lambda step, which: (0, step, 0))] * 2,
            scratch_shapes=[pltpu.VMEM((LANES * ROWS, depth), jnp.float32)],
        ),
        out_shape=[jax.ShapeDtypeStruct((share, cells, depth), raw.dtype)] * 2,
        compiler_params=pltpu.CompilerParams(vmem_limit_bytes=VMEM_BYTES),
        cost_estimate=pl.CostEstimate(flops=0, bytes_accessed=raw.size * 2, transcendentals=0),
        name="turn",
    )(jnp.stack([half, core]).astype(jnp.int32), raw)


DIMS = (((1,), (1,)), ((), ()))
BLOCK = 16


def multiply_body(slabs, core_ref, *refs):
    sources, pieces, rest = refs[:2], refs[2 : 2 + slabs], refs[2 + slabs :]
    right_ref = rest[-1]
    groups = (slabs * sources[0].shape[1] + LANES - 1) // LANES
    kept, sent = rest[-1 - 2 * groups : -1 - groups], rest[-1 - groups : -1]
    before = rest[: -1 - 2 * groups]
    block, cells, _ = sources[0].shape
    for place, piece in enumerate(pieces):
        side, other = divmod(place, 2)
        right_ref[2 * side + (core_ref[0] if other == 0 else 1 - core_ref[0])] = piece[...]
    for cross in range(block):
        left = jnp.concatenate([source[cross] for source in sources], axis=0)
        rows = pl.ds(cross * cells, cells)
        for group in range(groups):
            members = range(group * LANES // cells, min(slabs, (group + 1) * LANES // cells))
            right = jnp.concatenate([right_ref[slab, cross] for slab in members], axis=0)
            width = len(members) * cells
            value = lax.dot_general(left, right, DIMS, preferred_element_type=jnp.float32)
            for out, part in ((kept[group], value[:cells]), (sent[group], value[cells:])):
                if before:
                    part = part + before[group if out is kept[group] else groups + group][rows, :width]
                out[rows, :width] = part


def multiply(core, sources, pieces, before=()):
    share, cells, depth = sources[0].shape
    slabs = len(pieces)
    groups = -(-slabs * cells // LANES)
    slab = pl.BlockSpec((BLOCK, cells, depth), lambda step, core: (step, 0, 0))
    products = pl.BlockSpec((BLOCK * cells, LANES), lambda step, core: (step, 0))
    flops = 2 * share * 2 * cells * slabs * cells * depth
    return pl.pallas_call(
        functools.partial(multiply_body, slabs),
        grid_spec=pltpu.PrefetchScalarGridSpec(
            num_scalar_prefetch=1,
            grid=(share // BLOCK,),
            in_specs=[slab] * (2 + slabs) + [products] * len(before),
            out_specs=[products] * (2 * groups),
            scratch_shapes=[pltpu.VMEM((slabs, BLOCK, cells, depth), sources[0].dtype)],
        ),
        out_shape=[jax.ShapeDtypeStruct((share * cells, LANES), jnp.float32)] * (2 * groups),
        compiler_params=pltpu.CompilerParams(vmem_limit_bytes=VMEM_BYTES),
        cost_estimate=pl.CostEstimate(flops=flops, bytes_accessed=4 << 20, transcendentals=0),
        name="multiply",
    )(core.reshape(1), *sources, *pieces, *before)


def spread_body(scale, cells, where_ref, *refs):
    products, image_ref, skewed_ref, sem = refs[:4], *refs[4:]
    core = where_ref[6]
    for cell in range(cells):
        for group, count in ((0, 4), (1, 2)):
            kept, came = (ref[pl.ds(cell, LANES // 2, stride=cells), :] for ref in products[2 * group : 2 * group + 2])
            low = jnp.where(core == 0, kept, came)
            high = jnp.where(core == 0, came, kept)
            turned = jnp.concatenate([low, high], axis=0).T * scale
            for place in range(count):
                lag = (where_ref[4 * group + place] + 4) * cells - cell
                skewed_ref[pl.ds(lag * cells + cell, cells, stride=cells), :] = turned[
                    cells * place : cells * (place + 1)
                ]
    copy = pltpu.make_async_copy(skewed_ref.at[pl.ds(2 * cells * cells, image_ref.shape[0])], image_ref, sem)
    copy.start()
    copy.wait()


def spread(scale, cells, where, products):
    lags = 4 * cells + 1
    return pl.pallas_call(
        functools.partial(spread_body, scale, cells),
        grid_spec=pltpu.PrefetchScalarGridSpec(
            num_scalar_prefetch=1,
            grid=(1,),
            in_specs=[pl.BlockSpec(products[0].shape, lambda step, where: (0, 0))] * 4,
            out_specs=pl.BlockSpec(memory_space=pl.ANY),
            scratch_shapes=[
                pltpu.VMEM(((lags + 4 * cells) * cells, LANES), jnp.float32),
                pltpu.SemaphoreType.DMA(()),
            ],
        ),
        out_shape=jax.ShapeDtypeStruct((lags * cells, LANES), jnp.float32),
        compiler_params=pltpu.CompilerParams(vmem_limit_bytes=VMEM_BYTES),
        name="spread",
    )(where, *products).reshape(lags, cells, LANES)


def routed(source, receiver, scale):
    count = lax.axis_size("inline")
    cells = source.shape[1]
    own = lax.axis_index("inline")
    core, odd = own & 1, (own >> 1) & 1
    half = lax.axis_index("shot")

    def across(value):
        return lax.ppermute(value, "shot", [(0, 1), (1, 0)])

    def along_y(value):
        return lax.ppermute(value, "inline", [(index, index ^ 2) for index in range(count)])

    def along_z(value):
        pairs = [(index, index + (4 if index // 2 % 2 == 0 else -4)) for index in range(count)]
        return lax.ppermute(value, "inline", [pair for pair in pairs if 0 <= pair[1] < count])

    def to_core(value):
        return lax.ppermute(value, "inline", [(index, index ^ 1) for index in range(count)])

    def across_to_core(value):
        pairs = [(2 * index + side, 2 * (index ^ 1) + 1 - side) for index in range(count) for side in range(2)]
        return lax.ppermute(value, ("inline", "shot"), pairs)

    def barrier(*values):
        return lax.optimization_barrier(values)

    kept, lent = turn(receiver, half, core)
    y0 = along_y(kept)
    twin = to_core(lent)
    receiver, _ = barrier(receiver, kept)
    there, there_twin = turn(receiver, 1 - half, core)
    moved, moved_twin = across(there), across_to_core(there_twin)
    source, _ = barrier(source, there)
    left, left_lent = turn(source, half, core)
    far, far_lent = turn(source, 1 - half, core)
    left_twin = to_core(left_lent)
    y1 = along_y(twin)
    moved, y0 = barrier(moved, y0)
    y2, z0 = along_y(moved), along_z(y0)
    moved_twin, y1, far, far_lent = barrier(moved_twin, y1, far, far_lent)
    y3, z1 = along_y(moved_twin), along_z(y1)
    right, right_twin = across(far), across_to_core(far_lent)
    z2 = along_z(y2)
    z3 = along_z(y3)
    early = multiply(core, (left, left_twin), (kept, twin, y0, y1, z0, z1))
    middle = multiply(core, (right, right_twin), (moved, moved_twin, y2, y3), (early[0], early[2]))
    middle_came = to_core(middle[1])
    late = multiply(core, (right, right_twin), (z2, z3), (early[1], early[3]))
    late_came = to_core(late[1])
    side = 2 - 4 * odd
    where = jnp.stack([block + shift - core for shift in (0, side, -side) for block in (0, 1)] + [core])
    return spread(scale, cells, where.astype(jnp.int32), (middle[0], middle_came, late[0], late_came))


def on_device(source, receiver):
    shots, cells, times, cross = source.shape
    groups, count = lax.axis_size("shot"), lax.axis_size("inline")
    scale = 1.0 / (times * shots * groups) ** 0.5
    fits = (
        groups == 2
        and count % 4 == 0
        and cross == 2 * LANES
        and shots * times == LANES
        and 4 * cells == LANES
        and times % ROWS == 0
    )
    return routed(source, receiver, scale) if fits else plain(source, receiver, scale)


def solution(mesh):
    placed = (P("shot", "inline", None, None), P("shot", "inline", None, None))
    return jax.shard_map(
        on_device, mesh=mesh, in_specs=placed, out_specs=P(None, "inline", "shot"), check_vma=False
    )
```

time: 122 us -> 85.4 us (0.70)
  waiting for transfers between devices: 75.6 us -> 38.5 us
  starting transfers between devices: 16.1 us -> 21.9 us
  other arithmetic: 4.85 us -> 0.07 us
  local copies, waits for them, and re-layouts: 5.01 us -> 1.68 us
  Pallas kernels: 19.8 us -> 22.8 us
    ppermute x2, waiting for transfers between devices: 37 us -> 8.86 us  [across(): return lax.ppermute(value, 'shot', [(0, 1), (1, 0)])]
    ppermute x2 -> x4, waiting for transfers between devices: 18.9 us -> 6.2 us  [along_z(): lax.ppermute(value, 'inline', [pair for pair in pairs if 0 <= pair[1] < c...]
    ppermute x2 -> x4, starting transfers between devices: 8.07 us -> 14 us  [along_z(): lax.ppermute(value, 'inline', [pair for pair in pairs if 0 <= pair[1] < c...]
    select_n x2 -> x0, other arithmetic: 4.85 us -> none  [routed(): shared = jnp.where(core == odd, to_core(from_z), to_core(from_y))]
    ppermute x0 -> x2, waiting for transfers between devices: none -> 3.58 us  [across_to_core(): return lax.ppermute(value, ('inline', 'shot'), pairs)]
    unnamed x22 -> x6, local copies, waits for them, and re-layouts: 4.93 us -> 1.6 us
    ppermute x6 -> x4, waiting for transfers between devices: 0.02 us -> 2.92 us  [to_core(): lax.ppermute(value, 'inline', [(index, index ^ 1) for index in range(coun...]
    ppermute x2 -> x4, waiting for transfers between devices: 19.7 us -> 17 us  [along_y(): lax.ppermute(value, 'inline', [(index, index ^ 2) for index in range(coun...]
  transfers between devices with their start and end apart: 12 -> 16, of which waited for: 5 -> 8; matrix products, arithmetic and copies ran while one was open for 4% -> 0% of each run, Pallas kernels for 3% -> 15%
where the time goes in v3:
time: 85.4 us; the launch traced here: 85.1 us
  waiting for transfers between devices  38.5 us (45%)
  Pallas kernels  22.8 us (27%)
  starting transfers between devices  21.9 us (26%)
  local copies, waits for them, and re-layouts  1.68 us (2%)
    ppermute x4, waiting for transfers between devices, along_y(): lax.ppermute(value, 'inline', [(index, index ^ 2) for index in range(coun...  17 us
    ppermute x4, starting transfers between devices, along_z(): lax.ppermute(value, 'inline', [pair for pair in pairs if 0 <= pair[1] < c...  14 us
    ppermute x2, waiting for transfers between devices, across(): return lax.ppermute(value, 'shot', [(0, 1), (1, 0)])  8.86 us
    pallas_call x1, Pallas kernels, spread(): pl.pallas_call(functools.partial(spread_body, scale, cells), grid_spec=pl...  8.57 us
    pallas_call x3, Pallas kernels, multiply(): pl.pallas_call(functools.partial(multiply_body, slabs), grid_spec=pltpu.P...  7.57 us
    pallas_call x4, Pallas kernels, turn(): pl.pallas_call(turn_body, grid_spec=pltpu.PrefetchScalarGridSpec(num_scal...  6.65 us
    ppermute x4, waiting for transfers between devices, along_z(): lax.ppermute(value, 'inline', [pair for pair in pairs if 0 <= pair[1] < c...  6.2 us
    ppermute x2, waiting for transfers between devices, across_to_core(): return lax.ppermute(value, ('inline', 'shot'), pairs)  3.58 us
  transfers between devices with their start and end apart: 16, of which 8 were waited for; matrix products, arithmetic and copies ran while one was open for 0% of the time, Pallas kernels for 15%

profile of v3, /device:TPU:0, one launch (start us, length us, event | category | flops | bytes accessed | tf_op | source)
XLA Modules:
  0.0 85.1 jit_solution(7566655963937740971)
XLA Ops:
  0.0 0.1 pad_add_fusion
  0.1 0.0 copy-start
  0.1 1.6 %copy-done = bf16[4,32,32,256]{3,2,1,0:T(8,128)(2,1)S(1)} copy-done((bf16[4,32,32,256]{3,2,1,0:T(8,128)(2,1)S(1)}, bf16[4,32,32,256]{3,2,1,0:T(8,128)(2,1)}, u32[]{:S(2)}) %copy-start) | copy-done | bytes 2097176
  1.7 0.0 copy-start.1
  1.7 0.0 copy-start.2
  1.7 1.7 %turn.4 = (bf16[64,32,128]{2,1,0:T(8,128)(2,1)S(1)}, bf16[64,32,128]{2,1,0:T(8,128)(2,1)S(1)}) custom-call(s32[2]{0:T(128)S(1)} %get-tuple-element.54.which_ref, bf16[4,32,32,256]{3,2,1,0:T(8,128)(2,1)S(1)} %copy-done), custom_call_target="tpu_custom_call" | custom-call | bytes 2097152 | tf_op jit(solution)/shard_map/turn/pallas_call | solution.py:59
  3.3 0.5 collective-permute-start.1
  3.9 0.0 copy-done.1
  3.9 1.7 %turn.5 = (bf16[64,32,128]{2,1,0:T(8,128)(2,1)S(1)}, bf16[64,32,128]{2,1,0:T(8,128)(2,1)S(1)}) custom-call(s32[2]{0:T(128)S(1)} %get-tuple-element.53.which_ref, bf16[4,32,32,256]{3,2,1,0:T(8,128)(2,1)S(1)} %copy-done.1), custom_call_target="tpu_custom_call" | custom-call | bytes 2097152 | tf_op jit(solution)/shard_map/turn/pallas_call | solution.py:59
  5.5 2.6 %collective-permute-start.5 = (bf16[64,32,128]{2,1,0:T(8,128)(2,1)S(1)}, bf16[64,32,128]{2,1,0:T(8,128)(2,1)S(1)}, u32[]{:S(2)}, u32[]{:S(2)}) collective-permute-start(bf16[64,32,128]{2,1,0:T(8,128)(2,1)S(1)} %get-tuple-element.33), channel_id=1, source_target_pairs={{0,1},{1,0},{2,3},{3,2},{4,5},{5,4},{6,7},{7,6},{8,9},{9,8},{10,11... | collective-permute-start | bytes 1572872 | tf_op jit(solution)/shard_map/ppermute | solution.py:173
  8.1 1.5 %collective-permute-start.6 = (bf16[64,32,128]{2,1,0:T(8,128)(2,1)S(1)}, bf16[64,32,128]{2,1,0:T(8,128)(2,1)S(1)}, u32[]{:S(2)}, u32[]{:S(2)}) collective-permute-start(bf16[64,32,128]{2,1,0:T(8,128)(2,1)S(1)} %get-tuple-element.29.refs_2_), channel_id=1, source_target_pairs={{0,4},{2,6},{4,0},{6,2},{8,12},{10,14},{12,8},{14,10},{16,20},{18,... | collective-permute-start | bytes 1572872 | tf_op jit(solution)/shard_map/ppermute | solution.py:176
  9.6 0.1 collective-permute-start
  9.7 0.0 collective-permute-done.1.refs_3_
  9.7 0.4 collective-permute-start.2
  10.1 0.0 copy-done.2
  10.1 1.7 %turn.7 = (bf16[64,32,128]{2,1,0:T(8,128)(2,1)S(1)}, bf16[64,32,128]{2,1,0:T(8,128)(2,1)S(1)}) custom-call(s32[2]{0:T(128)S(1)} %get-tuple-element.54.which_ref, bf16[4,32,32,256]{3,2,1,0:T(8,128)(2,1)S(1)} %copy-done.2), custom_call_target="tpu_custom_call" | custom-call | bytes 2097152 | tf_op jit(solution)/shard_map/turn/pallas_call | solution.py:59
  11.8 0.2 collective-permute-start.9
  12.0 8.9 %collective-permute-done.5.refs_2_ = bf16[64,32,128]{2,1,0:T(8,128)(2,1)S(1)} collective-permute-done((bf16[64,32,128]{2,1,0:T(8,128)(2,1)S(1)}, bf16[64,32,128]{2,1,0:T(8,128)(2,1)S(1)}, u32[]{:S(2)}, u32[]{:S(2)}) %collective-permute-start.5) | collective-permute-done | bytes 524320 | tf_op jit(solution)/shard_map/ppermute | solution.py:173
  20.9 2.0 %collective-permute-done.6.refs_4_ = bf16[64,32,128]{2,1,0:T(8,128)(2,1)S(1)} collective-permute-done((bf16[64,32,128]{2,1,0:T(8,128)(2,1)S(1)}, bf16[64,32,128]{2,1,0:T(8,128)(2,1)S(1)}, u32[]{:S(2)}, u32[]{:S(2)}) %collective-permute-start.6) | collective-permute-done | bytes 524320 | tf_op jit(solution)/shard_map/ppermute | solution.py:176
  22.9 3.5 %collective-permute-start.10 = (bf16[64,32,128]{2,1,0:T(8,128)(2,1)S(1)}, bf16[64,32,128]{2,1,0:T(8,128)(2,1)S(1)}, u32[]{:S(2)}, u32[]{:S(2)}) collective-permute-start(bf16[64,32,128]{2,1,0:T(8,128)(2,1)S(1)} %collective-permute-done.6.refs_4_), channel_id=1, source_target_pairs={{0,8},{2,10},{8,16},{10,18},{12,4},{14,6},{16,24},{18,26},{20,12},... | collective-permute-start | bytes 1572872 | tf_op jit(solution)/shard_map/ppermute | solution.py:180
  26.4 1.7 %turn.6 = (bf16[64,32,128]{2,1,0:T(8,128)(2,1)S(1)}, bf16[64,32,128]{2,1,0:T(8,128)(2,1)S(1)}) custom-call(s32[2]{0:T(128)S(1)} %get-tuple-element.53.which_ref, bf16[4,32,32,256]{3,2,1,0:T(8,128)(2,1)S(1)} %copy-done.2), custom_call_target="tpu_custom_call" | custom-call | bytes 2097152 | tf_op jit(solution)/shard_map/turn/pallas_call | solution.py:59
  28.1 0.1 collective-permute-start.7
  28.1 3.6 %collective-permute-done.refs_3_ = bf16[64,32,128]{2,1,0:T(8,128)(2,1)S(1)} collective-permute-done((bf16[64,32,128]{2,1,0:T(8,128)(2,1)S(1)}, bf16[64,32,128]{2,1,0:T(8,128)(2,1)S(1)}, u32[]{:S(2)}, u32[]{:S(2)}) %collective-permute-start) | collective-permute-done | bytes 524320 | tf_op jit(solution)/shard_map/ppermute | solution.py:187
  31.7 2.4 %collective-permute-done.2.refs_5_ = bf16[64,32,128]{2,1,0:T(8,128)(2,1)S(1)} collective-permute-done((bf16[64,32,128]{2,1,0:T(8,128)(2,1)S(1)}, bf16[64,32,128]{2,1,0:T(8,128)(2,1)S(1)}, u32[]{:S(2)}, u32[]{:S(2)}) %collective-permute-start.2) | collective-permute-done | bytes 524320 | tf_op jit(solution)/shard_map/ppermute | solution.py:176
  34.1 1.5 %collective-permute-start.8 = (bf16[64,32,128]{2,1,0:T(8,128)(2,1)S(1)}, bf16[64,32,128]{2,1,0:T(8,128)(2,1)S(1)}, u32[]{:S(2)}, u32[]{:S(2)}) collective-permute-start(bf16[64,32,128]{2,1,0:T(8,128)(2,1)S(1)} %collective-permute-done.refs_3_), channel_id=1, source_target_pairs={{0,4},{2,6},{4,0},{6,2},{8,12},{10,14},{12,8},{14,10},{16,20},{18,... | collective-permute-start | bytes 1572872 | tf_op jit(solution)/shard_map/ppermute | solution.py:176
  35.6 3.5 %collective-permute-start.11 = (bf16[64,32,128]{2,1,0:T(8,128)(2,1)S(1)}, bf16[64,32,128]{2,1,0:T(8,128)(2,1)S(1)}, u32[]{:S(2)}, u32[]{:S(2)}) collective-permute-start(bf16[64,32,128]{2,1,0:T(8,128)(2,1)S(1)} %collective-permute-done.2.refs_5_), channel_id=1, source_target_pairs={{0,8},{2,10},{8,16},{10,18},{12,4},{14,6},{16,24},{18,26},{20,12},... | collective-permute-start | bytes 1572872 | tf_op jit(solution)/shard_map/ppermute | solution.py:180
  39.1 0.0 collective-permute-done.9.refs_1_
  39.1 0.6 collective-permute-start.3
  39.7 0.0 collective-permute-done.10.refs_6_
  39.7 0.0 collective-permute-start.4
  39.8 5.6 %collective-permute-done.7.refs_4_ = bf16[64,32,128]{2,1,0:T(8,128)(2,1)S(1)} collective-permute-done((bf16[64,32,128]{2,1,0:T(8,128)(2,1)S(1)}, bf16[64,32,128]{2,1,0:T(8,128)(2,1)S(1)}, u32[]{:S(2)}, u32[]{:S(2)}) %collective-permute-start.7) | collective-permute-done | bytes 524320 | tf_op jit(solution)/shard_map/ppermute | solution.py:176
  45.3 3.5 %collective-permute-start.13 = (bf16[64,32,128]{2,1,0:T(8,128)(2,1)S(1)}, bf16[64,32,128]{2,1,0:T(8,128)(2,1)S(1)}, u32[]{:S(2)}, u32[]{:S(2)}) collective-permute-start(bf16[64,32,128]{2,1,0:T(8,128)(2,1)S(1)} %collective-permute-done.7.refs_4_), channel_id=1, source_target_pairs={{0,8},{2,10},{8,16},{10,18},{12,4},{14,6},{16,24},{18,26},{20,12},... | collective-permute-start | bytes 1572872 | tf_op jit(solution)/shard_map/ppermute | solution.py:180
  48.9 7.0 %collective-permute-done.8.refs_5_ = bf16[64,32,128]{2,1,0:T(8,128)(2,1)S(1)} collective-permute-done((bf16[64,32,128]{2,1,0:T(8,128)(2,1)S(1)}, bf16[64,32,128]{2,1,0:T(8,128)(2,1)S(1)}, u32[]{:S(2)}, u32[]{:S(2)}) %collective-permute-start.8) | collective-permute-done | bytes 524320 | tf_op jit(solution)/shard_map/ppermute | solution.py:176
  55.8 3.5 %collective-permute-start.14 = (bf16[64,32,128]{2,1,0:T(8,128)(2,1)S(1)}, bf16[64,32,128]{2,1,0:T(8,128)(2,1)S(1)}, u32[]{:S(2)}, u32[]{:S(2)}) collective-permute-start(bf16[64,32,128]{2,1,0:T(8,128)(2,1)S(1)} %collective-permute-done.8.refs_5_), channel_id=1, source_target_pairs={{0,8},{2,10},{8,16},{10,18},{12,4},{14,6},{16,24},{18,26},{20,12},... | collective-permute-start | bytes 1572872 | tf_op jit(solution)/shard_map/ppermute | solution.py:180
  59.4 0.0 collective-permute-done.11.refs_7_
  59.4 2.4 %multiply.3 = (f32[2048,128]{1,0:T(8,128)S(1)}, f32[2048,128]{1,0:T(8,128)S(1)}, f32[2048,128]{1,0:T(8,128)S(1)}, f32[2048,128]{1,0:T(8,128)S(1)}) custom-call(s32[1]{0:T(128)} %bitcast.6.core_ref, bf16[64,32,128]{2,1,0:T(8,128)(2,1)S(1)} %get-tuple-element.41.refs_0_, bf16[64,32,128]{2,1,0:T(8,128)(2,1)S(1)} %collective-permute-done.9.refs_1_, ...), custom_call_target="tpu_custom_call" | custom-call | flops 201326592 | bytes 4194304 | tf_op jit(solution)/shard_map/multiply/pallas_call | solution.py:110
  61.7 0.0 collective-permute-done.3.refs_0_
  61.8 0.0 collective-permute-done.4.refs_1_
  61.8 2.9 %multiply.4 = (f32[2048,128]{1,0:T(8,128)S(1)}, f32[2048,128]{1,0:T(8,128)}) custom-call(s32[1]{0:T(128)} %bitcast.6.core_ref, bf16[64,32,128]{2,1,0:T(8,128)(2,1)S(1)} %collective-permute-done.3.refs_0_, bf16[64,32,128]{2,1,0:T(8,128)(2,1)S(1)} %collective-permute-done.4.refs_1_, bf16[64,32,128]{2,1,0:T(8,128)(2,1)S(1)} %collective-permute-done.5.refs_2_, ...), custom_call_target="tpu_custom_call" | custom-call | flops 134217728 | bytes 4194304 | tf_op jit(solution)/shard_map/multiply/pallas_call | solution.py:110
  64.7 0.4 collective-permute-start.12
  65.1 0.0 collective-permute-done.13.refs_2_
  65.1 6.2 %collective-permute-done.14.refs_3_ = bf16[64,32,128]{2,1,0:T(8,128)(2,1)S(1)} collective-permute-done((bf16[64,32,128]{2,1,0:T(8,128)(2,1)S(1)}, bf16[64,32,128]{2,1,0:T(8,128)(2,1)S(1)}, u32[]{:S(2)}, u32[]{:S(2)}) %collective-permute-start.14) | collective-permute-done | bytes 524320 | tf_op jit(solution)/shard_map/ppermute | solution.py:180
  71.3 2.3 %multiply.5 = (f32[2048,128]{1,0:T(8,128)S(1)}, f32[2048,128]{1,0:T(8,128)}) custom-call(s32[1]{0:T(128)} %bitcast.6.core_ref, bf16[64,32,128]{2,1,0:T(8,128)(2,1)S(1)} %collective-permute-done.3.refs_0_, bf16[64,32,128]{2,1,0:T(8,128)(2,1)S(1)} %collective-permute-done.4.refs_1_, bf16[64,32,128]{2,1,0:T(8,128)(2,1)S(1)} %collective-permute-done.13.refs_2_, ...), custom_call_target="tpu_custom_call" | custom-call | flops 67108864 | bytes 4194304 | tf_op jit(solution)/shard_map/multiply/pallas_call | solution.py:110
  73.6 0.0 collective-permute-start.15
  73.6 0.1 stack.51.where_ref
  73.6 0.0 collective-permute-done.12.refs_1_
  73.6 2.9 %collective-permute-done.15.refs_3_ = f32[2048,128]{1,0:T(8,128)} collective-permute-done((f32[2048,128]{1,0:T(8,128)}, f32[2048,128]{1,0:T(8,128)}, u32[]{:S(2)}, u32[]{:S(2)}) %collective-permute-start.15) | collective-permute-done | bytes 1048608 | tf_op jit(solution)/shard_map/ppermute | solution.py:183
  76.6 8.6 %spread.1 = f32[4128,128]{1,0:T(8,128)} custom-call(s32[7]{0:T(128)S(1)} %stack.51.where_ref, f32[2048,128]{1,0:T(8,128)S(1)} %get-tuple-element.47.refs_0_, f32[2048,128]{1,0:T(8,128)S(1)} %collective-permute-done.12.refs_1_, f32[2048,128]{1,0:T(8,128)S(1)} %get-tuple-element.51.refs_2_, f32[2048,128]{1,0:T(8,128)} %collective-permute-done.15.refs_3_), custom_call_target="tpu_custom_call" | custom-call | tf_op jit(solution)/shard_map/spread/pallas_call | solution.py:147
Async XLA Ops:
  0.1 1.6 %copy-start = (bf16[4,32,32,256]{3,2,1,0:T(8,128)(2,1)S(1)}, bf16[4,32,32,256]{3,2,1,0:T(8,128)(2,1)}, u32[]{:S(2)}) copy-start(bf16[4,32,32,256]{3,2,1,0:T(8,128)(2,1)} %raw_ref.2) | copy-start | bytes 6291460
  1.7 2.2 %copy-start.1 = (bf16[4,32,32,256]{3,2,1,0:T(8,128)(2,1)S(1)}, bf16[4,32,32,256]{3,2,1,0:T(8,128)(2,1)}, u32[]{:S(2)}) copy-start(bf16[4,32,32,256]{3,2,1,0:T(8,128)(2,1)} %raw_ref.2) | copy-start | bytes 6291460
  1.7 8.5 %copy-start.2 = (bf16[4,32,32,256]{3,2,1,0:T(8,128)(2,1)S(1)}, bf16[4,32,32,256]{3,2,1,0:T(8,128)(2,1)}, u32[]{:S(2)}) copy-start(bf16[4,32,32,256]{3,2,1,0:T(8,128)(2,1)} %raw_ref.4) | copy-start | bytes 6291460
  3.3 6.4 %collective-permute-start.1 = (bf16[64,32,128]{2,1,0:T(8,128)(2,1)S(1)}, bf16[64,32,128]{2,1,0:T(8,128)(2,1)S(1)}, u32[]{:S(2)}, u32[]{:S(2)}) collective-permute-start(bf16[64,32,128]{2,1,0:T(8,128)(2,1)S(1)} %get-tuple-element.32), channel_id=1, source_target_pairs={{0,2},{2,0},{4,6},{6,4},{8,10},{10,8},{12,14},{14,12},{16,18},{18,... | collective-permute-start | bytes 1572872 | tf_op jit(solution)/shard_map/ppermute | solution.py:183
  5.5 15.3 %collective-permute-start.5 = (bf16[64,32,128]{2,1,0:T(8,128)(2,1)S(1)}, bf16[64,32,128]{2,1,0:T(8,128)(2,1)S(1)}, u32[]{:S(2)}, u32[]{:S(2)}) collective-permute-start(bf16[64,32,128]{2,1,0:T(8,128)(2,1)S(1)} %get-tuple-element.33), channel_id=1, source_target_pairs={{0,1},{1,0},{2,3},{3,2},{4,5},{5,4},{6,7},{7,6},{8,9},{9,8},{10,11... | collective-permute-start | bytes 1572872 | tf_op jit(solution)/shard_map/ppermute | solution.py:173
  8.1 14.8 %collective-permute-start.6 = (bf16[64,32,128]{2,1,0:T(8,128)(2,1)S(1)}, bf16[64,32,128]{2,1,0:T(8,128)(2,1)S(1)}, u32[]{:S(2)}, u32[]{:S(2)}) collective-permute-start(bf16[64,32,128]{2,1,0:T(8,128)(2,1)S(1)} %get-tuple-element.29.refs_2_), channel_id=1, source_target_pairs={{0,4},{2,6},{4,0},{6,2},{8,12},{10,14},{12,8},{14,10},{16,20},{18,... | collective-permute-start | bytes 1572872 | tf_op jit(solution)/shard_map/ppermute | solution.py:176
  9.6 22.1 %collective-permute-start = (bf16[64,32,128]{2,1,0:T(8,128)(2,1)S(1)}, bf16[64,32,128]{2,1,0:T(8,128)(2,1)S(1)}, u32[]{:S(2)}, u32[]{:S(2)}) collective-permute-start(bf16[64,32,128]{2,1,0:T(8,128)(2,1)S(1)} %get-tuple-element.31), channel_id=1, source_target_pairs={{0,3},{1,2},{2,1},{3,0},{4,7},{5,6},{6,5},{7,4},{8,11},{9,10},{10,... | collective-permute-start | bytes 1572872 | tf_op jit(solution)/shard_map/ppermute | solution.py:187
  9.7 24.4 %collective-permute-start.2 = (bf16[64,32,128]{2,1,0:T(8,128)(2,1)S(1)}, bf16[64,32,128]{2,1,0:T(8,128)(2,1)S(1)}, u32[]{:S(2)}, u32[]{:S(2)}) collective-permute-start(bf16[64,32,128]{2,1,0:T(8,128)(2,1)S(1)} %collective-permute-done.1.refs_3_), channel_id=1, source_target_pairs={{0,4},{2,6},{4,0},{6,2},{8,12},{10,14},{12,8},{14,10},{16,20},{18,... | collective-permute-start | bytes 1572872 | tf_op jit(solution)/shard_map/ppermute | solution.py:176
  11.8 27.3 %collective-permute-start.9 = (bf16[64,32,128]{2,1,0:T(8,128)(2,1)S(1)}, bf16[64,32,128]{2,1,0:T(8,128)(2,1)S(1)}, u32[]{:S(2)}, u32[]{:S(2)}) collective-permute-start(bf16[64,32,128]{2,1,0:T(8,128)(2,1)S(1)} %get-tuple-element.42), channel_id=1, source_target_pairs={{0,2},{2,0},{4,6},{6,4},{8,10},{10,8},{12,14},{14,12},{16,18},{18,... | collective-permute-start | bytes 1572872 | tf_op jit(solution)/shard_map/ppermute | solution.py:183
  22.9 16.9 %collective-permute-start.10 = (bf16[64,32,128]{2,1,0:T(8,128)(2,1)S(1)}, bf16[64,32,128]{2,1,0:T(8,128)(2,1)S(1)}, u32[]{:S(2)}, u32[]{:S(2)}) collective-permute-start(bf16[64,32,128]{2,1,0:T(8,128)(2,1)S(1)} %collective-permute-done.6.refs_4_), channel_id=1, source_target_pairs={{0,8},{2,10},{8,16},{10,18},{12,4},{14,6},{16,24},{18,26},{20,12},... | collective-permute-start | bytes 1572872 | tf_op jit(solution)/shard_map/ppermute | solution.py:180
  28.1 17.3 %collective-permute-start.7 = (bf16[64,32,128]{2,1,0:T(8,128)(2,1)S(1)}, bf16[64,32,128]{2,1,0:T(8,128)(2,1)S(1)}, u32[]{:S(2)}, u32[]{:S(2)}) collective-permute-start(bf16[64,32,128]{2,1,0:T(8,128)(2,1)S(1)} %collective-permute-done.5.refs_2_), channel_id=1, source_target_pairs={{0,4},{2,6},{4,0},{6,2},{8,12},{10,14},{12,8},{14,10},{16,20},{18,... | collective-permute-start | bytes 1572872 | tf_op jit(solution)/shard_map/ppermute | solution.py:176
  34.1 21.7 %collective-permute-start.8 = (bf16[64,32,128]{2,1,0:T(8,128)(2,1)S(1)}, bf16[64,32,128]{2,1,0:T(8,128)(2,1)S(1)}, u32[]{:S(2)}, u32[]{:S(2)}) collective-permute-start(bf16[64,32,128]{2,1,0:T(8,128)(2,1)S(1)} %collective-permute-done.refs_3_), channel_id=1, source_target_pairs={{0,4},{2,6},{4,0},{6,2},{8,12},{10,14},{12,8},{14,10},{16,20},{18,... | collective-permute-start | bytes 1572872 | tf_op jit(solution)/shard_map/ppermute | solution.py:176
  35.6 23.7 %collective-permute-start.11 = (bf16[64,32,128]{2,1,0:T(8,128)(2,1)S(1)}, bf16[64,32,128]{2,1,0:T(8,128)(2,1)S(1)}, u32[]{:S(2)}, u32[]{:S(2)}) collective-permute-start(bf16[64,32,128]{2,1,0:T(8,128)(2,1)S(1)} %collective-permute-done.2.refs_5_), channel_id=1, source_target_pairs={{0,8},{2,10},{8,16},{10,18},{12,4},{14,6},{16,24},{18,26},{20,12},... | collective-permute-start | bytes 1572872 | tf_op jit(solution)/shard_map/ppermute | solution.py:180
  39.1 22.6 %collective-permute-start.3 = (bf16[64,32,128]{2,1,0:T(8,128)(2,1)S(1)}, bf16[64,32,128]{2,1,0:T(8,128)(2,1)S(1)}, u32[]{:S(2)}, u32[]{:S(2)}) collective-permute-start(bf16[64,32,128]{2,1,0:T(8,128)(2,1)S(1)} %get-tuple-element.37), channel_id=1, source_target_pairs={{0,1},{1,0},{2,3},{3,2},{4,5},{5,4},{6,7},{7,6},{8,9},{9,8},{10,11... | collective-permute-start | bytes 1572872 | tf_op jit(solution)/shard_map/ppermute | solution.py:173
  39.7 22.0 %collective-permute-start.4 = (bf16[64,32,128]{2,1,0:T(8,128)(2,1)S(1)}, bf16[64,32,128]{2,1,0:T(8,128)(2,1)S(1)}, u32[]{:S(2)}, u32[]{:S(2)}) collective-permute-start(bf16[64,32,128]{2,1,0:T(8,128)(2,1)S(1)} %get-tuple-element.38), channel_id=1, source_target_pairs={{0,3},{1,2},{2,1},{3,0},{4,7},{5,6},{6,5},{7,4},{8,11},{9,10},{10,... | collective-permute-start | bytes 1572872 | tf_op jit(solution)/shard_map/ppermute | solution.py:187
  45.3 19.7 %collective-permute-start.13 = (bf16[64,32,128]{2,1,0:T(8,128)(2,1)S(1)}, bf16[64,32,128]{2,1,0:T(8,128)(2,1)S(1)}, u32[]{:S(2)}, u32[]{:S(2)}) collective-permute-start(bf16[64,32,128]{2,1,0:T(8,128)(2,1)S(1)} %collective-permute-done.7.refs_4_), channel_id=1, source_target_pairs={{0,8},{2,10},{8,16},{10,18},{12,4},{14,6},{16,24},{18,26},{20,12},... | collective-permute-start | bytes 1572872 | tf_op jit(solution)/shard_map/ppermute | solution.py:180
  55.8 15.4 %collective-permute-start.14 = (bf16[64,32,128]{2,1,0:T(8,128)(2,1)S(1)}, bf16[64,32,128]{2,1,0:T(8,128)(2,1)S(1)}, u32[]{:S(2)}, u32[]{:S(2)}) collective-permute-start(bf16[64,32,128]{2,1,0:T(8,128)(2,1)S(1)} %collective-permute-done.8.refs_5_), channel_id=1, source_target_pairs={{0,8},{2,10},{8,16},{10,18},{12,4},{14,6},{16,24},{18,26},{20,12},... | collective-permute-start | bytes 1572872 | tf_op jit(solution)/shard_map/ppermute | solution.py:180
  64.7 9.0 %collective-permute-start.12 = (f32[2048,128]{1,0:T(8,128)}, f32[2048,128]{1,0:T(8,128)S(1)}, u32[]{:S(2)}, u32[]{:S(2)}) collective-permute-start(f32[2048,128]{1,0:T(8,128)} %get-tuple-element.48), channel_id=1, source_target_pairs={{0,2},{2,0},{4,6},{6,4},{8,10},{10,8},{12,14},{14,12},{16,18},{18,... | collective-permute-start | bytes 3145736 | tf_op jit(solution)/shard_map/ppermute | solution.py:183
  73.6 3.0 %collective-permute-start.15 = (f32[2048,128]{1,0:T(8,128)}, f32[2048,128]{1,0:T(8,128)}, u32[]{:S(2)}, u32[]{:S(2)}) collective-permute-start(f32[2048,128]{1,0:T(8,128)} %get-tuple-element.52), channel_id=1, source_target_pairs={{0,2},{2,0},{4,6},{6,4},{8,10},{10,8},{12,14},{14,12},{16,18},{18,... | collective-permute-start | bytes 3145736 | tf_op jit(solution)/shard_map/ppermute | solution.py:183

commit v4 on v0

v4 whole, which is shorter than its diff:
```python
import functools

import jax
import jax.numpy as jnp
from jax import lax
from jax.experimental import pallas as pl
from jax.experimental.pallas import tpu as pltpu
from jax.sharding import PartitionSpec as P

LANES = 128
ROWS = 16
VMEM_BYTES = 16 * 1024 * 1024


def shifted(value, axis, steps):
    count = lax.axis_size(axis)
    initial, last = (max(0, -steps), min(count, count - steps))
    return lax.ppermute(value, axis, [(source, source + steps) for source in range(initial, last)])


def band_rows(product, width, lags):
    rows = product.shape[0]
    cross = product.shape[2]
    flat = product.reshape(rows * width, cross)
    flat = jnp.pad(flat, ((0, rows), (0, 0)))
    skewed = flat.reshape(rows, width + 1, cross)[:, :lags, :]
    return jnp.transpose(skewed, (1, 0, 2))


def plain(source, receiver, scale):
    source, receiver = (
        lax.all_to_all(value, "shot", split_axis=3, concat_axis=0, tiled=True) for value in (source, receiver)
    )
    cells = source.shape[1]
    slabs = [receiver if step == 0 else shifted(receiver, "inline", -step) for step in (-2, -1, 0, 1, 2)]
    width = 5 * cells
    product = jnp.einsum(
        "sity,szty->izy", source, jnp.concatenate(slabs, axis=1), preferred_element_type=jnp.float32
    )
    return band_rows(product, width, 4 * cells + 1) * scale


def in_vmem(*values):
    return [pltpu.with_memory_space_constraint(value, pltpu.VMEM) for value in values]


def params():
    return pltpu.CompilerParams(vmem_limit_bytes=VMEM_BYTES)


SCALARS = pl.BlockSpec(memory_space=pltpu.SMEM)
WHOLE = pl.BlockSpec(memory_space=pltpu.VMEM)


def turn_body(which_ref, raw_ref, *refs):
    turned_refs, (buffer_ref, rows_ref, sems) = refs[:4], refs[4:]
    parts, shots, count, times, cross = buffer_ref.shape
    cells = parts * count
    copies = [
        pltpu.make_async_copy(raw_ref.at[:, pl.ds(part * count, count)], buffer_ref.at[part], sems.at[part])
        for part in range(parts)
    ]
    for copy in copies:
        copy.start()
    for part, copy in enumerate(copies):
        copy.wait()
        for cell in range(count):
            for lanes in range(0, cross, LANES):
                tile = buffer_ref[part, :, cell, :, lanes : lanes + LANES].reshape(shots * times, LANES)
                rows_ref[pl.ds(lanes * cells + part * count + cell, LANES, stride=cells), :] = tile.astype(jnp.float32).T
    share = cross // 4 * cells
    half, core = which_ref[0], which_ref[1]
    quarters = [2 * half + core, 2 * half + 1 - core, 2 - 2 * half + core, 3 - 2 * half - core]
    for turned_ref, quarter in zip(turned_refs, quarters):
        rows = rows_ref[pl.ds(pl.multiple_of(quarter * share, share), share), :]
        turned_ref[...] = rows.reshape(turned_ref.shape).astype(turned_ref.dtype)


def turn(raw, which):
    shots, cells, times, cross = raw.shape
    depth = shots * times
    parts = 4
    return pl.pallas_call(
        turn_body,
        in_specs=[SCALARS, pl.BlockSpec(memory_space=pl.ANY)],
        out_specs=[WHOLE] * 4,
        out_shape=[jax.ShapeDtypeStruct((cross // 4, cells, depth), raw.dtype)] * 4,
        scratch_shapes=[
            pltpu.VMEM((parts, shots, cells // parts, times, cross), raw.dtype),
            pltpu.VMEM((cross * cells, depth), jnp.float32),
            pltpu.SemaphoreType.DMA((parts,)),
        ],
        compiler_params=params(),
        cost_estimate=pl.CostEstimate(flops=0, bytes_accessed=raw.size * 4, transcendentals=0),
        name="turn",
    )(which, pltpu.with_memory_space_constraint(raw, pltpu.HBM))


DIMS = (((1,), (1,)), ((), ()))
BLOCK = 8


def multiply_body(pieces, core_ref, *refs):
    slabs = len(pieces)
    sources, right_ref = refs[:2], refs[-1]
    ins = refs[2 : 2 + sum(pieces)]
    share, cells, _ = sources[0].shape
    groups = (slabs * cells + LANES - 1) // LANES
    kept, sent = refs[-1 - 2 * groups : -1 - groups], refs[-1 - groups : -1]
    before = refs[2 + len(ins) : -1 - 2 * groups]
    for place, count in enumerate(pieces):
        side, other = divmod(place, 2)
        slab = 2 * side + (core_ref[0] if other == 0 else 1 - core_ref[0])
        for part in range(count):
            right_ref[slab, part * (share // count) : (part + 1) * (share // count)] = ins[part][...]
        ins = ins[count:]

    @pl.loop(0, share // BLOCK)
    def _(step):
        for place in range(BLOCK):
            cross = step * BLOCK + place
            left = jnp.concatenate([source[cross] for source in sources], axis=0)
            rows = pl.ds(pl.multiple_of(cross * cells, cells), cells)
            for group in range(groups):
                members = range(group * LANES // cells, min(slabs, (group + 1) * LANES // cells))
                right = jnp.concatenate([right_ref[slab, cross] for slab in members], axis=0)
                width = len(members) * cells
                value = lax.dot_general(left, right, DIMS, preferred_element_type=jnp.float32)
                for out, part, first in (
                    (kept[group], value[:cells], group),
                    (sent[group], value[cells:], groups + group),
                ):
                    if before:
                        part = part + before[first][rows, :width]
                    out[rows, :width] = part


def multiply(core, sources, pieces, before=()):
    share, cells, depth = sources[0].shape
    slabs = len(pieces)
    groups = -(-slabs * cells // LANES)
    flops = 2 * share * 2 * cells * slabs * cells * depth
    flat = [part for piece in pieces for part in piece]
    return pl.pallas_call(
        functools.partial(multiply_body, [len(piece) for piece in pieces]),
        in_specs=[SCALARS] + [WHOLE] * (2 + len(flat) + len(before)),
        out_specs=[WHOLE] * (2 * groups),
        out_shape=[jax.ShapeDtypeStruct((share * cells, LANES), jnp.float32)] * (2 * groups),
        scratch_shapes=[pltpu.VMEM((slabs, share, cells, depth), sources[0].dtype)],
        compiler_params=params(),
        cost_estimate=pl.CostEstimate(flops=flops, bytes_accessed=6 << 20, transcendentals=0),
        name="multiply",
    )(core.reshape(1), *in_vmem(*sources, *flat, *before))


def spread_cell(where_ref, cells, cell, kept_ref, came_ref, slabs, factor, skewed_ref):
    kept, came = (ref[pl.ds(cell, LANES // 2, stride=cells), :] for ref in (kept_ref, came_ref))
    core = where_ref[6]
    low = jnp.where(core == 0, kept, came)
    high = jnp.where(core == 0, came, kept)
    turned = jnp.concatenate([low, high], axis=0).T * factor
    for place, slab in enumerate(slabs):
        lag = (where_ref[slab] + 4) * cells - cell
        skewed_ref[pl.ds(lag * cells + cell, cells, stride=cells), :] = turned[cells * place : cells * (place + 1)]


def early_spread_body(scale, cells, where_ref, kept_ref, came_ref, skewed_ref):
    for cell in range(cells):
        spread_cell(where_ref, cells, cell, kept_ref, came_ref, range(4), scale, skewed_ref)


def early_spread(scale, cells, where, products):
    rows = (4 * cells + 1 + 4 * cells) * cells
    return pl.pallas_call(
        functools.partial(early_spread_body, scale, cells),
        in_specs=[SCALARS] + [WHOLE] * 2,
        out_specs=WHOLE,
        out_shape=jax.ShapeDtypeStruct((rows, LANES), jnp.float32),
        compiler_params=params(),
        cost_estimate=pl.CostEstimate(flops=0, bytes_accessed=6 << 20, transcendentals=0),
        name="early_spread",
    )(where, *in_vmem(*products))


def late_spread_body(scale, cells, where_ref, kept_ref, came_ref, _, skewed_ref, image_ref, sems):
    parts = sems.shape[0]
    count = cells // parts
    lags = image_ref.shape[0]
    factor = jnp.where(where_ref[7] == 1, scale, 0.0)
    shaped_ref = skewed_ref.reshape(skewed_ref.shape[0] // cells, cells, LANES)
    copies = []
    for part in range(parts):
        for cell in range(part * count, (part + 1) * count):
            spread_cell(where_ref, cells, cell, kept_ref, came_ref, (4, 5), factor, skewed_ref)
        rows = pl.ds(part * count, count)
        copies.append(
            pltpu.make_async_copy(shaped_ref.at[pl.ds(2 * cells, lags), rows], image_ref.at[:, rows], sems.at[part])
        )
        copies[-1].start()
    for copy in copies:
        copy.wait()


def late_spread(scale, cells, where, products, skewed):
    lags = 4 * cells + 1
    return pl.pallas_call(
        functools.partial(late_spread_body, scale, cells),
        in_specs=[SCALARS] + [WHOLE] * 3,
        out_specs=[WHOLE, pl.BlockSpec(memory_space=pl.ANY)],
        out_shape=[
            jax.ShapeDtypeStruct(skewed.shape, jnp.float32),
            jax.ShapeDtypeStruct((lags, cells, LANES), jnp.float32),
        ],
        input_output_aliases={3: 0},
        scratch_shapes=[pltpu.SemaphoreType.DMA((4,))],
        compiler_params=params(),
        name="late_spread",
    )(where, *in_vmem(*products, skewed))[1]


def routed(source, receiver, scale):
    count = lax.axis_size("inline")
    cells = source.shape[1]
    own = lax.axis_index("inline")
    core, odd = own & 1, (own >> 1) & 1
    half = lax.axis_index("shot")

    def across(value):
        return lax.ppermute(value, "shot", [(0, 1), (1, 0)])

    def along_y(value):
        return lax.ppermute(value, "inline", [(index, index ^ 2) for index in range(count)])

    def along_z(value):
        steps = (4, -4)
        return lax.ppermute(
            value, "inline", [(index, (index + steps[index // 2 % 2]) % count) for index in range(count)]
        )

    def to_core(value):
        return lax.ppermute(value, "inline", [(index, index ^ 1) for index in range(count)])

    def across_to_core(value):
        pairs = [(2 * index + side, 2 * (index ^ 1) + 1 - side) for index in range(count) for side in range(2)]
        return lax.ppermute(value, ("inline", "shot"), pairs)

    def barrier(*values):
        return lax.optimization_barrier(values)

    which = jnp.stack([half, core]).astype(jnp.int32)
    kept, lent, there, there_twin = turn(receiver, which)
    y0 = along_y(kept)
    twin = to_core(lent)
    moved, moved_twin = across(there), across_to_core(there_twin)
    source, _ = barrier(source, kept)
    left, left_lent, far, far_lent = turn(source, which)
    left_twin = to_core(left_lent)
    y1 = along_y(twin)
    moved, y0 = barrier(moved, y0)
    y2, z0 = along_y(moved), along_z(y0)
    moved_twin, y1, far, far_lent = barrier(moved_twin, y1, far, far_lent)
    middle_share = moved_twin.shape[0] // 2
    y3 = [along_y(moved_twin[:middle_share]), along_y(moved_twin[middle_share:])]
    z1 = along_z(y1)
    right, right_twin = across(far), across_to_core(far_lent)
    z2 = along_z(y2)
    early = multiply(core, (left, left_twin), [(piece,) for piece in (kept, twin, y0, y1, z0, z1)])
    y3[1], *early = barrier(y3[1], *early)
    z3 = [along_z(part) for part in y3]
    middle = multiply(core, (right, right_twin), ((moved,), (moved_twin,), (y2,), y3), (early[0], early[2]))
    middle_came = to_core(middle[1])
    side = 2 - 4 * odd
    end = jnp.where(odd == 0, own >> 1 == 0, own >> 1 == count // 2 - 1)
    where = jnp.stack([block + shift - core for shift in (0, side, -side) for block in (0, 1)] + [core, 1 - end])
    where = where.astype(jnp.int32)
    skewed = early_spread(scale, cells, where, (middle[0], middle_came))
    late = multiply(core, (right, right_twin), ((z2,), z3), (early[1], early[3]))
    late_came = to_core(late[1])
    return late_spread(scale, cells, where, (late[0], late_came), skewed)


def on_device(source, receiver):
    shots, cells, times, cross = source.shape
    groups, count = lax.axis_size("shot"), lax.axis_size("inline")
    scale = 1.0 / (times * shots * groups) ** 0.5
    fits = (
        groups == 2
        and count % 4 == 0
        and cross == 2 * LANES
        and shots * times == LANES
        and 4 * cells == LANES
        and times % ROWS == 0
    )
    return routed(source, receiver, scale) if fits else plain(source, receiver, scale)


def solution(mesh):
    placed = (P("shot", "inline", None, None), P("shot", "inline", None, None))
    return jax.shard_map(
        on_device, mesh=mesh, in_specs=placed, out_specs=P(None, "inline", "shot"), check_vma=False
    )
```

time: 341 us -> 88.1 us (0.26); the launches traced: 334 us -> 87.9 us
  local copies, waits for them, and re-layouts: 211 us -> 0.12 us
  blocking collectives: 59.2 us -> 0 us
  Pallas kernels: 0 us -> 27.6 us
  matrix products: 13.4 us -> 0 us
  starting transfers between devices: 10.4 us -> 22.2 us
    ppermute x4 -> x0, local copies, waits for them, and re-layouts: 61 us -> none  [shifted(): lax.ppermute(value, axis, [(source, source + steps) for source in range(i...]
    unnamed x8 -> x0, local copies, waits for them, and re-layouts: 60.1 us -> none
    all_to_all x2 -> x0, blocking collectives: 59.2 us -> none  [the longest x1 29.7 us: on_device(): lax.all_to_all(receiver, 'shot', split_axis=3, concat_axis=0, tiled=True)]
    concatenate x1 -> x0, local copies, waits for them, and re-layouts: 44.4 us -> none  [extend(): jnp.concatenate((far_left, near_left, receiver, near_right, far_right), a...]
    all_to_all x3 -> x0, local copies, waits for them, and re-layouts: 35.7 us -> none  [the longest x2 25.4 us: on_device(): lax.all_to_all(receiver, 'shot', split_axis=3, concat_axis=0, tiled=True)]
    pallas_call x0 -> x7, Pallas kernels: none -> 27.6 us  [the longest x2 10.8 us: turn(): pl.pallas_call(turn_body, in_specs=[SCALARS, pl.BlockSpec(memory_space=pl...]
    dot_general x1 -> x0, matrix products: 13.4 us -> none  [correlate(): jnp.einsum('sity,szty->izy', source, extended, preferred_element_type=jnp...]
    ppermute x4 -> x18, starting transfers between devices: 10.4 us -> 22.2 us  [the longest x5 8.65 us: along_y(): lax.ppermute(value, 'inline', [(index, index ^ 2) for index in range(coun...]
  transfers between devices with their start and end apart: 4 -> 18, of which waited for: 1 -> 10; matrix products, arithmetic and copies ran while one was open for 26% -> 0% of each run, Pallas kernels for 0% -> 20%
where the time goes in v4:
time: 88.1 us; the launch traced here: 87.9 us
  waiting for transfers between devices  37.6 us (43%)
  Pallas kernels  27.6 us (31%)
  starting transfers between devices  22.2 us (25%)
    ppermute x5, waiting for transfers between devices, along_y(): lax.ppermute(value, 'inline', [(index, index ^ 2) for index in range(coun...  14.1 us
    pallas_call x2, Pallas kernels, turn(): pl.pallas_call(turn_body, in_specs=[SCALARS, pl.BlockSpec(memory_space=pl...  10.8 us
    ppermute x5, waiting for transfers between devices, along_z(): lax.ppermute(value, 'inline', [(index, (index + steps[index // 2 % 2]) %...  10.6 us
    pallas_call x3, Pallas kernels, multiply(): pl.pallas_call(functools.partial(multiply_body, [len(piece) for piece in...  8.84 us
    ppermute x5, starting transfers between devices, along_y(): lax.ppermute(value, 'inline', [(index, index ^ 2) for index in range(coun...  8.65 us
    ppermute x5, starting transfers between devices, along_z(): lax.ppermute(value, 'inline', [(index, (index + steps[index // 2 % 2]) %...  8.12 us
    ppermute x2, waiting for transfers between devices, across_to_core(): return lax.ppermute(value, ('inline', 'shot'), pairs)  7.84 us
    ppermute x2, waiting for transfers between devices, across(): return lax.ppermute(value, 'shot', [(0, 1), (1, 0)])  5.14 us
  transfers between devices with their start and end apart: 18, of which 10 were waited for; matrix products, arithmetic and copies ran while one was open for 0% of the time, Pallas kernels for 20%

profile of v4, /device:TPU:0, one launch (start us, length us, event | category | flops | bytes accessed | tf_op | source)
XLA Modules:
  0.0 87.9 jit_solution(17965279218915918059)
XLA Ops:
  0.0 0.1 pad_add_fusion.which_ref
  0.1 5.4 %turn.2 = (bf16[64,32,128]{2,1,0:T(8,128)(2,1)S(1)}, bf16[64,32,128]{2,1,0:T(8,128)(2,1)S(1)}, bf16[64,32,128]{2,1,0:T(8,128)(2,1)S(1)}, bf16[64,32,128]{2,1,0:T(8,128)(2,1)S(1)}) custom-call(s32[2]{0:T(128)S(1)} %pad_add_fusion.which_ref, bf16[4,32,32,256]{3,2,1,0:T(8,128)(2,1)} %raw_ref.1), custom_call_target="tpu_custom_call" | custom-call | bytes 4194304 | tf_op jit(solution)/shard_map/turn/pallas_call | solution.py:83
  5.5 0.5 collective-permute-start.1
  6.0 2.6 %collective-permute-start.5 = (bf16[64,32,128]{2,1,0:T(8,128)(2,1)S(1)}, bf16[64,32,128]{2,1,0:T(8,128)(2,1)S(1)}, u32[]{:S(2)}, u32[]{:S(2)}) collective-permute-start(bf16[64,32,128]{2,1,0:T(8,128)(2,1)S(1)} %get-tuple-element.42), channel_id=1, source_target_pairs={{0,1},{1,0},{2,3},{3,2},{4,5},{5,4},{6,7},{7,6},{8,9},{9,8},{10,11... | collective-permute-start | bytes 1572872 | tf_op jit(solution)/shard_map/ppermute | solution.py:229
  8.6 1.5 %collective-permute-start.6 = (bf16[64,32,128]{2,1,0:T(8,128)(2,1)S(1)}, bf16[64,32,128]{2,1,0:T(8,128)(2,1)S(1)}, u32[]{:S(2)}, u32[]{:S(2)}) collective-permute-start(bf16[64,32,128]{2,1,0:T(8,128)(2,1)S(1)} %get-tuple-element.36.refs_2_), channel_id=1, source_target_pairs={{0,4},{2,6},{4,0},{6,2},{8,12},{10,14},{12,8},{14,10},{16,20},{18,... | collective-permute-start | bytes 1572872 | tf_op jit(solution)/shard_map/ppermute | solution.py:232
  10.1 0.0 collective-permute-start
  10.1 0.0 collective-permute-done.1.refs_3_
  10.1 0.5 collective-permute-start.2
  10.6 5.4 %turn.3 = (bf16[64,32,128]{2,1,0:T(8,128)(2,1)S(1)}, bf16[64,32,128]{2,1,0:T(8,128)(2,1)S(1)}, bf16[64,32,128]{2,1,0:T(8,128)(2,1)S(1)}, bf16[64,32,128]{2,1,0:T(8,128)(2,1)S(1)}) custom-call(s32[2]{0:T(128)S(1)} %pad_add_fusion.which_ref, bf16[4,32,32,256]{3,2,1,0:T(8,128)(2,1)} %raw_ref.2), custom_call_target="tpu_custom_call" | custom-call | bytes 4194304 | tf_op jit(solution)/shard_map/turn/pallas_call | solution.py:83
  16.0 0.2 collective-permute-start.12
  16.2 5.1 %collective-permute-done.5.refs_2_ = bf16[64,32,128]{2,1,0:T(8,128)(2,1)S(1)} collective-permute-done((bf16[64,32,128]{2,1,0:T(8,128)(2,1)S(1)}, bf16[64,32,128]{2,1,0:T(8,128)(2,1)S(1)}, u32[]{:S(2)}, u32[]{:S(2)}) %collective-permute-start.5) | collective-permute-done | bytes 524320 | tf_op jit(solution)/shard_map/ppermute | solution.py:229
  21.3 2.0 %collective-permute-done.6.refs_4_ = bf16[64,32,128]{2,1,0:T(8,128)(2,1)S(1)} collective-permute-done((bf16[64,32,128]{2,1,0:T(8,128)(2,1)S(1)}, bf16[64,32,128]{2,1,0:T(8,128)(2,1)S(1)}, u32[]{:S(2)}, u32[]{:S(2)}) %collective-permute-start.6) | collective-permute-done | bytes 524320 | tf_op jit(solution)/shard_map/ppermute | solution.py:232
  23.3 1.5 %collective-permute-start.7 = (bf16[64,32,128]{2,1,0:T(8,128)(2,1)S(1)}, bf16[64,32,128]{2,1,0:T(8,128)(2,1)S(1)}, u32[]{:S(2)}, u32[]{:S(2)}) collective-permute-start(bf16[64,32,128]{2,1,0:T(8,128)(2,1)S(1)} %collective-permute-done.5.refs_2_), channel_id=1, source_target_pairs={{0,4},{2,6},{4,0},{6,2},{8,12},{10,14},{12,8},{14,10},{16,20},{18,... | collective-permute-start | bytes 1572872 | tf_op jit(solution)/shard_map/ppermute | solution.py:232
  24.8 1.6 %collective-permute-start.13 = (bf16[64,32,128]{2,1,0:T(8,128)(2,1)S(1)}, bf16[64,32,128]{2,1,0:T(8,128)(2,1)S(1)}, u32[]{:S(2)}, u32[]{:S(2)}) collective-permute-start(bf16[64,32,128]{2,1,0:T(8,128)(2,1)S(1)} %collective-permute-done.6.refs_4_), channel_id=1, source_target_pairs={{0,8},{2,10},{4,28},{6,30},{8,16},{10,18},{12,4},{14,6},{16,24},{1... | collective-permute-start | bytes 1572872 | tf_op jit(solution)/shard_map/ppermute | solution.py:236
  26.4 5.6 %collective-permute-done.refs_3_ = bf16[64,32,128]{2,1,0:T(8,128)(2,1)S(1)} collective-permute-done((bf16[64,32,128]{2,1,0:T(8,128)(2,1)S(1)}, bf16[64,32,128]{2,1,0:T(8,128)(2,1)S(1)}, u32[]{:S(2)}, u32[]{:S(2)}) %collective-permute-start) | collective-permute-done | bytes 524320 | tf_op jit(solution)/shard_map/ppermute | solution.py:245
  32.0 2.5 %collective-permute-done.2.refs_5_ = bf16[64,32,128]{2,1,0:T(8,128)(2,1)S(1)} collective-permute-done((bf16[64,32,128]{2,1,0:T(8,128)(2,1)S(1)}, bf16[64,32,128]{2,1,0:T(8,128)(2,1)S(1)}, u32[]{:S(2)}, u32[]{:S(2)}) %collective-permute-start.2) | collective-permute-done | bytes 524320 | tf_op jit(solution)/shard_map/ppermute | solution.py:232
  34.6 1.6 %collective-permute-start.14 = (bf16[64,32,128]{2,1,0:T(8,128)(2,1)S(1)}, bf16[64,32,128]{2,1,0:T(8,128)(2,1)S(1)}, u32[]{:S(2)}, u32[]{:S(2)}) collective-permute-start(bf16[64,32,128]{2,1,0:T(8,128)(2,1)S(1)} %collective-permute-done.2.refs_5_), channel_id=1, source_target_pairs={{0,8},{2,10},{4,28},{6,30},{8,16},{10,18},{12,4},{14,6},{16,24},{1... | collective-permute-start | bytes 1572872 | tf_op jit(solution)/shard_map/ppermute | solution.py:236
  36.2 3.6 %collective-permute-start.9 = (bf16[32,32,128]{2,1,0:T(8,128)(2,1)S(1)}, bf16[32,32,128]{2,1,0:T(8,128)(2,1)S(1)}, u32[]{:S(2)}, u32[]{:S(2)}) collective-permute-start(bf16[32,32,128]{2,1,0:T(8,128)(2,1)S(1)} %get-tuple-element.64), channel_id=1, source_target_pairs={{0,4},{2,6},{4,0},{6,2},{8,12},{10,14},{12,8},{14,10},{16,20},{18,... | collective-permute-start | bytes 786440 | tf_op jit(solution)/shard_map/ppermute | solution.py:232
  39.8 0.0 collective-permute-done.12.refs_1_
  39.8 0.5 collective-permute-start.3
  40.3 5.5 %collective-permute-done.7.refs_4_ = bf16[64,32,128]{2,1,0:T(8,128)(2,1)S(1)} collective-permute-done((bf16[64,32,128]{2,1,0:T(8,128)(2,1)S(1)}, bf16[64,32,128]{2,1,0:T(8,128)(2,1)S(1)}, u32[]{:S(2)}, u32[]{:S(2)}) %collective-permute-start.7) | collective-permute-done | bytes 524320 | tf_op jit(solution)/shard_map/ppermute | solution.py:232
  45.8 0.0 collective-permute-start.4
  45.8 0.0 collective-permute-done.13.refs_6_
  45.8 1.5 %collective-permute-start.11 = (bf16[32,32,128]{2,1,0:T(8,128)(2,1)S(1)}, bf16[32,32,128]{2,1,0:T(8,128)(2,1)S(1)}, u32[]{:S(2)}, u32[]{:S(2)}) collective-permute-start(bf16[32,32,128]{2,1,0:T(8,128)(2,1)S(1)} %get-tuple-element.63), channel_id=1, source_target_pairs={{0,4},{2,6},{4,0},{6,2},{8,12},{10,14},{12,8},{14,10},{16,20},{18,... | collective-permute-start | bytes 786440 | tf_op jit(solution)/shard_map/ppermute | solution.py:232
  47.3 4.1 %collective-permute-done.9.refs_5_ = bf16[32,32,128]{2,1,0:T(8,128)(2,1)S(1)} collective-permute-done((bf16[32,32,128]{2,1,0:T(8,128)(2,1)S(1)}, bf16[32,32,128]{2,1,0:T(8,128)(2,1)S(1)}, u32[]{:S(2)}, u32[]{:S(2)}) %collective-permute-start.9) | collective-permute-done | bytes 262176 | tf_op jit(solution)/shard_map/ppermute | solution.py:232
  51.4 1.6 %collective-permute-start.8 = (bf16[64,32,128]{2,1,0:T(8,128)(2,1)S(1)}, bf16[64,32,128]{2,1,0:T(8,128)(2,1)S(1)}, u32[]{:S(2)}, u32[]{:S(2)}) collective-permute-start(bf16[64,32,128]{2,1,0:T(8,128)(2,1)S(1)} %collective-permute-done.7.refs_4_), channel_id=1, source_target_pairs={{0,8},{2,10},{4,28},{6,30},{8,16},{10,18},{12,4},{14,6},{16,24},{1... | collective-permute-start | bytes 1572872 | tf_op jit(solution)/shard_map/ppermute | solution.py:236
  53.0 0.0 collective-permute-done.14.refs_7_
  53.0 1.6 %collective-permute-start.10 = (bf16[32,32,128]{2,1,0:T(8,128)(2,1)S(1)}, bf16[32,32,128]{2,1,0:T(8,128)(2,1)S(1)}, u32[]{:S(2)}, u32[]{:S(2)}) collective-permute-start(bf16[32,32,128]{2,1,0:T(8,128)(2,1)S(1)} %collective-permute-done.9.refs_5_), channel_id=1, source_target_pairs={{0,8},{2,10},{4,28},{6,30},{8,16},{10,18},{12,4},{14,6},{16,24},{1... | collective-permute-start | bytes 786440 | tf_op jit(solution)/shard_map/ppermute | solution.py:236
  54.6 2.8 %multiply.3 = (f32[2048,128]{1,0:T(8,128)S(1)}, f32[2048,128]{1,0:T(8,128)S(1)}, f32[2048,128]{1,0:T(8,128)S(1)}, f32[2048,128]{1,0:T(8,128)S(1)}) custom-call(s32[1]{0:T(128)} %bitcast.6.core_ref, bf16[64,32,128]{2,1,0:T(8,128)(2,1)S(1)} %get-tuple-element.45.refs_0_, bf16[64,32,128]{2,1,0:T(8,128)(2,1)S(1)} %collective-permute-done.12.refs_1_, ...), custom_call_target="tpu_custom_call" | custom-call | flops 201326592 | bytes 6291456 | tf_op jit(solution)/shard_map/multiply/pallas_call | solution.py:144
  57.4 0.0 collective-permute-done.11.refs_6_
  57.4 1.8 %collective-permute-start.15 = (bf16[32,32,128]{2,1,0:T(8,128)(2,1)S(1)}, bf16[32,32,128]{2,1,0:T(8,128)(2,1)S(1)}, u32[]{:S(2)}, u32[]{:S(2)}) collective-permute-start(bf16[32,32,128]{2,1,0:T(8,128)(2,1)S(1)} %collective-permute-done.11.refs_6_), channel_id=1, source_target_pairs={{0,8},{2,10},{4,28},{6,30},{8,16},{10,18},{12,4},{14,6},{16,24},{1... | collective-permute-start | bytes 786440 | tf_op jit(solution)/shard_map/ppermute | solution.py:236
  59.2 0.0 collective-permute-done.3.refs_0_
  59.2 2.2 %collective-permute-done.4.refs_1_ = bf16[64,32,128]{2,1,0:T(8,128)(2,1)S(1)} collective-permute-done((bf16[64,32,128]{2,1,0:T(8,128)(2,1)S(1)}, bf16[64,32,128]{2,1,0:T(8,128)(2,1)S(1)}, u32[]{:S(2)}, u32[]{:S(2)}) %collective-permute-start.4) | collective-permute-done | bytes 524320 | tf_op jit(solution)/shard_map/ppermute | solution.py:245
  61.4 3.3 %multiply.5 = (f32[2048,128]{1,0:T(8,128)S(1)}, f32[2048,128]{1,0:T(8,128)}) custom-call(s32[1]{0:T(128)} %bitcast.6.core_ref, bf16[64,32,128]{2,1,0:T(8,128)(2,1)S(1)} %collective-permute-done.3.refs_0_, bf16[64,32,128]{2,1,0:T(8,128)(2,1)S(1)} %collective-permute-done.4.refs_1_, bf16[64,32,128]{2,1,0:T(8,128)(2,1)S(1)} %collective-permute-done.5.refs_2_, ...), custom_call_target="tpu_custom_call" | custom-call | flops 134217728 | bytes 6291456 | tf_op jit(solution)/shard_map/multiply/pallas_call | solution.py:144
  64.8 1.5 %collective-permute-start.17 = (f32[2048,128]{1,0:T(8,128)}, f32[2048,128]{1,0:T(8,128)S(1)}, u32[]{:S(2)}, u32[]{:S(2)}) collective-permute-start(f32[2048,128]{1,0:T(8,128)} %get-tuple-element.61), channel_id=1, source_target_pairs={{0,2},{2,0},{4,6},{6,4},{8,10},{10,8},{12,14},{14,12},{16,18},{18,... | collective-permute-start | bytes 3145736 | tf_op jit(solution)/shard_map/ppermute | solution.py:241
  66.3 1.8 %collective-permute-done.8.refs_2_ = bf16[64,32,128]{2,1,0:T(8,128)(2,1)S(1)} collective-permute-done((bf16[64,32,128]{2,1,0:T(8,128)(2,1)S(1)}, bf16[64,32,128]{2,1,0:T(8,128)(2,1)S(1)}, u32[]{:S(2)}, u32[]{:S(2)}) %collective-permute-start.8) | collective-permute-done | bytes 524320 | tf_op jit(solution)/shard_map/ppermute | solution.py:236
  68.1 5.6 %collective-permute-done.10.refs_3_ = bf16[32,32,128]{2,1,0:T(8,128)(2,1)S(1)} collective-permute-done((bf16[32,32,128]{2,1,0:T(8,128)(2,1)S(1)}, bf16[32,32,128]{2,1,0:T(8,128)(2,1)S(1)}, u32[]{:S(2)}, u32[]{:S(2)}) %collective-permute-start.10) | collective-permute-done | bytes 262176 | tf_op jit(solution)/shard_map/ppermute | solution.py:236
  73.7 3.2 %collective-permute-done.15.refs_4_ = bf16[32,32,128]{2,1,0:T(8,128)(2,1)S(1)} collective-permute-done((bf16[32,32,128]{2,1,0:T(8,128)(2,1)S(1)}, bf16[32,32,128]{2,1,0:T(8,128)(2,1)S(1)}, u32[]{:S(2)}, u32[]{:S(2)}) %collective-permute-start.15) | collective-permute-done | bytes 262176 | tf_op jit(solution)/shard_map/ppermute | solution.py:236
  76.9 2.7 %multiply.4 = (f32[2048,128]{1,0:T(8,128)S(1)}, f32[2048,128]{1,0:T(8,128)}) custom-call(s32[1]{0:T(128)} %bitcast.6.core_ref, bf16[64,32,128]{2,1,0:T(8,128)(2,1)S(1)} %collective-permute-done.3.refs_0_, bf16[64,32,128]{2,1,0:T(8,128)(2,1)S(1)} %collective-permute-done.4.refs_1_, bf16[64,32,128]{2,1,0:T(8,128)(2,1)S(1)} %collective-permute-done.8.refs_2_, ...), custom_call_target="tpu_custom_call" | custom-call | flops 67108864 | bytes 6291456 | tf_op jit(solution)/shard_map/multiply/pallas_call | solution.py:144
  79.6 0.0 collective-permute-start.16
  79.6 0.1 stack.42.where_ref
  79.7 0.0 collective-permute-done.17.came_ref
  79.7 3.7 %early_spread.1._ = f32[8224,128]{1,0:T(8,128)S(1)} custom-call(s32[8]{0:T(128)S(1)} %stack.42.where_ref, f32[2048,128]{1,0:T(8,128)S(1)} %get-tuple-element.60.kept_ref, f32[2048,128]{1,0:T(8,128)S(1)} %collective-permute-done.17.came_ref), custom_call_target="tpu_custom_call" | custom-call | bytes 6291456 | tf_op jit(solution)/shard_map/early_spread/pallas_call | solution.py:174
  83.4 0.0 collective-permute-done.16.came_ref
  83.4 4.3 %late_spread.1 = (f32[8224,128]{1,0:T(8,128)S(1)}, f32[129,32,128]{2,1,0:T(8,128)}) custom-call(s32[8]{0:T(128)S(1)} %stack.42.where_ref, f32[2048,128]{1,0:T(8,128)S(1)} %get-tuple-element.56.kept_ref, f32[2048,128]{1,0:T(8,128)} %collective-permute-done.16.came_ref, f32[8224,128]{1,0:T(8,128)S(1)} %early_spread.1._), custom_call_target="tpu_custom_call", output_to_operand_aliasing={{0}: (3, {})} | custom-call | tf_op jit(solution)/shard_map/late_spread/pallas_call | solution.py:206
  (1 shorter events, 0.0 us)
Async XLA Ops:
  5.5 4.6 %collective-permute-start.1 = (bf16[64,32,128]{2,1,0:T(8,128)(2,1)S(1)}, bf16[64,32,128]{2,1,0:T(8,128)(2,1)S(1)}, u32[]{:S(2)}, u32[]{:S(2)}) collective-permute-start(bf16[64,32,128]{2,1,0:T(8,128)(2,1)S(1)} %get-tuple-element.35), channel_id=1, source_target_pairs={{0,2},{2,0},{4,6},{6,4},{8,10},{10,8},{12,14},{14,12},{16,18},{18,... | collective-permute-start | bytes 1572872 | tf_op jit(solution)/shard_map/ppermute | solution.py:241
  6.0 15.3 %collective-permute-start.5 = (bf16[64,32,128]{2,1,0:T(8,128)(2,1)S(1)}, bf16[64,32,128]{2,1,0:T(8,128)(2,1)S(1)}, u32[]{:S(2)}, u32[]{:S(2)}) collective-permute-start(bf16[64,32,128]{2,1,0:T(8,128)(2,1)S(1)} %get-tuple-element.42), channel_id=1, source_target_pairs={{0,1},{1,0},{2,3},{3,2},{4,5},{5,4},{6,7},{7,6},{8,9},{9,8},{10,11... | collective-permute-start | bytes 1572872 | tf_op jit(solution)/shard_map/ppermute | solution.py:229
  8.6 14.8 %collective-permute-start.6 = (bf16[64,32,128]{2,1,0:T(8,128)(2,1)S(1)}, bf16[64,32,128]{2,1,0:T(8,128)(2,1)S(1)}, u32[]{:S(2)}, u32[]{:S(2)}) collective-permute-start(bf16[64,32,128]{2,1,0:T(8,128)(2,1)S(1)} %get-tuple-element.36.refs_2_), channel_id=1, source_target_pairs={{0,4},{2,6},{4,0},{6,2},{8,12},{10,14},{12,8},{14,10},{16,20},{18,... | collective-permute-start | bytes 1572872 | tf_op jit(solution)/shard_map/ppermute | solution.py:232
  10.1 22.0 %collective-permute-start = (bf16[64,32,128]{2,1,0:T(8,128)(2,1)S(1)}, bf16[64,32,128]{2,1,0:T(8,128)(2,1)S(1)}, u32[]{:S(2)}, u32[]{:S(2)}) collective-permute-start(bf16[64,32,128]{2,1,0:T(8,128)(2,1)S(1)} %get-tuple-element.34), channel_id=1, source_target_pairs={{0,3},{1,2},{2,1},{3,0},{4,7},{5,6},{6,5},{7,4},{8,11},{9,10},{10,... | collective-permute-start | bytes 1572872 | tf_op jit(solution)/shard_map/ppermute | solution.py:245
  10.1 24.5 %collective-permute-start.2 = (bf16[64,32,128]{2,1,0:T(8,128)(2,1)S(1)}, bf16[64,32,128]{2,1,0:T(8,128)(2,1)S(1)}, u32[]{:S(2)}, u32[]{:S(2)}) collective-permute-start(bf16[64,32,128]{2,1,0:T(8,128)(2,1)S(1)} %collective-permute-done.1.refs_3_), channel_id=1, source_target_pairs={{0,4},{2,6},{4,0},{6,2},{8,12},{10,14},{12,8},{14,10},{16,20},{18,... | collective-permute-start | bytes 1572872 | tf_op jit(solution)/shard_map/ppermute | solution.py:232
  16.0 23.8 %collective-permute-start.12 = (bf16[64,32,128]{2,1,0:T(8,128)(2,1)S(1)}, bf16[64,32,128]{2,1,0:T(8,128)(2,1)S(1)}, u32[]{:S(2)}, u32[]{:S(2)}) collective-permute-start(bf16[64,32,128]{2,1,0:T(8,128)(2,1)S(1)} %get-tuple-element.46), channel_id=1, source_target_pairs={{0,2},{2,0},{4,6},{6,4},{8,10},{10,8},{12,14},{14,12},{16,18},{18,... | collective-permute-start | bytes 1572872 | tf_op jit(solution)/shard_map/ppermute | solution.py:241
  23.3 22.5 %collective-permute-start.7 = (bf16[64,32,128]{2,1,0:T(8,128)(2,1)S(1)}, bf16[64,32,128]{2,1,0:T(8,128)(2,1)S(1)}, u32[]{:S(2)}, u32[]{:S(2)}) collective-permute-start(bf16[64,32,128]{2,1,0:T(8,128)(2,1)S(1)} %collective-permute-done.5.refs_2_), channel_id=1, source_target_pairs={{0,4},{2,6},{4,0},{6,2},{8,12},{10,14},{12,8},{14,10},{16,20},{18,... | collective-permute-start | bytes 1572872 | tf_op jit(solution)/shard_map/ppermute | solution.py:232
  24.8 21.0 %collective-permute-start.13 = (bf16[64,32,128]{2,1,0:T(8,128)(2,1)S(1)}, bf16[64,32,128]{2,1,0:T(8,128)(2,1)S(1)}, u32[]{:S(2)}, u32[]{:S(2)}) collective-permute-start(bf16[64,32,128]{2,1,0:T(8,128)(2,1)S(1)} %collective-permute-done.6.refs_4_), channel_id=1, source_target_pairs={{0,8},{2,10},{4,28},{6,30},{8,16},{10,18},{12,4},{14,6},{16,24},{1... | collective-permute-start | bytes 1572872 | tf_op jit(solution)/shard_map/ppermute | solution.py:236
  34.6 18.4 %collective-permute-start.14 = (bf16[64,32,128]{2,1,0:T(8,128)(2,1)S(1)}, bf16[64,32,128]{2,1,0:T(8,128)(2,1)S(1)}, u32[]{:S(2)}, u32[]{:S(2)}) collective-permute-start(bf16[64,32,128]{2,1,0:T(8,128)(2,1)S(1)} %collective-permute-done.2.refs_5_), channel_id=1, source_target_pairs={{0,8},{2,10},{4,28},{6,30},{8,16},{10,18},{12,4},{14,6},{16,24},{1... | collective-permute-start | bytes 1572872 | tf_op jit(solution)/shard_map/ppermute | solution.py:236
  36.2 15.2 %collective-permute-start.9 = (bf16[32,32,128]{2,1,0:T(8,128)(2,1)S(1)}, bf16[32,32,128]{2,1,0:T(8,128)(2,1)S(1)}, u32[]{:S(2)}, u32[]{:S(2)}) collective-permute-start(bf16[32,32,128]{2,1,0:T(8,128)(2,1)S(1)} %get-tuple-element.64), channel_id=1, source_target_pairs={{0,4},{2,6},{4,0},{6,2},{8,12},{10,14},{12,8},{14,10},{16,20},{18,... | collective-permute-start | bytes 786440 | tf_op jit(solution)/shard_map/ppermute | solution.py:232
  39.8 19.4 %collective-permute-start.3 = (bf16[64,32,128]{2,1,0:T(8,128)(2,1)S(1)}, bf16[64,32,128]{2,1,0:T(8,128)(2,1)S(1)}, u32[]{:S(2)}, u32[]{:S(2)}) collective-permute-start(bf16[64,32,128]{2,1,0:T(8,128)(2,1)S(1)} %get-tuple-element.40), channel_id=1, source_target_pairs={{0,1},{1,0},{2,3},{3,2},{4,5},{5,4},{6,7},{7,6},{8,9},{9,8},{10,11... | collective-permute-start | bytes 1572872 | tf_op jit(solution)/shard_map/ppermute | solution.py:229
  45.8 15.6 %collective-permute-start.4 = (bf16[64,32,128]{2,1,0:T(8,128)(2,1)S(1)}, bf16[64,32,128]{2,1,0:T(8,128)(2,1)S(1)}, u32[]{:S(2)}, u32[]{:S(2)}) collective-permute-start(bf16[64,32,128]{2,1,0:T(8,128)(2,1)S(1)} %get-tuple-element.41), channel_id=1, source_target_pairs={{0,3},{1,2},{2,1},{3,0},{4,7},{5,6},{6,5},{7,4},{8,11},{9,10},{10,... | collective-permute-start | bytes 1572872 | tf_op jit(solution)/shard_map/ppermute | solution.py:245
  45.8 11.6 %collective-permute-start.11 = (bf16[32,32,128]{2,1,0:T(8,128)(2,1)S(1)}, bf16[32,32,128]{2,1,0:T(8,128)(2,1)S(1)}, u32[]{:S(2)}, u32[]{:S(2)}) collective-permute-start(bf16[32,32,128]{2,1,0:T(8,128)(2,1)S(1)} %get-tuple-element.63), channel_id=1, source_target_pairs={{0,4},{2,6},{4,0},{6,2},{8,12},{10,14},{12,8},{14,10},{16,20},{18,... | collective-permute-start | bytes 786440 | tf_op jit(solution)/shard_map/ppermute | solution.py:232
  51.4 16.7 %collective-permute-start.8 = (bf16[64,32,128]{2,1,0:T(8,128)(2,1)S(1)}, bf16[64,32,128]{2,1,0:T(8,128)(2,1)S(1)}, u32[]{:S(2)}, u32[]{:S(2)}) collective-permute-start(bf16[64,32,128]{2,1,0:T(8,128)(2,1)S(1)} %collective-permute-done.7.refs_4_), channel_id=1, source_target_pairs={{0,8},{2,10},{4,28},{6,30},{8,16},{10,18},{12,4},{14,6},{16,24},{1... | collective-permute-start | bytes 1572872 | tf_op jit(solution)/shard_map/ppermute | solution.py:236
  53.0 20.7 %collective-permute-start.10 = (bf16[32,32,128]{2,1,0:T(8,128)(2,1)S(1)}, bf16[32,32,128]{2,1,0:T(8,128)(2,1)S(1)}, u32[]{:S(2)}, u32[]{:S(2)}) collective-permute-start(bf16[32,32,128]{2,1,0:T(8,128)(2,1)S(1)} %collective-permute-done.9.refs_5_), channel_id=1, source_target_pairs={{0,8},{2,10},{4,28},{6,30},{8,16},{10,18},{12,4},{14,6},{16,24},{1... | collective-permute-start | bytes 786440 | tf_op jit(solution)/shard_map/ppermute | solution.py:236
  57.4 19.5 %collective-permute-start.15 = (bf16[32,32,128]{2,1,0:T(8,128)(2,1)S(1)}, bf16[32,32,128]{2,1,0:T(8,128)(2,1)S(1)}, u32[]{:S(2)}, u32[]{:S(2)}) collective-permute-start(bf16[32,32,128]{2,1,0:T(8,128)(2,1)S(1)} %collective-permute-done.11.refs_6_), channel_id=1, source_target_pairs={{0,8},{2,10},{4,28},{6,30},{8,16},{10,18},{12,4},{14,6},{16,24},{1... | collective-permute-start | bytes 786440 | tf_op jit(solution)/shard_map/ppermute | solution.py:236
  64.8 14.9 %collective-permute-start.17 = (f32[2048,128]{1,0:T(8,128)}, f32[2048,128]{1,0:T(8,128)S(1)}, u32[]{:S(2)}, u32[]{:S(2)}) collective-permute-start(f32[2048,128]{1,0:T(8,128)} %get-tuple-element.61), channel_id=1, source_target_pairs={{0,2},{2,0},{4,6},{6,4},{8,10},{10,8},{12,14},{14,12},{16,18},{18,... | collective-permute-start | bytes 3145736 | tf_op jit(solution)/shard_map/ppermute | solution.py:241
  79.6 3.8 %collective-permute-start.16 = (f32[2048,128]{1,0:T(8,128)}, f32[2048,128]{1,0:T(8,128)}, u32[]{:S(2)}, u32[]{:S(2)}) collective-permute-start(f32[2048,128]{1,0:T(8,128)} %get-tuple-element.57), channel_id=1, source_target_pairs={{0,2},{2,0},{4,6},{6,4},{8,10},{10,8},{12,14},{14,12},{16,18},{18,... | collective-permute-start | bytes 3145736 | tf_op jit(solution)/shard_map/ppermute | solution.py:241

commit v5 on v4

--- a/solution.py
+++ b/solution.py
@@ -9,7 +9,7 @@
 
 LANES = 128
 ROWS = 16
-VMEM_BYTES = 16 * 1024 * 1024
+VMEM_BYTES = 24 * 1024 * 1024
 
 
 def shifted(value, axis, steps):
@@ -38,6 +38,14 @@
         "sity,szty->izy", source, jnp.concatenate(slabs, axis=1), preferred_element_type=jnp.float32
     )
     return band_rows(product, width, 4 * cells + 1) * scale
+
+
+GAP = 3
+
+
+def apart(count):
+    stride = GAP * count
+    return stride + 1 - stride % 2
 
 
 def in_vmem(*values):
@@ -67,13 +75,15 @@
         for cell in range(count):
             for lanes in range(0, cross, LANES):
                 tile = buffer_ref[part, :, cell, :, lanes : lanes + LANES].reshape(shots * times, LANES)
-                rows_ref[pl.ds(lanes * cells + part * count + cell, LANES, stride=cells), :] = tile.astype(jnp.float32).T
-    share = cross // 4 * cells
+                base = lanes * apart(cells) + GAP * (part * count + cell)
+                rows_ref[pl.ds(base, LANES, stride=apart(cells)), :] = tile.astype(jnp.float32).T
     half, core = which_ref[0], which_ref[1]
     quarters = [2 * half + core, 2 * half + 1 - core, 2 - 2 * half + core, 3 - 2 * half - core]
     for turned_ref, quarter in zip(turned_refs, quarters):
-        rows = rows_ref[pl.ds(pl.multiple_of(quarter * share, share), share), :]
-        turned_ref[...] = rows.reshape(turned_ref.shape).astype(turned_ref.dtype)
+        share = turned_ref.shape[0]
+        for place in range(share):
+            base = (quarter * share + place) * apart(cells)
+            turned_ref[place] = rows_ref[pl.ds(base, cells, stride=GAP), :].astype(turned_ref.dtype)
 
 
 def turn(raw, which):
@@ -87,7 +97,7 @@
         out_shape=[jax.ShapeDtypeStruct((cross // 4, cells, depth), raw.dtype)] * 4,
         scratch_shapes=[
             pltpu.VMEM((parts, shots, cells // parts, times, cross), raw.dtype),
-            pltpu.VMEM((cross * cells, depth), jnp.float32),
+            pltpu.VMEM((cross * apart(cells), depth), jnp.float32),
             pltpu.SemaphoreType.DMA((parts,)),
         ],
         compiler_params=params(),
@@ -153,49 +163,55 @@
     )(core.reshape(1), *in_vmem(*sources, *flat, *before))
 
 
-def spread_cell(where_ref, cells, cell, kept_ref, came_ref, slabs, factor, skewed_ref):
-    kept, came = (ref[pl.ds(cell, LANES // 2, stride=cells), :] for ref in (kept_ref, came_ref))
-    core = where_ref[6]
-    low = jnp.where(core == 0, kept, came)
-    high = jnp.where(core == 0, came, kept)
-    turned = jnp.concatenate([low, high], axis=0).T * factor
-    for place, slab in enumerate(slabs):
-        lag = (where_ref[slab] + 4) * cells - cell
-        skewed_ref[pl.ds(lag * cells + cell, cells, stride=cells), :] = turned[cells * place : cells * (place + 1)]
-
-
-def early_spread_body(scale, cells, where_ref, kept_ref, came_ref, skewed_ref):
+def gather_rows(where_ref, cells, kept_ref, came_ref, rows_ref):
+    share = kept_ref.shape[0] // cells
+    for ref, first in ((kept_ref, where_ref[6] * share), (came_ref, (1 - where_ref[6]) * share)):
+        for place in range(share):
+            base = (first + place) * apart(cells)
+            rows_ref[pl.ds(base, cells, stride=GAP), :] = ref[place * cells : (place + 1) * cells, :]
+
+
+def spread_rows(where_ref, cells, slabs, factor, rows_ref, skewed_ref):
+    line = skewed_ref.shape[0] // cells
     for cell in range(cells):
-        spread_cell(where_ref, cells, cell, kept_ref, came_ref, range(4), scale, skewed_ref)
+        turned = rows_ref[pl.ds(GAP * cell, LANES, stride=apart(cells)), :].T * factor
+        for place, slab in enumerate(slabs):
+            base = cell * line + GAP * ((where_ref[slab] + 4) * cells - cell)
+            skewed_ref[pl.ds(base, cells, stride=GAP), :] = turned[cells * place : cells * (place + 1)]
+
+
+def early_spread_body(scale, cells, where_ref, kept_ref, came_ref, skewed_ref, rows_ref):
+    gather_rows(where_ref, cells, kept_ref, came_ref, rows_ref)
+    spread_rows(where_ref, cells, range(4), scale, rows_ref, skewed_ref)
 
 
 def early_spread(scale, cells, where, products):
-    rows = (4 * cells + 1 + 4 * cells) * cells
+    rows = apart(4 * cells + 1 + 4 * cells) * cells
     return pl.pallas_call(
         functools.partial(early_spread_body, scale, cells),
         in_specs=[SCALARS] + [WHOLE] * 2,
         out_specs=WHOLE,
         out_shape=jax.ShapeDtypeStruct((rows, LANES), jnp.float32),
+        scratch_shapes=[pltpu.VMEM((LANES * apart(cells), LANES), jnp.float32)],
         compiler_params=params(),
         cost_estimate=pl.CostEstimate(flops=0, bytes_accessed=6 << 20, transcendentals=0),
         name="early_spread",
     )(where, *in_vmem(*products))
 
 
-def late_spread_body(scale, cells, where_ref, kept_ref, came_ref, _, skewed_ref, image_ref, sems):
-    parts = sems.shape[0]
-    count = cells // parts
-    lags = image_ref.shape[0]
+def late_spread_body(scale, cells, where_ref, kept_ref, came_ref, _, skewed_ref, image_ref, rows_ref, buffer_ref, sems):
     factor = jnp.where(where_ref[7] == 1, scale, 0.0)
-    shaped_ref = skewed_ref.reshape(skewed_ref.shape[0] // cells, cells, LANES)
+    gather_rows(where_ref, cells, kept_ref, came_ref, rows_ref)
+    spread_rows(where_ref, cells, (4, 5), factor, rows_ref, skewed_ref)
+    line = skewed_ref.shape[0] // cells
+    parts, lags = sems.shape[0], image_ref.shape[0]
+    cuts = [lags * part // parts for part in range(parts + 1)]
     copies = []
-    for part in range(parts):
-        for cell in range(part * count, (part + 1) * count):
-            spread_cell(where_ref, cells, cell, kept_ref, came_ref, (4, 5), factor, skewed_ref)
-        rows = pl.ds(part * count, count)
-        copies.append(
-            pltpu.make_async_copy(shaped_ref.at[pl.ds(2 * cells, lags), rows], image_ref.at[:, rows], sems.at[part])
-        )
+    for part, (start, stop) in enumerate(zip(cuts, cuts[1:])):
+        for lag in range(start, stop):
+            buffer_ref[lag] = skewed_ref[pl.ds(GAP * (2 * cells + lag), cells, stride=line), :]
+        block = pl.ds(start, stop - start)
+        copies.append(pltpu.make_async_copy(buffer_ref.at[block], image_ref.at[block], sems.at[part]))
         copies[-1].start()
     for copy in copies:
         copy.wait()
@@ -212,7 +228,11 @@
             jax.ShapeDtypeStruct((lags, cells, LANES), jnp.float32),
         ],
         input_output_aliases={3: 0},
-        scratch_shapes=[pltpu.SemaphoreType.DMA((4,))],
+        scratch_shapes=[
+            pltpu.VMEM((LANES * apart(cells), LANES), jnp.float32),
+            pltpu.VMEM((lags, cells, LANES), jnp.float32),
+            pltpu.SemaphoreType.DMA((4,)),
+        ],
         compiler_params=params(),
         name="late_spread",
     )(where, *in_vmem(*products, skewed))[1]
@@ -251,30 +271,30 @@
     kept, lent, there, there_twin = turn(receiver, which)
     y0 = along_y(kept)
     twin = to_core(lent)
-    moved, moved_twin = across(there), across_to_core(there_twin)
-    source, _ = barrier(source, kept)
+    there, twin = barrier(there, twin)
+    moved = across(there)
+    y1 = along_y(twin)
+    source, _ = barrier(source, twin)
     left, left_lent, far, far_lent = turn(source, which)
+    moved, y0, there_twin, left_lent = barrier(moved, y0, there_twin, left_lent)
     left_twin = to_core(left_lent)
-    y1 = along_y(twin)
-    moved, y0 = barrier(moved, y0)
     y2, z0 = along_y(moved), along_z(y0)
+    moved_twin = across_to_core(there_twin)
     moved_twin, y1, far, far_lent = barrier(moved_twin, y1, far, far_lent)
-    middle_share = moved_twin.shape[0] // 2
-    y3 = [along_y(moved_twin[:middle_share]), along_y(moved_twin[middle_share:])]
-    z1 = along_z(y1)
+    y3, z1 = along_y(moved_twin), along_z(y1)
     right, right_twin = across(far), across_to_core(far_lent)
     z2 = along_z(y2)
     early = multiply(core, (left, left_twin), [(piece,) for piece in (kept, twin, y0, y1, z0, z1)])
-    y3[1], *early = barrier(y3[1], *early)
-    z3 = [along_z(part) for part in y3]
-    middle = multiply(core, (right, right_twin), ((moved,), (moved_twin,), (y2,), y3), (early[0], early[2]))
+    y3, *early = barrier(y3, *early)
+    z3 = along_z(y3)
+    middle = multiply(core, (right, right_twin), ((moved,), (moved_twin,), (y2,), (y3,)), (early[0], early[2]))
     middle_came = to_core(middle[1])
     side = 2 - 4 * odd
     end = jnp.where(odd == 0, own >> 1 == 0, own >> 1 == count // 2 - 1)
     where = jnp.stack([block + shift - core for shift in (0, side, -side) for block in (0, 1)] + [core, 1 - end])
     where = where.astype(jnp.int32)
     skewed = early_spread(scale, cells, where, (middle[0], middle_came))
-    late = multiply(core, (right, right_twin), ((z2,), z3), (early[1], early[3]))
+    late = multiply(core, (right, right_twin), ((z2,), (z3,)), (early[1], early[3]))
     late_came = to_core(late[1])
     return late_spread(scale, cells, where, (late[0], late_came), skewed)
 

time: 88.1 us -> 81.9 us (0.930)
  Pallas kernels: 27.6 us -> 18.9 us
  waiting for transfers between devices: 37.6 us -> 40.3 us
    pallas_call x2, Pallas kernels: 10.8 us -> 5.38 us  [turn(): pl.pallas_call(turn_body, in_specs=[SCALARS, pl.BlockSpec(memory_space=pl...]
    ppermute x2, waiting for transfers between devices: 7.84 us -> 12.3 us  [across_to_core(): return lax.ppermute(value, ('inline', 'shot'), pairs)]
    ppermute x2, waiting for transfers between devices: 5.14 us -> 1.64 us  [across(): return lax.ppermute(value, 'shot', [(0, 1), (1, 0)])]
    ppermute x5 -> x4, starting transfers between devices: 8.12 us -> 5.67 us  [along_z(): lax.ppermute(value, 'inline', [(index, (index + steps[index // 2 % 2]) %...]
    pallas_call x1, Pallas kernels: 3.74 us -> 1.29 us  [early_spread(): pl.pallas_call(functools.partial(early_spread_body, scale, cells), in_spe...]
    ppermute x5 -> x4, waiting for transfers between devices: 10.6 us -> 12.3 us  [along_z(): lax.ppermute(value, 'inline', [(index, (index + steps[index // 2 % 2]) %...]
    ppermute x5 -> x4, waiting for transfers between devices: 14.1 us -> 12.4 us  [along_y(): lax.ppermute(value, 'inline', [(index, index ^ 2) for index in range(coun...]
    ppermute x4, waiting for transfers between devices: 0.01 us -> 1.62 us  [to_core(): lax.ppermute(value, 'inline', [(index, index ^ 1) for index in range(coun...]
  transfers between devices with their start and end apart: 18 -> 16, of which waited for: 10 -> 10; matrix products, arithmetic and copies ran while one was open for 0% -> 0% of each run, Pallas kernels for 20% -> 16%
where the time goes in v5:
time: 81.9 us; the launch traced here: 81.7 us
  waiting for transfers between devices  40.3 us (49%)
  starting transfers between devices  22.3 us (27%)
  Pallas kernels  18.9 us (23%)
    ppermute x4, waiting for transfers between devices, along_y(): lax.ppermute(value, 'inline', [(index, index ^ 2) for index in range(coun...  12.4 us
    ppermute x2, waiting for transfers between devices, across_to_core(): return lax.ppermute(value, ('inline', 'shot'), pairs)  12.3 us
    ppermute x4, waiting for transfers between devices, along_z(): lax.ppermute(value, 'inline', [(index, (index + steps[index // 2 % 2]) %...  12.3 us
    ppermute x4, starting transfers between devices, along_y(): lax.ppermute(value, 'inline', [(index, index ^ 2) for index in range(coun...  9.18 us
    pallas_call x3, Pallas kernels, multiply(): pl.pallas_call(functools.partial(multiply_body, [len(piece) for piece in...  8.84 us
    ppermute x4, starting transfers between devices, along_z(): lax.ppermute(value, 'inline', [(index, (index + steps[index // 2 % 2]) %...  5.67 us
    pallas_call x2, Pallas kernels, turn(): pl.pallas_call(turn_body, in_specs=[SCALARS, pl.BlockSpec(memory_space=pl...  5.38 us
    pallas_call x1, Pallas kernels, late_spread(): pl.pallas_call(functools.partial(late_spread_body, scale, cells), in_spec...  3.35 us
  transfers between devices with their start and end apart: 16, of which 10 were waited for; matrix products, arithmetic and copies ran while one was open for 0% of the time, Pallas kernels for 16%

profile of v5, /device:TPU:0, one launch (start us, length us, event | category | flops | bytes accessed | tf_op | source)
XLA Modules:
  0.0 81.7 jit_solution(845780359554868815)
XLA Ops:
  0.0 0.1 pad_add_fusion.which_ref
  0.1 2.7 %turn.2 = (bf16[64,32,128]{2,1,0:T(8,128)(2,1)S(1)}, bf16[64,32,128]{2,1,0:T(8,128)(2,1)S(1)}, bf16[64,32,128]{2,1,0:T(8,128)(2,1)S(1)}, bf16[64,32,128]{2,1,0:T(8,128)(2,1)S(1)}) custom-call(s32[2]{0:T(128)S(1)} %pad_add_fusion.which_ref, bf16[4,32,32,256]{3,2,1,0:T(8,128)(2,1)} %raw_ref.1), custom_call_target="tpu_custom_call" | custom-call | bytes 4194304 | tf_op jit(solution)/shard_map/turn/pallas_call | solution.py:93
  2.8 0.5 collective-permute-start
  3.3 2.6 %collective-permute-start.2 = (bf16[64,32,128]{2,1,0:T(8,128)(2,1)S(1)}, bf16[64,32,128]{2,1,0:T(8,128)(2,1)S(1)}, u32[]{:S(2)}, u32[]{:S(2)}) collective-permute-start(bf16[64,32,128]{2,1,0:T(8,128)(2,1)S(1)} %get-tuple-element.41.refs_2_), channel_id=1, source_target_pairs={{0,4},{2,6},{4,0},{6,2},{8,12},{10,14},{12,8},{14,10},{16,20},{18,... | collective-permute-start | bytes 1572872 | tf_op jit(solution)/shard_map/ppermute | solution.py:252
  5.9 0.0 collective-permute-done.refs_3_
  5.9 1.8 %collective-permute-start.1 = (bf16[64,32,128]{2,1,0:T(8,128)(2,1)S(1)}, bf16[64,32,128]{2,1,0:T(8,128)(2,1)S(1)}, u32[]{:S(2)}, u32[]{:S(2)}) collective-permute-start(bf16[64,32,128]{2,1,0:T(8,128)(2,1)S(1)} %get-tuple-element.40), channel_id=1, source_target_pairs={{0,1},{1,0},{2,3},{3,2},{4,5},{5,4},{6,7},{7,6},{8,9},{9,8},{10,11... | collective-permute-start | bytes 1572872 | tf_op jit(solution)/shard_map/ppermute | solution.py:249
  7.7 1.5 %collective-permute-start.4 = (bf16[64,32,128]{2,1,0:T(8,128)(2,1)S(1)}, bf16[64,32,128]{2,1,0:T(8,128)(2,1)S(1)}, u32[]{:S(2)}, u32[]{:S(2)}) collective-permute-start(bf16[64,32,128]{2,1,0:T(8,128)(2,1)S(1)} %collective-permute-done.refs_3_), channel_id=1, source_target_pairs={{0,4},{2,6},{4,0},{6,2},{8,12},{10,14},{12,8},{14,10},{16,20},{18,... | collective-permute-start | bytes 1572872 | tf_op jit(solution)/shard_map/ppermute | solution.py:252
  9.2 2.7 %turn.3 = (bf16[64,32,128]{2,1,0:T(8,128)(2,1)S(1)}, bf16[64,32,128]{2,1,0:T(8,128)(2,1)S(1)}, bf16[64,32,128]{2,1,0:T(8,128)(2,1)S(1)}, bf16[64,32,128]{2,1,0:T(8,128)(2,1)S(1)}) custom-call(s32[2]{0:T(128)S(1)} %pad_add_fusion.which_ref, bf16[4,32,32,256]{3,2,1,0:T(8,128)(2,1)} %raw_ref.2), custom_call_target="tpu_custom_call" | custom-call | bytes 4194304 | tf_op jit(solution)/shard_map/turn/pallas_call | solution.py:93
  11.9 6.8 %collective-permute-done.2.refs_4_ = bf16[64,32,128]{2,1,0:T(8,128)(2,1)S(1)} collective-permute-done((bf16[64,32,128]{2,1,0:T(8,128)(2,1)S(1)}, bf16[64,32,128]{2,1,0:T(8,128)(2,1)S(1)}, u32[]{:S(2)}, u32[]{:S(2)}) %collective-permute-start.2) | collective-permute-done | bytes 524320 | tf_op jit(solution)/shard_map/ppermute | solution.py:252
  18.7 1.3 %collective-permute-done.1.refs_2_ = bf16[64,32,128]{2,1,0:T(8,128)(2,1)S(1)} collective-permute-done((bf16[64,32,128]{2,1,0:T(8,128)(2,1)S(1)}, bf16[64,32,128]{2,1,0:T(8,128)(2,1)S(1)}, u32[]{:S(2)}, u32[]{:S(2)}) %collective-permute-start.1) | collective-permute-done | bytes 524320 | tf_op jit(solution)/shard_map/ppermute | solution.py:249
  19.9 0.7 collective-permute-start.3
  20.6 1.2 %collective-permute-start.10 = (bf16[64,32,128]{2,1,0:T(8,128)(2,1)S(1)}, bf16[64,32,128]{2,1,0:T(8,128)(2,1)S(1)}, u32[]{:S(2)}, u32[]{:S(2)}) collective-permute-start(bf16[64,32,128]{2,1,0:T(8,128)(2,1)S(1)} %get-tuple-element.54), channel_id=1, source_target_pairs={{0,2},{2,0},{4,6},{6,4},{8,10},{10,8},{12,14},{14,12},{16,18},{18,... | collective-permute-start | bytes 1572872 | tf_op jit(solution)/shard_map/ppermute | solution.py:261
  21.8 1.5 %collective-permute-start.7 = (bf16[64,32,128]{2,1,0:T(8,128)(2,1)S(1)}, bf16[64,32,128]{2,1,0:T(8,128)(2,1)S(1)}, u32[]{:S(2)}, u32[]{:S(2)}) collective-permute-start(bf16[64,32,128]{2,1,0:T(8,128)(2,1)S(1)} %collective-permute-done.1.refs_2_), channel_id=1, source_target_pairs={{0,4},{2,6},{4,0},{6,2},{8,12},{10,14},{12,8},{14,10},{16,20},{18,... | collective-permute-start | bytes 1572872 | tf_op jit(solution)/shard_map/ppermute | solution.py:252
  23.3 1.6 %collective-permute-start.11 = (bf16[64,32,128]{2,1,0:T(8,128)(2,1)S(1)}, bf16[64,32,128]{2,1,0:T(8,128)(2,1)S(1)}, u32[]{:S(2)}, u32[]{:S(2)}) collective-permute-start(bf16[64,32,128]{2,1,0:T(8,128)(2,1)S(1)} %collective-permute-done.2.refs_4_), channel_id=1, source_target_pairs={{0,8},{2,10},{4,28},{6,30},{8,16},{10,18},{12,4},{14,6},{16,24},{1... | collective-permute-start | bytes 1572872 | tf_op jit(solution)/shard_map/ppermute | solution.py:256
  24.9 5.0 %collective-permute-done.4.refs_5_ = bf16[64,32,128]{2,1,0:T(8,128)(2,1)S(1)} collective-permute-done((bf16[64,32,128]{2,1,0:T(8,128)(2,1)S(1)}, bf16[64,32,128]{2,1,0:T(8,128)(2,1)S(1)}, u32[]{:S(2)}, u32[]{:S(2)}) %collective-permute-start.4) | collective-permute-done | bytes 524320 | tf_op jit(solution)/shard_map/ppermute | solution.py:252
  29.9 3.9 %collective-permute-done.3.refs_3_ = bf16[64,32,128]{2,1,0:T(8,128)(2,1)S(1)} collective-permute-done((bf16[64,32,128]{2,1,0:T(8,128)(2,1)S(1)}, bf16[64,32,128]{2,1,0:T(8,128)(2,1)S(1)}, u32[]{:S(2)}, u32[]{:S(2)}) %collective-permute-start.3) | collective-permute-done | bytes 524320 | tf_op jit(solution)/shard_map/ppermute | solution.py:265
  33.8 2.1 %collective-permute-start.12 = (bf16[64,32,128]{2,1,0:T(8,128)(2,1)S(1)}, bf16[64,32,128]{2,1,0:T(8,128)(2,1)S(1)}, u32[]{:S(2)}, u32[]{:S(2)}) collective-permute-start(bf16[64,32,128]{2,1,0:T(8,128)(2,1)S(1)} %collective-permute-done.4.refs_5_), channel_id=1, source_target_pairs={{0,8},{2,10},{4,28},{6,30},{8,16},{10,18},{12,4},{14,6},{16,24},{1... | collective-permute-start | bytes 1572872 | tf_op jit(solution)/shard_map/ppermute | solution.py:256
  35.9 3.5 %collective-permute-start.9 = (bf16[64,32,128]{2,1,0:T(8,128)(2,1)S(1)}, bf16[64,32,128]{2,1,0:T(8,128)(2,1)S(1)}, u32[]{:S(2)}, u32[]{:S(2)}) collective-permute-start(bf16[64,32,128]{2,1,0:T(8,128)(2,1)S(1)} %collective-permute-done.3.refs_3_), channel_id=1, source_target_pairs={{0,4},{2,6},{4,0},{6,2},{8,12},{10,14},{12,8},{14,10},{16,20},{18,... | collective-permute-start | bytes 1572872 | tf_op jit(solution)/shard_map/ppermute | solution.py:252
  39.5 0.0 collective-permute-done.10.refs_1_
  39.5 1.0 %collective-permute-start.5 = (bf16[64,32,128]{2,1,0:T(8,128)(2,1)S(1)}, bf16[64,32,128]{2,1,0:T(8,128)(2,1)S(1)}, u32[]{:S(2)}, u32[]{:S(2)}) collective-permute-start(bf16[64,32,128]{2,1,0:T(8,128)(2,1)S(1)} %get-tuple-element.49), channel_id=1, source_target_pairs={{0,1},{1,0},{2,3},{3,2},{4,5},{5,4},{6,7},{7,6},{8,9},{9,8},{10,11... | collective-permute-start | bytes 1572872 | tf_op jit(solution)/shard_map/ppermute | solution.py:249
  40.5 0.6 collective-permute-done.7.refs_4_
  41.1 0.7 collective-permute-start.6
  41.9 0.0 collective-permute-done.11.refs_6_
  41.9 1.6 %collective-permute-start.8 = (bf16[64,32,128]{2,1,0:T(8,128)(2,1)S(1)}, bf16[64,32,128]{2,1,0:T(8,128)(2,1)S(1)}, u32[]{:S(2)}, u32[]{:S(2)}) collective-permute-start(bf16[64,32,128]{2,1,0:T(8,128)(2,1)S(1)} %collective-permute-done.7.refs_4_), channel_id=1, source_target_pairs={{0,8},{2,10},{4,28},{6,30},{8,16},{10,18},{12,4},{14,6},{16,24},{1... | collective-permute-start | bytes 1572872 | tf_op jit(solution)/shard_map/ppermute | solution.py:256
  43.4 7.2 %collective-permute-done.12.refs_7_ = bf16[64,32,128]{2,1,0:T(8,128)(2,1)S(1)} collective-permute-done((bf16[64,32,128]{2,1,0:T(8,128)(2,1)S(1)}, bf16[64,32,128]{2,1,0:T(8,128)(2,1)S(1)}, u32[]{:S(2)}, u32[]{:S(2)}) %collective-permute-start.12) | collective-permute-done | bytes 524320 | tf_op jit(solution)/shard_map/ppermute | solution.py:256
  50.7 2.8 %multiply.3 = (f32[2048,128]{1,0:T(8,128)S(1)}, f32[2048,128]{1,0:T(8,128)S(1)}, f32[2048,128]{1,0:T(8,128)S(1)}, f32[2048,128]{1,0:T(8,128)S(1)}) custom-call(s32[1]{0:T(128)} %bitcast.6.core_ref, bf16[64,32,128]{2,1,0:T(8,128)(2,1)S(1)} %get-tuple-element.53.refs_0_, bf16[64,32,128]{2,1,0:T(8,128)(2,1)S(1)} %collective-permute-done.10.refs_1_, ...), custom_call_target="tpu_custom_call" | custom-call | flops 201326592 | bytes 6291456 | tf_op jit(solution)/shard_map/multiply/pallas_call | solution.py:154
  53.5 0.0 collective-permute-done.9.refs_5_
  53.5 0.4 collective-permute-start.13
  53.9 0.4 collective-permute-done.5.refs_0_
  54.3 8.4 %collective-permute-done.6.refs_1_ = bf16[64,32,128]{2,1,0:T(8,128)(2,1)S(1)} collective-permute-done((bf16[64,32,128]{2,1,0:T(8,128)(2,1)S(1)}, bf16[64,32,128]{2,1,0:T(8,128)(2,1)S(1)}, u32[]{:S(2)}, u32[]{:S(2)}) %collective-permute-start.6) | collective-permute-done | bytes 524320 | tf_op jit(solution)/shard_map/ppermute | solution.py:265
  62.7 3.3 %multiply.5 = (f32[2048,128]{1,0:T(8,128)S(1)}, f32[2048,128]{1,0:T(8,128)}) custom-call(s32[1]{0:T(128)} %bitcast.6.core_ref, bf16[64,32,128]{2,1,0:T(8,128)(2,1)S(1)} %collective-permute-done.5.refs_0_, bf16[64,32,128]{2,1,0:T(8,128)(2,1)S(1)} %collective-permute-done.6.refs_1_, bf16[64,32,128]{2,1,0:T(8,128)(2,1)S(1)} %collective-permute-done.1.refs_2_, ...), custom_call_target="tpu_custom_call" | custom-call | flops 134217728 | bytes 6291456 | tf_op jit(solution)/shard_map/multiply/pallas_call | solution.py:154
  66.1 1.5 %collective-permute-start.15 = (f32[2048,128]{1,0:T(8,128)}, f32[2048,128]{1,0:T(8,128)S(1)}, u32[]{:S(2)}, u32[]{:S(2)}) collective-permute-start(f32[2048,128]{1,0:T(8,128)} %get-tuple-element.69), channel_id=1, source_target_pairs={{0,2},{2,0},{4,6},{6,4},{8,10},{10,8},{12,14},{14,12},{16,18},{18,... | collective-permute-start | bytes 3145736 | tf_op jit(solution)/shard_map/ppermute | solution.py:261
  67.6 0.0 collective-permute-done.8.refs_2_
  67.6 5.1 %collective-permute-done.13.refs_3_ = bf16[64,32,128]{2,1,0:T(8,128)(2,1)S(1)} collective-permute-done((bf16[64,32,128]{2,1,0:T(8,128)(2,1)S(1)}, bf16[64,32,128]{2,1,0:T(8,128)(2,1)S(1)}, u32[]{:S(2)}, u32[]{:S(2)}) %collective-permute-start.13) | collective-permute-done | bytes 524320 | tf_op jit(solution)/shard_map/ppermute | solution.py:256
  72.7 2.7 %multiply.4 = (f32[2048,128]{1,0:T(8,128)S(1)}, f32[2048,128]{1,0:T(8,128)}) custom-call(s32[1]{0:T(128)} %bitcast.6.core_ref, bf16[64,32,128]{2,1,0:T(8,128)(2,1)S(1)} %collective-permute-done.5.refs_0_, bf16[64,32,128]{2,1,0:T(8,128)(2,1)S(1)} %collective-permute-done.6.refs_1_, bf16[64,32,128]{2,1,0:T(8,128)(2,1)S(1)} %collective-permute-done.8.refs_2_, ...), custom_call_target="tpu_custom_call" | custom-call | flops 67108864 | bytes 6291456 | tf_op jit(solution)/shard_map/multiply/pallas_call | solution.py:154
  75.3 0.0 collective-permute-start.14
  75.3 0.1 stack.42.where_ref
  75.4 0.0 collective-permute-done.15.came_ref
  75.4 1.3 %early_spread.1._ = f32[24672,128]{1,0:T(8,128)S(1)} custom-call(s32[8]{0:T(128)S(1)} %stack.42.where_ref, f32[2048,128]{1,0:T(8,128)S(1)} %get-tuple-element.68.kept_ref, f32[2048,128]{1,0:T(8,128)S(1)} %collective-permute-done.15.came_ref), custom_call_target="tpu_custom_call" | custom-call | bytes 6291456 | tf_op jit(solution)/shard_map/early_spread/pallas_call | solution.py:190
  76.7 1.6 %collective-permute-done.14.came_ref = f32[2048,128]{1,0:T(8,128)} collective-permute-done((f32[2048,128]{1,0:T(8,128)}, f32[2048,128]{1,0:T(8,128)}, u32[]{:S(2)}, u32[]{:S(2)}) %collective-permute-start.14) | collective-permute-done | bytes 1048608 | tf_op jit(solution)/shard_map/ppermute | solution.py:261
  78.3 3.4 %late_spread.1 = (f32[24672,128]{1,0:T(8,128)S(1)}, f32[129,32,128]{2,1,0:T(8,128)}) custom-call(s32[8]{0:T(128)S(1)} %stack.42.where_ref, f32[2048,128]{1,0:T(8,128)S(1)} %get-tuple-element.64.kept_ref, f32[2048,128]{1,0:T(8,128)} %collective-permute-done.14.came_ref, f32[24672,128]{1,0:T(8,128)S(1)} %early_spread.1._), custom_call_target="tpu_custom_call", output_to_operand_aliasing={{0}: (3, {})} | custom-call | tf_op jit(solution)/shard_map/late_spread/pallas_call | solution.py:222
Async XLA Ops:
  2.8 3.1 %collective-permute-start = (bf16[64,32,128]{2,1,0:T(8,128)(2,1)S(1)}, bf16[64,32,128]{2,1,0:T(8,128)(2,1)S(1)}, u32[]{:S(2)}, u32[]{:S(2)}) collective-permute-start(bf16[64,32,128]{2,1,0:T(8,128)(2,1)S(1)} %get-tuple-element.39), channel_id=1, source_target_pairs={{0,2},{2,0},{4,6},{6,4},{8,10},{10,8},{12,14},{14,12},{16,18},{18,... | collective-permute-start | bytes 1572872 | tf_op jit(solution)/shard_map/ppermute | solution.py:261
  3.3 15.4 %collective-permute-start.2 = (bf16[64,32,128]{2,1,0:T(8,128)(2,1)S(1)}, bf16[64,32,128]{2,1,0:T(8,128)(2,1)S(1)}, u32[]{:S(2)}, u32[]{:S(2)}) collective-permute-start(bf16[64,32,128]{2,1,0:T(8,128)(2,1)S(1)} %get-tuple-element.41.refs_2_), channel_id=1, source_target_pairs={{0,4},{2,6},{4,0},{6,2},{8,12},{10,14},{12,8},{14,10},{16,20},{18,... | collective-permute-start | bytes 1572872 | tf_op jit(solution)/shard_map/ppermute | solution.py:252
  5.9 14.0 %collective-permute-start.1 = (bf16[64,32,128]{2,1,0:T(8,128)(2,1)S(1)}, bf16[64,32,128]{2,1,0:T(8,128)(2,1)S(1)}, u32[]{:S(2)}, u32[]{:S(2)}) collective-permute-start(bf16[64,32,128]{2,1,0:T(8,128)(2,1)S(1)} %get-tuple-element.40), channel_id=1, source_target_pairs={{0,1},{1,0},{2,3},{3,2},{4,5},{5,4},{6,7},{7,6},{8,9},{9,8},{10,11... | collective-permute-start | bytes 1572872 | tf_op jit(solution)/shard_map/ppermute | solution.py:249
  7.7 22.2 %collective-permute-start.4 = (bf16[64,32,128]{2,1,0:T(8,128)(2,1)S(1)}, bf16[64,32,128]{2,1,0:T(8,128)(2,1)S(1)}, u32[]{:S(2)}, u32[]{:S(2)}) collective-permute-start(bf16[64,32,128]{2,1,0:T(8,128)(2,1)S(1)} %collective-permute-done.refs_3_), channel_id=1, source_target_pairs={{0,4},{2,6},{4,0},{6,2},{8,12},{10,14},{12,8},{14,10},{16,20},{18,... | collective-permute-start | bytes 1572872 | tf_op jit(solution)/shard_map/ppermute | solution.py:252
  19.9 13.9 %collective-permute-start.3 = (bf16[64,32,128]{2,1,0:T(8,128)(2,1)S(1)}, bf16[64,32,128]{2,1,0:T(8,128)(2,1)S(1)}, u32[]{:S(2)}, u32[]{:S(2)}) collective-permute-start(bf16[64,32,128]{2,1,0:T(8,128)(2,1)S(1)} %get-tuple-element.46), channel_id=1, source_target_pairs={{0,3},{1,2},{2,1},{3,0},{4,7},{5,6},{6,5},{7,4},{8,11},{9,10},{10,... | collective-permute-start | bytes 1572872 | tf_op jit(solution)/shard_map/ppermute | solution.py:265
  20.6 18.9 %collective-permute-start.10 = (bf16[64,32,128]{2,1,0:T(8,128)(2,1)S(1)}, bf16[64,32,128]{2,1,0:T(8,128)(2,1)S(1)}, u32[]{:S(2)}, u32[]{:S(2)}) collective-permute-start(bf16[64,32,128]{2,1,0:T(8,128)(2,1)S(1)} %get-tuple-element.54), channel_id=1, source_target_pairs={{0,2},{2,0},{4,6},{6,4},{8,10},{10,8},{12,14},{14,12},{16,18},{18,... | collective-permute-start | bytes 1572872 | tf_op jit(solution)/shard_map/ppermute | solution.py:261
  21.8 19.4 %collective-permute-start.7 = (bf16[64,32,128]{2,1,0:T(8,128)(2,1)S(1)}, bf16[64,32,128]{2,1,0:T(8,128)(2,1)S(1)}, u32[]{:S(2)}, u32[]{:S(2)}) collective-permute-start(bf16[64,32,128]{2,1,0:T(8,128)(2,1)S(1)} %collective-permute-done.1.refs_2_), channel_id=1, source_target_pairs={{0,4},{2,6},{4,0},{6,2},{8,12},{10,14},{12,8},{14,10},{16,20},{18,... | collective-permute-start | bytes 1572872 | tf_op jit(solution)/shard_map/ppermute | solution.py:252
  23.3 18.6 %collective-permute-start.11 = (bf16[64,32,128]{2,1,0:T(8,128)(2,1)S(1)}, bf16[64,32,128]{2,1,0:T(8,128)(2,1)S(1)}, u32[]{:S(2)}, u32[]{:S(2)}) collective-permute-start(bf16[64,32,128]{2,1,0:T(8,128)(2,1)S(1)} %collective-permute-done.2.refs_4_), channel_id=1, source_target_pairs={{0,8},{2,10},{4,28},{6,30},{8,16},{10,18},{12,4},{14,6},{16,24},{1... | collective-permute-start | bytes 1572872 | tf_op jit(solution)/shard_map/ppermute | solution.py:256
  33.8 16.8 %collective-permute-start.12 = (bf16[64,32,128]{2,1,0:T(8,128)(2,1)S(1)}, bf16[64,32,128]{2,1,0:T(8,128)(2,1)S(1)}, u32[]{:S(2)}, u32[]{:S(2)}) collective-permute-start(bf16[64,32,128]{2,1,0:T(8,128)(2,1)S(1)} %collective-permute-done.4.refs_5_), channel_id=1, source_target_pairs={{0,8},{2,10},{4,28},{6,30},{8,16},{10,18},{12,4},{14,6},{16,24},{1... | collective-permute-start | bytes 1572872 | tf_op jit(solution)/shard_map/ppermute | solution.py:256
  35.9 17.6 %collective-permute-start.9 = (bf16[64,32,128]{2,1,0:T(8,128)(2,1)S(1)}, bf16[64,32,128]{2,1,0:T(8,128)(2,1)S(1)}, u32[]{:S(2)}, u32[]{:S(2)}) collective-permute-start(bf16[64,32,128]{2,1,0:T(8,128)(2,1)S(1)} %collective-permute-done.3.refs_3_), channel_id=1, source_target_pairs={{0,4},{2,6},{4,0},{6,2},{8,12},{10,14},{12,8},{14,10},{16,20},{18,... | collective-permute-start | bytes 1572872 | tf_op jit(solution)/shard_map/ppermute | solution.py:252
  39.5 14.8 %collective-permute-start.5 = (bf16[64,32,128]{2,1,0:T(8,128)(2,1)S(1)}, bf16[64,32,128]{2,1,0:T(8,128)(2,1)S(1)}, u32[]{:S(2)}, u32[]{:S(2)}) collective-permute-start(bf16[64,32,128]{2,1,0:T(8,128)(2,1)S(1)} %get-tuple-element.49), channel_id=1, source_target_pairs={{0,1},{1,0},{2,3},{3,2},{4,5},{5,4},{6,7},{7,6},{8,9},{9,8},{10,11... | collective-permute-start | bytes 1572872 | tf_op jit(solution)/shard_map/ppermute | solution.py:249
  41.1 21.6 %collective-permute-start.6 = (bf16[64,32,128]{2,1,0:T(8,128)(2,1)S(1)}, bf16[64,32,128]{2,1,0:T(8,128)(2,1)S(1)}, u32[]{:S(2)}, u32[]{:S(2)}) collective-permute-start(bf16[64,32,128]{2,1,0:T(8,128)(2,1)S(1)} %get-tuple-element.50), channel_id=1, source_target_pairs={{0,3},{1,2},{2,1},{3,0},{4,7},{5,6},{6,5},{7,4},{8,11},{9,10},{10,... | collective-permute-start | bytes 1572872 | tf_op jit(solution)/shard_map/ppermute | solution.py:265
  41.9 25.7 %collective-permute-start.8 = (bf16[64,32,128]{2,1,0:T(8,128)(2,1)S(1)}, bf16[64,32,128]{2,1,0:T(8,128)(2,1)S(1)}, u32[]{:S(2)}, u32[]{:S(2)}) collective-permute-start(bf16[64,32,128]{2,1,0:T(8,128)(2,1)S(1)} %collective-permute-done.7.refs_4_), channel_id=1, source_target_pairs={{0,8},{2,10},{4,28},{6,30},{8,16},{10,18},{12,4},{14,6},{16,24},{1... | collective-permute-start | bytes 1572872 | tf_op jit(solution)/shard_map/ppermute | solution.py:256
  53.5 19.2 %collective-permute-start.13 = (bf16[64,32,128]{2,1,0:T(8,128)(2,1)S(1)}, bf16[64,32,128]{2,1,0:T(8,128)(2,1)S(1)}, u32[]{:S(2)}, u32[]{:S(2)}) collective-permute-start(bf16[64,32,128]{2,1,0:T(8,128)(2,1)S(1)} %collective-permute-done.9.refs_5_), channel_id=1, source_target_pairs={{0,8},{2,10},{4,28},{6,30},{8,16},{10,18},{12,4},{14,6},{16,24},{1... | collective-permute-start | bytes 1572872 | tf_op jit(solution)/shard_map/ppermute | solution.py:256
  66.1 9.4 %collective-permute-start.15 = (f32[2048,128]{1,0:T(8,128)}, f32[2048,128]{1,0:T(8,128)S(1)}, u32[]{:S(2)}, u32[]{:S(2)}) collective-permute-start(f32[2048,128]{1,0:T(8,128)} %get-tuple-element.69), channel_id=1, source_target_pairs={{0,2},{2,0},{4,6},{6,4},{8,10},{10,8},{12,14},{14,12},{16,18},{18,... | collective-permute-start | bytes 3145736 | tf_op jit(solution)/shard_map/ppermute | solution.py:261
  75.3 3.0 %collective-permute-start.14 = (f32[2048,128]{1,0:T(8,128)}, f32[2048,128]{1,0:T(8,128)}, u32[]{:S(2)}, u32[]{:S(2)}) collective-permute-start(f32[2048,128]{1,0:T(8,128)} %get-tuple-element.65), channel_id=1, source_target_pairs={{0,2},{2,0},{4,6},{6,4},{8,10},{10,8},{12,14},{14,12},{16,18},{18,... | collective-permute-start | bytes 3145736 | tf_op jit(solution)/shard_map/ppermute | solution.py:261

commit v6 on v5

--- a/solution.py
+++ b/solution.py
@@ -200,9 +200,8 @@
 
 
 def late_spread_body(scale, cells, where_ref, kept_ref, came_ref, _, skewed_ref, image_ref, rows_ref, buffer_ref, sems):
-    factor = jnp.where(where_ref[7] == 1, scale, 0.0)
     gather_rows(where_ref, cells, kept_ref, came_ref, rows_ref)
-    spread_rows(where_ref, cells, (4, 5), factor, rows_ref, skewed_ref)
+    spread_rows(where_ref, cells, (4, 5), scale, rows_ref, skewed_ref)
     line = skewed_ref.shape[0] // cells
     parts, lags = sems.shape[0], image_ref.shape[0]
     cuts = [lags * part // parts for part in range(parts + 1)]
@@ -252,10 +251,8 @@
         return lax.ppermute(value, "inline", [(index, index ^ 2) for index in range(count)])
 
     def along_z(value):
-        steps = (4, -4)
-        return lax.ppermute(
-            value, "inline", [(index, (index + steps[index // 2 % 2]) % count) for index in range(count)]
-        )
+        pairs = [(index, index + (4, -4)[index // 2 % 2]) for index in range(count)]
+        return lax.ppermute(value, "inline", [pair for pair in pairs if 0 <= pair[1] < count])
 
     def to_core(value):
         return lax.ppermute(value, "inline", [(index, index ^ 1) for index in range(count)])
@@ -271,27 +268,28 @@
     kept, lent, there, there_twin = turn(receiver, which)
     y0 = along_y(kept)
     twin = to_core(lent)
-    there, twin = barrier(there, twin)
-    moved = across(there)
+    there, there_twin, twin = barrier(there, there_twin, twin)
+    moved, moved_twin = across(there), across_to_core(there_twin)
     y1 = along_y(twin)
     source, _ = barrier(source, twin)
     left, left_lent, far, far_lent = turn(source, which)
-    moved, y0, there_twin, left_lent = barrier(moved, y0, there_twin, left_lent)
+    moved, y0, left = barrier(moved, y0, left)
+    y2, z0 = along_y(moved), along_z(y0)
+    moved_twin, y1, far, left_lent = barrier(moved_twin, y1, far, left_lent)
+    y3, z1 = along_y(moved_twin), along_z(y1)
     left_twin = to_core(left_lent)
-    y2, z0 = along_y(moved), along_z(y0)
-    moved_twin = across_to_core(there_twin)
-    moved_twin, y1, far, far_lent = barrier(moved_twin, y1, far, far_lent)
-    y3, z1 = along_y(moved_twin), along_z(y1)
-    right, right_twin = across(far), across_to_core(far_lent)
+    right = across(far)
+    z0, far_lent, y2 = barrier(z0, far_lent, y2)
+    right_twin = across_to_core(far_lent)
     z2 = along_z(y2)
+    left_twin, right = barrier(left_twin, right)
     early = multiply(core, (left, left_twin), [(piece,) for piece in (kept, twin, y0, y1, z0, z1)])
     y3, *early = barrier(y3, *early)
     z3 = along_z(y3)
     middle = multiply(core, (right, right_twin), ((moved,), (moved_twin,), (y2,), (y3,)), (early[0], early[2]))
     middle_came = to_core(middle[1])
     side = 2 - 4 * odd
-    end = jnp.where(odd == 0, own >> 1 == 0, own >> 1 == count // 2 - 1)
-    where = jnp.stack([block + shift - core for shift in (0, side, -side) for block in (0, 1)] + [core, 1 - end])
+    where = jnp.stack([block + shift - core for shift in (0, side, -side) for block in (0, 1)] + [core])
     where = where.astype(jnp.int32)
     skewed = early_spread(scale, cells, where, (middle[0], middle_came))
     late = multiply(core, (right, right_twin), ((z2,), (z3,)), (early[1], early[3]))

time: 81.9 us -> 79.3 us (0.968)
  waiting for transfers between devices: 40.3 us -> 35 us
  starting transfers between devices: 22.3 us -> 24.9 us
    ppermute x4, starting transfers between devices: 5.67 us -> 14.6 us  [along_z(): lax.ppermute(value, 'inline', [pair for pair in pairs if 0 <= pair[1] < c...]
    ppermute x2, waiting for transfers between devices: 12.3 us -> 5.86 us  [across_to_core(): return lax.ppermute(value, ('inline', 'shot'), pairs)]
    ppermute x4, starting transfers between devices: 9.18 us -> 4.39 us  [along_y(): lax.ppermute(value, 'inline', [(index, index ^ 2) for index in range(coun...]
    ppermute x4, starting transfers between devices: 3.26 us -> 1.66 us  [to_core(): lax.ppermute(value, 'inline', [(index, index ^ 1) for index in range(coun...]
    ppermute x2, waiting for transfers between devices: 1.64 us -> 2.67 us  [across(): return lax.ppermute(value, 'shot', [(0, 1), (1, 0)])]
  transfers between devices with their start and end apart: 16 -> 16, of which waited for: 10 -> 9; matrix products, arithmetic and copies ran while one was open for 0% -> 0% of each run, Pallas kernels for 16% -> 16%
where the time goes in v6:
time: 79.3 us; the launch traced here: 79 us
  waiting for transfers between devices  35 us (44%)
  starting transfers between devices  24.9 us (31%)
  Pallas kernels  18.9 us (24%)
    ppermute x4, starting transfers between devices, along_z(): lax.ppermute(value, 'inline', [pair for pair in pairs if 0 <= pair[1] < c...  14.6 us
    ppermute x4, waiting for transfers between devices, along_z(): lax.ppermute(value, 'inline', [pair for pair in pairs if 0 <= pair[1] < c...  12.7 us
    ppermute x4, waiting for transfers between devices, along_y(): lax.ppermute(value, 'inline', [(index, index ^ 2) for index in range(coun...  12.2 us
    pallas_call x3, Pallas kernels, multiply(): pl.pallas_call(functools.partial(multiply_body, [len(piece) for piece in...  8.85 us
    ppermute x2, waiting for transfers between devices, across_to_core(): return lax.ppermute(value, ('inline', 'shot'), pairs)  5.86 us
    pallas_call x2, Pallas kernels, turn(): pl.pallas_call(turn_body, in_specs=[SCALARS, pl.BlockSpec(memory_space=pl...  5.38 us
    ppermute x4, starting transfers between devices, along_y(): lax.ppermute(value, 'inline', [(index, index ^ 2) for index in range(coun...  4.39 us
    ppermute x2, starting transfers between devices, across(): return lax.ppermute(value, 'shot', [(0, 1), (1, 0)])  3.54 us
  transfers between devices with their start and end apart: 16, of which 9 were waited for; matrix products, arithmetic and copies ran while one was open for 0% of the time, Pallas kernels for 16%

profile of v6, /device:TPU:0, one launch (start us, length us, event | category | flops | bytes accessed | tf_op | source)
XLA Modules:
  0.0 79.0 jit_solution(15910930775197635010)
XLA Ops:
  0.0 0.1 pad_add_fusion.which_ref
  0.1 2.7 %turn.2 = (bf16[64,32,128]{2,1,0:T(8,128)(2,1)S(1)}, bf16[64,32,128]{2,1,0:T(8,128)(2,1)S(1)}, bf16[64,32,128]{2,1,0:T(8,128)(2,1)S(1)}, bf16[64,32,128]{2,1,0:T(8,128)(2,1)S(1)}) custom-call(s32[2]{0:T(128)S(1)} %pad_add_fusion.which_ref, bf16[4,32,32,256]{3,2,1,0:T(8,128)(2,1)} %raw_ref.1), custom_call_target="tpu_custom_call" | custom-call | bytes 4194304 | tf_op jit(solution)/shard_map/turn/pallas_call | solution.py:93
  2.8 0.5 collective-permute-start
  3.3 2.6 %collective-permute-start.6 = (bf16[64,32,128]{2,1,0:T(8,128)(2,1)S(1)}, bf16[64,32,128]{2,1,0:T(8,128)(2,1)S(1)}, u32[]{:S(2)}, u32[]{:S(2)}) collective-permute-start(bf16[64,32,128]{2,1,0:T(8,128)(2,1)S(1)} %get-tuple-element.55.refs_2_), channel_id=1, source_target_pairs={{0,4},{2,6},{4,0},{6,2},{8,12},{10,14},{12,8},{14,10},{16,20},{18,... | collective-permute-start | bytes 1572872 | tf_op jit(solution)/shard_map/ppermute | solution.py:251
  5.9 0.0 collective-permute-done.refs_3_
  5.9 1.8 %collective-permute-start.5 = (bf16[64,32,128]{2,1,0:T(8,128)(2,1)S(1)}, bf16[64,32,128]{2,1,0:T(8,128)(2,1)S(1)}, u32[]{:S(2)}, u32[]{:S(2)}) collective-permute-start(bf16[64,32,128]{2,1,0:T(8,128)(2,1)S(1)} %get-tuple-element.54), channel_id=1, source_target_pairs={{0,1},{1,0},{2,3},{3,2},{4,5},{5,4},{6,7},{7,6},{8,9},{9,8},{10,11... | collective-permute-start | bytes 1572872 | tf_op jit(solution)/shard_map/ppermute | solution.py:248
  7.7 0.0 collective-permute-start.1
  7.7 1.6 %collective-permute-start.2 = (bf16[64,32,128]{2,1,0:T(8,128)(2,1)S(1)}, bf16[64,32,128]{2,1,0:T(8,128)(2,1)S(1)}, u32[]{:S(2)}, u32[]{:S(2)}) collective-permute-start(bf16[64,32,128]{2,1,0:T(8,128)(2,1)S(1)} %collective-permute-done.refs_3_), channel_id=1, source_target_pairs={{0,4},{2,6},{4,0},{6,2},{8,12},{10,14},{12,8},{14,10},{16,20},{18,... | collective-permute-start | bytes 1572872 | tf_op jit(solution)/shard_map/ppermute | solution.py:251
  9.2 2.7 %turn.3 = (bf16[64,32,128]{2,1,0:T(8,128)(2,1)S(1)}, bf16[64,32,128]{2,1,0:T(8,128)(2,1)S(1)}, bf16[64,32,128]{2,1,0:T(8,128)(2,1)S(1)}, bf16[64,32,128]{2,1,0:T(8,128)(2,1)S(1)}) custom-call(s32[2]{0:T(128)S(1)} %pad_add_fusion.which_ref, bf16[4,32,32,256]{3,2,1,0:T(8,128)(2,1)} %raw_ref.2), custom_call_target="tpu_custom_call" | custom-call | bytes 4194304 | tf_op jit(solution)/shard_map/turn/pallas_call | solution.py:93
  11.9 6.7 %collective-permute-done.6.refs_4_ = bf16[64,32,128]{2,1,0:T(8,128)(2,1)S(1)} collective-permute-done((bf16[64,32,128]{2,1,0:T(8,128)(2,1)S(1)}, bf16[64,32,128]{2,1,0:T(8,128)(2,1)S(1)}, u32[]{:S(2)}, u32[]{:S(2)}) %collective-permute-start.6) | collective-permute-done | bytes 524320 | tf_op jit(solution)/shard_map/ppermute | solution.py:251
  18.7 2.0 %collective-permute-done.5.refs_2_ = bf16[64,32,128]{2,1,0:T(8,128)(2,1)S(1)} collective-permute-done((bf16[64,32,128]{2,1,0:T(8,128)(2,1)S(1)}, bf16[64,32,128]{2,1,0:T(8,128)(2,1)S(1)}, u32[]{:S(2)}, u32[]{:S(2)}) %collective-permute-start.5) | collective-permute-done | bytes 524320 | tf_op jit(solution)/shard_map/ppermute | solution.py:248
  20.7 3.8 %collective-permute-start.7 = (bf16[64,32,128]{2,1,0:T(8,128)(2,1)S(1)}, bf16[64,32,128]{2,1,0:T(8,128)(2,1)S(1)}, u32[]{:S(2)}, u32[]{:S(2)}) collective-permute-start(bf16[64,32,128]{2,1,0:T(8,128)(2,1)S(1)} %collective-permute-done.6.refs_4_), channel_id=1, source_target_pairs={{0,8},{2,10},{8,16},{10,18},{12,4},{14,6},{16,24},{18,26},{20,12},... | collective-permute-start | bytes 1572872 | tf_op jit(solution)/shard_map/ppermute | solution.py:255
  24.5 0.1 collective-permute-start.8
  24.6 5.9 %collective-permute-done.1.refs_3_ = bf16[64,32,128]{2,1,0:T(8,128)(2,1)S(1)} collective-permute-done((bf16[64,32,128]{2,1,0:T(8,128)(2,1)S(1)}, bf16[64,32,128]{2,1,0:T(8,128)(2,1)S(1)}, u32[]{:S(2)}, u32[]{:S(2)}) %collective-permute-start.1) | collective-permute-done | bytes 524320 | tf_op jit(solution)/shard_map/ppermute | solution.py:262
  30.4 0.0 collective-permute-done.2.refs_5_
  30.4 0.9 %collective-permute-start.3 = (bf16[64,32,128]{2,1,0:T(8,128)(2,1)S(1)}, bf16[64,32,128]{2,1,0:T(8,128)(2,1)S(1)}, u32[]{:S(2)}, u32[]{:S(2)}) collective-permute-start(bf16[64,32,128]{2,1,0:T(8,128)(2,1)S(1)} %get-tuple-element.51), channel_id=1, source_target_pairs={{0,2},{2,0},{4,6},{6,4},{8,10},{10,8},{12,14},{14,12},{16,18},{18,... | collective-permute-start | bytes 1572872 | tf_op jit(solution)/shard_map/ppermute | solution.py:258
  31.3 1.7 %collective-permute-start.4 = (bf16[64,32,128]{2,1,0:T(8,128)(2,1)S(1)}, bf16[64,32,128]{2,1,0:T(8,128)(2,1)S(1)}, u32[]{:S(2)}, u32[]{:S(2)}) collective-permute-start(bf16[64,32,128]{2,1,0:T(8,128)(2,1)S(1)} %get-tuple-element.52), channel_id=1, source_target_pairs={{0,1},{1,0},{2,3},{3,2},{4,5},{5,4},{6,7},{7,6},{8,9},{9,8},{10,11... | collective-permute-start | bytes 1572872 | tf_op jit(solution)/shard_map/ppermute | solution.py:248
  33.0 3.5 %collective-permute-start.12 = (bf16[64,32,128]{2,1,0:T(8,128)(2,1)S(1)}, bf16[64,32,128]{2,1,0:T(8,128)(2,1)S(1)}, u32[]{:S(2)}, u32[]{:S(2)}) collective-permute-start(bf16[64,32,128]{2,1,0:T(8,128)(2,1)S(1)} %collective-permute-done.2.refs_5_), channel_id=1, source_target_pairs={{0,8},{2,10},{8,16},{10,18},{12,4},{14,6},{16,24},{18,26},{20,12},... | collective-permute-start | bytes 1572872 | tf_op jit(solution)/shard_map/ppermute | solution.py:255
  36.5 0.0 collective-permute-done.7.refs_6_
  36.5 0.2 collective-permute-start.11
  36.7 4.4 %collective-permute-done.8.refs_4_ = bf16[64,32,128]{2,1,0:T(8,128)(2,1)S(1)} collective-permute-done((bf16[64,32,128]{2,1,0:T(8,128)(2,1)S(1)}, bf16[64,32,128]{2,1,0:T(8,128)(2,1)S(1)}, u32[]{:S(2)}, u32[]{:S(2)}) %collective-permute-start.8) | collective-permute-done | bytes 524320 | tf_op jit(solution)/shard_map/ppermute | solution.py:251
  41.1 0.7 collective-permute-start.9
  41.9 0.0 collective-permute-done.3.refs_1_
  41.9 3.5 %collective-permute-start.10 = (bf16[64,32,128]{2,1,0:T(8,128)(2,1)S(1)}, bf16[64,32,128]{2,1,0:T(8,128)(2,1)S(1)}, u32[]{:S(2)}, u32[]{:S(2)}) collective-permute-start(bf16[64,32,128]{2,1,0:T(8,128)(2,1)S(1)} %collective-permute-done.8.refs_4_), channel_id=1, source_target_pairs={{0,8},{2,10},{8,16},{10,18},{12,4},{14,6},{16,24},{18,26},{20,12},... | collective-permute-start | bytes 1572872 | tf_op jit(solution)/shard_map/ppermute | solution.py:255
  45.4 0.7 collective-permute-done.4.refs_0_
  46.1 2.2 %collective-permute-done.12.refs_7_ = bf16[64,32,128]{2,1,0:T(8,128)(2,1)S(1)} collective-permute-done((bf16[64,32,128]{2,1,0:T(8,128)(2,1)S(1)}, bf16[64,32,128]{2,1,0:T(8,128)(2,1)S(1)}, u32[]{:S(2)}, u32[]{:S(2)}) %collective-permute-start.12) | collective-permute-done | bytes 524320 | tf_op jit(solution)/shard_map/ppermute | solution.py:255
  48.3 2.8 %multiply.3 = (f32[2048,128]{1,0:T(8,128)S(1)}, f32[2048,128]{1,0:T(8,128)S(1)}, f32[2048,128]{1,0:T(8,128)S(1)}, f32[2048,128]{1,0:T(8,128)S(1)}) custom-call(s32[1]{0:T(128)} %bitcast.6.core_ref, bf16[64,32,128]{2,1,0:T(8,128)(2,1)S(1)} %get-tuple-element.63.refs_0_, bf16[64,32,128]{2,1,0:T(8,128)(2,1)S(1)} %collective-permute-done.3.refs_1_, ...), custom_call_target="tpu_custom_call" | custom-call | flops 201326592 | bytes 6291456 | tf_op jit(solution)/shard_map/multiply/pallas_call | solution.py:154
  51.1 1.0 %collective-permute-done.11.refs_5_ = bf16[64,32,128]{2,1,0:T(8,128)(2,1)S(1)} collective-permute-done((bf16[64,32,128]{2,1,0:T(8,128)(2,1)S(1)}, bf16[64,32,128]{2,1,0:T(8,128)(2,1)S(1)}, u32[]{:S(2)}, u32[]{:S(2)}) %collective-permute-start.11) | collective-permute-done | bytes 524320 | tf_op jit(solution)/shard_map/ppermute | solution.py:251
  52.1 3.7 %collective-permute-start.13 = (bf16[64,32,128]{2,1,0:T(8,128)(2,1)S(1)}, bf16[64,32,128]{2,1,0:T(8,128)(2,1)S(1)}, u32[]{:S(2)}, u32[]{:S(2)}) collective-permute-start(bf16[64,32,128]{2,1,0:T(8,128)(2,1)S(1)} %collective-permute-done.11.refs_5_), channel_id=1, source_target_pairs={{0,8},{2,10},{8,16},{10,18},{12,4},{14,6},{16,24},{18,26},{20,12},... | collective-permute-start | bytes 1572872 | tf_op jit(solution)/shard_map/ppermute | solution.py:255
  55.9 0.0 collective-permute-done.9.refs_1_
  55.9 3.4 %multiply.5 = (f32[2048,128]{1,0:T(8,128)S(1)}, f32[2048,128]{1,0:T(8,128)}) custom-call(s32[1]{0:T(128)} %bitcast.6.core_ref, bf16[64,32,128]{2,1,0:T(8,128)(2,1)S(1)} %collective-permute-done.4.refs_0_, bf16[64,32,128]{2,1,0:T(8,128)(2,1)S(1)} %collective-permute-done.9.refs_1_, bf16[64,32,128]{2,1,0:T(8,128)(2,1)S(1)} %collective-permute-done.5.refs_2_, ...), custom_call_target="tpu_custom_call" | custom-call | flops 134217728 | bytes 6291456 | tf_op jit(solution)/shard_map/multiply/pallas_call | solution.py:154
  59.2 0.3 collective-permute-start.15
  59.5 0.0 collective-permute-done.10.refs_2_
  59.5 10.5 %collective-permute-done.13.refs_3_ = bf16[64,32,128]{2,1,0:T(8,128)(2,1)S(1)} collective-permute-done((bf16[64,32,128]{2,1,0:T(8,128)(2,1)S(1)}, bf16[64,32,128]{2,1,0:T(8,128)(2,1)S(1)}, u32[]{:S(2)}, u32[]{:S(2)}) %collective-permute-start.13) | collective-permute-done | bytes 524320 | tf_op jit(solution)/shard_map/ppermute | solution.py:255
  70.0 2.7 %multiply.4 = (f32[2048,128]{1,0:T(8,128)S(1)}, f32[2048,128]{1,0:T(8,128)}) custom-call(s32[1]{0:T(128)} %bitcast.6.core_ref, bf16[64,32,128]{2,1,0:T(8,128)(2,1)S(1)} %collective-permute-done.4.refs_0_, bf16[64,32,128]{2,1,0:T(8,128)(2,1)S(1)} %collective-permute-done.9.refs_1_, bf16[64,32,128]{2,1,0:T(8,128)(2,1)S(1)} %collective-permute-done.10.refs_2_, ...), custom_call_target="tpu_custom_call" | custom-call | flops 67108864 | bytes 6291456 | tf_op jit(solution)/shard_map/multiply/pallas_call | solution.py:154
  72.7 0.0 collective-permute-start.14
  72.7 0.1 stack.38.where_ref
  72.8 0.0 collective-permute-done.15.came_ref
  72.8 1.3 %early_spread.1._ = f32[24672,128]{1,0:T(8,128)S(1)} custom-call(s32[7]{0:T(128)S(1)} %stack.38.where_ref, f32[2048,128]{1,0:T(8,128)S(1)} %get-tuple-element.78.kept_ref, f32[2048,128]{1,0:T(8,128)S(1)} %collective-permute-done.15.came_ref), custom_call_target="tpu_custom_call" | custom-call | bytes 6291456 | tf_op jit(solution)/shard_map/early_spread/pallas_call | solution.py:190
  74.1 1.6 %collective-permute-done.14.came_ref = f32[2048,128]{1,0:T(8,128)} collective-permute-done((f32[2048,128]{1,0:T(8,128)}, f32[2048,128]{1,0:T(8,128)}, u32[]{:S(2)}, u32[]{:S(2)}) %collective-permute-start.14) | collective-permute-done | bytes 1048608 | tf_op jit(solution)/shard_map/ppermute | solution.py:258
  75.7 3.4 %late_spread.1 = (f32[24672,128]{1,0:T(8,128)S(1)}, f32[129,32,128]{2,1,0:T(8,128)}) custom-call(s32[7]{0:T(128)S(1)} %stack.38.where_ref, f32[2048,128]{1,0:T(8,128)S(1)} %get-tuple-element.74.kept_ref, f32[2048,128]{1,0:T(8,128)} %collective-permute-done.14.came_ref, f32[24672,128]{1,0:T(8,128)S(1)} %early_spread.1._), custom_call_target="tpu_custom_call", output_to_operand_aliasing={{0}: (3, {})} | custom-call | tf_op jit(solution)/shard_map/late_spread/pallas_call | solution.py:221
Async XLA Ops:
  2.8 3.1 %collective-permute-start = (bf16[64,32,128]{2,1,0:T(8,128)(2,1)S(1)}, bf16[64,32,128]{2,1,0:T(8,128)(2,1)S(1)}, u32[]{:S(2)}, u32[]{:S(2)}) collective-permute-start(bf16[64,32,128]{2,1,0:T(8,128)(2,1)S(1)} %get-tuple-element.45), channel_id=1, source_target_pairs={{0,2},{2,0},{4,6},{6,4},{8,10},{10,8},{12,14},{14,12},{16,18},{18,... | collective-permute-start | bytes 1572872 | tf_op jit(solution)/shard_map/ppermute | solution.py:258
  3.3 15.4 %collective-permute-start.6 = (bf16[64,32,128]{2,1,0:T(8,128)(2,1)S(1)}, bf16[64,32,128]{2,1,0:T(8,128)(2,1)S(1)}, u32[]{:S(2)}, u32[]{:S(2)}) collective-permute-start(bf16[64,32,128]{2,1,0:T(8,128)(2,1)S(1)} %get-tuple-element.55.refs_2_), channel_id=1, source_target_pairs={{0,4},{2,6},{4,0},{6,2},{8,12},{10,14},{12,8},{14,10},{16,20},{18,... | collective-permute-start | bytes 1572872 | tf_op jit(solution)/shard_map/ppermute | solution.py:251
  5.9 14.8 %collective-permute-start.5 = (bf16[64,32,128]{2,1,0:T(8,128)(2,1)S(1)}, bf16[64,32,128]{2,1,0:T(8,128)(2,1)S(1)}, u32[]{:S(2)}, u32[]{:S(2)}) collective-permute-start(bf16[64,32,128]{2,1,0:T(8,128)(2,1)S(1)} %get-tuple-element.54), channel_id=1, source_target_pairs={{0,1},{1,0},{2,3},{3,2},{4,5},{5,4},{6,7},{7,6},{8,9},{9,8},{10,11... | collective-permute-start | bytes 1572872 | tf_op jit(solution)/shard_map/ppermute | solution.py:248
  7.7 22.7 %collective-permute-start.1 = (bf16[64,32,128]{2,1,0:T(8,128)(2,1)S(1)}, bf16[64,32,128]{2,1,0:T(8,128)(2,1)S(1)}, u32[]{:S(2)}, u32[]{:S(2)}) collective-permute-start(bf16[64,32,128]{2,1,0:T(8,128)(2,1)S(1)} %get-tuple-element.46), channel_id=1, source_target_pairs={{0,3},{1,2},{2,1},{3,0},{4,7},{5,6},{6,5},{7,4},{8,11},{9,10},{10,... | collective-permute-start | bytes 1572872 | tf_op jit(solution)/shard_map/ppermute | solution.py:262
  7.7 22.7 %collective-permute-start.2 = (bf16[64,32,128]{2,1,0:T(8,128)(2,1)S(1)}, bf16[64,32,128]{2,1,0:T(8,128)(2,1)S(1)}, u32[]{:S(2)}, u32[]{:S(2)}) collective-permute-start(bf16[64,32,128]{2,1,0:T(8,128)(2,1)S(1)} %collective-permute-done.refs_3_), channel_id=1, source_target_pairs={{0,4},{2,6},{4,0},{6,2},{8,12},{10,14},{12,8},{14,10},{16,20},{18,... | collective-permute-start | bytes 1572872 | tf_op jit(solution)/shard_map/ppermute | solution.py:251
  20.7 15.9 %collective-permute-start.7 = (bf16[64,32,128]{2,1,0:T(8,128)(2,1)S(1)}, bf16[64,32,128]{2,1,0:T(8,128)(2,1)S(1)}, u32[]{:S(2)}, u32[]{:S(2)}) collective-permute-start(bf16[64,32,128]{2,1,0:T(8,128)(2,1)S(1)} %collective-permute-done.6.refs_4_), channel_id=1, source_target_pairs={{0,8},{2,10},{8,16},{10,18},{12,4},{14,6},{16,24},{18,26},{20,12},... | collective-permute-start | bytes 1572872 | tf_op jit(solution)/shard_map/ppermute | solution.py:255
  24.5 16.7 %collective-permute-start.8 = (bf16[64,32,128]{2,1,0:T(8,128)(2,1)S(1)}, bf16[64,32,128]{2,1,0:T(8,128)(2,1)S(1)}, u32[]{:S(2)}, u32[]{:S(2)}) collective-permute-start(bf16[64,32,128]{2,1,0:T(8,128)(2,1)S(1)} %collective-permute-done.5.refs_2_), channel_id=1, source_target_pairs={{0,4},{2,6},{4,0},{6,2},{8,12},{10,14},{12,8},{14,10},{16,20},{18,... | collective-permute-start | bytes 1572872 | tf_op jit(solution)/shard_map/ppermute | solution.py:251
  30.4 11.5 %collective-permute-start.3 = (bf16[64,32,128]{2,1,0:T(8,128)(2,1)S(1)}, bf16[64,32,128]{2,1,0:T(8,128)(2,1)S(1)}, u32[]{:S(2)}, u32[]{:S(2)}) collective-permute-start(bf16[64,32,128]{2,1,0:T(8,128)(2,1)S(1)} %get-tuple-element.51), channel_id=1, source_target_pairs={{0,2},{2,0},{4,6},{6,4},{8,10},{10,8},{12,14},{14,12},{16,18},{18,... | collective-permute-start | bytes 1572872 | tf_op jit(solution)/shard_map/ppermute | solution.py:258
  31.3 14.8 %collective-permute-start.4 = (bf16[64,32,128]{2,1,0:T(8,128)(2,1)S(1)}, bf16[64,32,128]{2,1,0:T(8,128)(2,1)S(1)}, u32[]{:S(2)}, u32[]{:S(2)}) collective-permute-start(bf16[64,32,128]{2,1,0:T(8,128)(2,1)S(1)} %get-tuple-element.52), channel_id=1, source_target_pairs={{0,1},{1,0},{2,3},{3,2},{4,5},{5,4},{6,7},{7,6},{8,9},{9,8},{10,11... | collective-permute-start | bytes 1572872 | tf_op jit(solution)/shard_map/ppermute | solution.py:248
  33.0 15.3 %collective-permute-start.12 = (bf16[64,32,128]{2,1,0:T(8,128)(2,1)S(1)}, bf16[64,32,128]{2,1,0:T(8,128)(2,1)S(1)}, u32[]{:S(2)}, u32[]{:S(2)}) collective-permute-start(bf16[64,32,128]{2,1,0:T(8,128)(2,1)S(1)} %collective-permute-done.2.refs_5_), channel_id=1, source_target_pairs={{0,8},{2,10},{8,16},{10,18},{12,4},{14,6},{16,24},{18,26},{20,12},... | collective-permute-start | bytes 1572872 | tf_op jit(solution)/shard_map/ppermute | solution.py:255
  36.5 15.6 %collective-permute-start.11 = (bf16[64,32,128]{2,1,0:T(8,128)(2,1)S(1)}, bf16[64,32,128]{2,1,0:T(8,128)(2,1)S(1)}, u32[]{:S(2)}, u32[]{:S(2)}) collective-permute-start(bf16[64,32,128]{2,1,0:T(8,128)(2,1)S(1)} %collective-permute-done.1.refs_3_), channel_id=1, source_target_pairs={{0,4},{2,6},{4,0},{6,2},{8,12},{10,14},{12,8},{14,10},{16,20},{18,... | collective-permute-start | bytes 1572872 | tf_op jit(solution)/shard_map/ppermute | solution.py:251
  41.1 14.7 %collective-permute-start.9 = (bf16[64,32,128]{2,1,0:T(8,128)(2,1)S(1)}, bf16[64,32,128]{2,1,0:T(8,128)(2,1)S(1)}, u32[]{:S(2)}, u32[]{:S(2)}) collective-permute-start(bf16[64,32,128]{2,1,0:T(8,128)(2,1)S(1)} %get-tuple-element.60), channel_id=1, source_target_pairs={{0,3},{1,2},{2,1},{3,0},{4,7},{5,6},{6,5},{7,4},{8,11},{9,10},{10,... | collective-permute-start | bytes 1572872 | tf_op jit(solution)/shard_map/ppermute | solution.py:262
  41.9 17.6 %collective-permute-start.10 = (bf16[64,32,128]{2,1,0:T(8,128)(2,1)S(1)}, bf16[64,32,128]{2,1,0:T(8,128)(2,1)S(1)}, u32[]{:S(2)}, u32[]{:S(2)}) collective-permute-start(bf16[64,32,128]{2,1,0:T(8,128)(2,1)S(1)} %collective-permute-done.8.refs_4_), channel_id=1, source_target_pairs={{0,8},{2,10},{8,16},{10,18},{12,4},{14,6},{16,24},{18,26},{20,12},... | collective-permute-start | bytes 1572872 | tf_op jit(solution)/shard_map/ppermute | solution.py:255
  52.1 17.9 %collective-permute-start.13 = (bf16[64,32,128]{2,1,0:T(8,128)(2,1)S(1)}, bf16[64,32,128]{2,1,0:T(8,128)(2,1)S(1)}, u32[]{:S(2)}, u32[]{:S(2)}) collective-permute-start(bf16[64,32,128]{2,1,0:T(8,128)(2,1)S(1)} %collective-permute-done.11.refs_5_), channel_id=1, source_target_pairs={{0,8},{2,10},{8,16},{10,18},{12,4},{14,6},{16,24},{18,26},{20,12},... | collective-permute-start | bytes 1572872 | tf_op jit(solution)/shard_map/ppermute | solution.py:255
  59.2 13.6 %collective-permute-start.15 = (f32[2048,128]{1,0:T(8,128)}, f32[2048,128]{1,0:T(8,128)S(1)}, u32[]{:S(2)}, u32[]{:S(2)}) collective-permute-start(f32[2048,128]{1,0:T(8,128)} %get-tuple-element.79), channel_id=1, source_target_pairs={{0,2},{2,0},{4,6},{6,4},{8,10},{10,8},{12,14},{14,12},{16,18},{18,... | collective-permute-start | bytes 3145736 | tf_op jit(solution)/shard_map/ppermute | solution.py:258
  72.7 3.0 %collective-permute-start.14 = (f32[2048,128]{1,0:T(8,128)}, f32[2048,128]{1,0:T(8,128)}, u32[]{:S(2)}, u32[]{:S(2)}) collective-permute-start(f32[2048,128]{1,0:T(8,128)} %get-tuple-element.75), channel_id=1, source_target_pairs={{0,2},{2,0},{4,6},{6,4},{8,10},{10,8},{12,14},{14,12},{16,18},{18,... | collective-permute-start | bytes 3145736 | tf_op jit(solution)/shard_map/ppermute | solution.py:258

commit v7 on v6

--- a/solution.py
+++ b/solution.py
@@ -89,16 +89,16 @@
 def turn(raw, which):
     shots, cells, times, cross = raw.shape
     depth = shots * times
-    parts = 4
+    chunks = 4
     return pl.pallas_call(
         turn_body,
         in_specs=[SCALARS, pl.BlockSpec(memory_space=pl.ANY)],
         out_specs=[WHOLE] * 4,
         out_shape=[jax.ShapeDtypeStruct((cross // 4, cells, depth), raw.dtype)] * 4,
         scratch_shapes=[
-            pltpu.VMEM((parts, shots, cells // parts, times, cross), raw.dtype),
+            pltpu.VMEM((chunks, shots, cells // chunks, times, cross), raw.dtype),
             pltpu.VMEM((cross * apart(cells), depth), jnp.float32),
-            pltpu.SemaphoreType.DMA((parts,)),
+            pltpu.SemaphoreType.DMA((chunks,)),
         ],
         compiler_params=params(),
         cost_estimate=pl.CostEstimate(flops=0, bytes_accessed=raw.size * 4, transcendentals=0),
@@ -107,17 +107,17 @@
 
 
 DIMS = (((1,), (1,)), ((), ()))
-BLOCK = 8
 
 
 def multiply_body(pieces, core_ref, *refs):
+    own, *pieces = pieces
     slabs = len(pieces)
-    sources, right_ref = refs[:2], refs[-1]
-    ins = refs[2 : 2 + sum(pieces)]
-    share, cells, _ = sources[0].shape
+    sources, right_ref = (refs[:own], refs[own]), refs[-1]
+    ins = refs[own + 1 : own + 1 + sum(pieces)]
+    share, cells, _ = refs[own].shape
     groups = (slabs * cells + LANES - 1) // LANES
     kept, sent = refs[-1 - 2 * groups : -1 - groups], refs[-1 - groups : -1]
-    before = refs[2 + len(ins) : -1 - 2 * groups]
+    before = refs[own + 1 + len(ins) : -1 - 2 * groups]
     for place, count in enumerate(pieces):
         side, other = divmod(place, 2)
         slab = 2 * side + (core_ref[0] if other == 0 else 1 - core_ref[0])
@@ -125,12 +125,12 @@
             right_ref[slab, part * (share // count) : (part + 1) * (share // count)] = ins[part][...]
         ins = ins[count:]
 
-    @pl.loop(0, share // BLOCK)
-    def _(step):
-        for place in range(BLOCK):
-            cross = step * BLOCK + place
-            left = jnp.concatenate([source[cross] for source in sources], axis=0)
-            rows = pl.ds(pl.multiple_of(cross * cells, cells), cells)
+    for cross_part in range(own):
+        first_cross = cross_part * (share // own)
+        for place in range(share // own):
+            cross = first_cross + place
+            left = jnp.concatenate([sources[0][cross_part][place], sources[1][cross]], axis=0)
+            rows = pl.ds(cross * cells, cells)
             for group in range(groups):
                 members = range(group * LANES // cells, min(slabs, (group + 1) * LANES // cells))
                 right = jnp.concatenate([right_ref[slab, cross] for slab in members], axis=0)
@@ -146,21 +146,22 @@
 
 
 def multiply(core, sources, pieces, before=()):
-    share, cells, depth = sources[0].shape
+    share, cells, depth = sources[1].shape
     slabs = len(pieces)
     groups = -(-slabs * cells // LANES)
     flops = 2 * share * 2 * cells * slabs * cells * depth
     flat = [part for piece in pieces for part in piece]
+    counts = [len(sources[0])] + [len(piece) for piece in pieces]
     return pl.pallas_call(
-        functools.partial(multiply_body, [len(piece) for piece in pieces]),
-        in_specs=[SCALARS] + [WHOLE] * (2 + len(flat) + len(before)),
+        functools.partial(multiply_body, counts),
+        in_specs=[SCALARS] + [WHOLE] * (1 + sum(counts) + len(before)),
         out_specs=[WHOLE] * (2 * groups),
         out_shape=[jax.ShapeDtypeStruct((share * cells, LANES), jnp.float32)] * (2 * groups),
-        scratch_shapes=[pltpu.VMEM((slabs, share, cells, depth), sources[0].dtype)],
+        scratch_shapes=[pltpu.VMEM((slabs, share, cells, depth), sources[1].dtype)],
         compiler_params=params(),
         cost_estimate=pl.CostEstimate(flops=flops, bytes_accessed=6 << 20, transcendentals=0),
         name="multiply",
-    )(core.reshape(1), *in_vmem(*sources, *flat, *before))
+    )(core.reshape(1), *in_vmem(*sources[0], sources[1], *flat, *before))
 
 
 def gather_rows(where_ref, cells, kept_ref, came_ref, rows_ref):
@@ -180,61 +181,70 @@
             skewed_ref[pl.ds(base, cells, stride=GAP), :] = turned[cells * place : cells * (place + 1)]
 
 
-def early_spread_body(scale, cells, where_ref, kept_ref, came_ref, skewed_ref, rows_ref):
+def write_lags(first, skewed_ref, image_ref, buffer_ref, sems):
+    cells = image_ref.shape[1]
+    line = skewed_ref.shape[0] // cells
+    parts, lags = sems.shape[0], buffer_ref.shape[0]
+    cuts = [lags * part // parts for part in range(parts + 1)]
+    copies = []
+    for part, (start, stop) in enumerate(zip(cuts, cuts[1:])):
+        for lag in range(start, stop):
+            buffer_ref[lag] = skewed_ref[pl.ds(GAP * (2 * cells + first + lag), cells, stride=line), :]
+        source, target = pl.ds(start, stop - start), pl.ds(first + start, stop - start)
+        copies.append(pltpu.make_async_copy(buffer_ref.at[source], image_ref.at[target], sems.at[part]))
+        copies[-1].start()
+    for copy in copies:
+        copy.wait()
+
+
+def early_spread_body(scale, cells, where_ref, kept_ref, came_ref, skewed_ref, image_ref, rows_ref, buffer_ref, sems):
     gather_rows(where_ref, cells, kept_ref, came_ref, rows_ref)
     spread_rows(where_ref, cells, range(4), scale, rows_ref, skewed_ref)
+    write_lags(where_ref[7] * 2 * cells, skewed_ref, image_ref, buffer_ref, sems)
+
+
+def spread_scratch(cells, lags):
+    return [
+        pltpu.VMEM((LANES * apart(cells), LANES), jnp.float32),
+        pltpu.VMEM((lags, cells, LANES), jnp.float32),
+        pltpu.SemaphoreType.DMA((2,)),
+    ]
 
 
 def early_spread(scale, cells, where, products):
-    rows = apart(4 * cells + 1 + 4 * cells) * cells
+    lags = 4 * cells + 1
     return pl.pallas_call(
         functools.partial(early_spread_body, scale, cells),
         in_specs=[SCALARS] + [WHOLE] * 2,
-        out_specs=WHOLE,
-        out_shape=jax.ShapeDtypeStruct((rows, LANES), jnp.float32),
-        scratch_shapes=[pltpu.VMEM((LANES * apart(cells), LANES), jnp.float32)],
+        out_specs=[WHOLE, pl.BlockSpec(memory_space=pl.ANY)],
+        out_shape=[
+            jax.ShapeDtypeStruct((apart(lags + 4 * cells) * cells, LANES), jnp.float32),
+            pltpu.HBM((lags, cells, LANES), jnp.float32),
+        ],
+        scratch_shapes=spread_scratch(cells, 2 * cells + 1),
         compiler_params=params(),
         cost_estimate=pl.CostEstimate(flops=0, bytes_accessed=6 << 20, transcendentals=0),
         name="early_spread",
     )(where, *in_vmem(*products))
 
 
-def late_spread_body(scale, cells, where_ref, kept_ref, came_ref, _, skewed_ref, image_ref, rows_ref, buffer_ref, sems):
+def late_spread_body(scale, cells, where_ref, kept_ref, came_ref, _, __, skewed_ref, image_ref, rows_ref, buffer_ref, sems):
     gather_rows(where_ref, cells, kept_ref, came_ref, rows_ref)
     spread_rows(where_ref, cells, (4, 5), scale, rows_ref, skewed_ref)
-    line = skewed_ref.shape[0] // cells
-    parts, lags = sems.shape[0], image_ref.shape[0]
-    cuts = [lags * part // parts for part in range(parts + 1)]
-    copies = []
-    for part, (start, stop) in enumerate(zip(cuts, cuts[1:])):
-        for lag in range(start, stop):
-            buffer_ref[lag] = skewed_ref[pl.ds(GAP * (2 * cells + lag), cells, stride=line), :]
-        block = pl.ds(start, stop - start)
-        copies.append(pltpu.make_async_copy(buffer_ref.at[block], image_ref.at[block], sems.at[part]))
-        copies[-1].start()
-    for copy in copies:
-        copy.wait()
-
-
-def late_spread(scale, cells, where, products, skewed):
-    lags = 4 * cells + 1
+    write_lags((1 - where_ref[7]) * (2 * cells + 1), skewed_ref, image_ref, buffer_ref, sems)
+
+
+def late_spread(scale, cells, where, products, skewed, image):
     return pl.pallas_call(
         functools.partial(late_spread_body, scale, cells),
-        in_specs=[SCALARS] + [WHOLE] * 3,
+        in_specs=[SCALARS] + [WHOLE] * 3 + [pl.BlockSpec(memory_space=pl.ANY)],
         out_specs=[WHOLE, pl.BlockSpec(memory_space=pl.ANY)],
-        out_shape=[
-            jax.ShapeDtypeStruct(skewed.shape, jnp.float32),
-            jax.ShapeDtypeStruct((lags, cells, LANES), jnp.float32),
-        ],
-        input_output_aliases={3: 0},
-        scratch_shapes=[
-            pltpu.VMEM((LANES * apart(cells), LANES), jnp.float32),
-            pltpu.VMEM((lags, cells, LANES), jnp.float32),
-            pltpu.SemaphoreType.DMA((4,)),
-        ],
+        out_shape=[jax.ShapeDtypeStruct(skewed.shape, jnp.float32), pltpu.HBM(image.shape, jnp.float32)],
+        input_output_aliases={3: 0, 4: 1},
+        scratch_shapes=spread_scratch(cells, 2 * cells),
         compiler_params=params(),
         name="late_spread",
-    )(where, *in_vmem(*products, skewed))[1]
+    )(where, *in_vmem(*products, skewed), image)[1]
 
 
 def routed(source, receiver, scale):
@@ -273,7 +283,7 @@
     y1 = along_y(twin)
     source, _ = barrier(source, twin)
     left, left_lent, far, far_lent = turn(source, which)
-    moved, y0, left = barrier(moved, y0, left)
+    y0, left = barrier(y0, left)
     y2, z0 = along_y(moved), along_z(y0)
     moved_twin, y1, far, left_lent = barrier(moved_twin, y1, far, left_lent)
     y3, z1 = along_y(moved_twin), along_z(y1)
@@ -281,20 +291,20 @@
     right = across(far)
     z0, far_lent, y2 = barrier(z0, far_lent, y2)
     right_twin = across_to_core(far_lent)
+    left_twin, right = barrier(left_twin, right)
     z2 = along_z(y2)
-    left_twin, right = barrier(left_twin, right)
-    early = multiply(core, (left, left_twin), [(piece,) for piece in (kept, twin, y0, y1, z0, z1)])
+    early = multiply(core, ([left], left_twin), [(piece,) for piece in (kept, twin, y0, y1, z0, z1)])
     y3, *early = barrier(y3, *early)
     z3 = along_z(y3)
-    middle = multiply(core, (right, right_twin), ((moved,), (moved_twin,), (y2,), (y3,)), (early[0], early[2]))
+    middle = multiply(core, ([right], right_twin), ((moved,), (moved_twin,), (y2,), (y3,)), (early[0], early[2]))
     middle_came = to_core(middle[1])
     side = 2 - 4 * odd
-    where = jnp.stack([block + shift - core for shift in (0, side, -side) for block in (0, 1)] + [core])
+    where = jnp.stack([block + shift - core for shift in (0, side, -side) for block in (0, 1)] + [core, 1 - odd])
     where = where.astype(jnp.int32)
-    skewed = early_spread(scale, cells, where, (middle[0], middle_came))
-    late = multiply(core, (right, right_twin), ((z2,), (z3,)), (early[1], early[3]))
+    skewed, image = early_spread(scale, cells, where, (middle[0], middle_came))
+    late = multiply(core, ([right], right_twin), ((z2,), (z3,)), (early[1], early[3]))
     late_came = to_core(late[1])
-    return late_spread(scale, cells, where, (late[0], late_came), skewed)
+    return late_spread(scale, cells, where, (late[0], late_came), skewed, image)
 
 
 def on_device(source, receiver):

time: 79.3 us -> 77.6 us (0.979)
  Pallas kernels: 18.9 us -> 17.1 us
    pallas_call x3, Pallas kernels: 8.85 us -> 6.39 us  [multiply(): pl.pallas_call(functools.partial(multiply_body, counts), in_specs=[SCALAR...]
    ppermute x2, waiting for transfers between devices: 2.67 us -> 0.68 us  [across(): return lax.ppermute(value, 'shot', [(0, 1), (1, 0)])]
    ppermute x2, waiting for transfers between devices: 5.86 us -> 7.72 us  [across_to_core(): return lax.ppermute(value, ('inline', 'shot'), pairs)]
    pallas_call x1, Pallas kernels: 1.29 us -> 3.01 us  [early_spread(): pl.pallas_call(functools.partial(early_spread_body, scale, cells), in_spe...]
    ppermute x4, waiting for transfers between devices: 1.62 us -> 0.01 us  [to_core(): lax.ppermute(value, 'inline', [(index, index ^ 1) for index in range(coun...]
    pallas_call x1, Pallas kernels: 3.35 us -> 2.3 us  [late_spread(): pl.pallas_call(functools.partial(late_spread_body, scale, cells), in_spec...]
    ppermute x4, waiting for transfers between devices: 12.2 us -> 13.1 us  [along_y(): lax.ppermute(value, 'inline', [(index, index ^ 2) for index in range(coun...]
  transfers between devices with their start and end apart: 16 -> 16, of which waited for: 9 -> 8; matrix products, arithmetic and copies ran while one was open for 0% -> 0% of each run, Pallas kernels for 16% -> 16%
where the time goes in v7:
time: 77.6 us; the launch traced here: 77.2 us
  waiting for transfers between devices  34.9 us (45%)
  starting transfers between devices  24.9 us (32%)
  Pallas kernels  17.1 us (22%)
    ppermute x4, starting transfers between devices, along_z(): lax.ppermute(value, 'inline', [pair for pair in pairs if 0 <= pair[1] < c...  14.7 us
    ppermute x4, waiting for transfers between devices, along_z(): lax.ppermute(value, 'inline', [pair for pair in pairs if 0 <= pair[1] < c...  13.4 us
    ppermute x4, waiting for transfers between devices, along_y(): lax.ppermute(value, 'inline', [(index, index ^ 2) for index in range(coun...  13.1 us
    ppermute x2, waiting for transfers between devices, across_to_core(): return lax.ppermute(value, ('inline', 'shot'), pairs)  7.72 us
    pallas_call x3, Pallas kernels, multiply(): pl.pallas_call(functools.partial(multiply_body, counts), in_specs=[SCALAR...  6.39 us
    pallas_call x2, Pallas kernels, turn(): pl.pallas_call(turn_body, in_specs=[SCALARS, pl.BlockSpec(memory_space=pl...  5.38 us
    ppermute x4, starting transfers between devices, along_y(): lax.ppermute(value, 'inline', [(index, index ^ 2) for index in range(coun...  4.28 us
    ppermute x2, starting transfers between devices, across(): return lax.ppermute(value, 'shot', [(0, 1), (1, 0)])  3.54 us
  transfers between devices with their start and end apart: 16, of which 8 were waited for; matrix products, arithmetic and copies ran while one was open for 0% of the time, Pallas kernels for 16%

profile of v7, /device:TPU:0, one launch (start us, length us, event | category | flops | bytes accessed | tf_op | source)
XLA Modules:
  0.0 77.2 jit_solution(13200599103046046024)
XLA Ops:
  0.0 0.1 pad_add_fusion.which_ref
  0.1 2.7 %turn.2 = (bf16[64,32,128]{2,1,0:T(8,128)(2,1)S(1)}, bf16[64,32,128]{2,1,0:T(8,128)(2,1)S(1)}, bf16[64,32,128]{2,1,0:T(8,128)(2,1)S(1)}, bf16[64,32,128]{2,1,0:T(8,128)(2,1)S(1)}) custom-call(s32[2]{0:T(128)S(1)} %pad_add_fusion.which_ref, bf16[4,32,32,256]{3,2,1,0:T(8,128)(2,1)} %raw_ref.1), custom_call_target="tpu_custom_call" | custom-call | bytes 4194304 | tf_op jit(solution)/shard_map/turn/pallas_call | solution.py:93
  2.8 0.5 collective-permute-start
  3.3 2.6 %collective-permute-start.5 = (bf16[64,32,128]{2,1,0:T(8,128)(2,1)S(1)}, bf16[64,32,128]{2,1,0:T(8,128)(2,1)S(1)}, u32[]{:S(2)}, u32[]{:S(2)}) collective-permute-start(bf16[64,32,128]{2,1,0:T(8,128)(2,1)S(1)} %get-tuple-element.55.refs_2_), channel_id=1, source_target_pairs={{0,4},{2,6},{4,0},{6,2},{8,12},{10,14},{12,8},{14,10},{16,20},{18,... | collective-permute-start | bytes 1572872 | tf_op jit(solution)/shard_map/ppermute | solution.py:261
  5.9 0.0 collective-permute-done.refs_3_
  5.9 1.8 %collective-permute-start.7 = (bf16[64,32,128]{2,1,0:T(8,128)(2,1)S(1)}, bf16[64,32,128]{2,1,0:T(8,128)(2,1)S(1)}, u32[]{:S(2)}, u32[]{:S(2)}) collective-permute-start(bf16[64,32,128]{2,1,0:T(8,128)(2,1)S(1)} %get-tuple-element.59), channel_id=1, source_target_pairs={{0,1},{1,0},{2,3},{3,2},{4,5},{5,4},{6,7},{7,6},{8,9},{9,8},{10,11... | collective-permute-start | bytes 1572872 | tf_op jit(solution)/shard_map/ppermute | solution.py:258
  7.7 0.0 collective-permute-start.1
  7.7 1.6 %collective-permute-start.2 = (bf16[64,32,128]{2,1,0:T(8,128)(2,1)S(1)}, bf16[64,32,128]{2,1,0:T(8,128)(2,1)S(1)}, u32[]{:S(2)}, u32[]{:S(2)}) collective-permute-start(bf16[64,32,128]{2,1,0:T(8,128)(2,1)S(1)} %collective-permute-done.refs_3_), channel_id=1, source_target_pairs={{0,4},{2,6},{4,0},{6,2},{8,12},{10,14},{12,8},{14,10},{16,20},{18,... | collective-permute-start | bytes 1572872 | tf_op jit(solution)/shard_map/ppermute | solution.py:261
  9.2 2.7 %turn.3 = (bf16[64,32,128]{2,1,0:T(8,128)(2,1)S(1)}, bf16[64,32,128]{2,1,0:T(8,128)(2,1)S(1)}, bf16[64,32,128]{2,1,0:T(8,128)(2,1)S(1)}, bf16[64,32,128]{2,1,0:T(8,128)(2,1)S(1)}) custom-call(s32[2]{0:T(128)S(1)} %pad_add_fusion.which_ref, bf16[4,32,32,256]{3,2,1,0:T(8,128)(2,1)} %raw_ref.2), custom_call_target="tpu_custom_call" | custom-call | bytes 4194304 | tf_op jit(solution)/shard_map/turn/pallas_call | solution.py:93
  11.9 6.7 %collective-permute-done.5.refs_4_ = bf16[64,32,128]{2,1,0:T(8,128)(2,1)S(1)} collective-permute-done((bf16[64,32,128]{2,1,0:T(8,128)(2,1)S(1)}, bf16[64,32,128]{2,1,0:T(8,128)(2,1)S(1)}, u32[]{:S(2)}, u32[]{:S(2)}) %collective-permute-start.5) | collective-permute-done | bytes 524320 | tf_op jit(solution)/shard_map/ppermute | solution.py:261
  18.7 3.9 %collective-permute-start.6 = (bf16[64,32,128]{2,1,0:T(8,128)(2,1)S(1)}, bf16[64,32,128]{2,1,0:T(8,128)(2,1)S(1)}, u32[]{:S(2)}, u32[]{:S(2)}) collective-permute-start(bf16[64,32,128]{2,1,0:T(8,128)(2,1)S(1)} %collective-permute-done.5.refs_4_), channel_id=1, source_target_pairs={{0,8},{2,10},{8,16},{10,18},{12,4},{14,6},{16,24},{18,26},{20,12},... | collective-permute-start | bytes 1572872 | tf_op jit(solution)/shard_map/ppermute | solution.py:265
  22.6 0.0 collective-permute-done.7.refs_2_
  22.6 0.1 collective-permute-start.8
  22.7 7.7 %collective-permute-done.1.refs_3_ = bf16[64,32,128]{2,1,0:T(8,128)(2,1)S(1)} collective-permute-done((bf16[64,32,128]{2,1,0:T(8,128)(2,1)S(1)}, bf16[64,32,128]{2,1,0:T(8,128)(2,1)S(1)}, u32[]{:S(2)}, u32[]{:S(2)}) %collective-permute-start.1) | collective-permute-done | bytes 524320 | tf_op jit(solution)/shard_map/ppermute | solution.py:272
  30.4 0.0 collective-permute-done.2.refs_5_
  30.4 0.9 %collective-permute-start.3 = (bf16[64,32,128]{2,1,0:T(8,128)(2,1)S(1)}, bf16[64,32,128]{2,1,0:T(8,128)(2,1)S(1)}, u32[]{:S(2)}, u32[]{:S(2)}) collective-permute-start(bf16[64,32,128]{2,1,0:T(8,128)(2,1)S(1)} %get-tuple-element.52), channel_id=1, source_target_pairs={{0,2},{2,0},{4,6},{6,4},{8,10},{10,8},{12,14},{14,12},{16,18},{18,... | collective-permute-start | bytes 1572872 | tf_op jit(solution)/shard_map/ppermute | solution.py:268
  31.3 1.7 %collective-permute-start.4 = (bf16[64,32,128]{2,1,0:T(8,128)(2,1)S(1)}, bf16[64,32,128]{2,1,0:T(8,128)(2,1)S(1)}, u32[]{:S(2)}, u32[]{:S(2)}) collective-permute-start(bf16[64,32,128]{2,1,0:T(8,128)(2,1)S(1)} %get-tuple-element.53), channel_id=1, source_target_pairs={{0,1},{1,0},{2,3},{3,2},{4,5},{5,4},{6,7},{7,6},{8,9},{9,8},{10,11... | collective-permute-start | bytes 1572872 | tf_op jit(solution)/shard_map/ppermute | solution.py:258
  33.0 3.5 %collective-permute-start.12 = (bf16[64,32,128]{2,1,0:T(8,128)(2,1)S(1)}, bf16[64,32,128]{2,1,0:T(8,128)(2,1)S(1)}, u32[]{:S(2)}, u32[]{:S(2)}) collective-permute-start(bf16[64,32,128]{2,1,0:T(8,128)(2,1)S(1)} %collective-permute-done.2.refs_5_), channel_id=1, source_target_pairs={{0,8},{2,10},{8,16},{10,18},{12,4},{14,6},{16,24},{18,26},{20,12},... | collective-permute-start | bytes 1572872 | tf_op jit(solution)/shard_map/ppermute | solution.py:265
  36.5 0.0 collective-permute-done.6.refs_6_
  36.5 0.1 collective-permute-start.11
  36.6 4.5 %collective-permute-done.8.refs_4_ = bf16[64,32,128]{2,1,0:T(8,128)(2,1)S(1)} collective-permute-done((bf16[64,32,128]{2,1,0:T(8,128)(2,1)S(1)}, bf16[64,32,128]{2,1,0:T(8,128)(2,1)S(1)}, u32[]{:S(2)}, u32[]{:S(2)}) %collective-permute-start.8) | collective-permute-done | bytes 524320 | tf_op jit(solution)/shard_map/ppermute | solution.py:261
  41.1 0.7 collective-permute-start.9
  41.9 0.0 collective-permute-done.3.refs_1_
  41.9 3.5 %collective-permute-start.10 = (bf16[64,32,128]{2,1,0:T(8,128)(2,1)S(1)}, bf16[64,32,128]{2,1,0:T(8,128)(2,1)S(1)}, u32[]{:S(2)}, u32[]{:S(2)}) collective-permute-start(bf16[64,32,128]{2,1,0:T(8,128)(2,1)S(1)} %collective-permute-done.8.refs_4_), channel_id=1, source_target_pairs={{0,8},{2,10},{8,16},{10,18},{12,4},{14,6},{16,24},{18,26},{20,12},... | collective-permute-start | bytes 1572872 | tf_op jit(solution)/shard_map/ppermute | solution.py:265
  45.4 0.7 collective-permute-done.4.refs_0_
  46.1 2.2 %collective-permute-done.12.refs_7_ = bf16[64,32,128]{2,1,0:T(8,128)(2,1)S(1)} collective-permute-done((bf16[64,32,128]{2,1,0:T(8,128)(2,1)S(1)}, bf16[64,32,128]{2,1,0:T(8,128)(2,1)S(1)}, u32[]{:S(2)}, u32[]{:S(2)}) %collective-permute-start.12) | collective-permute-done | bytes 524320 | tf_op jit(solution)/shard_map/ppermute | solution.py:265
  48.3 2.0 %multiply.3 = (f32[2048,128]{1,0:T(8,128)S(1)}, f32[2048,128]{1,0:T(8,128)S(1)}, f32[2048,128]{1,0:T(8,128)S(1)}, f32[2048,128]{1,0:T(8,128)S(1)}) custom-call(s32[1]{0:T(128)} %bitcast.6.core_ref, bf16[64,32,128]{2,1,0:T(8,128)(2,1)S(1)} %get-tuple-element.63.refs_0_, bf16[64,32,128]{2,1,0:T(8,128)(2,1)S(1)} %collective-permute-done.3.refs_1_, ...), custom_call_target="tpu_custom_call" | custom-call | flops 201326592 | bytes 6291456 | tf_op jit(solution)/shard_map/multiply/pallas_call | solution.py:155
  50.2 1.9 %collective-permute-done.11.refs_5_ = bf16[64,32,128]{2,1,0:T(8,128)(2,1)S(1)} collective-permute-done((bf16[64,32,128]{2,1,0:T(8,128)(2,1)S(1)}, bf16[64,32,128]{2,1,0:T(8,128)(2,1)S(1)}, u32[]{:S(2)}, u32[]{:S(2)}) %collective-permute-start.11) | collective-permute-done | bytes 524320 | tf_op jit(solution)/shard_map/ppermute | solution.py:261
  52.1 3.7 %collective-permute-start.13 = (bf16[64,32,128]{2,1,0:T(8,128)(2,1)S(1)}, bf16[64,32,128]{2,1,0:T(8,128)(2,1)S(1)}, u32[]{:S(2)}, u32[]{:S(2)}) collective-permute-start(bf16[64,32,128]{2,1,0:T(8,128)(2,1)S(1)} %collective-permute-done.11.refs_5_), channel_id=1, source_target_pairs={{0,8},{2,10},{8,16},{10,18},{12,4},{14,6},{16,24},{18,26},{20,12},... | collective-permute-start | bytes 1572872 | tf_op jit(solution)/shard_map/ppermute | solution.py:265
  55.9 0.0 collective-permute-done.9.refs_1_
  55.9 2.7 %multiply.5 = (f32[2048,128]{1,0:T(8,128)S(1)}, f32[2048,128]{1,0:T(8,128)}) custom-call(s32[1]{0:T(128)} %bitcast.6.core_ref, bf16[64,32,128]{2,1,0:T(8,128)(2,1)S(1)} %collective-permute-done.4.refs_0_, bf16[64,32,128]{2,1,0:T(8,128)(2,1)S(1)} %collective-permute-done.9.refs_1_, bf16[64,32,128]{2,1,0:T(8,128)(2,1)S(1)} %collective-permute-done.7.refs_2_, ...), custom_call_target="tpu_custom_call" | custom-call | flops 134217728 | bytes 6291456 | tf_op jit(solution)/shard_map/multiply/pallas_call | solution.py:155
  58.5 0.3 collective-permute-start.15
  58.8 0.7 collective-permute-done.10.refs_2_
  59.5 10.5 %collective-permute-done.13.refs_3_ = bf16[64,32,128]{2,1,0:T(8,128)(2,1)S(1)} collective-permute-done((bf16[64,32,128]{2,1,0:T(8,128)(2,1)S(1)}, bf16[64,32,128]{2,1,0:T(8,128)(2,1)S(1)}, u32[]{:S(2)}, u32[]{:S(2)}) %collective-permute-start.13) | collective-permute-done | bytes 524320 | tf_op jit(solution)/shard_map/ppermute | solution.py:265
  70.0 1.8 %multiply.4 = (f32[2048,128]{1,0:T(8,128)S(1)}, f32[2048,128]{1,0:T(8,128)}) custom-call(s32[1]{0:T(128)} %bitcast.6.core_ref, bf16[64,32,128]{2,1,0:T(8,128)(2,1)S(1)} %collective-permute-done.4.refs_0_, bf16[64,32,128]{2,1,0:T(8,128)(2,1)S(1)} %collective-permute-done.9.refs_1_, bf16[64,32,128]{2,1,0:T(8,128)(2,1)S(1)} %collective-permute-done.10.refs_2_, ...), custom_call_target="tpu_custom_call" | custom-call | flops 67108864 | bytes 6291456 | tf_op jit(solution)/shard_map/multiply/pallas_call | solution.py:155
  71.8 0.0 collective-permute-start.14
  71.8 0.1 stack.42.where_ref
  71.8 0.0 collective-permute-done.15.came_ref
  71.9 3.0 %early_spread.1 = (f32[24672,128]{1,0:T(8,128)S(1)}, f32[129,32,128]{2,1,0:T(8,128)}) custom-call(s32[8]{0:T(128)S(1)} %stack.42.where_ref, f32[2048,128]{1,0:T(8,128)S(1)} %get-tuple-element.78.kept_ref, f32[2048,128]{1,0:T(8,128)} %collective-permute-done.15.came_ref), custom_call_target="tpu_custom_call" | custom-call | bytes 6291456 | tf_op jit(solution)/shard_map/early_spread/pallas_call | solution.py:216
  74.9 0.0 collective-permute-done.14.came_ref
  74.9 2.3 %late_spread.1 = (f32[24672,128]{1,0:T(8,128)S(1)}, f32[129,32,128]{2,1,0:T(8,128)}) custom-call(s32[8]{0:T(128)S(1)} %stack.42.where_ref, f32[2048,128]{1,0:T(8,128)S(1)} %get-tuple-element.74.kept_ref, f32[2048,128]{1,0:T(8,128)S(1)} %collective-permute-done.14.came_ref, ...), custom_call_target="tpu_custom_call", output_to_operand_aliasing={{0}: (3, {}), {1}: (4, {})} | custom-call | tf_op jit(solution)/shard_map/late_spread/pallas_call | solution.py:238
Async XLA Ops:
  2.8 3.1 %collective-permute-start = (bf16[64,32,128]{2,1,0:T(8,128)(2,1)S(1)}, bf16[64,32,128]{2,1,0:T(8,128)(2,1)S(1)}, u32[]{:S(2)}, u32[]{:S(2)}) collective-permute-start(bf16[64,32,128]{2,1,0:T(8,128)(2,1)S(1)} %get-tuple-element.46), channel_id=1, source_target_pairs={{0,2},{2,0},{4,6},{6,4},{8,10},{10,8},{12,14},{14,12},{16,18},{18,... | collective-permute-start | bytes 1572872 | tf_op jit(solution)/shard_map/ppermute | solution.py:268
  3.3 15.4 %collective-permute-start.5 = (bf16[64,32,128]{2,1,0:T(8,128)(2,1)S(1)}, bf16[64,32,128]{2,1,0:T(8,128)(2,1)S(1)}, u32[]{:S(2)}, u32[]{:S(2)}) collective-permute-start(bf16[64,32,128]{2,1,0:T(8,128)(2,1)S(1)} %get-tuple-element.55.refs_2_), channel_id=1, source_target_pairs={{0,4},{2,6},{4,0},{6,2},{8,12},{10,14},{12,8},{14,10},{16,20},{18,... | collective-permute-start | bytes 1572872 | tf_op jit(solution)/shard_map/ppermute | solution.py:261
  5.9 16.7 %collective-permute-start.7 = (bf16[64,32,128]{2,1,0:T(8,128)(2,1)S(1)}, bf16[64,32,128]{2,1,0:T(8,128)(2,1)S(1)}, u32[]{:S(2)}, u32[]{:S(2)}) collective-permute-start(bf16[64,32,128]{2,1,0:T(8,128)(2,1)S(1)} %get-tuple-element.59), channel_id=1, source_target_pairs={{0,1},{1,0},{2,3},{3,2},{4,5},{5,4},{6,7},{7,6},{8,9},{9,8},{10,11... | collective-permute-start | bytes 1572872 | tf_op jit(solution)/shard_map/ppermute | solution.py:258
  7.7 22.7 %collective-permute-start.1 = (bf16[64,32,128]{2,1,0:T(8,128)(2,1)S(1)}, bf16[64,32,128]{2,1,0:T(8,128)(2,1)S(1)}, u32[]{:S(2)}, u32[]{:S(2)}) collective-permute-start(bf16[64,32,128]{2,1,0:T(8,128)(2,1)S(1)} %get-tuple-element.47), channel_id=1, source_target_pairs={{0,3},{1,2},{2,1},{3,0},{4,7},{5,6},{6,5},{7,4},{8,11},{9,10},{10,... | collective-permute-start | bytes 1572872 | tf_op jit(solution)/shard_map/ppermute | solution.py:272
  7.7 22.7 %collective-permute-start.2 = (bf16[64,32,128]{2,1,0:T(8,128)(2,1)S(1)}, bf16[64,32,128]{2,1,0:T(8,128)(2,1)S(1)}, u32[]{:S(2)}, u32[]{:S(2)}) collective-permute-start(bf16[64,32,128]{2,1,0:T(8,128)(2,1)S(1)} %collective-permute-done.refs_3_), channel_id=1, source_target_pairs={{0,4},{2,6},{4,0},{6,2},{8,12},{10,14},{12,8},{14,10},{16,20},{18,... | collective-permute-start | bytes 1572872 | tf_op jit(solution)/shard_map/ppermute | solution.py:261
  18.7 17.9 %collective-permute-start.6 = (bf16[64,32,128]{2,1,0:T(8,128)(2,1)S(1)}, bf16[64,32,128]{2,1,0:T(8,128)(2,1)S(1)}, u32[]{:S(2)}, u32[]{:S(2)}) collective-permute-start(bf16[64,32,128]{2,1,0:T(8,128)(2,1)S(1)} %collective-permute-done.5.refs_4_), channel_id=1, source_target_pairs={{0,8},{2,10},{8,16},{10,18},{12,4},{14,6},{16,24},{18,26},{20,12},... | collective-permute-start | bytes 1572872 | tf_op jit(solution)/shard_map/ppermute | solution.py:265
  22.6 18.5 %collective-permute-start.8 = (bf16[64,32,128]{2,1,0:T(8,128)(2,1)S(1)}, bf16[64,32,128]{2,1,0:T(8,128)(2,1)S(1)}, u32[]{:S(2)}, u32[]{:S(2)}) collective-permute-start(bf16[64,32,128]{2,1,0:T(8,128)(2,1)S(1)} %collective-permute-done.7.refs_2_), channel_id=1, source_target_pairs={{0,4},{2,6},{4,0},{6,2},{8,12},{10,14},{12,8},{14,10},{16,20},{18,... | collective-permute-start | bytes 1572872 | tf_op jit(solution)/shard_map/ppermute | solution.py:261
  30.4 11.5 %collective-permute-start.3 = (bf16[64,32,128]{2,1,0:T(8,128)(2,1)S(1)}, bf16[64,32,128]{2,1,0:T(8,128)(2,1)S(1)}, u32[]{:S(2)}, u32[]{:S(2)}) collective-permute-start(bf16[64,32,128]{2,1,0:T(8,128)(2,1)S(1)} %get-tuple-element.52), channel_id=1, source_target_pairs={{0,2},{2,0},{4,6},{6,4},{8,10},{10,8},{12,14},{14,12},{16,18},{18,... | collective-permute-start | bytes 1572872 | tf_op jit(solution)/shard_map/ppermute | solution.py:268
  31.3 14.8 %collective-permute-start.4 = (bf16[64,32,128]{2,1,0:T(8,128)(2,1)S(1)}, bf16[64,32,128]{2,1,0:T(8,128)(2,1)S(1)}, u32[]{:S(2)}, u32[]{:S(2)}) collective-permute-start(bf16[64,32,128]{2,1,0:T(8,128)(2,1)S(1)} %get-tuple-element.53), channel_id=1, source_target_pairs={{0,1},{1,0},{2,3},{3,2},{4,5},{5,4},{6,7},{7,6},{8,9},{9,8},{10,11... | collective-permute-start | bytes 1572872 | tf_op jit(solution)/shard_map/ppermute | solution.py:258
  33.0 15.3 %collective-permute-start.12 = (bf16[64,32,128]{2,1,0:T(8,128)(2,1)S(1)}, bf16[64,32,128]{2,1,0:T(8,128)(2,1)S(1)}, u32[]{:S(2)}, u32[]{:S(2)}) collective-permute-start(bf16[64,32,128]{2,1,0:T(8,128)(2,1)S(1)} %collective-permute-done.2.refs_5_), channel_id=1, source_target_pairs={{0,8},{2,10},{8,16},{10,18},{12,4},{14,6},{16,24},{18,26},{20,12},... | collective-permute-start | bytes 1572872 | tf_op jit(solution)/shard_map/ppermute | solution.py:265
  36.5 15.6 %collective-permute-start.11 = (bf16[64,32,128]{2,1,0:T(8,128)(2,1)S(1)}, bf16[64,32,128]{2,1,0:T(8,128)(2,1)S(1)}, u32[]{:S(2)}, u32[]{:S(2)}) collective-permute-start(bf16[64,32,128]{2,1,0:T(8,128)(2,1)S(1)} %collective-permute-done.1.refs_3_), channel_id=1, source_target_pairs={{0,4},{2,6},{4,0},{6,2},{8,12},{10,14},{12,8},{14,10},{16,20},{18,... | collective-permute-start | bytes 1572872 | tf_op jit(solution)/shard_map/ppermute | solution.py:261
  41.1 14.7 %collective-permute-start.9 = (bf16[64,32,128]{2,1,0:T(8,128)(2,1)S(1)}, bf16[64,32,128]{2,1,0:T(8,128)(2,1)S(1)}, u32[]{:S(2)}, u32[]{:S(2)}) collective-permute-start(bf16[64,32,128]{2,1,0:T(8,128)(2,1)S(1)} %get-tuple-element.60), channel_id=1, source_target_pairs={{0,3},{1,2},{2,1},{3,0},{4,7},{5,6},{6,5},{7,4},{8,11},{9,10},{10,... | collective-permute-start | bytes 1572872 | tf_op jit(solution)/shard_map/ppermute | solution.py:272
  41.9 17.6 %collective-permute-start.10 = (bf16[64,32,128]{2,1,0:T(8,128)(2,1)S(1)}, bf16[64,32,128]{2,1,0:T(8,128)(2,1)S(1)}, u32[]{:S(2)}, u32[]{:S(2)}) collective-permute-start(bf16[64,32,128]{2,1,0:T(8,128)(2,1)S(1)} %collective-permute-done.8.refs_4_), channel_id=1, source_target_pairs={{0,8},{2,10},{8,16},{10,18},{12,4},{14,6},{16,24},{18,26},{20,12},... | collective-permute-start | bytes 1572872 | tf_op jit(solution)/shard_map/ppermute | solution.py:265
  52.1 17.9 %collective-permute-start.13 = (bf16[64,32,128]{2,1,0:T(8,128)(2,1)S(1)}, bf16[64,32,128]{2,1,0:T(8,128)(2,1)S(1)}, u32[]{:S(2)}, u32[]{:S(2)}) collective-permute-start(bf16[64,32,128]{2,1,0:T(8,128)(2,1)S(1)} %collective-permute-done.11.refs_5_), channel_id=1, source_target_pairs={{0,8},{2,10},{8,16},{10,18},{12,4},{14,6},{16,24},{18,26},{20,12},... | collective-permute-start | bytes 1572872 | tf_op jit(solution)/shard_map/ppermute | solution.py:265
  58.5 13.3 %collective-permute-start.15 = (f32[2048,128]{1,0:T(8,128)}, f32[2048,128]{1,0:T(8,128)}, u32[]{:S(2)}, u32[]{:S(2)}) collective-permute-start(f32[2048,128]{1,0:T(8,128)} %get-tuple-element.79), channel_id=1, source_target_pairs={{0,2},{2,0},{4,6},{6,4},{8,10},{10,8},{12,14},{14,12},{16,18},{18,... | collective-permute-start | bytes 3145736 | tf_op jit(solution)/shard_map/ppermute | solution.py:268
  71.8 3.1 %collective-permute-start.14 = (f32[2048,128]{1,0:T(8,128)}, f32[2048,128]{1,0:T(8,128)S(1)}, u32[]{:S(2)}, u32[]{:S(2)}) collective-permute-start(f32[2048,128]{1,0:T(8,128)} %get-tuple-element.75), channel_id=1, source_target_pairs={{0,2},{2,0},{4,6},{6,4},{8,10},{10,8},{12,14},{14,12},{16,18},{18,... | collective-permute-start | bytes 3145736 | tf_op jit(solution)/shard_map/ppermute | solution.py:268

commit v8 on v6

--- a/solution.py
+++ b/solution.py
@@ -89,16 +89,16 @@
 def turn(raw, which):
     shots, cells, times, cross = raw.shape
     depth = shots * times
-    parts = 4
+    chunks = 4
     return pl.pallas_call(
         turn_body,
         in_specs=[SCALARS, pl.BlockSpec(memory_space=pl.ANY)],
         out_specs=[WHOLE] * 4,
         out_shape=[jax.ShapeDtypeStruct((cross // 4, cells, depth), raw.dtype)] * 4,
         scratch_shapes=[
-            pltpu.VMEM((parts, shots, cells // parts, times, cross), raw.dtype),
+            pltpu.VMEM((chunks, shots, cells // chunks, times, cross), raw.dtype),
             pltpu.VMEM((cross * apart(cells), depth), jnp.float32),
-            pltpu.SemaphoreType.DMA((parts,)),
+            pltpu.SemaphoreType.DMA((chunks,)),
         ],
         compiler_params=params(),
         cost_estimate=pl.CostEstimate(flops=0, bytes_accessed=raw.size * 4, transcendentals=0),
@@ -107,17 +107,17 @@
 
 
 DIMS = (((1,), (1,)), ((), ()))
-BLOCK = 8
 
 
 def multiply_body(pieces, core_ref, *refs):
+    own, *pieces = pieces
     slabs = len(pieces)
-    sources, right_ref = refs[:2], refs[-1]
-    ins = refs[2 : 2 + sum(pieces)]
-    share, cells, _ = sources[0].shape
+    sources, right_ref = (refs[:own], refs[own]), refs[-1]
+    ins = refs[own + 1 : own + 1 + sum(pieces)]
+    share, cells, _ = refs[own].shape
     groups = (slabs * cells + LANES - 1) // LANES
     kept, sent = refs[-1 - 2 * groups : -1 - groups], refs[-1 - groups : -1]
-    before = refs[2 + len(ins) : -1 - 2 * groups]
+    before = refs[own + 1 + len(ins) : -1 - 2 * groups]
     for place, count in enumerate(pieces):
         side, other = divmod(place, 2)
         slab = 2 * side + (core_ref[0] if other == 0 else 1 - core_ref[0])
@@ -125,12 +125,12 @@
             right_ref[slab, part * (share // count) : (part + 1) * (share // count)] = ins[part][...]
         ins = ins[count:]
 
-    @pl.loop(0, share // BLOCK)
-    def _(step):
-        for place in range(BLOCK):
-            cross = step * BLOCK + place
-            left = jnp.concatenate([source[cross] for source in sources], axis=0)
-            rows = pl.ds(pl.multiple_of(cross * cells, cells), cells)
+    for cross_part in range(own):
+        first_cross = cross_part * (share // own)
+        for place in range(share // own):
+            cross = first_cross + place
+            left = jnp.concatenate([sources[0][cross_part][place], sources[1][cross]], axis=0)
+            rows = pl.ds(cross * cells, cells)
             for group in range(groups):
                 members = range(group * LANES // cells, min(slabs, (group + 1) * LANES // cells))
                 right = jnp.concatenate([right_ref[slab, cross] for slab in members], axis=0)
@@ -146,21 +146,22 @@
 
 
 def multiply(core, sources, pieces, before=()):
-    share, cells, depth = sources[0].shape
+    share, cells, depth = sources[1].shape
     slabs = len(pieces)
     groups = -(-slabs * cells // LANES)
     flops = 2 * share * 2 * cells * slabs * cells * depth
     flat = [part for piece in pieces for part in piece]
+    counts = [len(sources[0])] + [len(piece) for piece in pieces]
     return pl.pallas_call(
-        functools.partial(multiply_body, [len(piece) for piece in pieces]),
-        in_specs=[SCALARS] + [WHOLE] * (2 + len(flat) + len(before)),
+        functools.partial(multiply_body, counts),
+        in_specs=[SCALARS] + [WHOLE] * (1 + sum(counts) + len(before)),
         out_specs=[WHOLE] * (2 * groups),
         out_shape=[jax.ShapeDtypeStruct((share * cells, LANES), jnp.float32)] * (2 * groups),
-        scratch_shapes=[pltpu.VMEM((slabs, share, cells, depth), sources[0].dtype)],
+        scratch_shapes=[pltpu.VMEM((slabs, share, cells, depth), sources[1].dtype)],
         compiler_params=params(),
         cost_estimate=pl.CostEstimate(flops=flops, bytes_accessed=6 << 20, transcendentals=0),
         name="multiply",
-    )(core.reshape(1), *in_vmem(*sources, *flat, *before))
+    )(core.reshape(1), *in_vmem(*sources[0], sources[1], *flat, *before))
 
 
 def gather_rows(where_ref, cells, kept_ref, came_ref, rows_ref):
@@ -200,18 +201,24 @@
 
 
 def late_spread_body(scale, cells, where_ref, kept_ref, came_ref, _, skewed_ref, image_ref, rows_ref, buffer_ref, sems):
+    line = skewed_ref.shape[0] // cells
+    side = 2 * cells
+
+    def send(first, count, sem):
+        for lag in range(count):
+            row = GAP * (2 * cells + first + lag)
+            buffer_ref[first + lag] = skewed_ref[pl.ds(row, cells, stride=line), :]
+        block = pl.ds(first, count)
+        copy = pltpu.make_async_copy(buffer_ref.at[block], image_ref.at[block], sem)
+        copy.start()
+        return copy
+
+    copies = [send(where_ref[7] * side, side + 1, sems.at[0])]
     gather_rows(where_ref, cells, kept_ref, came_ref, rows_ref)
     spread_rows(where_ref, cells, (4, 5), scale, rows_ref, skewed_ref)
-    line = skewed_ref.shape[0] // cells
-    parts, lags = sems.shape[0], image_ref.shape[0]
-    cuts = [lags * part // parts for part in range(parts + 1)]
-    copies = []
-    for part, (start, stop) in enumerate(zip(cuts, cuts[1:])):
-        for lag in range(start, stop):
-            buffer_ref[lag] = skewed_ref[pl.ds(GAP * (2 * cells + lag), cells, stride=line), :]
-        block = pl.ds(start, stop - start)
-        copies.append(pltpu.make_async_copy(buffer_ref.at[block], image_ref.at[block], sems.at[part]))
-        copies[-1].start()
+    for part in range(2):
+        first = (1 - where_ref[7]) * (side + 1) + part * (side // 2)
+        copies.append(send(first, side // 2, sems.at[1 + part]))
     for copy in copies:
         copy.wait()
 
@@ -230,7 +237,7 @@
         scratch_shapes=[
             pltpu.VMEM((LANES * apart(cells), LANES), jnp.float32),
             pltpu.VMEM((lags, cells, LANES), jnp.float32),
-            pltpu.SemaphoreType.DMA((4,)),
+            pltpu.SemaphoreType.DMA((3,)),
         ],
         compiler_params=params(),
         name="late_spread",
@@ -273,7 +280,7 @@
     y1 = along_y(twin)
     source, _ = barrier(source, twin)
     left, left_lent, far, far_lent = turn(source, which)
-    moved, y0, left = barrier(moved, y0, left)
+    y0, left = barrier(y0, left)
     y2, z0 = along_y(moved), along_z(y0)
     moved_twin, y1, far, left_lent = barrier(moved_twin, y1, far, left_lent)
     y3, z1 = along_y(moved_twin), along_z(y1)
@@ -281,18 +288,19 @@
     right = across(far)
     z0, far_lent, y2 = barrier(z0, far_lent, y2)
     right_twin = across_to_core(far_lent)
+    left_twin, right = barrier(left_twin, right)
     z2 = along_z(y2)
-    left_twin, right = barrier(left_twin, right)
-    early = multiply(core, (left, left_twin), [(piece,) for piece in (kept, twin, y0, y1, z0, z1)])
-    y3, *early = barrier(y3, *early)
+    y3, z1 = barrier(y3, z1)
     z3 = along_z(y3)
-    middle = multiply(core, (right, right_twin), ((moved,), (moved_twin,), (y2,), (y3,)), (early[0], early[2]))
+    left_twin, y3, z2 = barrier(left_twin, y3, z2)
+    early = multiply(core, ([left], left_twin), [(piece,) for piece in (kept, twin, y0, y1, z0, z1)])
+    middle = multiply(core, ([right], right_twin), ((moved,), (moved_twin,), (y2,), (y3,)), (early[0], early[2]))
     middle_came = to_core(middle[1])
     side = 2 - 4 * odd
-    where = jnp.stack([block + shift - core for shift in (0, side, -side) for block in (0, 1)] + [core])
+    where = jnp.stack([block + shift - core for shift in (0, side, -side) for block in (0, 1)] + [core, 1 - odd])
     where = where.astype(jnp.int32)
     skewed = early_spread(scale, cells, where, (middle[0], middle_came))
-    late = multiply(core, (right, right_twin), ((z2,), (z3,)), (early[1], early[3]))
+    late = multiply(core, ([right], right_twin), ((z2,), (z3,)), (early[1], early[3]))
     late_came = to_core(late[1])
     return late_spread(scale, cells, where, (late[0], late_came), skewed)
 

time: 79.3 us -> 78.3 us (0.987)
  Pallas kernels: 18.9 us -> 16.3 us
  starting transfers between devices: 24.9 us -> 26.1 us
    ppermute x4, waiting for transfers between devices: 12.7 us -> 3.69 us  [along_z(): lax.ppermute(value, 'inline', [pair for pair in pairs if 0 <= pair[1] < c...]
    ppermute x2, waiting for transfers between devices: 5.86 us -> 12.7 us  [across_to_core(): return lax.ppermute(value, ('inline', 'shot'), pairs)]
    ppermute x4, waiting for transfers between devices: 12.2 us -> 17.3 us  [along_y(): lax.ppermute(value, 'inline', [(index, index ^ 2) for index in range(coun...]
    ppermute x2, waiting for transfers between devices: 2.67 us -> 0.01 us  [across(): return lax.ppermute(value, 'shot', [(0, 1), (1, 0)])]
    pallas_call x3, Pallas kernels: 8.85 us -> 6.36 us  [multiply(): pl.pallas_call(functools.partial(multiply_body, counts), in_specs=[SCALAR...]
    ppermute x4, starting transfers between devices: 4.39 us -> 5.92 us  [along_y(): lax.ppermute(value, 'inline', [(index, index ^ 2) for index in range(coun...]
  transfers between devices with their start and end apart: 16 -> 16, of which waited for: 9 -> 8; matrix products, arithmetic and copies ran while one was open for 0% -> 0% of each run, Pallas kernels for 16% -> 13%
where the time goes in v8:
time: 78.3 us; the launch traced here: 78.1 us
  waiting for transfers between devices  35.3 us (45%)
  starting transfers between devices  26.1 us (33%)
  Pallas kernels  16.3 us (21%)
    ppermute x4, waiting for transfers between devices, along_y(): lax.ppermute(value, 'inline', [(index, index ^ 2) for index in range(coun...  17.3 us
    ppermute x4, starting transfers between devices, along_z(): lax.ppermute(value, 'inline', [pair for pair in pairs if 0 <= pair[1] < c...  14.9 us
    ppermute x2, waiting for transfers between devices, across_to_core(): return lax.ppermute(value, ('inline', 'shot'), pairs)  12.7 us
    pallas_call x3, Pallas kernels, multiply(): pl.pallas_call(functools.partial(multiply_body, counts), in_specs=[SCALAR...  6.36 us
    ppermute x4, starting transfers between devices, along_y(): lax.ppermute(value, 'inline', [(index, index ^ 2) for index in range(coun...  5.92 us
    pallas_call x2, Pallas kernels, turn(): pl.pallas_call(turn_body, in_specs=[SCALARS, pl.BlockSpec(memory_space=pl...  5.38 us
    ppermute x4, waiting for transfers between devices, along_z(): lax.ppermute(value, 'inline', [pair for pair in pairs if 0 <= pair[1] < c...  3.69 us
    pallas_call x1, Pallas kernels, late_spread(): pl.pallas_call(functools.partial(late_spread_body, scale, cells), in_spec...  3.31 us
  transfers between devices with their start and end apart: 16, of which 8 were waited for; matrix products, arithmetic and copies ran while one was open for 0% of the time, Pallas kernels for 13%

profile of v8, /device:TPU:0, one launch (start us, length us, event | category | flops | bytes accessed | tf_op | source)
XLA Modules:
  0.0 78.1 jit_solution(6016026269726769859)
XLA Ops:
  0.0 0.1 pad_add_fusion.which_ref
  0.1 2.7 %turn.2 = (bf16[64,32,128]{2,1,0:T(8,128)(2,1)S(1)}, bf16[64,32,128]{2,1,0:T(8,128)(2,1)S(1)}, bf16[64,32,128]{2,1,0:T(8,128)(2,1)S(1)}, bf16[64,32,128]{2,1,0:T(8,128)(2,1)S(1)}) custom-call(s32[2]{0:T(128)S(1)} %pad_add_fusion.which_ref, bf16[4,32,32,256]{3,2,1,0:T(8,128)(2,1)} %raw_ref.1), custom_call_target="tpu_custom_call" | custom-call | bytes 4194304 | tf_op jit(solution)/shard_map/turn/pallas_call | solution.py:93
  2.8 0.5 collective-permute-start
  3.3 2.6 %collective-permute-start.5 = (bf16[64,32,128]{2,1,0:T(8,128)(2,1)S(1)}, bf16[64,32,128]{2,1,0:T(8,128)(2,1)S(1)}, u32[]{:S(2)}, u32[]{:S(2)}) collective-permute-start(bf16[64,32,128]{2,1,0:T(8,128)(2,1)S(1)} %get-tuple-element.53.refs_2_), channel_id=1, source_target_pairs={{0,4},{2,6},{4,0},{6,2},{8,12},{10,14},{12,8},{14,10},{16,20},{18,... | collective-permute-start | bytes 1572872 | tf_op jit(solution)/shard_map/ppermute | solution.py:258
  5.9 0.0 collective-permute-done.refs_3_
  5.9 1.8 %collective-permute-start.7 = (bf16[64,32,128]{2,1,0:T(8,128)(2,1)S(1)}, bf16[64,32,128]{2,1,0:T(8,128)(2,1)S(1)}, u32[]{:S(2)}, u32[]{:S(2)}) collective-permute-start(bf16[64,32,128]{2,1,0:T(8,128)(2,1)S(1)} %get-tuple-element.57), channel_id=1, source_target_pairs={{0,1},{1,0},{2,3},{3,2},{4,5},{5,4},{6,7},{7,6},{8,9},{9,8},{10,11... | collective-permute-start | bytes 1572872 | tf_op jit(solution)/shard_map/ppermute | solution.py:255
  7.7 0.0 collective-permute-start.1
  7.7 1.6 %collective-permute-start.2 = (bf16[64,32,128]{2,1,0:T(8,128)(2,1)S(1)}, bf16[64,32,128]{2,1,0:T(8,128)(2,1)S(1)}, u32[]{:S(2)}, u32[]{:S(2)}) collective-permute-start(bf16[64,32,128]{2,1,0:T(8,128)(2,1)S(1)} %collective-permute-done.refs_3_), channel_id=1, source_target_pairs={{0,4},{2,6},{4,0},{6,2},{8,12},{10,14},{12,8},{14,10},{16,20},{18,... | collective-permute-start | bytes 1572872 | tf_op jit(solution)/shard_map/ppermute | solution.py:258
  9.2 2.7 %turn.3 = (bf16[64,32,128]{2,1,0:T(8,128)(2,1)S(1)}, bf16[64,32,128]{2,1,0:T(8,128)(2,1)S(1)}, bf16[64,32,128]{2,1,0:T(8,128)(2,1)S(1)}, bf16[64,32,128]{2,1,0:T(8,128)(2,1)S(1)}) custom-call(s32[2]{0:T(128)S(1)} %pad_add_fusion.which_ref, bf16[4,32,32,256]{3,2,1,0:T(8,128)(2,1)} %raw_ref.2), custom_call_target="tpu_custom_call" | custom-call | bytes 4194304 | tf_op jit(solution)/shard_map/turn/pallas_call | solution.py:93
  11.9 6.7 %collective-permute-done.5.refs_4_ = bf16[64,32,128]{2,1,0:T(8,128)(2,1)S(1)} collective-permute-done((bf16[64,32,128]{2,1,0:T(8,128)(2,1)S(1)}, bf16[64,32,128]{2,1,0:T(8,128)(2,1)S(1)}, u32[]{:S(2)}, u32[]{:S(2)}) %collective-permute-start.5) | collective-permute-done | bytes 524320 | tf_op jit(solution)/shard_map/ppermute | solution.py:258
  18.7 3.9 %collective-permute-start.6 = (bf16[64,32,128]{2,1,0:T(8,128)(2,1)S(1)}, bf16[64,32,128]{2,1,0:T(8,128)(2,1)S(1)}, u32[]{:S(2)}, u32[]{:S(2)}) collective-permute-start(bf16[64,32,128]{2,1,0:T(8,128)(2,1)S(1)} %collective-permute-done.5.refs_4_), channel_id=1, source_target_pairs={{0,8},{2,10},{8,16},{10,18},{12,4},{14,6},{16,24},{18,26},{20,12},... | collective-permute-start | bytes 1572872 | tf_op jit(solution)/shard_map/ppermute | solution.py:262
  22.6 0.0 collective-permute-done.7.refs_2_
  22.6 0.1 collective-permute-start.8
  22.7 7.7 %collective-permute-done.1.refs_3_ = bf16[64,32,128]{2,1,0:T(8,128)(2,1)S(1)} collective-permute-done((bf16[64,32,128]{2,1,0:T(8,128)(2,1)S(1)}, bf16[64,32,128]{2,1,0:T(8,128)(2,1)S(1)}, u32[]{:S(2)}, u32[]{:S(2)}) %collective-permute-start.1) | collective-permute-done | bytes 524320 | tf_op jit(solution)/shard_map/ppermute | solution.py:269
  30.4 0.0 collective-permute-done.2.refs_5_
  30.4 1.7 %collective-permute-start.10 = (bf16[64,32,128]{2,1,0:T(8,128)(2,1)S(1)}, bf16[64,32,128]{2,1,0:T(8,128)(2,1)S(1)}, u32[]{:S(2)}, u32[]{:S(2)}) collective-permute-start(bf16[64,32,128]{2,1,0:T(8,128)(2,1)S(1)} %collective-permute-done.1.refs_3_), channel_id=1, source_target_pairs={{0,4},{2,6},{4,0},{6,2},{8,12},{10,14},{12,8},{14,10},{16,20},{18,... | collective-permute-start | bytes 1572872 | tf_op jit(solution)/shard_map/ppermute | solution.py:258
  32.1 3.5 %collective-permute-start.11 = (bf16[64,32,128]{2,1,0:T(8,128)(2,1)S(1)}, bf16[64,32,128]{2,1,0:T(8,128)(2,1)S(1)}, u32[]{:S(2)}, u32[]{:S(2)}) collective-permute-start(bf16[64,32,128]{2,1,0:T(8,128)(2,1)S(1)} %collective-permute-done.2.refs_5_), channel_id=1, source_target_pairs={{0,8},{2,10},{8,16},{10,18},{12,4},{14,6},{16,24},{18,26},{20,12},... | collective-permute-start | bytes 1572872 | tf_op jit(solution)/shard_map/ppermute | solution.py:262
  35.6 0.4 collective-permute-start.3
  36.1 0.0 collective-permute-done.6.refs_6_
  36.1 1.5 %collective-permute-start.4 = (bf16[64,32,128]{2,1,0:T(8,128)(2,1)S(1)}, bf16[64,32,128]{2,1,0:T(8,128)(2,1)S(1)}, u32[]{:S(2)}, u32[]{:S(2)}) collective-permute-start(bf16[64,32,128]{2,1,0:T(8,128)(2,1)S(1)} %get-tuple-element.51), channel_id=1, source_target_pairs={{0,1},{1,0},{2,3},{3,2},{4,5},{5,4},{6,7},{7,6},{8,9},{9,8},{10,11... | collective-permute-start | bytes 1572872 | tf_op jit(solution)/shard_map/ppermute | solution.py:255
  37.5 3.6 %collective-permute-done.8.refs_4_ = bf16[64,32,128]{2,1,0:T(8,128)(2,1)S(1)} collective-permute-done((bf16[64,32,128]{2,1,0:T(8,128)(2,1)S(1)}, bf16[64,32,128]{2,1,0:T(8,128)(2,1)S(1)}, u32[]{:S(2)}, u32[]{:S(2)}) %collective-permute-start.8) | collective-permute-done | bytes 524320 | tf_op jit(solution)/shard_map/ppermute | solution.py:258
  41.1 3.9 %collective-permute-start.12 = (bf16[64,32,128]{2,1,0:T(8,128)(2,1)S(1)}, bf16[64,32,128]{2,1,0:T(8,128)(2,1)S(1)}, u32[]{:S(2)}, u32[]{:S(2)}) collective-permute-start(bf16[64,32,128]{2,1,0:T(8,128)(2,1)S(1)} %collective-permute-done.8.refs_4_), channel_id=1, source_target_pairs={{0,8},{2,10},{8,16},{10,18},{12,4},{14,6},{16,24},{18,26},{20,12},... | collective-permute-start | bytes 1572872 | tf_op jit(solution)/shard_map/ppermute | solution.py:262
  45.1 7.0 %collective-permute-done.10.refs_5_ = bf16[64,32,128]{2,1,0:T(8,128)(2,1)S(1)} collective-permute-done((bf16[64,32,128]{2,1,0:T(8,128)(2,1)S(1)}, bf16[64,32,128]{2,1,0:T(8,128)(2,1)S(1)}, u32[]{:S(2)}, u32[]{:S(2)}) %collective-permute-start.10) | collective-permute-done | bytes 524320 | tf_op jit(solution)/shard_map/ppermute | solution.py:258
  52.1 1.0 %collective-permute-start.9 = (bf16[64,32,128]{2,1,0:T(8,128)(2,1)S(1)}, bf16[64,32,128]{2,1,0:T(8,128)(2,1)S(1)}, u32[]{:S(2)}, u32[]{:S(2)}) collective-permute-start(bf16[64,32,128]{2,1,0:T(8,128)(2,1)S(1)} %get-tuple-element.58), channel_id=1, source_target_pairs={{0,3},{1,2},{2,1},{3,0},{4,7},{5,6},{6,5},{7,4},{8,11},{9,10},{10,... | collective-permute-start | bytes 1572872 | tf_op jit(solution)/shard_map/ppermute | solution.py:269
  53.1 0.0 collective-permute-done.11.refs_7_
  53.1 3.5 %collective-permute-start.13 = (bf16[64,32,128]{2,1,0:T(8,128)(2,1)S(1)}, bf16[64,32,128]{2,1,0:T(8,128)(2,1)S(1)}, u32[]{:S(2)}, u32[]{:S(2)}) collective-permute-start(bf16[64,32,128]{2,1,0:T(8,128)(2,1)S(1)} %collective-permute-done.10.refs_5_), channel_id=1, source_target_pairs={{0,8},{2,10},{8,16},{10,18},{12,4},{14,6},{16,24},{18,26},{20,12},... | collective-permute-start | bytes 1572872 | tf_op jit(solution)/shard_map/ppermute | solution.py:262
  56.6 0.0 collective-permute-done.3.refs_1_
  56.6 0.0 collective-permute-done.4.refs_0_
  56.6 2.5 %collective-permute-done.12.refs_2_ = bf16[64,32,128]{2,1,0:T(8,128)(2,1)S(1)} collective-permute-done((bf16[64,32,128]{2,1,0:T(8,128)(2,1)S(1)}, bf16[64,32,128]{2,1,0:T(8,128)(2,1)S(1)}, u32[]{:S(2)}, u32[]{:S(2)}) %collective-permute-start.12) | collective-permute-done | bytes 524320 | tf_op jit(solution)/shard_map/ppermute | solution.py:262
  59.1 2.0 %multiply.3 = (f32[2048,128]{1,0:T(8,128)S(1)}, f32[2048,128]{1,0:T(8,128)S(1)}, f32[2048,128]{1,0:T(8,128)S(1)}, f32[2048,128]{1,0:T(8,128)S(1)}) custom-call(s32[1]{0:T(128)} %bitcast.6.core_ref, bf16[64,32,128]{2,1,0:T(8,128)(2,1)S(1)} %get-tuple-element.65.refs_0_, bf16[64,32,128]{2,1,0:T(8,128)(2,1)S(1)} %collective-permute-done.3.refs_1_, ...), custom_call_target="tpu_custom_call" | custom-call | flops 201326592 | bytes 6291456 | tf_op jit(solution)/shard_map/multiply/pallas_call | solution.py:155
  61.1 5.0 %collective-permute-done.9.refs_1_ = bf16[64,32,128]{2,1,0:T(8,128)(2,1)S(1)} collective-permute-done((bf16[64,32,128]{2,1,0:T(8,128)(2,1)S(1)}, bf16[64,32,128]{2,1,0:T(8,128)(2,1)S(1)}, u32[]{:S(2)}, u32[]{:S(2)}) %collective-permute-start.9) | collective-permute-done | bytes 524320 | tf_op jit(solution)/shard_map/ppermute | solution.py:269
  66.0 2.7 %multiply.5 = (f32[2048,128]{1,0:T(8,128)S(1)}, f32[2048,128]{1,0:T(8,128)}) custom-call(s32[1]{0:T(128)} %bitcast.6.core_ref, bf16[64,32,128]{2,1,0:T(8,128)(2,1)S(1)} %collective-permute-done.4.refs_0_, bf16[64,32,128]{2,1,0:T(8,128)(2,1)S(1)} %collective-permute-done.9.refs_1_, bf16[64,32,128]{2,1,0:T(8,128)(2,1)S(1)} %collective-permute-done.7.refs_2_, ...), custom_call_target="tpu_custom_call" | custom-call | flops 134217728 | bytes 6291456 | tf_op jit(solution)/shard_map/multiply/pallas_call | solution.py:155
  68.7 0.1 collective-permute-start.15
  68.8 1.2 %collective-permute-done.13.refs_3_ = bf16[64,32,128]{2,1,0:T(8,128)(2,1)S(1)} collective-permute-done((bf16[64,32,128]{2,1,0:T(8,128)(2,1)S(1)}, bf16[64,32,128]{2,1,0:T(8,128)(2,1)S(1)}, u32[]{:S(2)}, u32[]{:S(2)}) %collective-permute-start.13) | collective-permute-done | bytes 524320 | tf_op jit(solution)/shard_map/ppermute | solution.py:262
  70.0 1.7 %multiply.4 = (f32[2048,128]{1,0:T(8,128)S(1)}, f32[2048,128]{1,0:T(8,128)}) custom-call(s32[1]{0:T(128)} %bitcast.6.core_ref, bf16[64,32,128]{2,1,0:T(8,128)(2,1)S(1)} %collective-permute-done.4.refs_0_, bf16[64,32,128]{2,1,0:T(8,128)(2,1)S(1)} %collective-permute-done.9.refs_1_, bf16[64,32,128]{2,1,0:T(8,128)(2,1)S(1)} %collective-permute-done.12.refs_2_, ...), custom_call_target="tpu_custom_call" | custom-call | flops 67108864 | bytes 6291456 | tf_op jit(solution)/shard_map/multiply/pallas_call | solution.py:155
  71.8 0.0 collective-permute-start.14
  71.8 0.1 stack.42.where_ref
  71.8 0.0 collective-permute-done.15.came_ref
  71.8 1.3 %early_spread.1._ = f32[24672,128]{1,0:T(8,128)S(1)} custom-call(s32[8]{0:T(128)S(1)} %stack.42.where_ref, f32[2048,128]{1,0:T(8,128)S(1)} %get-tuple-element.76.kept_ref, f32[2048,128]{1,0:T(8,128)S(1)} %collective-permute-done.15.came_ref), custom_call_target="tpu_custom_call" | custom-call | bytes 6291456 | tf_op jit(solution)/shard_map/early_spread/pallas_call | solution.py:191
  73.1 1.6 %collective-permute-done.14.came_ref = f32[2048,128]{1,0:T(8,128)} collective-permute-done((f32[2048,128]{1,0:T(8,128)}, f32[2048,128]{1,0:T(8,128)}, u32[]{:S(2)}, u32[]{:S(2)}) %collective-permute-start.14) | collective-permute-done | bytes 1048608 | tf_op jit(solution)/shard_map/ppermute | solution.py:265
  74.8 3.3 %late_spread.1 = (f32[24672,128]{1,0:T(8,128)S(1)}, f32[129,32,128]{2,1,0:T(8,128)}) custom-call(s32[8]{0:T(128)S(1)} %stack.42.where_ref, f32[2048,128]{1,0:T(8,128)S(1)} %get-tuple-element.71.kept_ref, f32[2048,128]{1,0:T(8,128)} %collective-permute-done.14.came_ref, f32[24672,128]{1,0:T(8,128)S(1)} %early_spread.1._), custom_call_target="tpu_custom_call", output_to_operand_aliasing={{0}: (3, {})} | custom-call | tf_op jit(solution)/shard_map/late_spread/pallas_call | solution.py:228
Async XLA Ops:
  2.8 3.1 %collective-permute-start = (bf16[64,32,128]{2,1,0:T(8,128)(2,1)S(1)}, bf16[64,32,128]{2,1,0:T(8,128)(2,1)S(1)}, u32[]{:S(2)}, u32[]{:S(2)}) collective-permute-start(bf16[64,32,128]{2,1,0:T(8,128)(2,1)S(1)} %get-tuple-element.44), channel_id=1, source_target_pairs={{0,2},{2,0},{4,6},{6,4},{8,10},{10,8},{12,14},{14,12},{16,18},{18,... | collective-permute-start | bytes 1572872 | tf_op jit(solution)/shard_map/ppermute | solution.py:265
  3.3 15.4 %collective-permute-start.5 = (bf16[64,32,128]{2,1,0:T(8,128)(2,1)S(1)}, bf16[64,32,128]{2,1,0:T(8,128)(2,1)S(1)}, u32[]{:S(2)}, u32[]{:S(2)}) collective-permute-start(bf16[64,32,128]{2,1,0:T(8,128)(2,1)S(1)} %get-tuple-element.53.refs_2_), channel_id=1, source_target_pairs={{0,4},{2,6},{4,0},{6,2},{8,12},{10,14},{12,8},{14,10},{16,20},{18,... | collective-permute-start | bytes 1572872 | tf_op jit(solution)/shard_map/ppermute | solution.py:258
  5.9 16.7 %collective-permute-start.7 = (bf16[64,32,128]{2,1,0:T(8,128)(2,1)S(1)}, bf16[64,32,128]{2,1,0:T(8,128)(2,1)S(1)}, u32[]{:S(2)}, u32[]{:S(2)}) collective-permute-start(bf16[64,32,128]{2,1,0:T(8,128)(2,1)S(1)} %get-tuple-element.57), channel_id=1, source_target_pairs={{0,1},{1,0},{2,3},{3,2},{4,5},{5,4},{6,7},{7,6},{8,9},{9,8},{10,11... | collective-permute-start | bytes 1572872 | tf_op jit(solution)/shard_map/ppermute | solution.py:255
  7.7 22.7 %collective-permute-start.1 = (bf16[64,32,128]{2,1,0:T(8,128)(2,1)S(1)}, bf16[64,32,128]{2,1,0:T(8,128)(2,1)S(1)}, u32[]{:S(2)}, u32[]{:S(2)}) collective-permute-start(bf16[64,32,128]{2,1,0:T(8,128)(2,1)S(1)} %get-tuple-element.45), channel_id=1, source_target_pairs={{0,3},{1,2},{2,1},{3,0},{4,7},{5,6},{6,5},{7,4},{8,11},{9,10},{10,... | collective-permute-start | bytes 1572872 | tf_op jit(solution)/shard_map/ppermute | solution.py:269
  7.7 22.7 %collective-permute-start.2 = (bf16[64,32,128]{2,1,0:T(8,128)(2,1)S(1)}, bf16[64,32,128]{2,1,0:T(8,128)(2,1)S(1)}, u32[]{:S(2)}, u32[]{:S(2)}) collective-permute-start(bf16[64,32,128]{2,1,0:T(8,128)(2,1)S(1)} %collective-permute-done.refs_3_), channel_id=1, source_target_pairs={{0,4},{2,6},{4,0},{6,2},{8,12},{10,14},{12,8},{14,10},{16,20},{18,... | collective-permute-start | bytes 1572872 | tf_op jit(solution)/shard_map/ppermute | solution.py:258
  18.7 17.4 %collective-permute-start.6 = (bf16[64,32,128]{2,1,0:T(8,128)(2,1)S(1)}, bf16[64,32,128]{2,1,0:T(8,128)(2,1)S(1)}, u32[]{:S(2)}, u32[]{:S(2)}) collective-permute-start(bf16[64,32,128]{2,1,0:T(8,128)(2,1)S(1)} %collective-permute-done.5.refs_4_), channel_id=1, source_target_pairs={{0,8},{2,10},{8,16},{10,18},{12,4},{14,6},{16,24},{18,26},{20,12},... | collective-permute-start | bytes 1572872 | tf_op jit(solution)/shard_map/ppermute | solution.py:262
  22.6 18.5 %collective-permute-start.8 = (bf16[64,32,128]{2,1,0:T(8,128)(2,1)S(1)}, bf16[64,32,128]{2,1,0:T(8,128)(2,1)S(1)}, u32[]{:S(2)}, u32[]{:S(2)}) collective-permute-start(bf16[64,32,128]{2,1,0:T(8,128)(2,1)S(1)} %collective-permute-done.7.refs_2_), channel_id=1, source_target_pairs={{0,4},{2,6},{4,0},{6,2},{8,12},{10,14},{12,8},{14,10},{16,20},{18,... | collective-permute-start | bytes 1572872 | tf_op jit(solution)/shard_map/ppermute | solution.py:258
  30.4 21.7 %collective-permute-start.10 = (bf16[64,32,128]{2,1,0:T(8,128)(2,1)S(1)}, bf16[64,32,128]{2,1,0:T(8,128)(2,1)S(1)}, u32[]{:S(2)}, u32[]{:S(2)}) collective-permute-start(bf16[64,32,128]{2,1,0:T(8,128)(2,1)S(1)} %collective-permute-done.1.refs_3_), channel_id=1, source_target_pairs={{0,4},{2,6},{4,0},{6,2},{8,12},{10,14},{12,8},{14,10},{16,20},{18,... | collective-permute-start | bytes 1572872 | tf_op jit(solution)/shard_map/ppermute | solution.py:258
  32.1 21.0 %collective-permute-start.11 = (bf16[64,32,128]{2,1,0:T(8,128)(2,1)S(1)}, bf16[64,32,128]{2,1,0:T(8,128)(2,1)S(1)}, u32[]{:S(2)}, u32[]{:S(2)}) collective-permute-start(bf16[64,32,128]{2,1,0:T(8,128)(2,1)S(1)} %collective-permute-done.2.refs_5_), channel_id=1, source_target_pairs={{0,8},{2,10},{8,16},{10,18},{12,4},{14,6},{16,24},{18,26},{20,12},... | collective-permute-start | bytes 1572872 | tf_op jit(solution)/shard_map/ppermute | solution.py:262
  35.6 21.0 %collective-permute-start.3 = (bf16[64,32,128]{2,1,0:T(8,128)(2,1)S(1)}, bf16[64,32,128]{2,1,0:T(8,128)(2,1)S(1)}, u32[]{:S(2)}, u32[]{:S(2)}) collective-permute-start(bf16[64,32,128]{2,1,0:T(8,128)(2,1)S(1)} %get-tuple-element.50), channel_id=1, source_target_pairs={{0,2},{2,0},{4,6},{6,4},{8,10},{10,8},{12,14},{14,12},{16,18},{18,... | collective-permute-start | bytes 1572872 | tf_op jit(solution)/shard_map/ppermute | solution.py:265
  36.1 20.6 %collective-permute-start.4 = (bf16[64,32,128]{2,1,0:T(8,128)(2,1)S(1)}, bf16[64,32,128]{2,1,0:T(8,128)(2,1)S(1)}, u32[]{:S(2)}, u32[]{:S(2)}) collective-permute-start(bf16[64,32,128]{2,1,0:T(8,128)(2,1)S(1)} %get-tuple-element.51), channel_id=1, source_target_pairs={{0,1},{1,0},{2,3},{3,2},{4,5},{5,4},{6,7},{7,6},{8,9},{9,8},{10,11... | collective-permute-start | bytes 1572872 | tf_op jit(solution)/shard_map/ppermute | solution.py:255
  41.1 18.0 %collective-permute-start.12 = (bf16[64,32,128]{2,1,0:T(8,128)(2,1)S(1)}, bf16[64,32,128]{2,1,0:T(8,128)(2,1)S(1)}, u32[]{:S(2)}, u32[]{:S(2)}) collective-permute-start(bf16[64,32,128]{2,1,0:T(8,128)(2,1)S(1)} %collective-permute-done.8.refs_4_), channel_id=1, source_target_pairs={{0,8},{2,10},{8,16},{10,18},{12,4},{14,6},{16,24},{18,26},{20,12},... | collective-permute-start | bytes 1572872 | tf_op jit(solution)/shard_map/ppermute | solution.py:262
  52.1 13.9 %collective-permute-start.9 = (bf16[64,32,128]{2,1,0:T(8,128)(2,1)S(1)}, bf16[64,32,128]{2,1,0:T(8,128)(2,1)S(1)}, u32[]{:S(2)}, u32[]{:S(2)}) collective-permute-start(bf16[64,32,128]{2,1,0:T(8,128)(2,1)S(1)} %get-tuple-element.58), channel_id=1, source_target_pairs={{0,3},{1,2},{2,1},{3,0},{4,7},{5,6},{6,5},{7,4},{8,11},{9,10},{10,... | collective-permute-start | bytes 1572872 | tf_op jit(solution)/shard_map/ppermute | solution.py:269
  53.1 16.9 %collective-permute-start.13 = (bf16[64,32,128]{2,1,0:T(8,128)(2,1)S(1)}, bf16[64,32,128]{2,1,0:T(8,128)(2,1)S(1)}, u32[]{:S(2)}, u32[]{:S(2)}) collective-permute-start(bf16[64,32,128]{2,1,0:T(8,128)(2,1)S(1)} %collective-permute-done.10.refs_5_), channel_id=1, source_target_pairs={{0,8},{2,10},{8,16},{10,18},{12,4},{14,6},{16,24},{18,26},{20,12},... | collective-permute-start | bytes 1572872 | tf_op jit(solution)/shard_map/ppermute | solution.py:262
  68.7 3.1 %collective-permute-start.15 = (f32[2048,128]{1,0:T(8,128)}, f32[2048,128]{1,0:T(8,128)S(1)}, u32[]{:S(2)}, u32[]{:S(2)}) collective-permute-start(f32[2048,128]{1,0:T(8,128)} %get-tuple-element.77), channel_id=1, source_target_pairs={{0,2},{2,0},{4,6},{6,4},{8,10},{10,8},{12,14},{14,12},{16,18},{18,... | collective-permute-start | bytes 3145736 | tf_op jit(solution)/shard_map/ppermute | solution.py:265
  71.8 3.0 %collective-permute-start.14 = (f32[2048,128]{1,0:T(8,128)}, f32[2048,128]{1,0:T(8,128)}, u32[]{:S(2)}, u32[]{:S(2)}) collective-permute-start(f32[2048,128]{1,0:T(8,128)} %get-tuple-element.72), channel_id=1, source_target_pairs={{0,2},{2,0},{4,6},{6,4},{8,10},{10,8},{12,14},{14,12},{16,18},{18,... | collective-permute-start | bytes 3145736 | tf_op jit(solution)/shard_map/ppermute | solution.py:265

commit v9 on v7

--- a/solution.py
+++ b/solution.py
@@ -60,50 +60,48 @@
 WHOLE = pl.BlockSpec(memory_space=pltpu.VMEM)
 
 
-def turn_body(which_ref, raw_ref, *refs):
-    turned_refs, (buffer_ref, rows_ref, sems) = refs[:4], refs[4:]
-    parts, shots, count, times, cross = buffer_ref.shape
-    cells = parts * count
+def turn_body(which_ref, raw_ref, own_ref, other_ref, buffer_ref, rows_ref, sems):
+    chunks, shots, count, times, cross = buffer_ref.shape
+    cells = chunks * count
+    lanes = pl.ds(pl.multiple_of(which_ref[0] * cross, cross), cross)
     copies = [
-        pltpu.make_async_copy(raw_ref.at[:, pl.ds(part * count, count)], buffer_ref.at[part], sems.at[part])
-        for part in range(parts)
+        pltpu.make_async_copy(
+            raw_ref.at[:, pl.ds(chunk * count, count), :, lanes], buffer_ref.at[chunk], sems.at[chunk]
+        )
+        for chunk in range(chunks)
     ]
     for copy in copies:
         copy.start()
-    for part, copy in enumerate(copies):
+    for chunk, copy in enumerate(copies):
         copy.wait()
         for cell in range(count):
-            for lanes in range(0, cross, LANES):
-                tile = buffer_ref[part, :, cell, :, lanes : lanes + LANES].reshape(shots * times, LANES)
-                base = lanes * apart(cells) + GAP * (part * count + cell)
-                rows_ref[pl.ds(base, LANES, stride=apart(cells)), :] = tile.astype(jnp.float32).T
-    half, core = which_ref[0], which_ref[1]
-    quarters = [2 * half + core, 2 * half + 1 - core, 2 - 2 * half + core, 3 - 2 * half - core]
-    for turned_ref, quarter in zip(turned_refs, quarters):
-        share = turned_ref.shape[0]
+            tile = buffer_ref[chunk, :, cell].reshape(shots * times, cross).astype(jnp.float32)
+            rows_ref[pl.ds(GAP * (chunk * count + cell), cross, stride=apart(cells)), :] = tile.T
+    share = cross // 2
+    for turned_ref, part in ((own_ref, which_ref[1]), (other_ref, 1 - which_ref[1])):
         for place in range(share):
-            base = (quarter * share + place) * apart(cells)
+            base = (part * share + place) * apart(cells)
             turned_ref[place] = rows_ref[pl.ds(base, cells, stride=GAP), :].astype(turned_ref.dtype)
 
 
-def turn(raw, which):
-    shots, cells, times, cross = raw.shape
+def turn(raw, half, core):
+    shots, cells, times, _ = raw.shape
     depth = shots * times
     chunks = 4
     return pl.pallas_call(
         turn_body,
         in_specs=[SCALARS, pl.BlockSpec(memory_space=pl.ANY)],
-        out_specs=[WHOLE] * 4,
-        out_shape=[jax.ShapeDtypeStruct((cross // 4, cells, depth), raw.dtype)] * 4,
+        out_specs=[WHOLE] * 2,
+        out_shape=[jax.ShapeDtypeStruct((LANES // 2, cells, depth), raw.dtype)] * 2,
         scratch_shapes=[
-            pltpu.VMEM((chunks, shots, cells // chunks, times, cross), raw.dtype),
-            pltpu.VMEM((cross * apart(cells), depth), jnp.float32),
+            pltpu.VMEM((chunks, shots, cells // chunks, times, LANES), raw.dtype),
+            pltpu.VMEM((LANES * apart(cells), depth), jnp.float32),
             pltpu.SemaphoreType.DMA((chunks,)),
         ],
         compiler_params=params(),
-        cost_estimate=pl.CostEstimate(flops=0, bytes_accessed=raw.size * 4, transcendentals=0),
+        cost_estimate=pl.CostEstimate(flops=0, bytes_accessed=raw.size * 2, transcendentals=0),
         name="turn",
-    )(which, pltpu.with_memory_space_constraint(raw, pltpu.HBM))
+    )(jnp.stack([half, core]).astype(jnp.int32), pltpu.with_memory_space_constraint(raw, pltpu.HBM))
 
 
 DIMS = (((1,), (1,)), ((), ()))
@@ -274,33 +272,45 @@
     def barrier(*values):
         return lax.optimization_barrier(values)
 
-    which = jnp.stack([half, core]).astype(jnp.int32)
-    kept, lent, there, there_twin = turn(receiver, which)
-    y0 = along_y(kept)
-    twin = to_core(lent)
-    there, there_twin, twin = barrier(there, there_twin, twin)
-    moved, moved_twin = across(there), across_to_core(there_twin)
-    y1 = along_y(twin)
-    source, _ = barrier(source, twin)
-    left, left_lent, far, far_lent = turn(source, which)
-    y0, left = barrier(y0, left)
-    y2, z0 = along_y(moved), along_z(y0)
-    moved_twin, y1, far, left_lent = barrier(moved_twin, y1, far, left_lent)
-    y3, z1 = along_y(moved_twin), along_z(y1)
-    left_twin = to_core(left_lent)
-    right = across(far)
-    z0, far_lent, y2 = barrier(z0, far_lent, y2)
-    right_twin = across_to_core(far_lent)
-    left_twin, right = barrier(left_twin, right)
-    z2 = along_z(y2)
-    early = multiply(core, ([left], left_twin), [(piece,) for piece in (kept, twin, y0, y1, z0, z1)])
-    y3, *early = barrier(y3, *early)
-    z3 = along_z(y3)
-    middle = multiply(core, ([right], right_twin), ((moved,), (moved_twin,), (y2,), (y3,)), (early[0], early[2]))
-    middle_came = to_core(middle[1])
+    receiver0, source0 = receiver, source
     side = 2 - 4 * odd
     where = jnp.stack([block + shift - core for shift in (0, side, -side) for block in (0, 1)] + [core, 1 - odd])
     where = where.astype(jnp.int32)
+    kept, lent = turn(receiver0, half, core)
+    y0 = along_y(kept)
+    twin = to_core(lent)
+    receiver_tied, *_ = barrier(receiver0, kept)
+    there, there_twin = turn(receiver_tied, 1 - half, core)
+    there_tied, *_ = barrier(there, twin)
+    moved = across(there_tied)
+    there_twin_tied, *_ = barrier(there_twin, twin)
+    moved_twin = across_to_core(there_twin_tied)
+    source_tied, *_ = barrier(source0, there)
+    left, left_lent = turn(source_tied, half, core)
+    source2_tied, *_ = barrier(source0, left)
+    far, far_lent = turn(source2_tied, 1 - half, core)
+    y1 = along_y(twin)
+    y2 = along_y(moved)
+    moved_twin_tied, *_ = barrier(moved_twin, y1)
+    y3 = along_y(moved_twin_tied)
+    y0_tied, *_ = barrier(y0, left)
+    z0 = along_z(y0_tied)
+    z1 = along_z(y1)
+    left_lent_tied, *_ = barrier(left_lent, moved_twin)
+    left_twin = to_core(left_lent_tied)
+    far_tied, *_ = barrier(far, y1)
+    right = across(far_tied)
+    far_lent_tied, *_ = barrier(far_lent, y2)
+    right_twin = across_to_core(far_lent_tied)
+    y2_tied, *_ = barrier(y2, z0)
+    z2 = along_z(y2_tied)
+    left_twin_tied, *_ = barrier(left_twin, right)
+    early = multiply(core, ([left], left_twin_tied), [(piece,) for piece in (kept, twin, y0, y1, z0, z1)])
+    y3_tied, *_ = barrier(y3, z1)
+    z3 = along_z(y3_tied)
+    right_twin_tied, *_ = barrier(right_twin, z2)
+    middle = multiply(core, ([right], right_twin_tied), ((moved,), (moved_twin,), (y2,), (y3,)), (early[0], early[2]))
+    middle_came = to_core(middle[1])
     skewed, image = early_spread(scale, cells, where, (middle[0], middle_came))
     late = multiply(core, ([right], right_twin), ((z2,), (z3,)), (early[1], early[3]))
     late_came = to_core(late[1])

time: 77.6 us -> 73.9 us (0.952)
  waiting for transfers between devices: 34.9 us -> 29.9 us
  Pallas kernels: 17.1 us -> 20.5 us
  starting transfers between devices: 24.9 us -> 22.8 us
    ppermute x4, waiting for transfers between devices: 13.4 us -> 2.53 us  [along_z(): lax.ppermute(value, 'inline', [pair for pair in pairs if 0 <= pair[1] < c...]
    ppermute x4, waiting for transfers between devices: 13.1 us -> 23.5 us  [along_y(): lax.ppermute(value, 'inline', [(index, index ^ 2) for index in range(coun...]
    ppermute x2, waiting for transfers between devices: 7.72 us -> 3.48 us  [across_to_core(): return lax.ppermute(value, ('inline', 'shot'), pairs)]
    pallas_call x2 -> x4, Pallas kernels: 5.38 us -> 8.83 us  [turn(): pl.pallas_call(turn_body, in_specs=[SCALARS, pl.BlockSpec(memory_space=pl...]
    ppermute x4, starting transfers between devices: 4.28 us -> 3.17 us  [along_y(): lax.ppermute(value, 'inline', [(index, index ^ 2) for index in range(coun...]
    ppermute x4, starting transfers between devices: 14.7 us -> 15.5 us  [along_z(): lax.ppermute(value, 'inline', [pair for pair in pairs if 0 <= pair[1] < c...]
    ppermute x4, starting transfers between devices: 1.66 us -> 0.88 us  [to_core(): lax.ppermute(value, 'inline', [(index, index ^ 1) for index in range(coun...]
  transfers between devices with their start and end apart: 16 -> 16, of which waited for: 8 -> 7; matrix products, arithmetic and copies ran while one was open for 0% -> 0% of each run, Pallas kernels for 16% -> 22%
where the time goes in v9:
time: 73.9 us; the launch traced here: 73.5 us
  waiting for transfers between devices  29.9 us (40%)
  starting transfers between devices  22.8 us (31%)
  Pallas kernels  20.5 us (28%)
    ppermute x4, waiting for transfers between devices, along_y(): lax.ppermute(value, 'inline', [(index, index ^ 2) for index in range(coun...  23.5 us
    ppermute x4, starting transfers between devices, along_z(): lax.ppermute(value, 'inline', [pair for pair in pairs if 0 <= pair[1] < c...  15.5 us
    pallas_call x4, Pallas kernels, turn(): pl.pallas_call(turn_body, in_specs=[SCALARS, pl.BlockSpec(memory_space=pl...  8.83 us
    pallas_call x3, Pallas kernels, multiply(): pl.pallas_call(functools.partial(multiply_body, counts), in_specs=[SCALAR...  6.39 us
    ppermute x2, waiting for transfers between devices, across_to_core(): return lax.ppermute(value, ('inline', 'shot'), pairs)  3.48 us
    ppermute x4, starting transfers between devices, along_y(): lax.ppermute(value, 'inline', [(index, index ^ 2) for index in range(coun...  3.17 us
    ppermute x2, starting transfers between devices, across(): return lax.ppermute(value, 'shot', [(0, 1), (1, 0)])  3.11 us
    pallas_call x1, Pallas kernels, early_spread(): pl.pallas_call(functools.partial(early_spread_body, scale, cells), in_spe...  3.01 us
  transfers between devices with their start and end apart: 16, of which 7 were waited for; matrix products, arithmetic and copies ran while one was open for 0% of the time, Pallas kernels for 22%

profile of v9, /device:TPU:0, one launch (start us, length us, event | category | flops | bytes accessed | tf_op | source)
XLA Modules:
  0.0 73.5 jit_solution(3590412991946047977)
XLA Ops:
  0.0 0.1 pad_add_fusion
  0.1 2.2 %turn.4 = (bf16[64,32,128]{2,1,0:T(8,128)(2,1)S(1)}, bf16[64,32,128]{2,1,0:T(8,128)(2,1)S(1)}) custom-call(s32[2]{0:T(128)S(1)} %get-tuple-element.72.which_ref, bf16[4,32,32,256]{3,2,1,0:T(8,128)(2,1)} %raw_ref.2), custom_call_target="tpu_custom_call" | custom-call | bytes 2097152 | tf_op jit(solution)/shard_map/turn/pallas_call | solution.py:91
  2.3 0.5 collective-permute-start
  2.8 2.6 %collective-permute-start.6 = (bf16[64,32,128]{2,1,0:T(8,128)(2,1)S(1)}, bf16[64,32,128]{2,1,0:T(8,128)(2,1)S(1)}, u32[]{:S(2)}, u32[]{:S(2)}) collective-permute-start(bf16[64,32,128]{2,1,0:T(8,128)(2,1)S(1)} %get-tuple-element.38.refs_2_), channel_id=1, source_target_pairs={{0,4},{2,6},{4,0},{6,2},{8,12},{10,14},{12,8},{14,10},{16,20},{18,... | collective-permute-start | bytes 1572872 | tf_op jit(solution)/shard_map/ppermute | solution.py:259
  5.4 2.2 %turn.5 = (bf16[64,32,128]{2,1,0:T(8,128)(2,1)S(1)}, bf16[64,32,128]{2,1,0:T(8,128)(2,1)S(1)}) custom-call(s32[2]{0:T(128)S(1)} %get-tuple-element.71.which_ref, bf16[4,32,32,256]{3,2,1,0:T(8,128)(2,1)} %raw_ref.2), custom_call_target="tpu_custom_call" | custom-call | bytes 2097152 | tf_op jit(solution)/shard_map/turn/pallas_call | solution.py:91
  7.6 0.0 collective-permute-done.refs_3_
  7.6 1.6 %collective-permute-start.3 = (bf16[64,32,128]{2,1,0:T(8,128)(2,1)S(1)}, bf16[64,32,128]{2,1,0:T(8,128)(2,1)S(1)}, u32[]{:S(2)}, u32[]{:S(2)}) collective-permute-start(bf16[64,32,128]{2,1,0:T(8,128)(2,1)S(1)} %get-tuple-element.48), channel_id=1, source_target_pairs={{0,1},{1,0},{2,3},{3,2},{4,5},{5,4},{6,7},{7,6},{8,9},{9,8},{10,11... | collective-permute-start | bytes 1572872 | tf_op jit(solution)/shard_map/ppermute | solution.py:256
  9.2 0.5 collective-permute-start.1
  9.7 0.0 collective-permute-start.9
  9.7 2.2 %turn.6 = (bf16[64,32,128]{2,1,0:T(8,128)(2,1)S(1)}, bf16[64,32,128]{2,1,0:T(8,128)(2,1)S(1)}) custom-call(s32[2]{0:T(128)S(1)} %get-tuple-element.72.which_ref, bf16[4,32,32,256]{3,2,1,0:T(8,128)(2,1)} %raw_ref.4), custom_call_target="tpu_custom_call" | custom-call | bytes 2097152 | tf_op jit(solution)/shard_map/turn/pallas_call | solution.py:91
  11.9 6.3 %collective-permute-done.6.refs_4_ = bf16[64,32,128]{2,1,0:T(8,128)(2,1)S(1)} collective-permute-done((bf16[64,32,128]{2,1,0:T(8,128)(2,1)S(1)}, bf16[64,32,128]{2,1,0:T(8,128)(2,1)S(1)}, u32[]{:S(2)}, u32[]{:S(2)}) %collective-permute-start.6) | collective-permute-done | bytes 524320 | tf_op jit(solution)/shard_map/ppermute | solution.py:259
  18.2 3.9 %collective-permute-start.7 = (bf16[64,32,128]{2,1,0:T(8,128)(2,1)S(1)}, bf16[64,32,128]{2,1,0:T(8,128)(2,1)S(1)}, u32[]{:S(2)}, u32[]{:S(2)}) collective-permute-start(bf16[64,32,128]{2,1,0:T(8,128)(2,1)S(1)} %collective-permute-done.6.refs_4_), channel_id=1, source_target_pairs={{0,8},{2,10},{8,16},{10,18},{12,4},{14,6},{16,24},{18,26},{20,12},... | collective-permute-start | bytes 1572872 | tf_op jit(solution)/shard_map/ppermute | solution.py:263
  22.1 0.3 collective-permute-done.3.refs_2_
  22.5 0.0 collective-permute-start.4
  22.5 6.9 %collective-permute-done.1.refs_5_ = bf16[64,32,128]{2,1,0:T(8,128)(2,1)S(1)} collective-permute-done((bf16[64,32,128]{2,1,0:T(8,128)(2,1)S(1)}, bf16[64,32,128]{2,1,0:T(8,128)(2,1)S(1)}, u32[]{:S(2)}, u32[]{:S(2)}) %collective-permute-start.1) | collective-permute-done | bytes 524320 | tf_op jit(solution)/shard_map/ppermute | solution.py:259
  29.4 3.9 %collective-permute-start.11 = (bf16[64,32,128]{2,1,0:T(8,128)(2,1)S(1)}, bf16[64,32,128]{2,1,0:T(8,128)(2,1)S(1)}, u32[]{:S(2)}, u32[]{:S(2)}) collective-permute-start(bf16[64,32,128]{2,1,0:T(8,128)(2,1)S(1)} %collective-permute-done.1.refs_5_), channel_id=1, source_target_pairs={{0,8},{2,10},{8,16},{10,18},{12,4},{14,6},{16,24},{18,26},{20,12},... | collective-permute-start | bytes 1572872 | tf_op jit(solution)/shard_map/ppermute | solution.py:263
  33.4 0.0 collective-permute-done.9.refs_3_
  33.4 0.1 collective-permute-start.10
  33.4 2.2 %turn.7 = (bf16[64,32,128]{2,1,0:T(8,128)(2,1)S(1)}, bf16[64,32,128]{2,1,0:T(8,128)(2,1)S(1)}) custom-call(s32[2]{0:T(128)S(1)} %get-tuple-element.71.which_ref, bf16[4,32,32,256]{3,2,1,0:T(8,128)(2,1)} %raw_ref.4), custom_call_target="tpu_custom_call" | custom-call | bytes 2097152 | tf_op jit(solution)/shard_map/turn/pallas_call | solution.py:91
  35.7 0.1 collective-permute-start.13
  35.7 0.0 collective-permute-done.7.refs_6_
  35.8 1.6 %collective-permute-start.2 = (bf16[64,32,128]{2,1,0:T(8,128)(2,1)S(1)}, bf16[64,32,128]{2,1,0:T(8,128)(2,1)S(1)}, u32[]{:S(2)}, u32[]{:S(2)}) collective-permute-start(bf16[64,32,128]{2,1,0:T(8,128)(2,1)S(1)} %get-tuple-element.46), channel_id=1, source_target_pairs={{0,1},{1,0},{2,3},{3,2},{4,5},{5,4},{6,7},{7,6},{8,9},{9,8},{10,11... | collective-permute-start | bytes 1572872 | tf_op jit(solution)/shard_map/ppermute | solution.py:256
  37.3 3.3 %collective-permute-done.4.refs_4_ = bf16[64,32,128]{2,1,0:T(8,128)(2,1)S(1)} collective-permute-done((bf16[64,32,128]{2,1,0:T(8,128)(2,1)S(1)}, bf16[64,32,128]{2,1,0:T(8,128)(2,1)S(1)}, u32[]{:S(2)}, u32[]{:S(2)}) %collective-permute-start.4) | collective-permute-done | bytes 524320 | tf_op jit(solution)/shard_map/ppermute | solution.py:259
  40.6 3.9 %collective-permute-start.8 = (bf16[64,32,128]{2,1,0:T(8,128)(2,1)S(1)}, bf16[64,32,128]{2,1,0:T(8,128)(2,1)S(1)}, u32[]{:S(2)}, u32[]{:S(2)}) collective-permute-start(bf16[64,32,128]{2,1,0:T(8,128)(2,1)S(1)} %collective-permute-done.4.refs_4_), channel_id=1, source_target_pairs={{0,8},{2,10},{8,16},{10,18},{12,4},{14,6},{16,24},{18,26},{20,12},... | collective-permute-start | bytes 1572872 | tf_op jit(solution)/shard_map/ppermute | solution.py:263
  44.6 0.0 collective-permute-done.11.refs_7_
  44.6 0.1 collective-permute-start.5
  44.7 6.9 %collective-permute-done.10.refs_5_ = bf16[64,32,128]{2,1,0:T(8,128)(2,1)S(1)} collective-permute-done((bf16[64,32,128]{2,1,0:T(8,128)(2,1)S(1)}, bf16[64,32,128]{2,1,0:T(8,128)(2,1)S(1)}, u32[]{:S(2)}, u32[]{:S(2)}) %collective-permute-start.10) | collective-permute-done | bytes 524320 | tf_op jit(solution)/shard_map/ppermute | solution.py:259
  51.6 3.7 %collective-permute-start.12 = (bf16[64,32,128]{2,1,0:T(8,128)(2,1)S(1)}, bf16[64,32,128]{2,1,0:T(8,128)(2,1)S(1)}, u32[]{:S(2)}, u32[]{:S(2)}) collective-permute-start(bf16[64,32,128]{2,1,0:T(8,128)(2,1)S(1)} %collective-permute-done.10.refs_5_), channel_id=1, source_target_pairs={{0,8},{2,10},{8,16},{10,18},{12,4},{14,6},{16,24},{18,26},{20,12},... | collective-permute-start | bytes 1572872 | tf_op jit(solution)/shard_map/ppermute | solution.py:263
  55.4 0.0 collective-permute-done.13.refs_1_
  55.4 0.0 collective-permute-done.2.refs_0_
  55.4 2.0 %multiply.3 = (f32[2048,128]{1,0:T(8,128)S(1)}, f32[2048,128]{1,0:T(8,128)S(1)}, f32[2048,128]{1,0:T(8,128)S(1)}, f32[2048,128]{1,0:T(8,128)S(1)}) custom-call(s32[1]{0:T(128)} %bitcast.6.core_ref, bf16[64,32,128]{2,1,0:T(8,128)(2,1)S(1)} %get-tuple-element.42.refs_0_, bf16[64,32,128]{2,1,0:T(8,128)(2,1)S(1)} %collective-permute-done.13.refs_1_, ...), custom_call_target="tpu_custom_call" | custom-call | flops 201326592 | bytes 6291456 | tf_op jit(solution)/shard_map/multiply/pallas_call | solution.py:153
  57.4 0.0 collective-permute-done.8.refs_2_
  57.4 3.5 %collective-permute-done.5.refs_1_ = bf16[64,32,128]{2,1,0:T(8,128)(2,1)S(1)} collective-permute-done((bf16[64,32,128]{2,1,0:T(8,128)(2,1)S(1)}, bf16[64,32,128]{2,1,0:T(8,128)(2,1)S(1)}, u32[]{:S(2)}, u32[]{:S(2)}) %collective-permute-start.5) | collective-permute-done | bytes 524320 | tf_op jit(solution)/shard_map/ppermute | solution.py:270
  60.9 2.7 %multiply.5 = (f32[2048,128]{1,0:T(8,128)S(1)}, f32[2048,128]{1,0:T(8,128)}) custom-call(s32[1]{0:T(128)} %bitcast.6.core_ref, bf16[64,32,128]{2,1,0:T(8,128)(2,1)S(1)} %collective-permute-done.2.refs_0_, bf16[64,32,128]{2,1,0:T(8,128)(2,1)S(1)} %collective-permute-done.5.refs_1_, bf16[64,32,128]{2,1,0:T(8,128)(2,1)S(1)} %collective-permute-done.3.refs_2_, ...), custom_call_target="tpu_custom_call" | custom-call | flops 134217728 | bytes 6291456 | tf_op jit(solution)/shard_map/multiply/pallas_call | solution.py:153
  63.5 0.3 collective-permute-start.15
  63.8 2.5 %collective-permute-done.12.refs_3_ = bf16[64,32,128]{2,1,0:T(8,128)(2,1)S(1)} collective-permute-done((bf16[64,32,128]{2,1,0:T(8,128)(2,1)S(1)}, bf16[64,32,128]{2,1,0:T(8,128)(2,1)S(1)}, u32[]{:S(2)}, u32[]{:S(2)}) %collective-permute-start.12) | collective-permute-done | bytes 524320 | tf_op jit(solution)/shard_map/ppermute | solution.py:263
  66.3 1.8 %multiply.4 = (f32[2048,128]{1,0:T(8,128)S(1)}, f32[2048,128]{1,0:T(8,128)}) custom-call(s32[1]{0:T(128)} %bitcast.6.core_ref, bf16[64,32,128]{2,1,0:T(8,128)(2,1)S(1)} %collective-permute-done.2.refs_0_, bf16[64,32,128]{2,1,0:T(8,128)(2,1)S(1)} %collective-permute-done.5.refs_1_, bf16[64,32,128]{2,1,0:T(8,128)(2,1)S(1)} %collective-permute-done.8.refs_2_, ...), custom_call_target="tpu_custom_call" | custom-call | flops 67108864 | bytes 6291456 | tf_op jit(solution)/shard_map/multiply/pallas_call | solution.py:153
  68.1 0.0 collective-permute-start.14
  68.1 0.1 stack.55.where_ref
  68.2 0.0 collective-permute-done.15.came_ref
  68.2 3.0 %early_spread.1 = (f32[24672,128]{1,0:T(8,128)S(1)}, f32[129,32,128]{2,1,0:T(8,128)}) custom-call(s32[8]{0:T(128)S(1)} %stack.55.where_ref, f32[2048,128]{1,0:T(8,128)S(1)} %get-tuple-element.66.kept_ref, f32[2048,128]{1,0:T(8,128)} %collective-permute-done.15.came_ref), custom_call_target="tpu_custom_call" | custom-call | bytes 6291456 | tf_op jit(solution)/shard_map/early_spread/pallas_call | solution.py:214
  71.2 0.0 collective-permute-done.14.came_ref
  71.2 2.3 %late_spread.1 = (f32[24672,128]{1,0:T(8,128)S(1)}, f32[129,32,128]{2,1,0:T(8,128)}) custom-call(s32[8]{0:T(128)S(1)} %stack.55.where_ref, f32[2048,128]{1,0:T(8,128)S(1)} %get-tuple-element.61.kept_ref, f32[2048,128]{1,0:T(8,128)S(1)} %collective-permute-done.14.came_ref, ...), custom_call_target="tpu_custom_call", output_to_operand_aliasing={{0}: (3, {}), {1}: (4, {})} | custom-call | tf_op jit(solution)/shard_map/late_spread/pallas_call | solution.py:236
Async XLA Ops:
  2.3 5.3 %collective-permute-start = (bf16[64,32,128]{2,1,0:T(8,128)(2,1)S(1)}, bf16[64,32,128]{2,1,0:T(8,128)(2,1)S(1)}, u32[]{:S(2)}, u32[]{:S(2)}) collective-permute-start(bf16[64,32,128]{2,1,0:T(8,128)(2,1)S(1)} %get-tuple-element.45), channel_id=1, source_target_pairs={{0,2},{2,0},{4,6},{6,4},{8,10},{10,8},{12,14},{14,12},{16,18},{18,... | collective-permute-start | bytes 1572872 | tf_op jit(solution)/shard_map/ppermute | solution.py:266
  2.8 15.4 %collective-permute-start.6 = (bf16[64,32,128]{2,1,0:T(8,128)(2,1)S(1)}, bf16[64,32,128]{2,1,0:T(8,128)(2,1)S(1)}, u32[]{:S(2)}, u32[]{:S(2)}) collective-permute-start(bf16[64,32,128]{2,1,0:T(8,128)(2,1)S(1)} %get-tuple-element.38.refs_2_), channel_id=1, source_target_pairs={{0,4},{2,6},{4,0},{6,2},{8,12},{10,14},{12,8},{14,10},{16,20},{18,... | collective-permute-start | bytes 1572872 | tf_op jit(solution)/shard_map/ppermute | solution.py:259
  7.6 14.8 %collective-permute-start.3 = (bf16[64,32,128]{2,1,0:T(8,128)(2,1)S(1)}, bf16[64,32,128]{2,1,0:T(8,128)(2,1)S(1)}, u32[]{:S(2)}, u32[]{:S(2)}) collective-permute-start(bf16[64,32,128]{2,1,0:T(8,128)(2,1)S(1)} %get-tuple-element.48), channel_id=1, source_target_pairs={{0,1},{1,0},{2,3},{3,2},{4,5},{5,4},{6,7},{7,6},{8,9},{9,8},{10,11... | collective-permute-start | bytes 1572872 | tf_op jit(solution)/shard_map/ppermute | solution.py:256
  9.2 20.2 %collective-permute-start.1 = (bf16[64,32,128]{2,1,0:T(8,128)(2,1)S(1)}, bf16[64,32,128]{2,1,0:T(8,128)(2,1)S(1)}, u32[]{:S(2)}, u32[]{:S(2)}) collective-permute-start(bf16[64,32,128]{2,1,0:T(8,128)(2,1)S(1)} %collective-permute-done.refs_3_), channel_id=1, source_target_pairs={{0,4},{2,6},{4,0},{6,2},{8,12},{10,14},{12,8},{14,10},{16,20},{18,... | collective-permute-start | bytes 1572872 | tf_op jit(solution)/shard_map/ppermute | solution.py:259
  9.7 23.7 %collective-permute-start.9 = (bf16[64,32,128]{2,1,0:T(8,128)(2,1)S(1)}, bf16[64,32,128]{2,1,0:T(8,128)(2,1)S(1)}, u32[]{:S(2)}, u32[]{:S(2)}) collective-permute-start(bf16[64,32,128]{2,1,0:T(8,128)(2,1)S(1)} %get-tuple-element.53), channel_id=1, source_target_pairs={{0,3},{1,2},{2,1},{3,0},{4,7},{5,6},{6,5},{7,4},{8,11},{9,10},{10,... | collective-permute-start | bytes 1572872 | tf_op jit(solution)/shard_map/ppermute | solution.py:270
  18.2 17.6 %collective-permute-start.7 = (bf16[64,32,128]{2,1,0:T(8,128)(2,1)S(1)}, bf16[64,32,128]{2,1,0:T(8,128)(2,1)S(1)}, u32[]{:S(2)}, u32[]{:S(2)}) collective-permute-start(bf16[64,32,128]{2,1,0:T(8,128)(2,1)S(1)} %collective-permute-done.6.refs_4_), channel_id=1, source_target_pairs={{0,8},{2,10},{8,16},{10,18},{12,4},{14,6},{16,24},{18,26},{20,12},... | collective-permute-start | bytes 1572872 | tf_op jit(solution)/shard_map/ppermute | solution.py:263
  22.5 18.2 %collective-permute-start.4 = (bf16[64,32,128]{2,1,0:T(8,128)(2,1)S(1)}, bf16[64,32,128]{2,1,0:T(8,128)(2,1)S(1)}, u32[]{:S(2)}, u32[]{:S(2)}) collective-permute-start(bf16[64,32,128]{2,1,0:T(8,128)(2,1)S(1)} %collective-permute-done.3.refs_2_), channel_id=1, source_target_pairs={{0,4},{2,6},{4,0},{6,2},{8,12},{10,14},{12,8},{14,10},{16,20},{18,... | collective-permute-start | bytes 1572872 | tf_op jit(solution)/shard_map/ppermute | solution.py:259
  29.4 15.2 %collective-permute-start.11 = (bf16[64,32,128]{2,1,0:T(8,128)(2,1)S(1)}, bf16[64,32,128]{2,1,0:T(8,128)(2,1)S(1)}, u32[]{:S(2)}, u32[]{:S(2)}) collective-permute-start(bf16[64,32,128]{2,1,0:T(8,128)(2,1)S(1)} %collective-permute-done.1.refs_5_), channel_id=1, source_target_pairs={{0,8},{2,10},{8,16},{10,18},{12,4},{14,6},{16,24},{18,26},{20,12},... | collective-permute-start | bytes 1572872 | tf_op jit(solution)/shard_map/ppermute | solution.py:263
  33.4 18.3 %collective-permute-start.10 = (bf16[64,32,128]{2,1,0:T(8,128)(2,1)S(1)}, bf16[64,32,128]{2,1,0:T(8,128)(2,1)S(1)}, u32[]{:S(2)}, u32[]{:S(2)}) collective-permute-start(bf16[64,32,128]{2,1,0:T(8,128)(2,1)S(1)} %collective-permute-done.9.refs_3_), channel_id=1, source_target_pairs={{0,4},{2,6},{4,0},{6,2},{8,12},{10,14},{12,8},{14,10},{16,20},{18,... | collective-permute-start | bytes 1572872 | tf_op jit(solution)/shard_map/ppermute | solution.py:259
  35.7 19.7 %collective-permute-start.13 = (bf16[64,32,128]{2,1,0:T(8,128)(2,1)S(1)}, bf16[64,32,128]{2,1,0:T(8,128)(2,1)S(1)}, u32[]{:S(2)}, u32[]{:S(2)}) collective-permute-start(bf16[64,32,128]{2,1,0:T(8,128)(2,1)S(1)} %get-tuple-element.57), channel_id=1, source_target_pairs={{0,2},{2,0},{4,6},{6,4},{8,10},{10,8},{12,14},{14,12},{16,18},{18,... | collective-permute-start | bytes 1572872 | tf_op jit(solution)/shard_map/ppermute | solution.py:266
  35.8 19.6 %collective-permute-start.2 = (bf16[64,32,128]{2,1,0:T(8,128)(2,1)S(1)}, bf16[64,32,128]{2,1,0:T(8,128)(2,1)S(1)}, u32[]{:S(2)}, u32[]{:S(2)}) collective-permute-start(bf16[64,32,128]{2,1,0:T(8,128)(2,1)S(1)} %get-tuple-element.46), channel_id=1, source_target_pairs={{0,1},{1,0},{2,3},{3,2},{4,5},{5,4},{6,7},{7,6},{8,9},{9,8},{10,11... | collective-permute-start | bytes 1572872 | tf_op jit(solution)/shard_map/ppermute | solution.py:256
  40.6 16.7 %collective-permute-start.8 = (bf16[64,32,128]{2,1,0:T(8,128)(2,1)S(1)}, bf16[64,32,128]{2,1,0:T(8,128)(2,1)S(1)}, u32[]{:S(2)}, u32[]{:S(2)}) collective-permute-start(bf16[64,32,128]{2,1,0:T(8,128)(2,1)S(1)} %collective-permute-done.4.refs_4_), channel_id=1, source_target_pairs={{0,8},{2,10},{8,16},{10,18},{12,4},{14,6},{16,24},{18,26},{20,12},... | collective-permute-start | bytes 1572872 | tf_op jit(solution)/shard_map/ppermute | solution.py:263
  44.6 16.3 %collective-permute-start.5 = (bf16[64,32,128]{2,1,0:T(8,128)(2,1)S(1)}, bf16[64,32,128]{2,1,0:T(8,128)(2,1)S(1)}, u32[]{:S(2)}, u32[]{:S(2)}) collective-permute-start(bf16[64,32,128]{2,1,0:T(8,128)(2,1)S(1)} %get-tuple-element.49), channel_id=1, source_target_pairs={{0,3},{1,2},{2,1},{3,0},{4,7},{5,6},{6,5},{7,4},{8,11},{9,10},{10,... | collective-permute-start | bytes 1572872 | tf_op jit(solution)/shard_map/ppermute | solution.py:270
  51.6 14.7 %collective-permute-start.12 = (bf16[64,32,128]{2,1,0:T(8,128)(2,1)S(1)}, bf16[64,32,128]{2,1,0:T(8,128)(2,1)S(1)}, u32[]{:S(2)}, u32[]{:S(2)}) collective-permute-start(bf16[64,32,128]{2,1,0:T(8,128)(2,1)S(1)} %collective-permute-done.10.refs_5_), channel_id=1, source_target_pairs={{0,8},{2,10},{8,16},{10,18},{12,4},{14,6},{16,24},{18,26},{20,12},... | collective-permute-start | bytes 1572872 | tf_op jit(solution)/shard_map/ppermute | solution.py:263
  63.5 4.7 %collective-permute-start.15 = (f32[2048,128]{1,0:T(8,128)}, f32[2048,128]{1,0:T(8,128)}, u32[]{:S(2)}, u32[]{:S(2)}) collective-permute-start(f32[2048,128]{1,0:T(8,128)} %get-tuple-element.67), channel_id=1, source_target_pairs={{0,2},{2,0},{4,6},{6,4},{8,10},{10,8},{12,14},{14,12},{16,18},{18,... | collective-permute-start | bytes 3145736 | tf_op jit(solution)/shard_map/ppermute | solution.py:266
  68.1 3.1 %collective-permute-start.14 = (f32[2048,128]{1,0:T(8,128)}, f32[2048,128]{1,0:T(8,128)S(1)}, u32[]{:S(2)}, u32[]{:S(2)}) collective-permute-start(f32[2048,128]{1,0:T(8,128)} %get-tuple-element.62), channel_id=1, source_target_pairs={{0,2},{2,0},{4,6},{6,4},{8,10},{10,8},{12,14},{14,12},{16,18},{18,... | collective-permute-start | bytes 3145736 | tf_op jit(solution)/shard_map/ppermute | solution.py:266

commit v10 on v9

--- a/solution.py
+++ b/solution.py
@@ -205,7 +205,7 @@
     return [
         pltpu.VMEM((LANES * apart(cells), LANES), jnp.float32),
         pltpu.VMEM((lags, cells, LANES), jnp.float32),
-        pltpu.SemaphoreType.DMA((2,)),
+        pltpu.SemaphoreType.DMA((4,)),
     ]
 
 

time: 73.9 us -> 73.9 us (level)
  no operation moved by 1% of the time
where the time goes in v10:
time: 73.9 us; the launch traced here: 73.5 us
  waiting for transfers between devices  29.9 us (40%)
  starting transfers between devices  22.8 us (31%)
  Pallas kernels  20.5 us (28%)
    ppermute x4, waiting for transfers between devices, along_y(): lax.ppermute(value, 'inline', [(index, index ^ 2) for index in range(coun...  23.5 us
    ppermute x4, starting transfers between devices, along_z(): lax.ppermute(value, 'inline', [pair for pair in pairs if 0 <= pair[1] < c...  15.5 us
    pallas_call x4, Pallas kernels, turn(): pl.pallas_call(turn_body, in_specs=[SCALARS, pl.BlockSpec(memory_space=pl...  8.83 us
    pallas_call x3, Pallas kernels, multiply(): pl.pallas_call(functools.partial(multiply_body, counts), in_specs=[SCALAR...  6.39 us
    ppermute x2, waiting for transfers between devices, across_to_core(): return lax.ppermute(value, ('inline', 'shot'), pairs)  3.48 us
    ppermute x4, starting transfers between devices, along_y(): lax.ppermute(value, 'inline', [(index, index ^ 2) for index in range(coun...  3.17 us
    ppermute x2, starting transfers between devices, across(): return lax.ppermute(value, 'shot', [(0, 1), (1, 0)])  3.11 us
    pallas_call x1, Pallas kernels, early_spread(): pl.pallas_call(functools.partial(early_spread_body, scale, cells), in_spe...  3.01 us
  transfers between devices with their start and end apart: 16, of which 7 were waited for; matrix products, arithmetic and copies ran while one was open for 0% of the time, Pallas kernels for 22%

profile of v10, /device:TPU:0, one launch (start us, length us, event | category | flops | bytes accessed | tf_op | source)
XLA Modules:
  0.0 73.5 jit_solution(6200733582296502577)
XLA Ops:
  0.0 0.1 pad_add_fusion
  0.1 2.2 %turn.4 = (bf16[64,32,128]{2,1,0:T(8,128)(2,1)S(1)}, bf16[64,32,128]{2,1,0:T(8,128)(2,1)S(1)}) custom-call(s32[2]{0:T(128)S(1)} %get-tuple-element.72.which_ref, bf16[4,32,32,256]{3,2,1,0:T(8,128)(2,1)} %raw_ref.2), custom_call_target="tpu_custom_call" | custom-call | bytes 2097152 | tf_op jit(solution)/shard_map/turn/pallas_call | solution.py:91
  2.3 0.5 collective-permute-start
  2.8 2.6 %collective-permute-start.6 = (bf16[64,32,128]{2,1,0:T(8,128)(2,1)S(1)}, bf16[64,32,128]{2,1,0:T(8,128)(2,1)S(1)}, u32[]{:S(2)}, u32[]{:S(2)}) collective-permute-start(bf16[64,32,128]{2,1,0:T(8,128)(2,1)S(1)} %get-tuple-element.38.refs_2_), channel_id=1, source_target_pairs={{0,4},{2,6},{4,0},{6,2},{8,12},{10,14},{12,8},{14,10},{16,20},{18,... | collective-permute-start | bytes 1572872 | tf_op jit(solution)/shard_map/ppermute | solution.py:259
  5.4 2.2 %turn.5 = (bf16[64,32,128]{2,1,0:T(8,128)(2,1)S(1)}, bf16[64,32,128]{2,1,0:T(8,128)(2,1)S(1)}) custom-call(s32[2]{0:T(128)S(1)} %get-tuple-element.71.which_ref, bf16[4,32,32,256]{3,2,1,0:T(8,128)(2,1)} %raw_ref.2), custom_call_target="tpu_custom_call" | custom-call | bytes 2097152 | tf_op jit(solution)/shard_map/turn/pallas_call | solution.py:91
  7.6 0.0 collective-permute-done.refs_3_
  7.6 1.6 %collective-permute-start.3 = (bf16[64,32,128]{2,1,0:T(8,128)(2,1)S(1)}, bf16[64,32,128]{2,1,0:T(8,128)(2,1)S(1)}, u32[]{:S(2)}, u32[]{:S(2)}) collective-permute-start(bf16[64,32,128]{2,1,0:T(8,128)(2,1)S(1)} %get-tuple-element.48), channel_id=1, source_target_pairs={{0,1},{1,0},{2,3},{3,2},{4,5},{5,4},{6,7},{7,6},{8,9},{9,8},{10,11... | collective-permute-start | bytes 1572872 | tf_op jit(solution)/shard_map/ppermute | solution.py:256
  9.2 0.5 collective-permute-start.1
  9.7 0.0 collective-permute-start.9
  9.7 2.2 %turn.6 = (bf16[64,32,128]{2,1,0:T(8,128)(2,1)S(1)}, bf16[64,32,128]{2,1,0:T(8,128)(2,1)S(1)}) custom-call(s32[2]{0:T(128)S(1)} %get-tuple-element.72.which_ref, bf16[4,32,32,256]{3,2,1,0:T(8,128)(2,1)} %raw_ref.4), custom_call_target="tpu_custom_call" | custom-call | bytes 2097152 | tf_op jit(solution)/shard_map/turn/pallas_call | solution.py:91
  11.9 6.3 %collective-permute-done.6.refs_4_ = bf16[64,32,128]{2,1,0:T(8,128)(2,1)S(1)} collective-permute-done((bf16[64,32,128]{2,1,0:T(8,128)(2,1)S(1)}, bf16[64,32,128]{2,1,0:T(8,128)(2,1)S(1)}, u32[]{:S(2)}, u32[]{:S(2)}) %collective-permute-start.6) | collective-permute-done | bytes 524320 | tf_op jit(solution)/shard_map/ppermute | solution.py:259
  18.2 3.9 %collective-permute-start.7 = (bf16[64,32,128]{2,1,0:T(8,128)(2,1)S(1)}, bf16[64,32,128]{2,1,0:T(8,128)(2,1)S(1)}, u32[]{:S(2)}, u32[]{:S(2)}) collective-permute-start(bf16[64,32,128]{2,1,0:T(8,128)(2,1)S(1)} %collective-permute-done.6.refs_4_), channel_id=1, source_target_pairs={{0,8},{2,10},{8,16},{10,18},{12,4},{14,6},{16,24},{18,26},{20,12},... | collective-permute-start | bytes 1572872 | tf_op jit(solution)/shard_map/ppermute | solution.py:263
  22.1 0.3 collective-permute-done.3.refs_2_
  22.5 0.0 collective-permute-start.4
  22.5 6.9 %collective-permute-done.1.refs_5_ = bf16[64,32,128]{2,1,0:T(8,128)(2,1)S(1)} collective-permute-done((bf16[64,32,128]{2,1,0:T(8,128)(2,1)S(1)}, bf16[64,32,128]{2,1,0:T(8,128)(2,1)S(1)}, u32[]{:S(2)}, u32[]{:S(2)}) %collective-permute-start.1) | collective-permute-done | bytes 524320 | tf_op jit(solution)/shard_map/ppermute | solution.py:259
  29.4 3.9 %collective-permute-start.11 = (bf16[64,32,128]{2,1,0:T(8,128)(2,1)S(1)}, bf16[64,32,128]{2,1,0:T(8,128)(2,1)S(1)}, u32[]{:S(2)}, u32[]{:S(2)}) collective-permute-start(bf16[64,32,128]{2,1,0:T(8,128)(2,1)S(1)} %collective-permute-done.1.refs_5_), channel_id=1, source_target_pairs={{0,8},{2,10},{8,16},{10,18},{12,4},{14,6},{16,24},{18,26},{20,12},... | collective-permute-start | bytes 1572872 | tf_op jit(solution)/shard_map/ppermute | solution.py:263
  33.4 0.0 collective-permute-done.9.refs_3_
  33.4 0.1 collective-permute-start.10
  33.4 2.2 %turn.7 = (bf16[64,32,128]{2,1,0:T(8,128)(2,1)S(1)}, bf16[64,32,128]{2,1,0:T(8,128)(2,1)S(1)}) custom-call(s32[2]{0:T(128)S(1)} %get-tuple-element.71.which_ref, bf16[4,32,32,256]{3,2,1,0:T(8,128)(2,1)} %raw_ref.4), custom_call_target="tpu_custom_call" | custom-call | bytes 2097152 | tf_op jit(solution)/shard_map/turn/pallas_call | solution.py:91
  35.7 0.1 collective-permute-start.13
  35.7 0.0 collective-permute-done.7.refs_6_
  35.8 1.6 %collective-permute-start.2 = (bf16[64,32,128]{2,1,0:T(8,128)(2,1)S(1)}, bf16[64,32,128]{2,1,0:T(8,128)(2,1)S(1)}, u32[]{:S(2)}, u32[]{:S(2)}) collective-permute-start(bf16[64,32,128]{2,1,0:T(8,128)(2,1)S(1)} %get-tuple-element.46), channel_id=1, source_target_pairs={{0,1},{1,0},{2,3},{3,2},{4,5},{5,4},{6,7},{7,6},{8,9},{9,8},{10,11... | collective-permute-start | bytes 1572872 | tf_op jit(solution)/shard_map/ppermute | solution.py:256
  37.3 3.3 %collective-permute-done.4.refs_4_ = bf16[64,32,128]{2,1,0:T(8,128)(2,1)S(1)} collective-permute-done((bf16[64,32,128]{2,1,0:T(8,128)(2,1)S(1)}, bf16[64,32,128]{2,1,0:T(8,128)(2,1)S(1)}, u32[]{:S(2)}, u32[]{:S(2)}) %collective-permute-start.4) | collective-permute-done | bytes 524320 | tf_op jit(solution)/shard_map/ppermute | solution.py:259
  40.6 3.9 %collective-permute-start.8 = (bf16[64,32,128]{2,1,0:T(8,128)(2,1)S(1)}, bf16[64,32,128]{2,1,0:T(8,128)(2,1)S(1)}, u32[]{:S(2)}, u32[]{:S(2)}) collective-permute-start(bf16[64,32,128]{2,1,0:T(8,128)(2,1)S(1)} %collective-permute-done.4.refs_4_), channel_id=1, source_target_pairs={{0,8},{2,10},{8,16},{10,18},{12,4},{14,6},{16,24},{18,26},{20,12},... | collective-permute-start | bytes 1572872 | tf_op jit(solution)/shard_map/ppermute | solution.py:263
  44.6 0.0 collective-permute-done.11.refs_7_
  44.6 0.1 collective-permute-start.5
  44.7 6.9 %collective-permute-done.10.refs_5_ = bf16[64,32,128]{2,1,0:T(8,128)(2,1)S(1)} collective-permute-done((bf16[64,32,128]{2,1,0:T(8,128)(2,1)S(1)}, bf16[64,32,128]{2,1,0:T(8,128)(2,1)S(1)}, u32[]{:S(2)}, u32[]{:S(2)}) %collective-permute-start.10) | collective-permute-done | bytes 524320 | tf_op jit(solution)/shard_map/ppermute | solution.py:259
  51.6 3.7 %collective-permute-start.12 = (bf16[64,32,128]{2,1,0:T(8,128)(2,1)S(1)}, bf16[64,32,128]{2,1,0:T(8,128)(2,1)S(1)}, u32[]{:S(2)}, u32[]{:S(2)}) collective-permute-start(bf16[64,32,128]{2,1,0:T(8,128)(2,1)S(1)} %collective-permute-done.10.refs_5_), channel_id=1, source_target_pairs={{0,8},{2,10},{8,16},{10,18},{12,4},{14,6},{16,24},{18,26},{20,12},... | collective-permute-start | bytes 1572872 | tf_op jit(solution)/shard_map/ppermute | solution.py:263
  55.4 0.0 collective-permute-done.13.refs_1_
  55.4 0.0 collective-permute-done.2.refs_0_
  55.4 2.0 %multiply.3 = (f32[2048,128]{1,0:T(8,128)S(1)}, f32[2048,128]{1,0:T(8,128)S(1)}, f32[2048,128]{1,0:T(8,128)S(1)}, f32[2048,128]{1,0:T(8,128)S(1)}) custom-call(s32[1]{0:T(128)} %bitcast.6.core_ref, bf16[64,32,128]{2,1,0:T(8,128)(2,1)S(1)} %get-tuple-element.42.refs_0_, bf16[64,32,128]{2,1,0:T(8,128)(2,1)S(1)} %collective-permute-done.13.refs_1_, ...), custom_call_target="tpu_custom_call" | custom-call | flops 201326592 | bytes 6291456 | tf_op jit(solution)/shard_map/multiply/pallas_call | solution.py:153
  57.4 0.0 collective-permute-done.8.refs_2_
  57.4 3.5 %collective-permute-done.5.refs_1_ = bf16[64,32,128]{2,1,0:T(8,128)(2,1)S(1)} collective-permute-done((bf16[64,32,128]{2,1,0:T(8,128)(2,1)S(1)}, bf16[64,32,128]{2,1,0:T(8,128)(2,1)S(1)}, u32[]{:S(2)}, u32[]{:S(2)}) %collective-permute-start.5) | collective-permute-done | bytes 524320 | tf_op jit(solution)/shard_map/ppermute | solution.py:270
  60.9 2.7 %multiply.5 = (f32[2048,128]{1,0:T(8,128)S(1)}, f32[2048,128]{1,0:T(8,128)}) custom-call(s32[1]{0:T(128)} %bitcast.6.core_ref, bf16[64,32,128]{2,1,0:T(8,128)(2,1)S(1)} %collective-permute-done.2.refs_0_, bf16[64,32,128]{2,1,0:T(8,128)(2,1)S(1)} %collective-permute-done.5.refs_1_, bf16[64,32,128]{2,1,0:T(8,128)(2,1)S(1)} %collective-permute-done.3.refs_2_, ...), custom_call_target="tpu_custom_call" | custom-call | flops 134217728 | bytes 6291456 | tf_op jit(solution)/shard_map/multiply/pallas_call | solution.py:153
  63.5 0.3 collective-permute-start.15
  63.8 2.5 %collective-permute-done.12.refs_3_ = bf16[64,32,128]{2,1,0:T(8,128)(2,1)S(1)} collective-permute-done((bf16[64,32,128]{2,1,0:T(8,128)(2,1)S(1)}, bf16[64,32,128]{2,1,0:T(8,128)(2,1)S(1)}, u32[]{:S(2)}, u32[]{:S(2)}) %collective-permute-start.12) | collective-permute-done | bytes 524320 | tf_op jit(solution)/shard_map/ppermute | solution.py:263
  66.3 1.8 %multiply.4 = (f32[2048,128]{1,0:T(8,128)S(1)}, f32[2048,128]{1,0:T(8,128)}) custom-call(s32[1]{0:T(128)} %bitcast.6.core_ref, bf16[64,32,128]{2,1,0:T(8,128)(2,1)S(1)} %collective-permute-done.2.refs_0_, bf16[64,32,128]{2,1,0:T(8,128)(2,1)S(1)} %collective-permute-done.5.refs_1_, bf16[64,32,128]{2,1,0:T(8,128)(2,1)S(1)} %collective-permute-done.8.refs_2_, ...), custom_call_target="tpu_custom_call" | custom-call | flops 67108864 | bytes 6291456 | tf_op jit(solution)/shard_map/multiply/pallas_call | solution.py:153
  68.1 0.0 collective-permute-start.14
  68.1 0.1 stack.55.where_ref
  68.2 0.0 collective-permute-done.15.came_ref
  68.2 3.0 %early_spread.1 = (f32[24672,128]{1,0:T(8,128)S(1)}, f32[129,32,128]{2,1,0:T(8,128)}) custom-call(s32[8]{0:T(128)S(1)} %stack.55.where_ref, f32[2048,128]{1,0:T(8,128)S(1)} %get-tuple-element.66.kept_ref, f32[2048,128]{1,0:T(8,128)} %collective-permute-done.15.came_ref), custom_call_target="tpu_custom_call" | custom-call | bytes 6291456 | tf_op jit(solution)/shard_map/early_spread/pallas_call | solution.py:214
  71.2 0.0 collective-permute-done.14.came_ref
  71.2 2.3 %late_spread.1 = (f32[24672,128]{1,0:T(8,128)S(1)}, f32[129,32,128]{2,1,0:T(8,128)}) custom-call(s32[8]{0:T(128)S(1)} %stack.55.where_ref, f32[2048,128]{1,0:T(8,128)S(1)} %get-tuple-element.61.kept_ref, f32[2048,128]{1,0:T(8,128)S(1)} %collective-permute-done.14.came_ref, ...), custom_call_target="tpu_custom_call", output_to_operand_aliasing={{0}: (3, {}), {1}: (4, {})} | custom-call | tf_op jit(solution)/shard_map/late_spread/pallas_call | solution.py:236
Async XLA Ops:
  2.3 5.3 %collective-permute-start = (bf16[64,32,128]{2,1,0:T(8,128)(2,1)S(1)}, bf16[64,32,128]{2,1,0:T(8,128)(2,1)S(1)}, u32[]{:S(2)}, u32[]{:S(2)}) collective-permute-start(bf16[64,32,128]{2,1,0:T(8,128)(2,1)S(1)} %get-tuple-element.45), channel_id=1, source_target_pairs={{0,2},{2,0},{4,6},{6,4},{8,10},{10,8},{12,14},{14,12},{16,18},{18,... | collective-permute-start | bytes 1572872 | tf_op jit(solution)/shard_map/ppermute | solution.py:266
  2.8 15.4 %collective-permute-start.6 = (bf16[64,32,128]{2,1,0:T(8,128)(2,1)S(1)}, bf16[64,32,128]{2,1,0:T(8,128)(2,1)S(1)}, u32[]{:S(2)}, u32[]{:S(2)}) collective-permute-start(bf16[64,32,128]{2,1,0:T(8,128)(2,1)S(1)} %get-tuple-element.38.refs_2_), channel_id=1, source_target_pairs={{0,4},{2,6},{4,0},{6,2},{8,12},{10,14},{12,8},{14,10},{16,20},{18,... | collective-permute-start | bytes 1572872 | tf_op jit(solution)/shard_map/ppermute | solution.py:259
  7.6 14.8 %collective-permute-start.3 = (bf16[64,32,128]{2,1,0:T(8,128)(2,1)S(1)}, bf16[64,32,128]{2,1,0:T(8,128)(2,1)S(1)}, u32[]{:S(2)}, u32[]{:S(2)}) collective-permute-start(bf16[64,32,128]{2,1,0:T(8,128)(2,1)S(1)} %get-tuple-element.48), channel_id=1, source_target_pairs={{0,1},{1,0},{2,3},{3,2},{4,5},{5,4},{6,7},{7,6},{8,9},{9,8},{10,11... | collective-permute-start | bytes 1572872 | tf_op jit(solution)/shard_map/ppermute | solution.py:256
  9.2 20.2 %collective-permute-start.1 = (bf16[64,32,128]{2,1,0:T(8,128)(2,1)S(1)}, bf16[64,32,128]{2,1,0:T(8,128)(2,1)S(1)}, u32[]{:S(2)}, u32[]{:S(2)}) collective-permute-start(bf16[64,32,128]{2,1,0:T(8,128)(2,1)S(1)} %collective-permute-done.refs_3_), channel_id=1, source_target_pairs={{0,4},{2,6},{4,0},{6,2},{8,12},{10,14},{12,8},{14,10},{16,20},{18,... | collective-permute-start | bytes 1572872 | tf_op jit(solution)/shard_map/ppermute | solution.py:259
  9.7 23.7 %collective-permute-start.9 = (bf16[64,32,128]{2,1,0:T(8,128)(2,1)S(1)}, bf16[64,32,128]{2,1,0:T(8,128)(2,1)S(1)}, u32[]{:S(2)}, u32[]{:S(2)}) collective-permute-start(bf16[64,32,128]{2,1,0:T(8,128)(2,1)S(1)} %get-tuple-element.53), channel_id=1, source_target_pairs={{0,3},{1,2},{2,1},{3,0},{4,7},{5,6},{6,5},{7,4},{8,11},{9,10},{10,... | collective-permute-start | bytes 1572872 | tf_op jit(solution)/shard_map/ppermute | solution.py:270
  18.2 17.6 %collective-permute-start.7 = (bf16[64,32,128]{2,1,0:T(8,128)(2,1)S(1)}, bf16[64,32,128]{2,1,0:T(8,128)(2,1)S(1)}, u32[]{:S(2)}, u32[]{:S(2)}) collective-permute-start(bf16[64,32,128]{2,1,0:T(8,128)(2,1)S(1)} %collective-permute-done.6.refs_4_), channel_id=1, source_target_pairs={{0,8},{2,10},{8,16},{10,18},{12,4},{14,6},{16,24},{18,26},{20,12},... | collective-permute-start | bytes 1572872 | tf_op jit(solution)/shard_map/ppermute | solution.py:263
  22.5 18.2 %collective-permute-start.4 = (bf16[64,32,128]{2,1,0:T(8,128)(2,1)S(1)}, bf16[64,32,128]{2,1,0:T(8,128)(2,1)S(1)}, u32[]{:S(2)}, u32[]{:S(2)}) collective-permute-start(bf16[64,32,128]{2,1,0:T(8,128)(2,1)S(1)} %collective-permute-done.3.refs_2_), channel_id=1, source_target_pairs={{0,4},{2,6},{4,0},{6,2},{8,12},{10,14},{12,8},{14,10},{16,20},{18,... | collective-permute-start | bytes 1572872 | tf_op jit(solution)/shard_map/ppermute | solution.py:259
  29.4 15.2 %collective-permute-start.11 = (bf16[64,32,128]{2,1,0:T(8,128)(2,1)S(1)}, bf16[64,32,128]{2,1,0:T(8,128)(2,1)S(1)}, u32[]{:S(2)}, u32[]{:S(2)}) collective-permute-start(bf16[64,32,128]{2,1,0:T(8,128)(2,1)S(1)} %collective-permute-done.1.refs_5_), channel_id=1, source_target_pairs={{0,8},{2,10},{8,16},{10,18},{12,4},{14,6},{16,24},{18,26},{20,12},... | collective-permute-start | bytes 1572872 | tf_op jit(solution)/shard_map/ppermute | solution.py:263
  33.4 18.3 %collective-permute-start.10 = (bf16[64,32,128]{2,1,0:T(8,128)(2,1)S(1)}, bf16[64,32,128]{2,1,0:T(8,128)(2,1)S(1)}, u32[]{:S(2)}, u32[]{:S(2)}) collective-permute-start(bf16[64,32,128]{2,1,0:T(8,128)(2,1)S(1)} %collective-permute-done.9.refs_3_), channel_id=1, source_target_pairs={{0,4},{2,6},{4,0},{6,2},{8,12},{10,14},{12,8},{14,10},{16,20},{18,... | collective-permute-start | bytes 1572872 | tf_op jit(solution)/shard_map/ppermute | solution.py:259
  35.7 19.7 %collective-permute-start.13 = (bf16[64,32,128]{2,1,0:T(8,128)(2,1)S(1)}, bf16[64,32,128]{2,1,0:T(8,128)(2,1)S(1)}, u32[]{:S(2)}, u32[]{:S(2)}) collective-permute-start(bf16[64,32,128]{2,1,0:T(8,128)(2,1)S(1)} %get-tuple-element.57), channel_id=1, source_target_pairs={{0,2},{2,0},{4,6},{6,4},{8,10},{10,8},{12,14},{14,12},{16,18},{18,... | collective-permute-start | bytes 1572872 | tf_op jit(solution)/shard_map/ppermute | solution.py:266
  35.8 19.6 %collective-permute-start.2 = (bf16[64,32,128]{2,1,0:T(8,128)(2,1)S(1)}, bf16[64,32,128]{2,1,0:T(8,128)(2,1)S(1)}, u32[]{:S(2)}, u32[]{:S(2)}) collective-permute-start(bf16[64,32,128]{2,1,0:T(8,128)(2,1)S(1)} %get-tuple-element.46), channel_id=1, source_target_pairs={{0,1},{1,0},{2,3},{3,2},{4,5},{5,4},{6,7},{7,6},{8,9},{9,8},{10,11... | collective-permute-start | bytes 1572872 | tf_op jit(solution)/shard_map/ppermute | solution.py:256
  40.6 16.7 %collective-permute-start.8 = (bf16[64,32,128]{2,1,0:T(8,128)(2,1)S(1)}, bf16[64,32,128]{2,1,0:T(8,128)(2,1)S(1)}, u32[]{:S(2)}, u32[]{:S(2)}) collective-permute-start(bf16[64,32,128]{2,1,0:T(8,128)(2,1)S(1)} %collective-permute-done.4.refs_4_), channel_id=1, source_target_pairs={{0,8},{2,10},{8,16},{10,18},{12,4},{14,6},{16,24},{18,26},{20,12},... | collective-permute-start | bytes 1572872 | tf_op jit(solution)/shard_map/ppermute | solution.py:263
  44.6 16.3 %collective-permute-start.5 = (bf16[64,32,128]{2,1,0:T(8,128)(2,1)S(1)}, bf16[64,32,128]{2,1,0:T(8,128)(2,1)S(1)}, u32[]{:S(2)}, u32[]{:S(2)}) collective-permute-start(bf16[64,32,128]{2,1,0:T(8,128)(2,1)S(1)} %get-tuple-element.49), channel_id=1, source_target_pairs={{0,3},{1,2},{2,1},{3,0},{4,7},{5,6},{6,5},{7,4},{8,11},{9,10},{10,... | collective-permute-start | bytes 1572872 | tf_op jit(solution)/shard_map/ppermute | solution.py:270
  51.6 14.7 %collective-permute-start.12 = (bf16[64,32,128]{2,1,0:T(8,128)(2,1)S(1)}, bf16[64,32,128]{2,1,0:T(8,128)(2,1)S(1)}, u32[]{:S(2)}, u32[]{:S(2)}) collective-permute-start(bf16[64,32,128]{2,1,0:T(8,128)(2,1)S(1)} %collective-permute-done.10.refs_5_), channel_id=1, source_target_pairs={{0,8},{2,10},{8,16},{10,18},{12,4},{14,6},{16,24},{18,26},{20,12},... | collective-permute-start | bytes 1572872 | tf_op jit(solution)/shard_map/ppermute | solution.py:263
  63.5 4.7 %collective-permute-start.15 = (f32[2048,128]{1,0:T(8,128)}, f32[2048,128]{1,0:T(8,128)}, u32[]{:S(2)}, u32[]{:S(2)}) collective-permute-start(f32[2048,128]{1,0:T(8,128)} %get-tuple-element.67), channel_id=1, source_target_pairs={{0,2},{2,0},{4,6},{6,4},{8,10},{10,8},{12,14},{14,12},{16,18},{18,... | collective-permute-start | bytes 3145736 | tf_op jit(solution)/shard_map/ppermute | solution.py:266
  68.1 3.1 %collective-permute-start.14 = (f32[2048,128]{1,0:T(8,128)}, f32[2048,128]{1,0:T(8,128)S(1)}, u32[]{:S(2)}, u32[]{:S(2)}) collective-permute-start(f32[2048,128]{1,0:T(8,128)} %get-tuple-element.62), channel_id=1, source_target_pairs={{0,2},{2,0},{4,6},{6,4},{8,10},{10,8},{12,14},{14,12},{16,18},{18,... | collective-permute-start | bytes 3145736 | tf_op jit(solution)/shard_map/ppermute | solution.py:266
